TPU v7x, 32 devices: a whole 2x2x4 slice. The times are simulated.
32 devices in a mesh: grp: 4 (over x, core), tok: 8 (over z, y).
Axes of the slice: x: 2, y: 2, z: 4, core: 2. Of those that a mesh axis runs over, the one named last changes fastest.
Arguments:
- kept_tokens: float32 [32, 768, 1152], P('grp', 'tok'), may hold values from -6 to 6
- kept_index: int32 [32, 768], P(('grp', 'tok')), may hold values from 0 to 1023, as said below
- kept_count: int32 [32], P(('grp', 'tok')), may hold values from 256 to 768, as said below
- condition: float32 [32, 1152], P(('grp', 'tok')), may hold values from -6 to 6
- mask_token: float32 [1152], P('tok'), may hold values from -6 to 6
- position_table: float32 [1024, 1152], P('tok'), may hold values from -3 to 3
- modulation_weight: float32 [1152, 6912], P(None, 'tok'), may hold values from -0.1875 to 0.1875
- modulation_bias: float32 [6912], P('tok'), may hold values from -3 to 3
- input_weight: float32 [1152, 3456], P('tok'), may hold values from -0.1875 to 0.1875
- query_bias: float32 [1152], P('tok'), may hold values from -2 to 2
- value_bias: float32 [1152], P('tok'), may hold values from -2 to 2
- output_weight: float32 [1152, 1152], P('tok'), may hold values from -3 to 3
- output_bias: float32 [1152], P('tok'), may hold values from -2 to 2
- up_weight: float32 [1152, 4608], P('tok'), may hold values from -0.1875 to 0.1875
- up_bias: float32 [4608], P('tok'), may hold values from -2 to 2
- down_weight: float32 [4608, 1152], P('tok'), may hold values from -0.09375 to 0.09375
- down_bias: float32 [1152], P('tok'), may hold values from -2 to 2
- cotangent: float32 [32, 1024, 1152], P(('grp', 'tok')), may hold values from -6 to 6
Outputs:
- block_output: float32 [32, 1024, 1152], P(('grp', 'tok'))
- kept_grad: float32 [32, 768, 1152], P('grp', 'tok')
- condition_grad: float32 [32, 1152], P(('grp', 'tok'))
- mask_grad: float32 [1152], P('tok')
- position_grad: float32 [1024, 1152], P('tok')
- modulation_weight_grad: float32 [1152, 6912], P(None, 'tok')
- modulation_bias_grad: float32 [6912], P('tok')
- input_weight_grad: float32 [1152, 3456], P('tok')
- query_bias_grad: float32 [1152], P('tok')
- value_bias_grad: float32 [1152], P('tok')
- output_weight_grad: float32 [1152, 1152], P('tok')
- output_bias_grad: float32 [1152], P('tok')
- up_weight_grad: float32 [1152, 4608], P('tok')
- up_bias_grad: float32 [4608], P('tok')
- down_weight_grad: float32 [4608, 1152], P('tok')
- down_bias_grad: float32 [1152], P('tok')
Inputs may be any that keep to these rules, and one draw needn't show every extreme that they name: `kept_index`: each image's row holds 768 distinct positions; its first kept_count entries are the positions that the image keeps. `kept_count`: in every group of 8 consecutive images, one image keeps 768 positions and another keeps a quarter of 1024.
All inputs are finite; a program needn't handle non-finite values.
Results may differ from a plain program's by a relative error of at most 0.019.
The roundings to bfloat16 on the way count: a program that leaves them out, or rounds other values in their place, can miss the bound.
Values may be sent and summed in bfloat16 or wider, within the bound.
No kernel may reach another device: no remote copies, remote signals or barrier semaphores. Data moves between devices by JAX's collectives and lax.ppermute only.
A program may use at most 384 MiB of HBM per device.

v0:
```python
import math

import jax
import jax.numpy as jnp
from jax import lax
from jax.sharding import PartitionSpec as P

H = 16
HD = 72


epsilon = 1e-06
block_limit = 512


def layer_norm(values):
    center = values - jnp.mean(values, axis=-1, keepdims=True)
    spread = jnp.mean(center * center, axis=-1, keepdims=True)
    return center * lax.rsqrt(spread + epsilon)


def modulate(values, scale_part, shift_part):
    return layer_norm(values) * (1.0 + scale_part) + shift_part


def gelu_tanh(values):
    return jax.nn.gelu(values, approximate=True)


def attend_image(query_rows, key_rows, value_rows, factor):
    seq_len, head_count, head_width = query_rows.shape
    block_size = min(block_limit, seq_len)
    query_blocks = query_rows.reshape(seq_len // block_size, block_size, head_count, head_width)

    def one_block(query_block):
        scores = (
            jnp.einsum("qhd,khd->hqk", query_block, key_rows, preferred_element_type=jnp.float32)
            * factor
        )
        row_max = jnp.max(scores, axis=-1, keepdims=True)
        weights = jnp.exp(scores - row_max)
        row_total = jnp.sum(weights, axis=-1, keepdims=True)
        probabilities = (weights / row_total).astype(jnp.bfloat16)
        mixture = jnp.einsum(
            "hqk,khd->qhd", probabilities, value_rows, preferred_element_type=jnp.float32
        )
        return (mixture.astype(jnp.bfloat16), (row_max + jnp.log(row_total))[..., 0])

    mixture, log_totals = lax.map(one_block, query_blocks)
    return (mixture.reshape(query_rows.shape), log_totals)


def attend_back(query_rows, key_rows, value_rows, log_totals, grad_rows, factor):
    seq_len, head_count, head_width = query_rows.shape
    block_size = min(block_limit, seq_len)
    query_blocks = query_rows.reshape(seq_len // block_size, block_size, head_count, head_width)
    grad_blocks = grad_rows.reshape(seq_len // block_size, block_size, head_count, head_width)

    def back_block(running, inputs):
        key_grad, value_grad = running
        query_block, grad_block, log_block = inputs
        scores = (
            jnp.einsum("qhd,khd->hqk", query_block, key_rows, preferred_element_type=jnp.float32)
            * factor
        )
        probabilities = jnp.exp(scores - log_block[..., None])
        value_grad = value_grad + jnp.einsum(
            "hqk,qhd->khd",
            probabilities.astype(jnp.bfloat16),
            grad_block,
            preferred_element_type=jnp.float32,
        )
        prob_grad = jnp.einsum(
            "qhd,khd->hqk", grad_block, value_rows, preferred_element_type=jnp.float32
        )
        inner = jnp.sum(probabilities * prob_grad, axis=-1, keepdims=True)
        score_grad = (probabilities * (prob_grad - inner)).astype(jnp.bfloat16)
        query_grad = (
            jnp.einsum("hqk,khd->qhd", score_grad, key_rows, preferred_element_type=jnp.float32)
            * factor
        )
        key_grad = (
            key_grad
            + jnp.einsum(
                "hqk,qhd->khd", score_grad, query_block, preferred_element_type=jnp.float32
            )
            * factor
        )
        return ((key_grad, value_grad), query_grad.astype(jnp.bfloat16))

    empty_grad = jnp.zeros((seq_len, head_count, head_width), jnp.float32)
    (key_grad, value_grad), query_grad = lax.scan(
        back_block, (empty_grad, empty_grad), (query_blocks, grad_blocks, log_totals)
    )
    return (
        query_grad.reshape(query_rows.shape),
        key_grad.astype(jnp.bfloat16),
        value_grad.astype(jnp.bfloat16),
    )


def on_device(
    kept_tokens,
    kept_index,
    kept_count,
    condition,
    mask_token,
    position_table,
    modulation_weight,
    modulation_bias,
    input_weight,
    query_bias,
    value_bias,
    output_weight,
    output_bias,
    up_weight,
    up_bias,
    down_weight,
    down_bias,
    cotangent,
):
    images_here, seq_len, model_width = cotangent.shape
    slot_count = kept_index.shape[1]
    factor = 1.0 / math.sqrt(HD)
    (
        input_full,
        output_full,
        up_full,
        down_full,
        position_full,
        query_bias_full,
        value_bias_full,
        output_bias_full,
        up_bias_full,
        down_bias_full,
        mask_full,
    ) = (
        lax.all_gather(input_weight.astype(jnp.bfloat16), "tok", axis=0, tiled=True),
        lax.all_gather(output_weight.astype(jnp.bfloat16), "tok", axis=0, tiled=True),
        lax.all_gather(up_weight.astype(jnp.bfloat16), "tok", axis=0, tiled=True),
        lax.all_gather(down_weight.astype(jnp.bfloat16), "tok", axis=0, tiled=True),
        lax.all_gather(position_table.astype(jnp.bfloat16), "tok", axis=0, tiled=True),
        lax.all_gather(query_bias.astype(jnp.bfloat16), "tok", axis=0, tiled=True),
        lax.all_gather(value_bias.astype(jnp.bfloat16), "tok", axis=0, tiled=True),
        lax.all_gather(output_bias.astype(jnp.bfloat16), "tok", axis=0, tiled=True),
        lax.all_gather(up_bias.astype(jnp.bfloat16), "tok", axis=0, tiled=True),
        lax.all_gather(down_bias.astype(jnp.bfloat16), "tok", axis=0, tiled=True),
        lax.all_gather(mask_token.astype(jnp.bfloat16), "tok", axis=0, tiled=True),
    )
    condition_low = jax.nn.silu(condition).astype(jnp.bfloat16)
    modulation_full, modulation_bias_full = (
        lax.all_gather(modulation_weight.astype(jnp.bfloat16), "tok", axis=1, tiled=True),
        lax.all_gather(modulation_bias.astype(jnp.bfloat16), "tok", axis=0, tiled=True),
    )
    modulation = jnp.dot(
        condition_low, modulation_full, preferred_element_type=jnp.float32
    ) + modulation_bias_full.astype(jnp.float32)
    shift_one, scale_one, gate_one, shift_two, scale_two, gate_two = (
        modulation[:, None, number * model_width : (number + 1) * model_width]
        for number in range(6)
    )
    routed = lax.all_to_all(
        kept_tokens.astype(jnp.bfloat16), "tok", split_axis=0, concat_axis=1, tiled=True
    )
    live_mask = jnp.arange(slot_count)[None, :] < kept_count[:, None]

    def place_rows(index_row, live_row, routed_rows):
        values = jnp.where(live_row[:, None], routed_rows.astype(jnp.float32), 0.0)
        filled = jnp.zeros((seq_len, model_width), jnp.float32).at[index_row].set(values)
        marker = jnp.zeros((seq_len,), jnp.float32).at[index_row].set(live_row.astype(jnp.float32))
        return (filled, marker)

    filled, marker = jax.vmap(place_rows)(kept_index, live_mask, routed)
    empty_rows = (1.0 - marker)[..., None]
    start_rows = (
        filled
        + empty_rows * mask_full.astype(jnp.float32)
        + position_full.astype(jnp.float32)[None]
    )
    normed_one = modulate(start_rows, scale_one, shift_one).astype(jnp.bfloat16)
    projected_bias = jnp.concatenate(
        [
            query_bias_full.astype(jnp.float32),
            jnp.zeros((model_width,), jnp.float32),
            value_bias_full.astype(jnp.float32),
        ]
    )
    projected = (
        jnp.einsum("isd,de->ise", normed_one, input_full, preferred_element_type=jnp.float32)
        + projected_bias
    )
    head_shape = (images_here, seq_len, H, HD)
    queries = projected[..., :model_width].astype(jnp.bfloat16).reshape(head_shape)
    keys_all = (
        projected[..., model_width : 2 * model_width].astype(jnp.bfloat16).reshape(head_shape)
    )
    values_all = projected[..., 2 * model_width :].astype(jnp.bfloat16).reshape(head_shape)

    def attend_item(triple):
        return attend_image(triple[0], triple[1], triple[2], factor)

    mixture, log_totals = lax.map(attend_item, (queries, keys_all, values_all))
    mixture = mixture.reshape(images_here, seq_len, model_width)
    branch_one = jnp.einsum(
        "isd,de->ise", mixture, output_full, preferred_element_type=jnp.float32
    ) + output_bias_full.astype(jnp.float32)
    middle = start_rows + gate_one * branch_one
    normed_two = modulate(middle, scale_two, shift_two).astype(jnp.bfloat16)
    hidden_pre = jnp.einsum(
        "isd,df->isf", normed_two, up_full, preferred_element_type=jnp.float32
    ) + up_bias_full.astype(jnp.float32)
    hidden = gelu_tanh(hidden_pre).astype(jnp.bfloat16)
    branch_two = jnp.einsum(
        "isf,fd->isd", hidden, down_full, preferred_element_type=jnp.float32
    ) + down_bias_full.astype(jnp.float32)
    block_output = middle + gate_two * branch_two
    grad_two = (gate_two * cotangent).astype(jnp.bfloat16)
    gate_two_grad = jnp.sum(cotangent * branch_two, axis=1)
    down_bias_term = jnp.sum(grad_two.astype(jnp.float32), axis=(0, 1))
    hidden_grad = jnp.einsum("isd,fd->isf", grad_two, down_full, preferred_element_type=jnp.float32)
    _, gelu_back = jax.vjp(gelu_tanh, hidden_pre)
    pre_grad = gelu_back(hidden_grad)[0].astype(jnp.bfloat16)
    up_bias_term = jnp.sum(pre_grad.astype(jnp.float32), axis=(0, 1))
    normed_two_grad = jnp.einsum(
        "isf,df->isd", pre_grad, up_full, preferred_element_type=jnp.float32
    )
    _, norm_two_back = jax.vjp(modulate, middle, scale_two, shift_two)
    middle_part, scale_two_grad, shift_two_grad = norm_two_back(normed_two_grad)
    middle_grad = cotangent + middle_part
    grad_one = (gate_one * middle_grad).astype(jnp.bfloat16)
    gate_one_grad = jnp.sum(middle_grad * branch_one, axis=1)
    output_bias_term = jnp.sum(grad_one.astype(jnp.float32), axis=(0, 1))
    mixture_grad = (
        jnp.einsum("ise,de->isd", grad_one, output_full, preferred_element_type=jnp.float32)
        .astype(jnp.bfloat16)
        .reshape(head_shape)
    )

    def back_item(group_rows):
        return attend_back(
            group_rows[0], group_rows[1], group_rows[2], group_rows[3], group_rows[4], factor
        )

    queries_grad, keys_grad, values_grad = lax.map(
        back_item, (queries, keys_all, values_all, log_totals, mixture_grad)
    )
    flat_shape = (images_here, seq_len, model_width)
    projected_grad = jnp.concatenate(
        [
            queries_grad.reshape(flat_shape),
            keys_grad.reshape(flat_shape),
            values_grad.reshape(flat_shape),
        ],
        axis=-1,
    )
    query_bias_term = jnp.sum(queries_grad.reshape(flat_shape).astype(jnp.float32), axis=(0, 1))
    value_bias_term = jnp.sum(values_grad.reshape(flat_shape).astype(jnp.float32), axis=(0, 1))
    normed_one_grad = jnp.einsum(
        "ise,de->isd", projected_grad, input_full, preferred_element_type=jnp.float32
    )
    _, norm_one_back = jax.vjp(modulate, start_rows, scale_one, shift_one)
    start_part, scale_one_grad, shift_one_grad = norm_one_back(normed_one_grad)
    start_grad = middle_grad + start_part
    modulation_grad = jnp.concatenate(
        [
            shift_one_grad[:, 0],
            scale_one_grad[:, 0],
            gate_one_grad,
            shift_two_grad[:, 0],
            scale_two_grad[:, 0],
            gate_two_grad,
        ],
        axis=1,
    ).astype(jnp.bfloat16)
    position_term = jnp.sum(start_grad, axis=0)
    mask_term = jnp.sum(start_grad * empty_rows, axis=(0, 1))

    def pick_rows(grad_rows, index_row, live_row):
        return jnp.where(live_row[:, None], grad_rows[index_row], 0.0)

    slot_grad = jax.vmap(pick_rows)(start_grad, kept_index, live_mask)
    kept_grad = lax.all_to_all(
        slot_grad.astype(jnp.bfloat16), "tok", split_axis=1, concat_axis=0, tiled=True
    ).astype(slot_grad.dtype)
    modulation_term = jnp.einsum(
        "id,ie->de", condition_low, modulation_grad, preferred_element_type=jnp.float32
    )
    modulation_bias_term = jnp.sum(modulation_grad.astype(jnp.float32), axis=0)
    condition_low_grad = jnp.einsum(
        "ie,de->id", modulation_grad, modulation_full, preferred_element_type=jnp.float32
    )
    modulation_shard, modulation_bias_shard = (
        lax.psum_scatter(
            modulation_term.astype(jnp.bfloat16), "tok", scatter_dimension=1, tiled=True
        ).astype(jnp.float32),
        lax.psum_scatter(
            modulation_bias_term.astype(jnp.bfloat16), "tok", scatter_dimension=0, tiled=True
        ).astype(jnp.float32),
    )
    _, silu_back = jax.vjp(jax.nn.silu, condition)
    condition_grad = silu_back(condition_low_grad)[0]
    input_term = jnp.einsum(
        "isd,ise->de", normed_one, projected_grad, preferred_element_type=jnp.float32
    )
    output_term = jnp.einsum("isd,ise->de", mixture, grad_one, preferred_element_type=jnp.float32)
    up_term = jnp.einsum("isd,isf->df", normed_two, pre_grad, preferred_element_type=jnp.float32)
    down_term = jnp.einsum("isf,isd->fd", hidden, grad_two, preferred_element_type=jnp.float32)
    (
        input_shard,
        output_shard,
        up_shard,
        down_shard,
        position_shard,
        query_bias_shard,
        value_bias_shard,
        output_bias_shard,
        up_bias_shard,
        down_bias_shard,
        mask_shard,
    ) = (
        lax.psum_scatter(
            input_term.astype(jnp.bfloat16), "tok", scatter_dimension=0, tiled=True
        ).astype(jnp.float32),
        lax.psum_scatter(
            output_term.astype(jnp.bfloat16), "tok", scatter_dimension=0, tiled=True
        ).astype(jnp.float32),
        lax.psum_scatter(
            up_term.astype(jnp.bfloat16), "tok", scatter_dimension=0, tiled=True
        ).astype(jnp.float32),
        lax.psum_scatter(
            down_term.astype(jnp.bfloat16), "tok", scatter_dimension=0, tiled=True
        ).astype(jnp.float32),
        lax.psum_scatter(
            position_term.astype(jnp.bfloat16), "tok", scatter_dimension=0, tiled=True
        ).astype(jnp.float32),
        lax.psum_scatter(
            query_bias_term.astype(jnp.bfloat16), "tok", scatter_dimension=0, tiled=True
        ).astype(jnp.float32),
        lax.psum_scatter(
            value_bias_term.astype(jnp.bfloat16), "tok", scatter_dimension=0, tiled=True
        ).astype(jnp.float32),
        lax.psum_scatter(
            output_bias_term.astype(jnp.bfloat16), "tok", scatter_dimension=0, tiled=True
        ).astype(jnp.float32),
        lax.psum_scatter(
            up_bias_term.astype(jnp.bfloat16), "tok", scatter_dimension=0, tiled=True
        ).astype(jnp.float32),
        lax.psum_scatter(
            down_bias_term.astype(jnp.bfloat16), "tok", scatter_dimension=0, tiled=True
        ).astype(jnp.float32),
        lax.psum_scatter(
            mask_term.astype(jnp.bfloat16), "tok", scatter_dimension=0, tiled=True
        ).astype(jnp.float32),
    )
    (
        input_total,
        output_total,
        up_total,
        down_total,
        position_total,
        query_bias_total,
        value_bias_total,
        output_bias_total,
        up_bias_total,
        down_bias_total,
        mask_total,
        modulation_total,
        modulation_bias_total,
    ) = (
        lax.psum(input_shard.astype(jnp.bfloat16), "grp").astype(jnp.float32),
        lax.psum(output_shard.astype(jnp.bfloat16), "grp").astype(jnp.float32),
        lax.psum(up_shard.astype(jnp.bfloat16), "grp").astype(jnp.float32),
        lax.psum(down_shard.astype(jnp.bfloat16), "grp").astype(jnp.float32),
        lax.psum(position_shard.astype(jnp.bfloat16), "grp").astype(jnp.float32),
        lax.psum(query_bias_shard.astype(jnp.bfloat16), "grp").astype(jnp.float32),
        lax.psum(value_bias_shard.astype(jnp.bfloat16), "grp").astype(jnp.float32),
        lax.psum(output_bias_shard.astype(jnp.bfloat16), "grp").astype(jnp.float32),
        lax.psum(up_bias_shard.astype(jnp.bfloat16), "grp").astype(jnp.float32),
        lax.psum(down_bias_shard.astype(jnp.bfloat16), "grp").astype(jnp.float32),
        lax.psum(mask_shard.astype(jnp.bfloat16), "grp").astype(jnp.float32),
        lax.psum(modulation_shard.astype(jnp.bfloat16), "grp").astype(jnp.float32),
        lax.psum(modulation_bias_shard.astype(jnp.bfloat16), "grp").astype(jnp.float32),
    )
    return (
        block_output,
        kept_grad,
        condition_grad,
        mask_total,
        position_total,
        modulation_total,
        modulation_bias_total,
        input_total,
        query_bias_total,
        value_bias_total,
        output_total,
        output_bias_total,
        up_total,
        up_bias_total,
        down_total,
        down_bias_total,
    )


def solution(mesh):
    return jax.shard_map(
        on_device,
        mesh=mesh,
        in_specs=(
            P("grp", "tok", None),
            P(("grp", "tok"), None),
            P(("grp", "tok")),
            P(("grp", "tok"), None),
            P("tok"),
            P("tok", None),
            P(None, "tok"),
            P("tok"),
            P("tok", None),
            P("tok"),
            P("tok"),
            P("tok", None),
            P("tok"),
            P("tok", None),
            P("tok"),
            P("tok", None),
            P("tok"),
            P(("grp", "tok"), None, None),
        ),
        out_specs=(
            P(("grp", "tok"), None, None),
            P("grp", "tok", None),
            P(("grp", "tok"), None),
            P("tok"),
            P("tok", None),
            P(None, "tok"),
            P("tok"),
            P("tok", None),
            P("tok"),
            P("tok"),
            P("tok", None),
            P("tok"),
            P("tok", None),
            P("tok"),
            P("tok", None),
            P("tok"),
        ),
        check_vma=False,
    )
```

profile of v0, /device:TPU:0, one launch (start us, length us, event | category | flops | bytes accessed | tf_op | source)
XLA Modules:
  0.0 2226.7 jit_solution(13797572448008390052)
XLA Ops:
  37.6 79.5 %all-reduce.15 = (bf16[1152]{0:T(1024)(128)(2,1)S(1)}, bf16[1152]{0:T(1024)(128)(2,1)S(1)}, bf16[1152]{0:T(1024)(128)(2,1)S(1)}, bf16[6912]{0:T(1024)(128)(2,1)S...) all-reduce(bf16[1152]{0:T(1024)(128)(2,1)S(1)} %dynamic-update-slic, ...), channel_id=1, replica_groups=mesh['grp'=4,'tok'=8] {'tok'}, use_global_device_ids=true, to_apply=%add | all-reduce | flops 17280 | bytes 69120
  139.4 172.4 %all-gather.9.cloned.1.call-done = bf16[1152,6912]{0,1:T(8,128)(2,1)} async-done(((bf16[1152,864]{0,1:T(8,128)(2,1)}), bf16[1152,6912]{0,1:T(8,128)(2,1)}) %all-gather.9.cloned.1.call-update) | async-done | bytes 15925264 | tf_op jit(solution)/shard_map/all_gather | solution.py:152
  322.3 110.1 %all-gather.11.cloned.1.call-done = bf16[1152,3456]{1,0:T(8,128)(2,1)} async-done(((bf16[144,3456]{1,0:T(8,128)(2,1)}), bf16[1152,3456]{1,0:T(8,128)(2,1)}) %all-gather.11.cloned.1.call-update) | async-done | bytes 7962640 | tf_op jit(solution)/shard_map/all_gather | solution.py:138
  473.2 95.2 %while.47 = (s32[]{:T(128)}, bf16[2,512,16,72]{1,3,2,0:T(8,128)(2,1)S(1)}, f32[2,16,512]{2,1,0:T(8,128)S(1)}, bf16[2,512,16,72]{1,3,2,0:T(8,128)(2,1)}, bf16[102...) while((s32[]{:T(128)}, bf16[2,512,16,72]{1,3,2,0:T(8,128)(2,1)S(1)}, ...), condition=%wide.region_7.8_spmd, body=%wide.region_4.7_spmd.sunk | while | flops 2491998208 | bytes 108003424 | solution.py:49
  473.6 17.7 multiply_reduce_fusion.7
  520.9 17.8 multiply_reduce_fusion.7
  538.8 15.1 fusion.136
  585.0 56.3 %all-gather.15.cloned.1.call-done = bf16[1152,4608]{1,0:T(8,128)(2,1)} async-done(((bf16[144,4608]{1,0:T(8,128)(2,1)}), bf16[1152,4608]{1,0:T(8,128)(2,1)}) %all-gather.15.cloned.1.call-update) | async-done | bytes 10616848 | tf_op jit(solution)/shard_map/all_gather | solution.py:140
  641.3 20.7 fusion.83
  662.0 132.0 %all-gather.17.cloned.1.call-done = bf16[4608,1152]{1,0:T(8,128)(2,1)} async-done(((bf16[576,1152]{1,0:T(8,128)(2,1)}), bf16[4608,1152]{1,0:T(8,128)(2,1)}) %all-gather.17.cloned.1.call-update) | async-done | bytes 10616848 | tf_op jit(solution)/shard_map/all_gather | solution.py:141
  794.0 29.1 %fusion.96 = (bf16[4608]{0:T(1024)(128)(2,1)}, bf16[1024,4608]{1,0:T(8,128)(2,1)}) fusion(f32[1024,4608]{1,0:T(8,128)} %fusion.83, f32[4608]{0:T(1024)S(1)} %copy-done.32, bf16[4608,1152]{1,0:T(8,128)(2,1)} %all-gather.17.cloned.1.call-done, bf16[1,1024,1152]{2,1,0:T(8,128)(2,1)S(1)} %get-tuple-element.297), kind=kOutput, calls=%fused_computation.164 | convolution fusion | flops 10975440896 | bytes 41315328 | tf_op jit(solution)/shard_map/isd,fd->isf/dot_general | solution.py:220
  823.1 21.1 fusion.43
  844.3 28.4 %fusion.42 = (bf16[1152]{0:T(1024)(128)(2,1)}, f32[1,1024,1152]{2,1,0:T(8,128)}, f32[1024]{0:T(1024)S(1)}, f32[1,1024,1152]{2,1,0:T(8,128)}) fusion(f32[1,1024,1152]{2,1,0:T(8,128)} %param.39, f32[1,1024,1152]{2,1,0:T(8,128)} %copy-done.5, f32[1152]{0:T(1024)S(1)} %copy-done.31, f32[1024]{0:T(1024)S(1)} %multiply_multiply_fusion.3, ...), kind=kOutput, calls=%fused_computation.68 | convolution fusion | flops 10932975616 | bytes 53135104 | tf_op jit(solution)/shard_map/isf,fd->isd/dot_general | solution.py:213
  902.4 213.4 %while.48 = (s32[]{:T(128)}, f32[1024,16,72]{0,2,1:T(8,128)}, f32[1024,16,72]{0,2,1:T(8,128)}, bf16[2,512,16,72]{1,3,2,0:T(8,128)(2,1)}, bf16[2,512,16,72]{1,3,2...) while((s32[]{:T(128)}, f32[1024,16,72]{0,2,1:T(8,128)}, ...), condition=%wide.region_14.15_spmd.clone, body=%wide.region_12.14_spmd.clone.sunk | while | flops 6147530752 | bytes 350847136 | solution.py:92
  902.6 17.7 fusion.147
  920.3 16.5 bitcast_add_fusion.9
  936.7 24.6 %multiply_reduce_fusion.8 = (f32[16,512]{1,0:T(8,128)S(1)}, f32[16,512,1024]{2,1,0:T(8,128)}) fusion(f32[16,512,1024]{2,1,0:T(8,128)} %fusion.147, f32[16,512]{1,0:T(8,128)S(1)} %dynamic-slice_bitcast_fusion.2, bf16[1024,16,72]{0,2,1:T(8,128)(2,1)} %get-tuple-element.481, bf16[2,512,16,72]{1,3,2,0:T(8,128)(2,1)} %get-tuple-element.480, s32[]{:T(128)S(6)} %copy.91), kind=kOutput, calls=%fused_computation.18.clone.1 | convolution fusion | flops 1241505792 | bytes 70713344 | tf_op jit(solution)/shard_map/while/body/eval_jaxpr/while/body/eval_jaxpr/qhd,khd->hqk/dot_general | solution.py:73
  961.4 27.9 %multiply_convert_fusion.11 = bf16[16,512,1024]{2,1,0:T(8,128)(2,1)} fusion(f32[16,512,1024]{2,1,0:T(8,128)} %get-tuple-element.428, f32[16,512,1024]{2,1,0:T(8,128)} %fusion.147, f32[16,512]{1,0:T(8,128)S(1)} %get-tuple-element.429, f32[16,512]{1,0:T(8,128)S(1)} %dynamic-slice_bitcast_fusion.2), kind=kLoop, calls=%fused_computation.17.clone.1 | loop fusion | flops 41943040 | bytes 83951616 | tf_op jit(solution)/shard_map/while/body/eval_jaxpr/while/body/eval_jaxpr/convert_element_type | solution.py:77
  1007.6 17.6 fusion.147
  1025.3 17.8 bitcast_add_fusion.9
  1043.1 24.6 %multiply_reduce_fusion.8 = (f32[16,512]{1,0:T(8,128)S(1)}, f32[16,512,1024]{2,1,0:T(8,128)}) fusion(f32[16,512,1024]{2,1,0:T(8,128)} %fusion.147, f32[16,512]{1,0:T(8,128)S(1)} %dynamic-slice_bitcast_fusion.2, bf16[1024,16,72]{0,2,1:T(8,128)(2,1)} %get-tuple-element.481, bf16[2,512,16,72]{1,3,2,0:T(8,128)(2,1)} %get-tuple-element.480, s32[]{:T(128)S(6)} %copy.91), kind=kOutput, calls=%fused_computation.18.clone.1 | convolution fusion | flops 1241505792 | bytes 70713344 | tf_op jit(solution)/shard_map/while/body/eval_jaxpr/while/body/eval_jaxpr/qhd,khd->hqk/dot_general | solution.py:73
  1067.8 27.9 %multiply_convert_fusion.11 = bf16[16,512,1024]{2,1,0:T(8,128)(2,1)} fusion(f32[16,512,1024]{2,1,0:T(8,128)} %get-tuple-element.428, f32[16,512,1024]{2,1,0:T(8,128)} %fusion.147, f32[16,512]{1,0:T(8,128)S(1)} %get-tuple-element.429, f32[16,512]{1,0:T(8,128)S(1)} %dynamic-slice_bitcast_fusion.2), kind=kLoop, calls=%fused_computation.17.clone.1 | loop fusion | flops 41943040 | bytes 83951616 | tf_op jit(solution)/shard_map/while/body/eval_jaxpr/while/body/eval_jaxpr/convert_element_type | solution.py:77
  1130.2 17.7 fusion.45
  1166.2 16.9 convolution_convert_fusion.2
  1183.8 18.2 convolution_convert_fusion.1
  1203.7 22.2 convolution_convert_fusion
  1249.4 51.8 %reduce-scatter.13.cloned.1.call-done = bf16[144,1152]{1,0:T(8,128)(2,1)} async-done(((bf16[1152,1152]{1,0:T(8,128)(2,1)}), bf16[144,1152]{1,0:T(8,128)(2,1)}) %reduce-scatter.13.cloned.1.call-update) | async-done | bytes 331792 | tf_op jit(solution)/shard_map/reduce_scatter | solution.py:324
  1301.2 145.6 %reduce-scatter.11.cloned.1.call-done = bf16[144,3456]{1,0:T(8,128)(2,1)} async-done(((bf16[1152,3456]{1,0:T(8,128)(2,1)}), bf16[144,3456]{1,0:T(8,128)(2,1)}) %reduce-scatter.11.cloned.1.call-update) | async-done | bytes 995344 | tf_op jit(solution)/shard_map/reduce_scatter | solution.py:321
  1446.8 183.0 %reduce-scatter.15.cloned.1.call-done = bf16[144,4608]{1,0:T(8,128)(2,1)} async-done(((bf16[1152,4608]{1,0:T(8,128)(2,1)}), bf16[144,4608]{1,0:T(8,128)(2,1)}) %reduce-scatter.15.cloned.1.call-update) | async-done | bytes 1327120 | tf_op jit(solution)/shard_map/reduce_scatter | solution.py:327
  1629.8 182.7 %reduce-scatter.17.cloned.1.call-done = bf16[576,1152]{1,0:T(8,128)(2,1)} async-done(((bf16[4608,1152]{1,0:T(8,128)(2,1)}), bf16[576,1152]{1,0:T(8,128)(2,1)}) %reduce-scatter.17.cloned.1.call-update) | async-done | bytes 1327120 | tf_op jit(solution)/shard_map/reduce_scatter | solution.py:330
  1812.4 272.6 %reduce-scatter.9.cloned.1.call-done = bf16[1152,864]{0,1:T(8,128)(2,1)} async-done(((bf16[1152,6912]{0,1:T(8,128)(2,1)}), bf16[1152,864]{0,1:T(8,128)(2,1)}) %reduce-scatter.9.cloned.1.call-update) | async-done | bytes 1990672 | tf_op jit(solution)/shard_map/reduce_scatter | solution.py:293
  2116.2 59.5 %all-reduce.14 = (bf16[1152]{0:T(1024)(128)(2,1)S(1)}, bf16[6912]{0:T(1024)(128)(2,1)S(1)}, bf16[1152]{0:T(1024)(128)(2,1)S(1)}, bf16[1152]{0:T(1024)(128)(2,1)S...) all-reduce(bf16[1152]{0:T(1024)(128)(2,1)S(1)} %multiply_reduce_fus, ...), channel_id=2, replica_groups=mesh['grp'=4,'tok'=8] {'tok'}, use_global_device_ids=true, to_apply=%region_24.25.clone | all-reduce | flops 17280 | bytes 69120
  (325 shorter events, 360.9 us)
Async XLA Ops:
  7.2 125.4 %all-gather.7.cloned.1.call-start = ((), (), s32[]{:S(2)}) async-start(), calls=%async_computation.8 | async-start | bytes 2654208 | tf_op jit(solution)/shard_map/all_gather | solution.py:142
  9.1 302.8 %all-gather.9.cloned.1.call-start = ((), (), s32[]{:S(2)}) async-start(), calls=%async_computation.9 | async-start | bytes 17915904 | tf_op jit(solution)/shard_map/all_gather | solution.py:152
  12.8 419.6 %all-gather.11.cloned.1.call-start = ((), (), s32[]{:S(2)}) async-start(), calls=%async_computation.10 | async-start | bytes 8957952 | tf_op jit(solution)/shard_map/all_gather | solution.py:138
  15.6 555.9 %all-gather.13.cloned.1.call-start = ((), (), s32[]{:S(2)}) async-start(), calls=%async_computation.11 | async-start | bytes 2985984 | tf_op jit(solution)/shard_map/all_gather | solution.py:139
  17.5 623.8 %all-gather.15.cloned.1.call-start = ((), (), s32[]{:S(2)}) async-start(), calls=%async_computation.12 | async-start | bytes 11943936 | tf_op jit(solution)/shard_map/all_gather | solution.py:140
  22.0 96.9 %copy-start.59 = (s32[1,768]{1,0:T(1,128)S(1)}, s32[1,768]{1,0:T(1,128)}, u32[]{:S(2)}) copy-start(s32[1,768]{1,0:T(1,128)} %param.23) | copy-start | bytes 9220
  22.0 101.0 %copy-start.17 = (f32[1,1152]{1,0:T(1,128)S(1)}, f32[1,1152]{1,0:T(1,128)}, u32[]{:S(2)}) copy-start(f32[1,1152]{1,0:T(1,128)} %param.25) | copy-start | bytes 13828
  22.0 101.7 %all-to-all-start = ((bf16[8,96,1152]{2,1,0:T(8,128)(2,1)}), bf16[8,96,1152]{2,1,0:T(8,128)(2,1)S(1)}, u32[]{:S(2)}, u32[]{:S(2)}) async-start(bf16[8,96,1152]{2,1,0:T(8,128)(2,1)} %convert_element_type.276), calls=%async_computation | async-start | bytes 3538944 | tf_op jit(solution)/shard_map/all_to_all | solution.py:162
  29.5 764.5 %all-gather.17.cloned.1.call-start = ((), (), s32[]{:S(2)}) async-start(), calls=%async_computation.13 | async-start | bytes 11943936 | tf_op jit(solution)/shard_map/all_gather | solution.py:141
  32.5 1216.9 %reduce-scatter.7.cloned.1.call-start = ((), (), s32[]{:S(2)}) async-start(), calls=%async_computation.14 | async-start | bytes 2654208 | tf_op jit(solution)/shard_map/reduce_scatter | solution.py:333
  123.7 188.1 %copy-start.19 = (f32[1,1152]{1,0:T(1,128)}, f32[1,1152]{1,0:T(1,128)S(1)}, u32[]{:S(2)}) copy-start(f32[1,1152]{1,0:T(1,128)S(1)} %get-tuple-element.293) | copy-start | bytes 13828
  136.6 295.8 %copy-start.25 = (f32[1024]{0:T(1024)}, f32[1024]{0:T(1024)S(1)}, u32[]{:S(2)}) copy-start(f32[1024]{0:T(1024)S(1)} %broadcast_multiply_fusion.1) | copy-start | bytes 12292
  139.4 182.2 %copy-start.23 = (f32[1024]{0:T(1024)}, f32[1024]{0:T(1024)S(1)}, u32[]{:S(2)}) copy-start(f32[1024]{0:T(1024)S(1)} %multiply_reduce_fusion.4) | copy-start | bytes 12292
  139.4 293.0 %copy-start.40 = (f32[1024]{0:T(1024)}, f32[1024]{0:T(1024)S(1)}, u32[]{:S(2)}) copy-start(f32[1024]{0:T(1024)S(1)} %fusion.72) | copy-start | bytes 12292
  322.3 110.1 %copy-start.27 = (f32[1152]{0:T(1024)}, f32[1152]{0:T(1024)S(1)}, u32[]{:S(2)}) copy-start(f32[1152]{0:T(1024)S(1)} %get-tuple-element.231) | copy-start | bytes 13828
  322.3 110.1 %copy-start.47 = (f32[1152]{0:T(1024)}, f32[1152]{0:T(1024)S(1)}, u32[]{:S(2)}) copy-start(f32[1152]{0:T(1024)S(1)} %get-tuple-element.230) | copy-start | bytes 13828
  580.8 263.4 %copy-start.35 = (f32[1024]{0:T(1024)}, f32[1024]{0:T(1024)S(1)}, u32[]{:S(2)}) copy-start(f32[1024]{0:T(1024)S(1)} %broadcast_multiply_fusion) | copy-start | bytes 12292
  583.7 57.7 %copy-start.43 = (f32[1152]{0:T(1024)S(1)}, f32[1152]{0:T(1024)}, u32[]{:S(2)}) copy-start(f32[1152]{0:T(1024)} %get-tuple-element.228) | copy-start | bytes 13828
  583.7 57.7 %copy-start.45 = (f32[1152]{0:T(1024)S(1)}, f32[1152]{0:T(1024)}, u32[]{:S(2)}) copy-start(f32[1152]{0:T(1024)} %get-tuple-element.229) | copy-start | bytes 13828
  583.7 260.6 %copy-start.55 = (f32[1024]{0:T(1024)}, f32[1024]{0:T(1024)S(1)}, u32[]{:S(2)}) copy-start(f32[1024]{0:T(1024)S(1)} %fusion.73) | copy-start | bytes 12292
  585.0 209.0 %copy-start.10 = (bf16[1,1024,1152]{2,1,0:T(8,128)(2,1)}, bf16[1,1024,1152]{2,1,0:T(8,128)(2,1)S(1)}, u32[]{:S(2)}) copy-start(bf16[1,1024,1152]{2,1,0:T(8,128)(2,1)S(1)} %get-tuple-element.297) | copy-start | bytes 7077892
  641.3 152.7 %copy-start.32 = (f32[4608]{0:T(1024)S(1)}, f32[4608]{0:T(1024)}, u32[]{:S(2)}) copy-start(f32[4608]{0:T(1024)} %convert_element_type.299) | copy-start | bytes 55300
  1159.5 141.7 %reduce-scatter.13.cloned.1.call-start = ((), (), s32[]{:S(2)}) async-start(), calls=%async_computation.17 | async-start | bytes 2985984 | tf_op jit(solution)/shard_map/reduce_scatter | solution.py:324
  1166.1 280.7 %reduce-scatter.11.cloned.1.call-start = ((), (), s32[]{:S(2)}) async-start(), calls=%async_computation.16 | async-start | bytes 8957952 | tf_op jit(solution)/shard_map/reduce_scatter | solution.py:321
  1183.2 446.6 %reduce-scatter.15.cloned.1.call-start = ((), (), s32[]{:S(2)}) async-start(), calls=%async_computation.18 | async-start | bytes 11943936 | tf_op jit(solution)/shard_map/reduce_scatter | solution.py:327
  1202.1 610.3 %reduce-scatter.17.cloned.1.call-start = ((), (), s32[]{:S(2)}) async-start(), calls=%async_computation.19 | async-start | bytes 11943936 | tf_op jit(solution)/shard_map/reduce_scatter | solution.py:330
  1226.0 859.1 %reduce-scatter.9.cloned.1.call-start = ((), (), s32[]{:S(2)}) async-start(), calls=%async_computation.15 | async-start | bytes 17915904 | tf_op jit(solution)/shard_map/reduce_scatter | solution.py:293
  1239.7 968.1 %all-reduce.20.cloned.1.call-start = ((), (), s32[]{:S(2)}) async-start(), calls=%async_computation.20 | async-start | bytes 12533760 | tf_op jit(solution)/shard_map/psum | solution.py:374
  1249.4 835.7 %copy-start.58 = (pred[768]{0:T(1024)(128)(4,1)S(1)}, pred[768]{0:T(1024)(128)(4,1)}, u32[]{:S(2)}) copy-start(pred[768]{0:T(1024)(128)(4,1)} %copy-done.57) | copy-start | bytes 2308
  2106.2 80.8 %copy-start.18 = (f32[1,1152]{1,0:T(1,128)S(1)}, f32[1,1152]{1,0:T(1,128)}, u32[]{:S(2)}) copy-start(f32[1,1152]{1,0:T(1,128)} %param.25) | copy-start | bytes 13828
  2106.2 80.8 %copy-start.20 = (f32[1,1152]{1,0:T(1,128)S(1)}, f32[1,1152]{1,0:T(1,128)}, u32[]{:S(2)}) copy-start(f32[1,1152]{1,0:T(1,128)} %copy-done.19) | copy-start | bytes 13828
  2106.2 89.3 %all-to-all-start.1 = ((bf16[8,2,55296]{2,1,0:T(2,128)(2,1)}), bf16[8,2,55296]{2,1,0:T(2,128)(2,1)}, u32[]{:S(2)}, u32[]{:S(2)}) async-start(bf16[8,2,55296]{2,1,0:T(2,128)(2,1)} %reshape.683), calls=%async_computation.1 | async-start | bytes 3538944 | tf_op jit(solution)/shard_map/all_to_all | solution.py:282
  (55 other events, 484.5 us)
Sparse Core Ops, SparseCore 0:
  10.8 82.8 all-gather.6
  96.5 215.3 all-gather.8
  314.6 117.7 all-gather.10
  435.0 53.1 all-gather.12
  490.3 151.0 all-gather.14
  643.4 150.6 all-gather.16
  1159.6 67.3 reduce-scatter.6
  1231.2 69.9 reduce-scatter.12
  1305.2 141.5 reduce-scatter.10
  1450.7 179.0 reduce-scatter.14
  1633.4 179.0 reduce-scatter.16
  1816.6 268.3 reduce-scatter.8
  2088.1 119.7 all-reduce.19
where the time goes:
time: 2240 us; the launch traced here: 2230 us
  waiting for transfers between devices  1310 us (58%)
  matrix products  445 us (20%)
  other arithmetic  193 us (9%)
  blocking collectives  146 us (7%)
  local copies, waits for them, and re-layouts  96.6 us (4%)
    reduce_scatter x1, waiting for transfers between devices, on_device(): lax.psum_scatter(modulation_term.astype(jnp.bfloat16), 'tok', scatter_dim...  273 us
    reduce_scatter x1, waiting for transfers between devices, on_device(): lax.psum_scatter(up_term.astype(jnp.bfloat16), 'tok', scatter_dimension=0...  183 us
    reduce_scatter x1, waiting for transfers between devices, on_device(): lax.psum_scatter(down_term.astype(jnp.bfloat16), 'tok', scatter_dimension...  183 us
    all_gather x1, waiting for transfers between devices, on_device(): lax.all_gather(modulation_weight.astype(jnp.bfloat16), 'tok', axis=1, til...  172 us
    reduce_scatter x1, waiting for transfers between devices, on_device(): lax.psum_scatter(input_term.astype(jnp.bfloat16), 'tok', scatter_dimensio...  146 us
    unnamed x2, blocking collectives  139 us
    all_gather x1, waiting for transfers between devices, on_device(): lax.all_gather(down_weight.astype(jnp.bfloat16), 'tok', axis=0, tiled=True)  132 us
    all_gather x1, waiting for transfers between devices, on_device(): lax.all_gather(input_weight.astype(jnp.bfloat16), 'tok', axis=0, tiled=True)  110 us
  transfers between devices with their start and end apart: 15, of which 10 were waited for; matrix products, arithmetic and copies ran while one was open for 16% of the time, Pallas kernels for 0%

commit v1 on v0

--- a/solution.py
+++ b/solution.py
@@ -122,39 +122,42 @@
     images_here, seq_len, model_width = cotangent.shape
     slot_count = kept_index.shape[1]
     factor = 1.0 / math.sqrt(HD)
-    (
-        input_full,
-        output_full,
-        up_full,
-        down_full,
-        position_full,
-        query_bias_full,
-        value_bias_full,
-        output_bias_full,
-        up_bias_full,
-        down_bias_full,
-        mask_full,
-    ) = (
-        lax.all_gather(input_weight.astype(jnp.bfloat16), "tok", axis=0, tiled=True),
-        lax.all_gather(output_weight.astype(jnp.bfloat16), "tok", axis=0, tiled=True),
-        lax.all_gather(up_weight.astype(jnp.bfloat16), "tok", axis=0, tiled=True),
-        lax.all_gather(down_weight.astype(jnp.bfloat16), "tok", axis=0, tiled=True),
-        lax.all_gather(position_table.astype(jnp.bfloat16), "tok", axis=0, tiled=True),
-        lax.all_gather(query_bias.astype(jnp.bfloat16), "tok", axis=0, tiled=True),
-        lax.all_gather(value_bias.astype(jnp.bfloat16), "tok", axis=0, tiled=True),
-        lax.all_gather(output_bias.astype(jnp.bfloat16), "tok", axis=0, tiled=True),
-        lax.all_gather(up_bias.astype(jnp.bfloat16), "tok", axis=0, tiled=True),
-        lax.all_gather(down_bias.astype(jnp.bfloat16), "tok", axis=0, tiled=True),
-        lax.all_gather(mask_token.astype(jnp.bfloat16), "tok", axis=0, tiled=True),
-    )
-    condition_low = jax.nn.silu(condition).astype(jnp.bfloat16)
-    modulation_full, modulation_bias_full = (
-        lax.all_gather(modulation_weight.astype(jnp.bfloat16), "tok", axis=1, tiled=True),
-        lax.all_gather(modulation_bias.astype(jnp.bfloat16), "tok", axis=0, tiled=True),
-    )
-    modulation = jnp.dot(
-        condition_low, modulation_full, preferred_element_type=jnp.float32
-    ) + modulation_bias_full.astype(jnp.float32)
+    grp_count, tok_count = lax.axis_size("grp"), lax.axis_size("tok")
+    grp_index = lax.axis_index("grp")
+    low = jnp.bfloat16
+
+    def gather_rows(shard):
+        if shard.shape[0] % grp_count:
+            return lax.all_gather(shard.astype(low), "tok", axis=0, tiled=True)
+        quarter = shard.shape[0] // grp_count
+        part = lax.dynamic_slice_in_dim(shard, grp_index * quarter, quarter, 0).astype(low)
+        return lax.all_gather(part, ("tok", "grp"), axis=0, tiled=True)
+
+    condition_low = jax.nn.silu(condition).astype(low)
+    condition_group = lax.all_gather(condition_low, "tok", axis=0, tiled=True)
+    modulation_low = modulation_weight.astype(low)
+    modulation_part = jnp.dot(
+        condition_group, modulation_low, preferred_element_type=jnp.float32
+    ) + modulation_bias.astype(low).astype(jnp.float32)
+    modulation = lax.all_to_all(
+        modulation_part, "tok", split_axis=0, concat_axis=1, tiled=True
+    )
+    small_parts = [mask_token, query_bias, value_bias, output_bias, down_bias, up_bias]
+    small_widths = [part.shape[0] for part in small_parts]
+    small_full = lax.all_gather(jnp.concatenate(small_parts).astype(low), "tok", axis=0)
+
+    def small_piece(number):
+        start = sum(small_widths[:number])
+        return small_full[:, start : start + small_widths[number]].reshape(-1)
+
+    mask_full, query_bias_full, value_bias_full, output_bias_full, down_bias_full, up_bias_full = (
+        small_piece(number) for number in range(6)
+    )
+    position_full = gather_rows(position_table)
+    input_full = gather_rows(input_weight)
+    output_full = gather_rows(output_weight)
+    up_full = gather_rows(up_weight)
+    down_full = gather_rows(down_weight)
     shift_one, scale_one, gate_one, shift_two, scale_two, gate_two = (
         modulation[:, None, number * model_width : (number + 1) * model_width]
         for number in range(6)
@@ -282,20 +285,22 @@
     kept_grad = lax.all_to_all(
         slot_grad.astype(jnp.bfloat16), "tok", split_axis=1, concat_axis=0, tiled=True
     ).astype(slot_grad.dtype)
-    modulation_term = jnp.einsum(
-        "id,ie->de", condition_low, modulation_grad, preferred_element_type=jnp.float32
-    )
-    modulation_bias_term = jnp.sum(modulation_grad.astype(jnp.float32), axis=0)
-    condition_low_grad = jnp.einsum(
-        "ie,de->id", modulation_grad, modulation_full, preferred_element_type=jnp.float32
-    )
-    modulation_shard, modulation_bias_shard = (
-        lax.psum_scatter(
-            modulation_term.astype(jnp.bfloat16), "tok", scatter_dimension=1, tiled=True
-        ).astype(jnp.float32),
-        lax.psum_scatter(
-            modulation_bias_term.astype(jnp.bfloat16), "tok", scatter_dimension=0, tiled=True
-        ).astype(jnp.float32),
+    condition_all = lax.all_gather(condition_group, "grp", axis=0, tiled=True)
+    modulation_grad_group = lax.all_to_all(
+        modulation_grad, "tok", split_axis=1, concat_axis=0, tiled=True
+    )
+    modulation_grad_all = lax.all_gather(modulation_grad_group, "grp", axis=0, tiled=True)
+    modulation_total = jnp.einsum(
+        "id,ie->de", condition_all, modulation_grad_all, preferred_element_type=jnp.float32
+    )
+    modulation_bias_total = jnp.sum(modulation_grad_all.astype(jnp.float32), axis=0)
+    condition_part = jnp.einsum(
+        "ie,de->id", modulation_grad_group, modulation_low, preferred_element_type=jnp.float32
+    )
+    condition_low_grad = jnp.sum(
+        lax.all_to_all(condition_part, "tok", split_axis=0, concat_axis=0, tiled=True),
+        axis=0,
+        keepdims=True,
     )
     _, silu_back = jax.vjp(jax.nn.silu, condition)
     condition_grad = silu_back(condition_low_grad)[0]
@@ -305,82 +310,49 @@
     output_term = jnp.einsum("isd,ise->de", mixture, grad_one, preferred_element_type=jnp.float32)
     up_term = jnp.einsum("isd,isf->df", normed_two, pre_grad, preferred_element_type=jnp.float32)
     down_term = jnp.einsum("isf,isd->fd", hidden, grad_two, preferred_element_type=jnp.float32)
+    swap = lambda bit: [(g, g ^ bit) for g in range(grp_count)]
+    core = grp_index % 2
+
+    def reduce_rows(term):
+        halves = term.reshape(term.shape[0], 2, term.shape[1] // 2)
+        mine = lax.dynamic_index_in_dim(halves, core, 1, keepdims=False)
+        other = lax.dynamic_index_in_dim(halves, 1 - core, 1, keepdims=False).astype(low)
+        got = lax.ppermute(other, "grp", swap(1))
+        chip = (mine + got.astype(jnp.float32)).astype(low)
+        shard = lax.psum_scatter(chip, "tok", scatter_dimension=0, tiled=True)
+        bit = 2
+        while bit < grp_count:
+            got = lax.ppermute(shard, "grp", swap(bit))
+            shard = (shard.astype(jnp.float32) + got.astype(jnp.float32)).astype(low)
+            bit *= 2
+        got = lax.ppermute(shard, "grp", swap(1))
+        left = jnp.where(core == 0, shard, got)
+        right = jnp.where(core == 0, got, shard)
+        return jnp.concatenate([left, right], axis=1).astype(jnp.float32)
+
+    down_total = reduce_rows(down_term)
+    up_total = reduce_rows(up_term)
+    output_total = reduce_rows(output_term)
+    input_total = reduce_rows(input_term)
+    position_total = reduce_rows(position_term)
+    small_terms = [
+        mask_term, query_bias_term, value_bias_term, output_bias_term, down_bias_term, up_bias_term
+    ]
+    small_term = jnp.concatenate(
+        [term.reshape(tok_count, -1) for term in small_terms], axis=1
+    )
+    small_sum = lax.psum(
+        lax.psum_scatter(small_term, "tok", scatter_dimension=0), "grp"
+    )
+    cut = [sum(small_widths[:number]) for number in range(7)]
     (
-        input_shard,
-        output_shard,
-        up_shard,
-        down_shard,
-        position_shard,
-        query_bias_shard,
-        value_bias_shard,
-        output_bias_shard,
-        up_bias_shard,
-        down_bias_shard,
-        mask_shard,
-    ) = (
-        lax.psum_scatter(
-            input_term.astype(jnp.bfloat16), "tok", scatter_dimension=0, tiled=True
-        ).astype(jnp.float32),
-        lax.psum_scatter(
-            output_term.astype(jnp.bfloat16), "tok", scatter_dimension=0, tiled=True
-        ).astype(jnp.float32),
-        lax.psum_scatter(
-            up_term.astype(jnp.bfloat16), "tok", scatter_dimension=0, tiled=True
-        ).astype(jnp.float32),
-        lax.psum_scatter(
-            down_term.astype(jnp.bfloat16), "tok", scatter_dimension=0, tiled=True
-        ).astype(jnp.float32),
-        lax.psum_scatter(
-            position_term.astype(jnp.bfloat16), "tok", scatter_dimension=0, tiled=True
-        ).astype(jnp.float32),
-        lax.psum_scatter(
-            query_bias_term.astype(jnp.bfloat16), "tok", scatter_dimension=0, tiled=True
-        ).astype(jnp.float32),
-        lax.psum_scatter(
-            value_bias_term.astype(jnp.bfloat16), "tok", scatter_dimension=0, tiled=True
-        ).astype(jnp.float32),
-        lax.psum_scatter(
-            output_bias_term.astype(jnp.bfloat16), "tok", scatter_dimension=0, tiled=True
-        ).astype(jnp.float32),
-        lax.psum_scatter(
-            up_bias_term.astype(jnp.bfloat16), "tok", scatter_dimension=0, tiled=True
-        ).astype(jnp.float32),
-        lax.psum_scatter(
-            down_bias_term.astype(jnp.bfloat16), "tok", scatter_dimension=0, tiled=True
-        ).astype(jnp.float32),
-        lax.psum_scatter(
-            mask_term.astype(jnp.bfloat16), "tok", scatter_dimension=0, tiled=True
-        ).astype(jnp.float32),
-    )
-    (
-        input_total,
-        output_total,
-        up_total,
-        down_total,
-        position_total,
+        mask_total,
         query_bias_total,
         value_bias_total,
         output_bias_total,
+        down_bias_total,
         up_bias_total,
-        down_bias_total,
-        mask_total,
-        modulation_total,
-        modulation_bias_total,
-    ) = (
-        lax.psum(input_shard.astype(jnp.bfloat16), "grp").astype(jnp.float32),
-        lax.psum(output_shard.astype(jnp.bfloat16), "grp").astype(jnp.float32),
-        lax.psum(up_shard.astype(jnp.bfloat16), "grp").astype(jnp.float32),
-        lax.psum(down_shard.astype(jnp.bfloat16), "grp").astype(jnp.float32),
-        lax.psum(position_shard.astype(jnp.bfloat16), "grp").astype(jnp.float32),
-        lax.psum(query_bias_shard.astype(jnp.bfloat16), "grp").astype(jnp.float32),
-        lax.psum(value_bias_shard.astype(jnp.bfloat16), "grp").astype(jnp.float32),
-        lax.psum(output_bias_shard.astype(jnp.bfloat16), "grp").astype(jnp.float32),
-        lax.psum(up_bias_shard.astype(jnp.bfloat16), "grp").astype(jnp.float32),
-        lax.psum(down_bias_shard.astype(jnp.bfloat16), "grp").astype(jnp.float32),
-        lax.psum(mask_shard.astype(jnp.bfloat16), "grp").astype(jnp.float32),
-        lax.psum(modulation_shard.astype(jnp.bfloat16), "grp").astype(jnp.float32),
-        lax.psum(modulation_bias_shard.astype(jnp.bfloat16), "grp").astype(jnp.float32),
-    )
+    ) = (small_sum[cut[number] : cut[number + 1]] for number in range(6))
     return (
         block_output,
         kept_grad,

time: 2240 us -> 1340 us (0.60)
  waiting for transfers between devices: 1310 us -> 209 us
  local copies, waits for them, and re-layouts: 96.6 us -> 228 us
  blocking collectives: 146 us -> 190 us
  other arithmetic: 193 us -> 217 us
    reduce_scatter x6 -> x2, waiting for transfers between devices: 836 us -> 102 us  [reduce_rows(): shard = lax.psum_scatter(chip, 'tok', scatter_dimension=0, tiled=True)]
    all_gather x6 -> x5, waiting for transfers between devices: 471 us -> 59.1 us  [gather_rows(): return lax.all_gather(part, ('tok', 'grp'), axis=0, tiled=True)]
    all_gather x0 -> x4, blocking collectives: none -> 100 us  [the longest x1 57.3 us: on_device(): lax.all_gather(jnp.concatenate(small_parts).astype(low), 'tok', axis=0)]
    unnamed x173 -> x188, local copies, waits for them, and re-layouts: 34 us -> 105 us
    unnamed x2 -> x1, blocking collectives: 139 us -> 83.8 us
    ppermute x0 -> x15, waiting for transfers between devices: none -> 42.5 us  [the longest x5 31.4 us: reduce_rows(): got = lax.ppermute(shard, 'grp', swap(bit))]
    convert_element_type x0 -> x15, local copies, waits for them, and re-layouts: none -> 26.4 us  [the longest x5 19.5 us: reduce_rows(): lax.dynamic_index_in_dim(halves, 1 - core, 1, keepdims=False).astype(low)]
    convert_element_type x33 -> x17, other arithmetic: 47.2 us -> 59.3 us  [the longest x5 30 us: reduce_rows(): chip = (mine + got.astype(jnp.float32)).astype(low)]
  transfers between devices with their start and end apart: 15 -> 30, of which waited for: 10 -> 9; matrix products, arithmetic and copies ran while one was open for 16% -> 36% of each run, Pallas kernels for 0% -> 0%
where the time goes in v1:
time: 1340 us; the launch traced here: 1320 us
  matrix products  427 us (32%)
  local copies, waits for them, and re-layouts  228 us (17%)
  other arithmetic  217 us (16%)
  waiting for transfers between devices  209 us (16%)
  blocking collectives  190 us (14%)
  starting transfers between devices  35.3 us (3%)
  between operations  16.4 us (1%)
    unnamed x188, local copies, waits for them, and re-layouts  105 us
    reduce_scatter x2, waiting for transfers between devices, reduce_rows(): shard = lax.psum_scatter(chip, 'tok', scatter_dimension=0, tiled=True)  102 us
    unnamed x1, blocking collectives  83.8 us
    all_gather x5, waiting for transfers between devices, gather_rows(): return lax.all_gather(part, ('tok', 'grp'), axis=0, tiled=True)  59.1 us
    all_gather x1, blocking collectives, on_device(): lax.all_gather(jnp.concatenate(small_parts).astype(low), 'tok', axis=0)  57.3 us
    convert_element_type x2, other arithmetic, back_block(): score_grad = (probabilities * (prob_grad - inner)).astype(jnp.bfloat16)  55.8 us
    dot_general x2, matrix products, back_block(): jnp.einsum('qhd,khd->hqk', grad_block, value_rows, preferred_element_type...  45.7 us
    dot_general x2, matrix products, back_block(): jnp.einsum('hqk,qhd->khd', probabilities.astype(jnp.bfloat16), grad_block...  34.1 us
  transfers between devices with their start and end apart: 30, of which 9 were waited for; matrix products, arithmetic and copies ran while one was open for 36% of the time, Pallas kernels for 0%

profile of v1, /device:TPU:0, one launch (start us, length us, event | category | flops | bytes accessed | tf_op | source)
XLA Modules:
  0.0 1324.9 jit_solution(17139382764220286800)
XLA Ops:
  14.8 32.5 %all-gather.2 = bf16[8,1,1152]{2,1,0:T(2,128)(2,1)S(1)} all-gather(bf16[1,1,1152]{2,1,0:T(2,128)(2,1)S(1)} %get-tuple-element.363), channel_id=1, replica_groups=mesh['grp'=4,'tok'=8] {'tok'}, dimensions={0}, use_global_device_ids=true | all-gather | bytes 20736 | tf_op jit(solution)/shard_map/all_gather | solution.py:137
  69.5 57.3 %all-gather.1 = bf16[8,1,1296]{2,1,0:T(2,128)(2,1)S(1)} all-gather(bf16[1,1,1296]{2,1,0:T(2,128)(2,1)S(1)} %bitcast.339), channel_id=1, replica_groups=mesh['grp'=4,'tok'=8] {'tok'}, dimensions={0}, use_global_device_ids=true | all-gather | bytes 23328 | tf_op jit(solution)/shard_map/all_gather | solution.py:147
  166.9 59.0 %all-gather.16.cloned.1.call-done = bf16[32,36,3456]{2,1,0:T(8,128)(2,1)} async-done(((bf16[1,36,3456]{2,1,0:T(8,128)(2,1)}), bf16[32,36,3456]{2,1,0:T(8,128)(2,1)}) %all-gather.16.cloned.1.call-update) | async-done | bytes 7962640 | tf_op jit(solution)/shard_map/all_gather | solution.py:134
  279.4 88.6 %while.47 = (s32[]{:T(128)}, bf16[2,512,16,72]{1,3,2,0:T(8,128)(2,1)}, f32[2,16,512]{2,1,0:T(8,128)S(1)}, bf16[2,512,16,72]{1,3,2,0:T(8,128)(2,1)}, bf16[1024,16...) while((s32[]{:T(128)}, bf16[2,512,16,72]{1,3,2,0:T(8,128)(2,1)}, ...), condition=%wide.region_7.8_spmd, body=%wide.region_4.7_spmd.sunk | while | flops 2491998208 | bytes 117441648 | solution.py:49
  279.9 15.1 %multiply_reduce_fusion.7 = (f32[16,512]{1,0:T(8,128)S(1)}, f32[16,512,1024]{2,1,0:T(8,128)}) fusion(bf16[1024,16,72]{0,2,1:T(8,128)(2,1)S(1)} %get-tuple-element.519, bf16[2,512,16,72]{1,3,2,0:T(8,128)(2,1)} %get-tuple-element.518, s32[]{:T(128)} %get-tuple-element.508), kind=kOutput, calls=%fused_computation.5.clone.1 | convolution fusion | flops 1224728576 | bytes 37126656 | tf_op jit(solution)/shard_map/while/body/eval_jaxpr/while/body/eval_jaxpr/qhd,khd->hqk/dot_general | solution.py:37
  295.0 14.5 %fusion.159 = f32[16,512]{1,0:T(8,128)S(1)} fusion(f32[16,512,1024]{2,1,0:T(8,128)} %get-tuple-element.488, f32[16,512]{1,0:T(8,128)S(1)} %get-tuple-element.489), kind=kLoop, calls=%fused_computation.6.clone.1 | loop fusion | flops 25157632 | bytes 33619968 | tf_op jit(solution)/shard_map/while/body/eval_jaxpr/while/body/eval_jaxpr/reduce_sum | solution.py:42
  309.5 14.9 %fusion.160 = bf16[2,512,16,72]{1,3,2,0:T(8,128)(2,1)} fusion(bf16[2,512,16,72]{1,3,2,0:T(8,128)(2,1)} %get-tuple-element.509, s32[]{:T(128)} %get-tuple-element.508, bf16[1024,16,72]{0,2,1:T(8,128)(2,1)S(1)} %copy-done.5, f32[16,512,1024]{2,1,0:T(8,128)} %get-tuple-element.488, f32[16,512]{1,0:T(8,128)S(1)} %fusion.159, ...), kind=kOutput, calls=%fused_computation.10.clone.1 | convolution fusion | flops 1242103808 | bytes 37159424 | tf_op jit(solution)/shard_map/while/body/eval_jaxpr/while/body/eval_jaxpr/hqk,khd->qhd/dot_general | solution.py:44
  324.4 14.8 %multiply_reduce_fusion.7 = (f32[16,512]{1,0:T(8,128)S(1)}, f32[16,512,1024]{2,1,0:T(8,128)}) fusion(bf16[1024,16,72]{0,2,1:T(8,128)(2,1)S(1)} %get-tuple-element.519, bf16[2,512,16,72]{1,3,2,0:T(8,128)(2,1)} %get-tuple-element.518, s32[]{:T(128)} %get-tuple-element.508), kind=kOutput, calls=%fused_computation.5.clone.1 | convolution fusion | flops 1224728576 | bytes 37126656 | tf_op jit(solution)/shard_map/while/body/eval_jaxpr/while/body/eval_jaxpr/qhd,khd->hqk/dot_general | solution.py:37
  339.2 14.4 %fusion.159 = f32[16,512]{1,0:T(8,128)S(1)} fusion(f32[16,512,1024]{2,1,0:T(8,128)} %get-tuple-element.488, f32[16,512]{1,0:T(8,128)S(1)} %get-tuple-element.489), kind=kLoop, calls=%fused_computation.6.clone.1 | loop fusion | flops 25157632 | bytes 33619968 | tf_op jit(solution)/shard_map/while/body/eval_jaxpr/while/body/eval_jaxpr/reduce_sum | solution.py:42
  353.7 14.4 %fusion.160 = bf16[2,512,16,72]{1,3,2,0:T(8,128)(2,1)} fusion(bf16[2,512,16,72]{1,3,2,0:T(8,128)(2,1)} %get-tuple-element.509, s32[]{:T(128)} %get-tuple-element.508, bf16[1024,16,72]{0,2,1:T(8,128)(2,1)S(1)} %copy-done.5, f32[16,512,1024]{2,1,0:T(8,128)} %get-tuple-element.488, f32[16,512]{1,0:T(8,128)S(1)} %fusion.159, ...), kind=kOutput, calls=%fused_computation.10.clone.1 | convolution fusion | flops 1242103808 | bytes 37159424 | tf_op jit(solution)/shard_map/while/body/eval_jaxpr/while/body/eval_jaxpr/hqk,khd->qhd/dot_general | solution.py:44
  382.4 14.3 %reshape.784 = bf16[1152,4608]{1,0:T(8,128)(2,1)} reshape(bf16[32,36,4608]{2,1,0:T(8,128)(2,1)} %all-gather.20.cloned.1.call-done) | data formatting | bytes 21233664
  396.7 20.9 %fusion.83 = f32[1024,4608]{1,0:T(8,128)} fusion(bf16[1152,4608]{1,0:T(8,128)(2,1)} %reshape.784, f32[1,1024,1152]{2,1,0:T(8,128)} %copy-done.16, f32[1152]{0:T(1024)S(1)} %copy-done.52, f32[1152]{0:T(1024)S(1)} %copy-done.54, f32[1024]{0:T(1024)S(1)} %fusion.106, f32[1024]{0:T(1024)S(1)} %broadcast_multiply_fusion), kind=kOutput, calls=%fused_computation.142 | convolution fusion | flops 10877534208 | bytes 34227200 | tf_op jit(solution)/shard_map/isd,df->isf/dot_general | solution.py:212
  417.6 30.8 %convert_reduce_fusion = (f32[4608]{0:T(1024)}, bf16[1024,4608]{1,0:T(8,128)(2,1)}, f32[1024,4608]{1,0:T(8,128)}) fusion(f32[1024,4608]{1,0:T(8,128)} %fusion.83, f32[4608]{0:T(1024)S(1)} %copy-done.29, bf16[4608,1152]{1,0:T(8,128)(2,1)} %all-gather.14.cloned.1.call-done, bf16[1,1024,1152]{1,2,0:T(8,128)(2,1)S(1)} %copy-done.21), kind=kOutput, calls=%fused_computation.68 | convolution fusion | flops 10980159488 | bytes 60198912 | tf_op jit(solution)/shard_map/isd,fd->isf/dot_general | solution.py:223
  448.4 21.6 %fusion.62 = (bf16[1152]{0:T(1024)(128)(2,1)}, f32[1024]{0:T(1024)S(1)}, f32[1024,1152]{1,0:T(8,128)}) fusion(f32[1,1024,1152]{2,1,0:T(8,128)} %copy-done.16, f32[1024]{0:T(1024)S(1)} %fusion.106, f32[1024]{0:T(1024)S(1)} %broadcast_multiply_fusion, f32[1152]{0:T(1024)S(1)} %copy-done.54, bf16[1024,4608]{1,0:T(8,128)(2,1)} %get-tuple-element.345, ...), kind=kOutput, calls=%fused_computation.95 | convolution fusion | flops 10879891456 | bytes 29510400 | tf_op jit(solution)/shard_map/isf,df->isd/dot_general | solution.py:227
  470.0 27.7 %fusion.61 = (bf16[1152]{0:T(1024)(128)(2,1)}, f32[1,1024,1152]{2,1,0:T(8,128)}, f32[1024]{0:T(1024)S(1)}, f32[1,1024,1152]{2,1,0:T(8,128)}) fusion(f32[1,1024,1152]{2,1,0:T(8,128)} %param.39, f32[1,1024,1152]{2,1,0:T(8,128)} %copy-done.16, f32[1152]{0:T(1024)S(1)} %copy-done.41, f32[1024]{0:T(1024)S(1)} %multiply_multiply_fusion.5, ...), kind=kOutput, calls=%fused_computation.93 | convolution fusion | flops 10932975616 | bytes 53135104 | tf_op jit(solution)/shard_map/isf,fd->isd/dot_general | solution.py:216
  528.5 209.0 %while.48 = (s32[]{:T(128)}, f32[1024,16,72]{0,2,1:T(8,128)}, f32[1024,16,72]{0,2,1:T(8,128)}, bf16[2,512,16,72]{1,3,2,0:T(8,128)(2,1)}, bf16[2,512,16,72]{1,3,2...) while((s32[]{:T(128)}, f32[1024,16,72]{0,2,1:T(8,128)}, ...), condition=%wide.region_14.15_spmd.clone, body=%wide.region_12.14_spmd.clone.sunk | while | flops 6147530752 | bytes 302614688 | solution.py:92
  528.7 14.6 %fusion.170 = f32[16,512,1024]{2,1,0:T(8,128)} fusion(bf16[1024,16,72]{0,2,1:T(8,128)(2,1)S(1)} %get-tuple-element.549, bf16[2,512,16,72]{1,3,2,0:T(8,128)(2,1)} %get-tuple-element.548, s32[]{:T(128)} %get-tuple-element.533), kind=kOutput, calls=%fused_computation.33.clone.1 | convolution fusion | flops 1207959552 | bytes 37093888 | tf_op jit(solution)/shard_map/while/body/eval_jaxpr/while/body/eval_jaxpr/qhd,khd->hqk/dot_general | solution.py:63
  543.3 22.8 %multiply_reduce_fusion.8 = (f32[16,512]{1,0:T(8,128)S(1)}, f32[16,512,1024]{2,1,0:T(8,128)}) fusion(f32[16,512,1024]{2,1,0:T(8,128)} %fusion.170, f32[16,512]{1,0:T(8,128)S(1)} %dynamic-slice_bitcast_fusion.2, bf16[1024,16,72]{0,2,1:T(8,128)(2,1)S(1)} %copy-done.6, bf16[2,512,16,72]{1,3,2,0:T(8,128)(2,1)S(1)} %copy-done.7, s32[]{:T(128)} %get-tuple-element.533), kind=kOutput, calls=%fused_computation.18.clone.1 | convolution fusion | flops 1241505792 | bytes 70713344 | tf_op jit(solution)/shard_map/while/body/eval_jaxpr/while/body/eval_jaxpr/qhd,khd->hqk/dot_general | solution.py:73
  566.2 27.9 %multiply_convert_fusion.10 = bf16[16,512,1024]{2,1,0:T(8,128)(2,1)} fusion(f32[16,512,1024]{2,1,0:T(8,128)} %get-tuple-element.499, f32[16,512,1024]{2,1,0:T(8,128)} %fusion.170, f32[16,512]{1,0:T(8,128)S(1)} %get-tuple-element.500, f32[16,512]{1,0:T(8,128)S(1)} %dynamic-slice_bitcast_fusion.2), kind=kLoop, calls=%fused_computation.17.clone.1 | loop fusion | flops 41943040 | bytes 83951616 | tf_op jit(solution)/shard_map/while/body/eval_jaxpr/while/body/eval_jaxpr/convert_element_type | solution.py:77
  615.3 16.4 %bitcast_add_fusion.14 = f32[1024,16,72]{0,2,1:T(8,128)} fusion(f32[1024,16,72]{0,2,1:T(8,128)} %get-tuple-element.535, pred[]{:T(512)S(6)} %compare.9, f32[16,512,1024]{2,1,0:T(8,128)} %fusion.170, f32[16,512]{1,0:T(8,128)S(1)} %dynamic-slice_bitcast_fusion.2, bf16[2,512,16,72]{1,3,2,0:T(8,128)(2,1)} %get-tuple-element.551, s32[]{:T(128)} %get-tuple-element.533), kind=kOutput, calls=%fused_computation.24.clone.1 | convolution fusion | flops 1235484672 | bytes 44204544 | tf_op jit(solution)/shard_map/while/body/eval_jaxpr/while/body/eval_jaxpr/hqk,qhd->khd/dot_general | solution.py:67
  631.6 14.6 %fusion.170 = f32[16,512,1024]{2,1,0:T(8,128)} fusion(bf16[1024,16,72]{0,2,1:T(8,128)(2,1)S(1)} %get-tuple-element.549, bf16[2,512,16,72]{1,3,2,0:T(8,128)(2,1)} %get-tuple-element.548, s32[]{:T(128)} %get-tuple-element.533), kind=kOutput, calls=%fused_computation.33.clone.1 | convolution fusion | flops 1207959552 | bytes 37093888 | tf_op jit(solution)/shard_map/while/body/eval_jaxpr/while/body/eval_jaxpr/qhd,khd->hqk/dot_general | solution.py:63
  646.3 22.8 %multiply_reduce_fusion.8 = (f32[16,512]{1,0:T(8,128)S(1)}, f32[16,512,1024]{2,1,0:T(8,128)}) fusion(f32[16,512,1024]{2,1,0:T(8,128)} %fusion.170, f32[16,512]{1,0:T(8,128)S(1)} %dynamic-slice_bitcast_fusion.2, bf16[1024,16,72]{0,2,1:T(8,128)(2,1)S(1)} %copy-done.6, bf16[2,512,16,72]{1,3,2,0:T(8,128)(2,1)S(1)} %copy-done.7, s32[]{:T(128)} %get-tuple-element.533), kind=kOutput, calls=%fused_computation.18.clone.1 | convolution fusion | flops 1241505792 | bytes 70713344 | tf_op jit(solution)/shard_map/while/body/eval_jaxpr/while/body/eval_jaxpr/qhd,khd->hqk/dot_general | solution.py:73
  669.1 27.9 %multiply_convert_fusion.10 = bf16[16,512,1024]{2,1,0:T(8,128)(2,1)} fusion(f32[16,512,1024]{2,1,0:T(8,128)} %get-tuple-element.499, f32[16,512,1024]{2,1,0:T(8,128)} %fusion.170, f32[16,512]{1,0:T(8,128)S(1)} %get-tuple-element.500, f32[16,512]{1,0:T(8,128)S(1)} %dynamic-slice_bitcast_fusion.2), kind=kLoop, calls=%fused_computation.17.clone.1 | loop fusion | flops 41943040 | bytes 83951616 | tf_op jit(solution)/shard_map/while/body/eval_jaxpr/while/body/eval_jaxpr/convert_element_type | solution.py:77
  719.6 17.7 %bitcast_add_fusion.14 = f32[1024,16,72]{0,2,1:T(8,128)} fusion(f32[1024,16,72]{0,2,1:T(8,128)} %get-tuple-element.535, pred[]{:T(512)S(6)} %compare.9, f32[16,512,1024]{2,1,0:T(8,128)} %fusion.170, f32[16,512]{1,0:T(8,128)S(1)} %dynamic-slice_bitcast_fusion.2, bf16[2,512,16,72]{1,3,2,0:T(8,128)(2,1)} %get-tuple-element.551, s32[]{:T(128)} %get-tuple-element.533), kind=kOutput, calls=%fused_computation.24.clone.1 | convolution fusion | flops 1235484672 | bytes 44204544 | tf_op jit(solution)/shard_map/while/body/eval_jaxpr/while/body/eval_jaxpr/hqk,qhd->khd/dot_general | solution.py:67
  754.4 17.9 %fusion.64 = (bf16[1152]{0:T(1024)(128)(2,1)}, f32[1024]{0:T(1024)S(1)}, f32[1024,1152]{1,0:T(8,128)}) fusion(f32[1,1024,1152]{2,1,0:T(8,128)} %copy-done.8, f32[1024]{0:T(1024)S(1)} %copy-done.51, f32[1024]{0:T(1024)S(1)} %copy-done.36, f32[1152]{0:T(1024)S(1)} %copy-done.38, bf16[1152,3456]{1,0:T(8,128)(2,1)} %reshape.780, ...), kind=kOutput, calls=%fused_computation.99 | convolution fusion | flops 8183216128 | bytes 24496896 | tf_op jit(solution)/shard_map/ise,de->isd/dot_general | solution.py:261
  772.3 17.9 %fusion.77 = f32[1152,2,1728]{0,2,1:T(8,128)} fusion(bf16[2,1728,1024]{2,1,0:T(8,128)(2,1)} %bitcast.326, f32[1,1024,1152]{2,1,0:T(8,128)} %copy-done.8, f32[1152]{0:T(1024)S(1)} %copy-done.57, f32[1152]{0:T(1024)S(1)} %copy-done.38, f32[1024]{0:T(1024)S(1)} %copy-done.51, f32[1024]{0:T(1024)S(1)} %copy-done.36), kind=kOutput, calls=%fused_computation.135 | convolution fusion | flops 8159625216 | bytes 27739136 | tf_op jit(solution)/shard_map/isd,ise->de/dot_general | solution.py:307
  842.6 19.6 %fusion.53 = f32[4608,2,576]{0,2,1:T(8,128)} fusion(bf16[2,576,1024]{2,1,0:T(8,128)(2,1)S(1)} %bitcast.329, f32[1024,4608]{1,0:T(8,128)} %fusion.83, f32[4608]{0:T(1024)S(1)} %copy-done.30), kind=kOutput, calls=%fused_computation.77 | convolution fusion | flops 10918821888 | bytes 42485760 | tf_op jit(solution)/shard_map/isf,isd->fd/dot_general | solution.py:312
  872.7 21.1 %fusion.47 = bf16[4608,1024]{0,1:T(8,128)(2,1)} fusion(f32[1024,4608]{1,0:T(8,128)} %get-tuple-element.398, f32[1024,4608]{1,0:T(8,128)} %fusion.83, f32[4608]{0:T(1024)S(1)} %copy-done.30), kind=kLoop, calls=%fused_computation.62 | loop fusion | flops 99090432 | bytes 47204352 | tf_op jit(solution)/shard_map/convert_element_type | solution.py:225
  925.5 20.6 %fusion.73 = f32[1152,2,2304]{2,0,1:T(8,128)} fusion(bf16[2,2304,1024]{2,1,0:T(8,128)(2,1)} %bitcast.321, f32[1,1024,1152]{2,1,0:T(8,128)} %copy-done.16, f32[1152]{0:T(1024)S(1)} %copy-done.53, f32[1152]{0:T(1024)S(1)} %copy-done.55, f32[1024]{0:T(1024)S(1)} %copy-done.64, f32[1024]{0:T(1024)S(1)} %copy-done.49), kind=kOutput, calls=%fused_computation.131 | convolution fusion | flops 10877534208 | bytes 35406848 | tf_op jit(solution)/shard_map/isd,isf->df/dot_general | solution.py:311
  1037.5 83.8 %all-reduce = f32[8,1296]{1,0:T(8,128)S(1)} all-reduce(f32[8,1296]{1,0:T(8,128)S(1)} %concatenate.81), channel_id=3, replica_groups=mesh['grp'=4,'tok'=8] {'tok'}, use_global_device_ids=true, to_apply=%region_30.31.clone | all-reduce | flops 10368 | bytes 82944
  1155.3 16.3 %collective-permute-done.7 = bf16[144,576]{0,1:T(8,128)(2,1)S(1)} collective-permute-done((bf16[144,576]{0,1:T(8,128)(2,1)S(1)}, bf16[144,576]{0,1:T(8,128)(2,1)S(1)}, u32[]{:S(2)}, u32[]{:S(2)}) %collective-permute-start.7) | collective-permute-done | bytes 165920 | tf_op jit(solution)/shard_map/ppermute | solution.py:325
  1183.6 102.3 %reduce-scatter.14.cloned.1.call-done = bf16[144,2304]{1,0:T(8,128)(2,1)} async-done(((bf16[1152,2304]{1,0:T(8,128)(2,1)}), bf16[144,2304]{1,0:T(8,128)(2,1)}) %reduce-scatter.14.cloned.1.call-update) | async-done | bytes 663568 | tf_op jit(solution)/shard_map/reduce_scatter | solution.py:322
  (414 shorter events, 491.2 us)
Async XLA Ops:
  7.2 147.6 %all-gather.12.cloned.1.call-start = ((), (), s32[]{:S(2)}) async-start(), calls=%async_computation.10 | async-start | bytes 2433024 | tf_op jit(solution)/shard_map/all_gather | solution.py:134
  9.0 152.8 %all-gather.18.cloned.1.call-start = ((), (), s32[]{:S(2)}) async-start(), calls=%async_computation.14 | async-start | bytes 3041280 | tf_op jit(solution)/shard_map/all_gather | solution.py:134
  10.7 215.3 %all-gather.16.cloned.1.call-start = ((), (), s32[]{:S(2)}) async-start(), calls=%async_computation.13 | async-start | bytes 9123840 | tf_op jit(solution)/shard_map/all_gather | solution.py:134
  12.6 369.8 %all-gather.20.cloned.1.call-start = ((), (), s32[]{:S(2)}) async-start(), calls=%async_computation.15 | async-start | bytes 12165120 | tf_op jit(solution)/shard_map/all_gather | solution.py:134
  51.4 12.2 all-to-all-start.1
  63.5 82.3 %all-to-all-start = ((bf16[8,96,1152]{2,1,0:T(8,128)(2,1)}), bf16[8,96,1152]{2,1,0:T(8,128)(2,1)S(1)}, u32[]{:S(2)}, u32[]{:S(2)}) async-start(bf16[8,96,1152]{2,1,0:T(8,128)(2,1)} %convert_element_type.350), calls=%async_computation | async-start | bytes 3538944 | tf_op jit(solution)/shard_map/all_to_all | solution.py:165
  67.1 350.5 %all-gather.14.cloned.1.call-start = ((), (), s32[]{:S(2)}) async-start(), calls=%async_computation.11 | async-start | bytes 10948608 | tf_op jit(solution)/shard_map/all_gather | solution.py:134
  69.1 1065.6 %reduce-scatter.16.cloned.1.call-start = ((), (), s32[]{:S(2)}) async-start(), calls=%async_computation.16 | async-start | bytes 1474560
  796.1 21.1 %collective-permute-start.3 = (bf16[1152,1728]{0,1:T(8,128)(2,1)}, bf16[1152,1728]{0,1:T(8,128)(2,1)}, u32[]{:S(2)}, u32[]{:S(2)}) collective-permute-start(bf16[1152,1728]{0,1:T(8,128)(2,1)} %fusion.67), channel_id=1, source_target_pairs={{0,8},{8,0},{16,24},{24,16},{1,9},{9,1},{17,25},{25,17},{2,10},{10... | collective-permute-start | bytes 11943944 | tf_op jit(solution)/shard_map/ppermute | solution.py:320
  810.6 3.0 collective-permute-start
  817.2 333.8 %reduce-scatter.18.cloned.1.call-start = ((), (), s32[]{:S(2)}) async-start(), calls=%async_computation.17 | async-start | bytes 4644864 | tf_op jit(solution)/shard_map/reduce_scatter | solution.py:322
  831.1 321.4 %reduce-scatter.20.cloned.1.call-start = ((), (), s32[]{:S(2)}) async-start(), calls=%async_computation.18 | async-start | bytes 1658880
  842.1 27.3 %collective-permute-start.6 = (bf16[1152,576]{0,1:T(8,128)(2,1)S(1)}, bf16[1152,576]{0,1:T(8,128)(2,1)}, u32[]{:S(2)}, u32[]{:S(2)}) collective-permute-start(bf16[1152,576]{0,1:T(8,128)(2,1)S(1)} %fusion.90), channel_id=1, source_target_pairs={{0,8},{8,0},{16,24},{24,16},{1,9},{9,1},{17,25},{25,17},{2,10},{10... | collective-permute-start | bytes 3981320 | tf_op jit(solution)/shard_map/ppermute | solution.py:320
  869.4 37.1 %collective-permute-start.12 = (bf16[4608,576]{0,1:T(8,128)(2,1)}, bf16[4608,576]{0,1:T(8,128)(2,1)}, u32[]{:S(2)}, u32[]{:S(2)}) collective-permute-start(bf16[4608,576]{0,1:T(8,128)(2,1)} %fusion.60), channel_id=1, source_target_pairs={{0,8},{8,0},{16,24},{24,16},{1,9},{9,1},{17,25},{25,17},{2,10},{10... | collective-permute-start | bytes 15925256 | tf_op jit(solution)/shard_map/ppermute | solution.py:320
  872.7 305.3 %reduce-scatter.22.cloned.1.call-start = ((), (), s32[]{:S(2)}) async-start(), calls=%async_computation.19 | async-start | bytes 6635520
  924.8 361.1 %reduce-scatter.14.cloned.1.call-start = ((), (), s32[]{:S(2)}) async-start(), calls=%async_computation.12 | async-start | bytes 5971968 | tf_op jit(solution)/shard_map/reduce_scatter | solution.py:322
  950.7 8.9 collective-permute-start.9
  976.5 15.7 %all-to-all-start.3 = ((bf16[8,2,432]{2,1,0:T(2,128)(2,1)}), bf16[8,2,432]{2,1,0:T(2,128)(2,1)S(1)}, u32[]{:S(2)}, u32[]{:S(2)}) async-start(bf16[8,2,432]{2,1,0:T(2,128)(2,1)} %reshape.818), calls=%async_computation.3 | async-start | bytes 32768 | tf_op jit(solution)/shard_map/all_to_all | solution.py:289
  995.5 27.5 %all-to-all-start.4 = ((f32[8,1,1152]{2,1,0:T(1,128)}), f32[8,1,1152]{2,1,0:T(1,128)S(1)}, u32[]{:S(2)}, u32[]{:S(2)}) async-start(f32[8,1,1152]{2,1,0:T(1,128)} %copy.108), calls=%async_computation.4 | async-start | bytes 73728 | tf_op jit(solution)/shard_map/all_to_all | solution.py:301
  1022.9 119.7 %all-to-all-start.2 = ((bf16[8,2,55296]{2,1,0:T(2,128)(2,1)}), bf16[8,2,55296]{2,1,0:T(2,128)(2,1)S(1)}, u32[]{:S(2)}, u32[]{:S(2)}) async-start(bf16[8,2,55296]{2,1,0:T(2,128)(2,1)} %reshape.816), calls=%async_computation.2 | async-start | bytes 3538944 | tf_op jit(solution)/shard_map/all_to_all | solution.py:285
  1028.9 113.1 %copy-start.46 = (f32[1,1152]{1,0:T(1,128)S(1)}, f32[1,1152]{1,0:T(1,128)}, u32[]{:S(2)}) copy-start(f32[1,1152]{1,0:T(1,128)} %param.25) | copy-start | bytes 13828
  1028.9 113.1 %copy-start.47 = (f32[1,1152]{1,0:T(1,128)S(1)}, f32[1,1152]{1,0:T(1,128)}, u32[]{:S(2)}) copy-start(f32[1,1152]{1,0:T(1,128)} %get-tuple-element.364) | copy-start | bytes 13828
  1135.7 6.2 collective-permute-start.1
  1141.9 10.5 collective-permute-start.2
  1151.0 22.2 %collective-permute-start.4 = (bf16[144,1728]{1,0:T(8,128)(2,1)}, bf16[144,1728]{1,0:T(8,128)(2,1)S(1)}, u32[]{:S(2)}, u32[]{:S(2)}) collective-permute-start(bf16[144,1728]{1,0:T(8,128)(2,1)} %reduce-scatter.18.cloned.1.call-done), channel_id=1, source_target_pairs={{0,16},{8,24},{16,0},{24,8},{1,17},{9,25},{17,1},{25,9},{2,18},{10... | collective-permute-start | bytes 1493000 | tf_op jit(solution)/shard_map/ppermute | solution.py:325
  1153.6 18.1 %collective-permute-start.7 = (bf16[144,576]{0,1:T(8,128)(2,1)S(1)}, bf16[144,576]{0,1:T(8,128)(2,1)S(1)}, u32[]{:S(2)}, u32[]{:S(2)}) collective-permute-start(bf16[144,576]{0,1:T(8,128)(2,1)S(1)} %copy.136), channel_id=1, source_target_pairs={{0,16},{8,24},{16,0},{24,8},{1,17},{9,25},{17,1},{25,9},{2,18},{10... | collective-permute-start | bytes 497672 | tf_op jit(solution)/shard_map/ppermute | solution.py:325
  1171.7 3.5 collective-permute-start.8
  1174.7 7.5 collective-permute-start.5
  1179.4 108.1 %collective-permute-start.13 = (bf16[576,576]{0,1:T(8,128)(2,1)S(1)}, bf16[576,576]{0,1:T(8,128)(2,1)}, u32[]{:S(2)}, u32[]{:S(2)}) collective-permute-start(bf16[576,576]{0,1:T(8,128)(2,1)S(1)} %copy.138), channel_id=1, source_target_pairs={{0,16},{8,24},{16,0},{24,8},{1,17},{9,25},{17,1},{25,9},{2,18},{10... | collective-permute-start | bytes 1990664 | tf_op jit(solution)/shard_map/ppermute | solution.py:325
  1285.9 16.7 %collective-permute-start.10 = (bf16[144,2304]{1,0:T(8,128)(2,1)}, bf16[144,2304]{1,0:T(8,128)(2,1)S(1)}, u32[]{:S(2)}, u32[]{:S(2)}) collective-permute-start(bf16[144,2304]{1,0:T(8,128)(2,1)} %reduce-scatter.14.cloned.1.call-done), channel_id=1, source_target_pairs={{0,16},{8,24},{16,0},{24,8},{1,17},{9,25},{17,1},{25,9},{2,18},{10... | collective-permute-start | bytes 1990664 | tf_op jit(solution)/shard_map/ppermute | solution.py:325
  1288.8 19.5 %collective-permute-start.14 = (bf16[576,576]{0,1:T(8,128)(2,1)S(1)}, bf16[576,576]{0,1:T(8,128)(2,1)}, u32[]{:S(2)}, u32[]{:S(2)}) collective-permute-start(bf16[576,576]{0,1:T(8,128)(2,1)S(1)} %add_convert_fusion.4), channel_id=1, source_target_pairs={{0,8},{8,0},{16,24},{24,16},{1,9},{9,1},{17,25},{25,17},{2,10},{10... | collective-permute-start | bytes 1990664 | tf_op jit(solution)/shard_map/ppermute | solution.py:328
  1302.8 12.2 collective-permute-start.11
  (80 other events, 1363.1 us)
Sparse Core Ops, SparseCore 0:
  11.5 62.6 all-gather.11
  77.7 66.6 all-gather.17
  147.9 77.9 all-gather.15
  229.3 91.0 all-gather.19
  323.7 85.4 all-gather.13
  817.3 63.9 reduce-scatter.15
  884.8 86.6 reduce-scatter.17
  975.9 65.5 reduce-scatter.19
  1045.7 132.2 reduce-scatter.21
  1181.9 103.9 reduce-scatter.13

commit v2 on v1

v2 whole, which is shorter than its diff:
```python
import functools
import math

import jax
import jax.numpy as jnp
from jax import lax
from jax.experimental import pallas as pl
from jax.experimental.pallas import tpu as pltpu
from jax.sharding import PartitionSpec as P

H = 16
HD = 72
LANES = 128

epsilon = 1e-06
f32 = jnp.float32
bf16 = jnp.bfloat16
plain = (((1,), (0,)), ((), ()))
right_turned = (((1,), (1,)), ((), ()))
left_turned = (((0,), (0,)), ((), ()))
vmem_limit = 60 << 20


def product(left, right, dims=plain):
    return lax.dot_general(left, right, dims, preferred_element_type=f32)


def whole_block(array):
    zeros = (0,) * array.ndim
    return pl.BlockSpec(array.shape, lambda *_: zeros)


def row_block(rows, *rest):
    return pl.BlockSpec((rows,) + rest, lambda i: (i,) + (0,) * len(rest))


smem = pl.BlockSpec(memory_space=pltpu.SMEM)
anywhere = pl.BlockSpec(memory_space=pl.ANY)


def params():
    return pltpu.CompilerParams(vmem_limit_bytes=vmem_limit)


def cost(flops, moved, exps=0):
    return pl.CostEstimate(flops=int(flops), bytes_accessed=int(moved), transcendentals=int(exps))


def column_sum(values):
    return jnp.sum(values, axis=0, keepdims=True)


def normalize(values):
    center = values - jnp.mean(values, axis=-1, keepdims=True)
    spread = jnp.mean(center * center, axis=-1, keepdims=True)
    inverse = lax.rsqrt(spread + epsilon)
    return center * inverse, inverse


def normalize_back(grad, unit, inverse, scale):
    scaled = grad * (1.0 + scale)
    first = jnp.mean(scaled, axis=-1, keepdims=True)
    second = jnp.mean(scaled * unit, axis=-1, keepdims=True)
    return (scaled - first - unit * second) * inverse


def start_kernel(count_ref, index_ref, kept_ref, position_ref, mask_ref, mod_ref, start_ref, norm_ref):
    rows, slots = position_ref.shape[0], kept_ref.shape[0]
    base = pl.program_id(0) * rows
    here = lax.broadcasted_iota(jnp.int32, (rows, slots), 0) + base
    slot = lax.broadcasted_iota(jnp.int32, (rows, slots), 1)
    chosen = jnp.where((index_ref[...] == here) & (slot < count_ref[0]), 1.0, 0.0)
    filled = product(chosen.astype(bf16), kept_ref[...])
    empty = 1.0 - jnp.sum(chosen, axis=1, keepdims=True)
    start = filled + empty * mask_ref[...] + position_ref[...].astype(f32)
    start_ref[...] = start
    unit, _ = normalize(start)
    norm_ref[...] = (unit * (1.0 + mod_ref[1:2]) + mod_ref[0:1]).astype(bf16)


def start_call(count, index, kept, position, mask, mod):
    seq_len, width = position.shape
    rows = seq_len // 4
    return pl.pallas_call(
        start_kernel,
        grid=(4,),
        in_specs=[
            smem,
            whole_block(index),
            whole_block(kept),
            row_block(rows, width),
            whole_block(mask),
            whole_block(mod),
        ],
        out_specs=[row_block(rows, width)] * 2,
        out_shape=[
            jax.ShapeDtypeStruct((seq_len, width), f32),
            jax.ShapeDtypeStruct((seq_len, width), bf16),
        ],
        compiler_params=params(),
        cost_estimate=cost(2 * seq_len * width * kept.shape[0], 14 * seq_len * width),
    )(count, index, kept, position, mask, mod)


def block_copy(core_ref, mine_ref, other_ref, block, target, sem):
    owner, place = block // 2, block % 2

    @pl.when(core_ref[0] == owner)
    def _():
        pltpu.make_async_copy(mine_ref.at[place], target, sem).start()

    @pl.when(core_ref[0] != owner)
    def _():
        pltpu.make_async_copy(other_ref.at[place], target, sem).start()


def block_wait(mine_ref, target, sem):
    pltpu.make_async_copy(mine_ref.at[0], target, sem).wait()


def split_heads(values, store):
    rows = values.shape[0]
    blank = jnp.zeros((rows, LANES - HD), values.dtype)
    for head in range(H):
        store(head, jnp.concatenate([values[:, head * HD : (head + 1) * HD], blank], axis=1))


def project_kernel(core_ref, norm_ref, mine_ref, other_ref, bias_ref, out_ref, weight, sems):
    step = pl.program_id(0)

    @pl.when(step == 0)
    def _():
        for block in range(3):
            block_copy(core_ref, mine_ref, other_ref, block, weight.at[block], sems.at[block])

    block_wait(mine_ref, weight.at[step], sems.at[step])
    half = norm_ref.shape[0] // 2
    for part in range(2):
        rows = slice(part * half, (part + 1) * half)
        result = product(norm_ref[rows], weight[step]) + bias_ref[0]

        def store(head, value):
            out_ref[0, head, rows] = value

        split_heads(result.astype(bf16), store)


def project_call(core, norm, mine, other, bias):
    seq_len, width = norm.shape
    return pl.pallas_call(
        project_kernel,
        grid=(3,),
        in_specs=[
            smem,
            whole_block(norm),
            anywhere,
            anywhere,
            pl.BlockSpec((1, 1, width), lambda i: (i, 0, 0)),
        ],
        out_specs=pl.BlockSpec((1, H, seq_len, LANES), lambda i: (i, 0, 0, 0)),
        out_shape=jax.ShapeDtypeStruct((3, H, seq_len, LANES), bf16),
        scratch_shapes=[pltpu.VMEM((3, width, width), bf16), pltpu.SemaphoreType.DMA((3,))],
        compiler_params=params(),
        cost_estimate=cost(6 * seq_len * width * width, 12 * seq_len * width + 6 * width * width),
    )(core, norm, mine, other, bias)


def attend_kernel(query_ref, key_ref, value_ref, mix_ref, log_ref, *, size, factor):
    turned_value = value_ref[0, 0].T
    for part in range(query_ref.shape[2] // size):
        rows = slice(part * size, (part + 1) * size)
        scores = product(key_ref[0, 0], query_ref[0, 0, rows], right_turned)
        top = jnp.max(scores, axis=0, keepdims=True)
        weights = jnp.exp2((scores - top) * factor)
        total = jnp.sum(weights, axis=0, keepdims=True)
        mix = product(turned_value, weights.astype(bf16))
        mix_ref[0, rows] = (mix / total).T.astype(bf16)
        log_ref[0, :, rows] = top * factor + jnp.log2(total)


def head_block(place, seq_len):
    return pl.BlockSpec((1, 1, seq_len, LANES), lambda h: (place, h, 0, 0))


def attend_call(projected):
    seq_len = projected.shape[2]
    flat = pl.BlockSpec((1, seq_len, LANES), lambda h: (h, 0, 0))
    return pl.pallas_call(
        functools.partial(
            attend_kernel, size=seq_len, factor=math.log2(math.e) / math.sqrt(HD)
        ),
        grid=(H,),
        in_specs=[head_block(place, seq_len) for place in range(3)],
        out_specs=[flat, pl.BlockSpec((1, 1, seq_len), lambda h: (h, 0, 0))],
        out_shape=[
            jax.ShapeDtypeStruct((H, seq_len, LANES), bf16),
            jax.ShapeDtypeStruct((H, 1, seq_len), f32),
        ],
        compiler_params=params(),
        cost_estimate=cost(4 * H * seq_len * seq_len * 256, 8 * H * seq_len * LANES, H * seq_len * seq_len),
    )(projected, projected, projected)


def attend_back_kernel(
    query_ref, key_ref, value_ref, mix_ref, log_ref, grad_ref, query_grad_ref, key_grad_ref,
    value_grad_ref, key_sum, value_sum, *, size, factor
):
    key, value = key_ref[0, 0], value_ref[0, 0]
    turned_key = key.T
    base_two = factor * math.log2(math.e)
    for part in range(query_ref.shape[2] // size):
        rows = slice(part * size, (part + 1) * size)
        query, grad = query_ref[0, 0, rows], grad_ref[0, rows]
        scores = product(key, query, right_turned)
        weights = jnp.exp2(scores * base_two - log_ref[0, :, rows])
        value_part = product(weights.astype(bf16), grad)
        weight_grad = product(value, grad, right_turned)
        inner = column_sum((grad.astype(f32) * mix_ref[0, rows].astype(f32)).T)
        score_grad = (weights * (weight_grad - inner)).astype(bf16)
        key_part = product(score_grad, query)
        query_grad_ref[0, rows] = (product(turned_key, score_grad) * factor).T.astype(bf16)
        if part == 0:
            key_sum[...] = key_part
            value_sum[...] = value_part
        else:
            key_sum[...] += key_part
            value_sum[...] += value_part
    key_grad_ref[0] = (key_sum[...] * factor).astype(bf16)
    value_grad_ref[0] = value_sum[...].astype(bf16)


def attend_back_call(projected, mix, logs, grad):
    seq_len = projected.shape[2]
    flat = pl.BlockSpec((1, seq_len, LANES), lambda h: (h, 0, 0))
    return pl.pallas_call(
        functools.partial(attend_back_kernel, size=seq_len // 2, factor=1.0 / math.sqrt(HD)),
        grid=(H,),
        in_specs=[head_block(place, seq_len) for place in range(3)]
        + [flat, pl.BlockSpec((1, 1, seq_len), lambda h: (h, 0, 0)), flat],
        out_specs=[flat] * 3,
        out_shape=[jax.ShapeDtypeStruct((H, seq_len, LANES), bf16)] * 3,
        scratch_shapes=[pltpu.VMEM((seq_len, LANES), f32)] * 2,
        compiler_params=params(),
        cost_estimate=cost(10 * H * seq_len * seq_len * 256, 16 * H * seq_len * LANES, H * seq_len * seq_len),
    )(projected, projected, projected, mix, logs, grad)


def join_heads(read):
    return jnp.concatenate([read(head)[:, :HD] for head in range(H)], axis=1)


def mix_kernel(
    core_ref, mix_ref, start_ref, mine_ref, other_ref, bias_ref, mod_ref, joined_ref, branch_ref,
    middle_ref, norm_ref, weight, sem
):
    @pl.when(pl.program_id(0) == 0)
    def _():
        block_copy(core_ref, mine_ref, other_ref, 3, weight, sem)
        block_wait(mine_ref, weight, sem)

    joined = join_heads(lambda head: mix_ref[head])
    joined_ref[...] = joined
    branch = product(joined, weight[...]) + bias_ref[...]
    branch_ref[...] = branch
    middle = start_ref[...] + mod_ref[2:3] * branch
    middle_ref[...] = middle
    unit, _ = normalize(middle)
    norm_ref[...] = (unit * (1.0 + mod_ref[4:5]) + mod_ref[3:4]).astype(bf16)


def mix_call(core, mix, start, mine, other, bias, mod):
    seq_len, width = start.shape
    rows = seq_len // 4
    block = row_block(rows, width)
    return pl.pallas_call(
        mix_kernel,
        grid=(4,),
        in_specs=[
            smem,
            pl.BlockSpec((H, rows, LANES), lambda i: (0, i, 0)),
            block,
            anywhere,
            anywhere,
            whole_block(bias),
            whole_block(mod),
        ],
        out_specs=[block] * 4,
        out_shape=[
            jax.ShapeDtypeStruct((seq_len, width), kind) for kind in (bf16, f32, f32, bf16)
        ],
        scratch_shapes=[pltpu.VMEM((width, width), bf16), pltpu.SemaphoreType.DMA],
        compiler_params=params(),
        cost_estimate=cost(2 * seq_len * width * width, 18 * seq_len * width),
    )(core, mix, start, mine, other, bias, mod)


def gelu_parts(values):
    inner = 0.7978845608028654 * (values + 0.044715 * values * values * values)
    turned = jnp.tanh(inner)
    half = 0.5 * (1.0 + turned)
    slope = half + 0.5 * values * (1.0 - turned * turned) * (
        0.7978845608028654 * (1.0 + 0.134145 * values * values)
    )
    return values * half, slope


def feed_kernel(
    norm_ref, middle_ref, cot_ref, branch_ref, mod_ref, up_bias_ref, down_bias_ref, up_mine, up_other,
    down_mine, down_other, out_ref, hidden_ref, pre_ref, grad_two_ref, middle_grad_ref, grad_one_ref,
    sums_ref, up_sums_ref, up, down, slopes, sems
):
    step = pl.program_id(0)
    chunks = 4

    def copies(chunk):
        up_from, down_from = (up_mine, down_mine) if chunk < 2 else (up_other, down_other)
        place = chunk % 2
        return (
            pltpu.make_async_copy(up_from.at[place], up.at[chunk], sems.at[0, chunk]),
            pltpu.make_async_copy(down_from.at[place], down.at[chunk], sems.at[1, chunk]),
        )

    @pl.when(step == 0)
    def _():
        for chunk in range(chunks):
            for copy in copies(chunk):
                copy.start()
        sums_ref[...] = jnp.zeros_like(sums_ref)
        up_sums_ref[...] = jnp.zeros_like(up_sums_ref)

    norm = norm_ref[...]
    total = None
    for chunk in range(chunks):

        @pl.when(step == 0)
        def _():
            for copy in copies(chunk):
                copy.wait()

        before = product(norm, up[chunk]) + up_bias_ref[chunk]
        hidden, slope = gelu_parts(before)
        hidden = hidden.astype(bf16)
        hidden_ref[chunk] = hidden
        slopes[chunk] = slope.astype(slopes.dtype)
        part = product(hidden, down[chunk])
        total = part if total is None else total + part
    branch_two = total + down_bias_ref[...]
    middle, cot = middle_ref[...], cot_ref[...]
    gate_two = mod_ref[5:6]
    out_ref[...] = middle + gate_two * branch_two
    grad_two = (gate_two * cot).astype(bf16)
    grad_two_ref[...] = grad_two
    sums_ref[0:1] += column_sum(cot * branch_two)
    sums_ref[1:2] += column_sum(grad_two.astype(f32))
    total = None
    for chunk in range(chunks):
        pre = (product(grad_two, down[chunk], right_turned) * slopes[chunk].astype(f32)).astype(bf16)
        pre_ref[chunk] = pre
        up_sums_ref[chunk] += column_sum(pre.astype(f32))
        part = product(pre, up[chunk], right_turned)
        total = part if total is None else total + part
    unit, inverse = normalize(middle)
    sums_ref[2:3] += column_sum(total * unit)
    sums_ref[3:4] += column_sum(total)
    middle_grad = cot + normalize_back(total, unit, inverse, mod_ref[4:5])
    middle_grad_ref[...] = middle_grad
    sums_ref[4:5] += column_sum(middle_grad * branch_ref[...])
    grad_one = (mod_ref[2:3] * middle_grad).astype(bf16)
    grad_one_ref[...] = grad_one
    sums_ref[5:6] += column_sum(grad_one.astype(f32))


def feed_call(norm, middle, cot, branch, mod, up_bias, down_bias, up_mine, up_other, down_mine, down_other):
    seq_len, width = middle.shape
    steps = 4
    rows = seq_len // steps
    block = row_block(rows, width)
    chunked = pl.BlockSpec((4, rows, width), lambda i: (0, i, 0))
    wide = jax.ShapeDtypeStruct((4, seq_len, width), bf16)
    return pl.pallas_call(
        feed_kernel,
        grid=(steps,),
        in_specs=[
            block,
            block,
            block,
            block,
            whole_block(mod),
            whole_block(up_bias),
            whole_block(down_bias),
            anywhere,
            anywhere,
            anywhere,
            anywhere,
        ],
        out_specs=[
            block,
            chunked,
            chunked,
            block,
            block,
            block,
            pl.BlockSpec((8, width), lambda i: (0, 0)),
            pl.BlockSpec((4, 1, width), lambda i: (0, 0, 0)),
        ],
        out_shape=[
            jax.ShapeDtypeStruct((seq_len, width), f32),
            wide,
            wide,
            jax.ShapeDtypeStruct((seq_len, width), bf16),
            jax.ShapeDtypeStruct((seq_len, width), f32),
            jax.ShapeDtypeStruct((seq_len, width), bf16),
            jax.ShapeDtypeStruct((8, width), f32),
            jax.ShapeDtypeStruct((4, 1, width), f32),
        ],
        scratch_shapes=[
            pltpu.VMEM((4, width, width), bf16),
            pltpu.VMEM((4, width, width), bf16),
            pltpu.VMEM((4, rows, width), f32),
            pltpu.SemaphoreType.DMA((2, 4)),
        ],
        compiler_params=params(),
        cost_estimate=cost(32 * seq_len * width * width, 60 * seq_len * width, 4 * seq_len * width),
    )(norm, middle, cot, branch, mod, up_bias, down_bias, up_mine, up_other, down_mine, down_other)


def feed_weight_kernel(norm_ref, pre_ref, hidden_ref, grad_ref, out_ref):
    step = pl.program_id(0)

    @pl.when(step < 2)
    def _():
        out_ref[0] = product(norm_ref[...], pre_ref[0], left_turned).astype(bf16)

    @pl.when(step >= 2)
    def _():
        out_ref[0] = product(hidden_ref[0], grad_ref[...], left_turned).astype(bf16)


def feed_weight_call(norm, pre, hidden, grad, first):
    seq_len, width = norm.shape
    block = (1, seq_len, width)
    return pl.pallas_call(
        feed_weight_kernel,
        grid=(4,),
        in_specs=[
            whole_block(norm),
            pl.BlockSpec(block, lambda i: (first + jnp.minimum(i, 1), 0, 0)),
            pl.BlockSpec(block, lambda i: (first + jnp.maximum(i - 2, 0), 0, 0)),
            whole_block(grad),
        ],
        out_specs=pl.BlockSpec((1, width, width), lambda i: (i, 0, 0)),
        out_shape=jax.ShapeDtypeStruct((4, width, width), bf16),
        compiler_params=params(),
        cost_estimate=cost(8 * seq_len * width * width, 12 * seq_len * width + 8 * width * width),
    )(norm, pre, hidden, grad)


def attention_weight_kernel(block_ref, norm_ref, joined_ref, projected_ref, grad_ref, out_ref):
    block = block_ref[pl.program_id(0)]

    @pl.when(block < 3)
    def _():
        out_ref[0] = product(norm_ref[...], projected_ref[0], left_turned).astype(bf16)

    @pl.when(block == 3)
    def _():
        out_ref[0] = product(joined_ref[...], grad_ref[...], left_turned).astype(bf16)


def attention_weight_call(blocks, norm, joined, projected_grad, grad_one):
    seq_len, width = norm.shape
    full = pl.BlockSpec((seq_len, width), lambda i, b: (0, 0))
    return pl.pallas_call(
        attention_weight_kernel,
        grid_spec=pltpu.PrefetchScalarGridSpec(
            num_scalar_prefetch=1,
            grid=(2,),
            in_specs=[
                full,
                full,
                pl.BlockSpec((1, seq_len, width), lambda i, b: (jnp.minimum(b[i], 2), 0, 0)),
                full,
            ],
            out_specs=pl.BlockSpec((1, width, width), lambda i, b: (i, 0, 0)),
        ),
        out_shape=jax.ShapeDtypeStruct((2, width, width), bf16),
        compiler_params=params(),
        cost_estimate=cost(4 * seq_len * width * width, 10 * seq_len * width + 4 * width * width),
    )(blocks, norm, joined, projected_grad, grad_one)


def mix_grad_kernel(core_ref, grad_ref, mine_ref, other_ref, out_ref, weight, sem):
    @pl.when(pl.program_id(0) == 0)
    def _():
        block_copy(core_ref, mine_ref, other_ref, 3, weight, sem)
        block_wait(mine_ref, weight, sem)

    def store(head, value):
        out_ref[head] = value

    split_heads(product(grad_ref[...], weight[...], right_turned).astype(bf16), store)


def mix_grad_call(core, grad_one, mine, other):
    seq_len, width = grad_one.shape
    rows = seq_len // 2
    return pl.pallas_call(
        mix_grad_kernel,
        grid=(2,),
        in_specs=[smem, row_block(rows, width), anywhere, anywhere],
        out_specs=pl.BlockSpec((H, rows, LANES), lambda i: (0, i, 0)),
        out_shape=jax.ShapeDtypeStruct((H, seq_len, LANES), bf16),
        scratch_shapes=[pltpu.VMEM((width, width), bf16), pltpu.SemaphoreType.DMA],
        compiler_params=params(),
        cost_estimate=cost(2 * seq_len * width * width, 8 * seq_len * width),
    )(core, grad_one, mine, other)


def start_back_kernel(
    core_ref, count_ref, index_row_ref, index_ref, query_ref, key_ref, value_ref, mine_ref, other_ref,
    middle_grad_ref, start_ref, mod_ref, joined_ref, row_grad_ref, slot_ref, sums_ref, weight, slots, sems
):
    step = pl.program_id(0)
    rows, width = start_ref.shape
    slot_count = slots.shape[0]

    @pl.when(step == 0)
    def _():
        for block in range(3):
            block_copy(core_ref, mine_ref, other_ref, block, weight.at[block], sems.at[block])
        sums_ref[...] = jnp.zeros_like(sums_ref)

    total = None
    for block, ref in enumerate((query_ref, key_ref, value_ref)):
        joined = join_heads(lambda head: ref[head])
        joined_ref[block] = joined
        if block != 1:
            place = block // 2
            sums_ref[place : place + 1] += column_sum(joined.astype(f32))

        @pl.when(step == 0)
        def _():
            block_wait(mine_ref, weight.at[block], sems.at[block])

        part = product(joined, weight[block], right_turned)
        total = part if total is None else total + part
    unit, inverse = normalize(start_ref[...])
    sums_ref[2:3] += column_sum(total * unit)
    sums_ref[3:4] += column_sum(total)
    row_grad = middle_grad_ref[...] + normalize_back(total, unit, inverse, mod_ref[1:2])
    row_low = row_grad.astype(bf16)
    row_grad_ref[...] = row_low
    base = step * rows
    place = lax.broadcasted_iota(jnp.int32, (slot_count, rows), 1) + base
    slot = lax.broadcasted_iota(jnp.int32, (slot_count, rows), 0)
    chosen = jnp.where((index_ref[...] == place) & (slot < count_ref[0]), 1.0, 0.0)
    part = product(chosen.astype(bf16), row_low)

    @pl.when(step == 0)
    def _():
        slots[...] = part

    @pl.when(step > 0)
    def _():
        slots[...] += part

    here = lax.broadcasted_iota(jnp.int32, (rows, slot_count), 0) + base
    lane = lax.broadcasted_iota(jnp.int32, (rows, slot_count), 1)
    taken = jnp.where((index_row_ref[...] == here) & (lane < count_ref[0]), 1.0, 0.0)
    empty = 1.0 - jnp.sum(taken, axis=1, keepdims=True)
    sums_ref[4:5] += column_sum(row_grad * empty)

    @pl.when(step == pl.num_programs(0) - 1)
    def _():
        slot_ref[...] = slots[...].astype(bf16)


def start_back_call(core, count, index, query_grad, key_grad, value_grad, mine, other, middle_grad, start, mod):
    seq_len, width = start.shape
    slot_count = index.shape[1]
    steps = 4
    rows = seq_len // steps
    heads = pl.BlockSpec((H, rows, LANES), lambda i: (0, i, 0))
    block = row_block(rows, width)
    column = index.reshape(slot_count, 1)
    return pl.pallas_call(
        start_back_kernel,
        grid=(steps,),
        in_specs=[
            smem,
            smem,
            whole_block(index),
            whole_block(column),
            heads,
            heads,
            heads,
            anywhere,
            anywhere,
            block,
            block,
            whole_block(mod),
        ],
        out_specs=[
            pl.BlockSpec((3, rows, width), lambda i: (0, i, 0)),
            block,
            pl.BlockSpec((slot_count, width), lambda i: (0, 0)),
            pl.BlockSpec((8, width), lambda i: (0, 0)),
        ],
        out_shape=[
            jax.ShapeDtypeStruct((3, seq_len, width), bf16),
            jax.ShapeDtypeStruct((seq_len, width), bf16),
            jax.ShapeDtypeStruct((slot_count, width), bf16),
            jax.ShapeDtypeStruct((8, width), f32),
        ],
        scratch_shapes=[
            pltpu.VMEM((3, width, width), bf16),
            pltpu.VMEM((slot_count, width), f32),
            pltpu.SemaphoreType.DMA((3,)),
        ],
        compiler_params=params(),
        cost_estimate=cost(8 * seq_len * width * width, 26 * seq_len * width),
    )(core, count, index, column, query_grad, key_grad, value_grad, mine, other, middle_grad, start, mod)


def swap_pairs(size, bit):
    return [(place, place ^ bit) for place in range(size)]


def swap_core(values):
    return lax.ppermute(values, "grp", swap_pairs(lax.axis_size("grp"), 1))


def add_low(*parts):
    total = parts[0].astype(f32)
    for part in parts[1:]:
        total = total + part.astype(f32)
    return total.astype(bf16)


def gather_blocks(shard):
    return lax.all_gather(shard, "tok", axis=1, tiled=True)


def scatter_blocks(mine, other):
    chip = add_low(mine, swap_core(other))
    shard = lax.psum_scatter(chip, "tok", scatter_dimension=1, tiled=True)
    bit = 2
    while bit < lax.axis_size("grp"):
        shard = add_low(shard, lax.ppermute(shard, "grp", swap_pairs(lax.axis_size("grp"), bit)))
        bit *= 2
    return shard


def on_device(
    kept_tokens,
    kept_index,
    kept_count,
    condition,
    mask_token,
    position_table,
    modulation_weight,
    modulation_bias,
    input_weight,
    query_bias,
    value_bias,
    output_weight,
    output_bias,
    up_weight,
    up_bias,
    down_weight,
    down_bias,
    cotangent,
):
    _, seq_len, width = cotangent.shape
    tok_count = lax.axis_size("tok")
    core = lax.axis_index("grp") % 2
    core_row = core.reshape(1)
    share = input_weight.shape[0]
    position_rows = position_table.shape[0]

    def by_core(first, second):
        return jnp.where(core == 0, first, second)

    condition_low = jax.nn.silu(condition).astype(bf16)
    condition_group = lax.all_gather(condition_low, "tok", axis=0, tiled=True)
    modulation_low = modulation_weight.astype(bf16)
    modulation_part = jnp.dot(
        condition_group, modulation_low, preferred_element_type=f32
    ) + modulation_bias.astype(bf16).astype(f32)
    modulation = lax.all_to_all(modulation_part, "tok", split_axis=0, concat_axis=1, tiled=True)
    mod = modulation.reshape(6, width)

    routed = lax.all_to_all(
        kept_tokens.astype(bf16), "tok", split_axis=0, concat_axis=1, tiled=True
    )[0]

    small_parts = [mask_token, query_bias, value_bias, output_bias, down_bias, up_bias]
    small_widths = [part.shape[0] for part in small_parts]
    cuts = [sum(small_widths[:number]) for number in range(len(small_widths) + 1)]
    small_rows = position_rows // 8
    table_rows = position_rows + small_rows
    table_half = table_rows // 2

    def as_rows(parts):
        flat = jnp.concatenate(parts, axis=-1)
        lead = flat.shape[:-1]
        flat = jnp.pad(flat, [(0, 0)] * len(lead) + [(0, small_rows * width - flat.shape[-1])])
        return flat.reshape(lead + (small_rows, width))

    table_shard = jnp.concatenate([position_table, as_rows(small_parts)]).astype(bf16)
    table_mine = gather_blocks(
        lax.dynamic_slice_in_dim(table_shard, core * table_half, table_half, 0)[None]
    )[0].reshape(tok_count, table_half, width)
    table_other = swap_core(table_mine)
    table = jnp.concatenate(
        [by_core(table_mine, table_other), by_core(table_other, table_mine)], axis=1
    )
    position = table[:, :position_rows].reshape(seq_len, width)
    small = table[:, position_rows:].reshape(tok_count, -1)
    mask_full, query_bias_full, value_bias_full, output_bias_full, down_bias_full = (
        small[:, cuts[number] : cuts[number + 1]].reshape(1, width).astype(f32)
        for number in range(5)
    )
    up_bias_full = (
        small[:, cuts[5] : cuts[6]].reshape(tok_count, 4, share).transpose(1, 0, 2).reshape(4, 1, width)
    ).astype(f32)
    up_bias_here = jnp.concatenate(
        [by_core(up_bias_full[:2], up_bias_full[2:]), by_core(up_bias_full[2:], up_bias_full[:2])]
    )

    input_low = input_weight.astype(bf16)
    input_blocks = [input_low[:, number * width : (number + 1) * width] for number in range(3)]
    attention_blocks = jnp.stack(input_blocks + [output_weight.astype(bf16)])
    up_blocks = up_weight.astype(bf16).reshape(share, tok_count, 4, share).transpose(2, 0, 1, 3)
    up_blocks = up_blocks.reshape(4, share, width)
    down_blocks = down_weight.astype(bf16).reshape(4, share, width)
    attention_mine = gather_blocks(by_core(attention_blocks[:2], attention_blocks[2:]))
    attention_other = swap_core(attention_mine)
    up_mine = gather_blocks(by_core(up_blocks[:2], up_blocks[2:]))
    up_other = swap_core(up_mine)
    down_mine = gather_blocks(by_core(down_blocks[:2], down_blocks[2:]))
    down_other = swap_core(down_mine)

    start, norm_one = start_call(kept_count, kept_index, routed, position, mask_full, mod)
    blank = jnp.zeros_like(query_bias_full)
    projected_bias = jnp.stack([query_bias_full, blank, value_bias_full])
    projected = project_call(core_row, norm_one, attention_mine, attention_other, projected_bias)
    mix, logs = attend_call(projected)
    joined, branch_one, middle, norm_two = mix_call(
        core_row, mix, start, attention_mine, attention_other, output_bias_full, mod
    )
    (
        block_output,
        hidden,
        pre_grad,
        grad_two,
        middle_grad,
        grad_one,
        feed_sums,
        up_bias_sum,
    ) = feed_call(
        norm_two, middle, cotangent[0], branch_one, mod, up_bias_here, down_bias_full, up_mine, up_other,
        down_mine, down_other,
    )
    feed_other = feed_weight_call(norm_two, pre_grad, hidden, grad_two, 2)
    feed_mine = feed_weight_call(norm_two, pre_grad, hidden, grad_two, 0)
    feed_shard = scatter_blocks(feed_mine, feed_other)
    mix_grad = mix_grad_call(core_row, grad_one, attention_mine, attention_other)
    query_grad, key_grad, value_grad = attend_back_call(projected, mix, logs, mix_grad)
    projected_grad, row_grad, slot_grad, start_sums = start_back_call(
        core_row, kept_count, kept_index, query_grad, key_grad, value_grad, attention_mine,
        attention_other, middle_grad, start, mod,
    )
    pair = jnp.arange(2, dtype=jnp.int32)
    attention_shard = scatter_blocks(
        attention_weight_call(pair + 2 * core, norm_one, joined, projected_grad, grad_one),
        attention_weight_call(pair + 2 * (1 - core), norm_one, joined, projected_grad, grad_one),
    )
    kept_grad = lax.all_to_all(
        slot_grad[None], "tok", split_axis=1, concat_axis=0, tiled=True
    ).astype(f32)

    up_sums = jnp.concatenate(
        [by_core(up_bias_sum[:2], up_bias_sum[2:]), by_core(up_bias_sum[2:], up_bias_sum[:2])]
    )
    up_sums = up_sums.reshape(4, tok_count, share).transpose(1, 0, 2).reshape(tok_count, -1)
    rows_of = lambda row: row.reshape(tok_count, -1)
    small_grads = as_rows(
        [
            rows_of(start_sums[4]),
            rows_of(start_sums[0]),
            rows_of(start_sums[1]),
            rows_of(feed_sums[5]),
            rows_of(feed_sums[1]),
            up_sums,
        ]
    ).astype(bf16)
    table_grad = jnp.concatenate(
        [row_grad.reshape(tok_count, position_rows, width), small_grads], axis=1
    )
    halves = [
        table_grad[:, :table_half].reshape(1, -1, width),
        table_grad[:, table_half:].reshape(1, -1, width),
    ]
    table_shard_grad = scatter_blocks(by_core(halves[0], halves[1]), by_core(halves[1], halves[0]))[0]

    def both_cores(shard):
        got = swap_core(shard)
        return by_core(shard, got).astype(f32), by_core(got, shard).astype(f32)

    table_total = jnp.concatenate(both_cores(table_shard_grad))
    position_total = table_total[:position_rows]
    small_total = table_total[position_rows:].reshape(-1)
    (
        mask_total,
        query_bias_total,
        value_bias_total,
        output_bias_total,
        down_bias_total,
        up_bias_total,
    ) = (small_total[cuts[number] : cuts[number + 1]] for number in range(6))
    first, second = both_cores(attention_shard)
    input_total = jnp.concatenate([first[0], first[1], second[0]], axis=1)
    output_total = second[1]
    first, second = both_cores(feed_shard)
    up_total = jnp.concatenate([first[:2], second[:2]]).reshape(4, share, tok_count, share)
    up_total = up_total.transpose(1, 2, 0, 3).reshape(share, -1)
    down_total = jnp.concatenate([first[2:], second[2:]]).reshape(-1, width)

    modulation_grad = jnp.concatenate(
        [start_sums[3], start_sums[2], feed_sums[4], feed_sums[3], feed_sums[2], feed_sums[0]]
    ).astype(bf16)[None]
    condition_all = lax.all_gather(condition_group, "grp", axis=0, tiled=True)
    modulation_grad_group = lax.all_to_all(
        modulation_grad, "tok", split_axis=1, concat_axis=0, tiled=True
    )
    modulation_grad_all = lax.all_gather(modulation_grad_group, "grp", axis=0, tiled=True)
    modulation_total = jnp.einsum(
        "id,ie->de", condition_all, modulation_grad_all, preferred_element_type=f32
    )
    modulation_bias_total = jnp.sum(modulation_grad_all.astype(f32), axis=0)
    condition_part = jnp.einsum(
        "ie,de->id", modulation_grad_group, modulation_low, preferred_element_type=f32
    )
    condition_low_grad = jnp.sum(
        lax.all_to_all(condition_part, "tok", split_axis=0, concat_axis=0, tiled=True),
        axis=0,
        keepdims=True,
    )
    _, silu_back = jax.vjp(jax.nn.silu, condition)
    condition_grad = silu_back(condition_low_grad)[0]
    return (
        block_output[None],
        kept_grad,
        condition_grad,
        mask_total,
        position_total,
        modulation_total,
        modulation_bias_total,
        input_total,
        query_bias_total,
        value_bias_total,
        output_total,
        output_bias_total,
        up_total,
        up_bias_total,
        down_total,
        down_bias_total,
    )


def solution(mesh):
    return jax.shard_map(
        on_device,
        mesh=mesh,
        in_specs=(
            P("grp", "tok", None),
            P(("grp", "tok"), None),
            P(("grp", "tok")),
            P(("grp", "tok"), None),
            P("tok"),
            P("tok", None),
            P(None, "tok"),
            P("tok"),
            P("tok", None),
            P("tok"),
            P("tok"),
            P("tok", None),
            P("tok"),
            P("tok", None),
            P("tok"),
            P("tok", None),
            P("tok"),
            P(("grp", "tok"), None, None),
        ),
        out_specs=(
            P(("grp", "tok"), None, None),
            P("grp", "tok", None),
            P(("grp", "tok"), None),
            P("tok"),
            P("tok", None),
            P(None, "tok"),
            P("tok"),
            P("tok", None),
            P("tok"),
            P("tok"),
            P("tok", None),
            P("tok"),
            P("tok", None),
            P("tok"),
            P("tok", None),
            P("tok"),
        ),
        check_vma=False,
    )
```

time: 1340 us -> 1080 us (0.81)
  matrix products: 427 us -> 7.9 us
  waiting for transfers between devices: 209 us -> 564 us
  Pallas kernels: 0 us -> 286 us
  local copies, waits for them, and re-layouts: 228 us -> 56.2 us
  other arithmetic: 217 us -> 67.3 us
  blocking collectives: 190 us -> 51.2 us
    dot_general x27 -> x1, matrix products: 422 us -> 2.74 us  [on_device(): jnp.dot(condition_group, modulation_low, preferred_element_type=f32)]
    pallas_call x0 -> x12, Pallas kernels: none -> 286 us  [the longest x1 73.3 us: feed_call(): pl.pallas_call(feed_kernel, grid=(steps,), in_specs=[block, block, block,...]
    all_gather x5 -> x4, waiting for transfers between devices: 59.1 us -> 276 us  [gather_blocks(): return lax.all_gather(shard, 'tok', axis=1, tiled=True)]
    reduce_scatter x2, waiting for transfers between devices: 102 us -> 242 us  [scatter_blocks(): shard = lax.psum_scatter(chip, 'tok', scatter_dimension=1, tiled=True)]
    unnamed x188 -> x60, local copies, waits for them, and re-layouts: 105 us -> 14.3 us
    convert_element_type x25 -> x15, other arithmetic: 121 us -> 34 us  [the longest x5 25.3 us: add_low(): return total.astype(bf16)]
    unnamed x1 -> x0, blocking collectives: 83.8 us -> none
    reduce_sum x14 -> x1, other arithmetic: 64.6 us -> 0.61 us  [on_device(): modulation_bias_total = jnp.sum(modulation_grad_all.astype(f32), axis=0)]
  transfers between devices with their start and end apart: 30 -> 24, of which waited for: 9 -> 11; matrix products, arithmetic and copies ran while one was open for 36% -> 10% of each run, Pallas kernels for 0% -> 18%
where the time goes in v2:
time: 1080 us; the launch traced here: 1070 us
  waiting for transfers between devices  564 us (52%)
  Pallas kernels  286 us (26%)
  other arithmetic  67.3 us (6%)
  local copies, waits for them, and re-layouts  56.2 us (5%)
  blocking collectives  51.2 us (5%)
  starting transfers between devices  24.4 us (2%)
  between operations  15.7 us (1%)
    all_gather x4, waiting for transfers between devices, gather_blocks(): return lax.all_gather(shard, 'tok', axis=1, tiled=True)  276 us
    reduce_scatter x2, waiting for transfers between devices, scatter_blocks(): shard = lax.psum_scatter(chip, 'tok', scatter_dimension=1, tiled=True)  242 us
    pallas_call x1, Pallas kernels, feed_call(): pl.pallas_call(feed_kernel, grid=(steps,), in_specs=[block, block, block,...  73.3 us
    pallas_call x1, Pallas kernels, attend_back_call(): pl.pallas_call(functools.partial(attend_back_kernel, size=seq_len // 2, f...  46.6 us
    pallas_call x2, Pallas kernels, feed_weight_call(): pl.pallas_call(feed_weight_kernel, grid=(4,), in_specs=[whole_block(norm)...  37.1 us
    ppermute x3, waiting for transfers between devices, scatter_blocks(): lax.ppermute(shard, 'grp', swap_pairs(lax.axis_size('grp'), bit))  32.1 us
    all_gather x1, blocking collectives, on_device(): condition_group = lax.all_gather(condition_low, 'tok', axis=0, tiled=True)  31 us
    pallas_call x1, Pallas kernels, start_back_call(): pl.pallas_call(start_back_kernel, grid=(steps,), in_specs=[smem, smem, wh...  30 us
  transfers between devices with their start and end apart: 24, of which 11 were waited for; matrix products, arithmetic and copies ran while one was open for 10% of the time, Pallas kernels for 18%

profile of v2, /device:TPU:0, one launch (start us, length us, event | category | flops | bytes accessed | tf_op | source)
XLA Modules:
  0.0 1072.9 jit_solution(11762361566628579950)
XLA Ops:
  24.6 76.1 %all-gather.8.cloned.1.call-done.mine_ref = bf16[2,1152,1152]{2,1,0:T(8,128)(2,1)} async-done(((bf16[2,144,1152]{2,1,0:T(8,128)(2,1)}), bf16[2,1152,1152]{2,1,0:T(8,128)(2,1)}) %all-gather.8.cloned.1.call-update) | async-done | bytes 5308432 | tf_op jit(solution)/shard_map/all_gather | solution.py:641
  101.3 42.6 %all-gather.14.cloned.1.call-done = bf16[576,1152]{1,0:T(8,128)(2,1)} async-done(((bf16[72,1152]{1,0:T(8,128)(2,1)}), bf16[576,1152]{1,0:T(8,128)(2,1)}) %all-gather.14.cloned.1.call-update) | async-done | bytes 1327120 | tf_op jit(solution)/shard_map/all_gather | solution.py:641
  144.5 31.0 %all-gather.2 = bf16[8,1,1152]{2,1,0:T(2,128)(2,1)S(1)} all-gather(bf16[1,1,1152]{2,1,0:T(2,128)(2,1)S(1)} %get-tuple-element.67), channel_id=1, replica_groups=mesh['grp'=4,'tok'=8] {'tok'}, dimensions={0}, use_global_device_ids=true | all-gather | bytes 20736 | tf_op jit(solution)/shard_map/all_gather | solution.py:685
  185.0 5.7 all-to-all-done.1
  199.0 67.9 %all-gather.10.cloned.1.call-done.up_mine = bf16[2,1152,1152]{2,1,0:T(8,128)(2,1)} async-done(((bf16[2,144,1152]{2,1,0:T(8,128)(2,1)}), bf16[2,1152,1152]{2,1,0:T(8,128)(2,1)}) %all-gather.10.cloned.1.call-update) | async-done | bytes 5308432 | tf_op jit(solution)/shard_map/all_gather | solution.py:641
  266.9 89.8 %all-gather.12.cloned.1.call-done.down_mine = bf16[2,1152,1152]{2,1,0:T(8,128)(2,1)} async-done(((bf16[2,144,1152]{2,1,0:T(8,128)(2,1)}), bf16[2,1152,1152]{2,1,0:T(8,128)(2,1)}) %all-gather.12.cloned.1.call-update) | async-done | bytes 5308432 | tf_op jit(solution)/shard_map/all_gather | solution.py:641
  363.2 7.1 shard_map.297
  371.6 16.5 %shard_map.298.query_ref.key_ref.value_ref = bf16[3,16,1024,128]{3,2,1,0:T(8,128)(2,1)} custom-call(s32[1]{0:T(128)} %bitcast.core_ref, bf16[1024,1152]{1,0:T(8,128)(2,1)} %get-tuple-element.39.norm_ref, bf16[2,1152,1152]{2,1,0:T(8,128)(2,1)} %all-gather.8.cloned.1.call-done.mine_ref, bf16[2,1152,1152]{2,1,0:T(8,128)(2,1)} %collective-permute-done.1.other_ref, ...), custom_call_target="tpu_custom_call" | custom-call | flops 8153726976 | bytes 22118400 | tf_op jit(solution)/shard_map/pallas_call | solution.py:150
  388.2 29.4 %shard_map.299 = (bf16[16,1024,128]{2,1,0:T(8,128)(2,1)}, f32[16,1,1024]{2,1,0:T(1,128)}) custom-call(bf16[3,16,1024,128]{3,2,1,0:T(8,128)(2,1)} %shard_map.298.query_ref.key_ref.value_ref, bf16[3,16,1024,128]{3,2,1,0:T(8,128)(2,1)} %shard_map.298.query_ref.key_ref.value_ref, bf16[3,16,1024,128]{3,2,1,0:T(8,128)(2,1)} %shard_map.298.query_ref.key_ref.value_ref), custom_call_target="tpu_custom_call" | custom-call | flops 17179869184 | bytes 16777216 | tf_op jit(solution)/shard_map/pallas_call | solution.py:188
  417.6 12.4 %shard_map.300 = (bf16[1024,1152]{1,0:T(8,128)(2,1)}, f32[1024,1152]{1,0:T(8,128)}, f32[1024,1152]{1,0:T(8,128)}, bf16[1024,1152]{1,0:T(8,128)(2,1)}) custom-call(s32[1]{0:T(128)} %bitcast.core_ref, bf16[16,1024,128]{2,1,0:T(8,128)(2,1)} %get-tuple-element.40.mix_ref, f32[1024,1152]{1,0:T(8,128)} %get-tuple-element.41.start_ref, ...), custom_call_target="tpu_custom_call" | custom-call | flops 2717908992 | bytes 21233664 | tf_op jit(solution)/shard_map/pallas_call | solution.py:275
  430.0 73.3 %shard_map.301 = (f32[1024,1152]{1,0:T(8,128)}, bf16[4,1024,1152]{2,1,0:T(8,128)(2,1)}, bf16[4,1024,1152]{2,1,0:T(8,128)(2,1)}, bf16[1024,1152]{1,0:T(8,128)(2,1...) custom-call(bf16[1024,1152]{1,0:T(8,128)(2,1)} %get-tuple-element.42.norm_ref,, ...), custom_call_target="tpu_custom_call" | custom-call | flops 43486543872 | bytes 70778880 | tf_op jit(solution)/shard_map/pallas_call | solution.py:380
  503.3 18.5 %shard_map.308 = bf16[4,1152,1152]{2,1,0:T(8,128)(2,1)} custom-call(bf16[1024,1152]{1,0:T(8,128)(2,1)} %get-tuple-element.42.norm_ref, bf16[4,1024,1152]{2,1,0:T(8,128)(2,1)} %get-tuple-element.59.pre_ref, bf16[4,1024,1152]{2,1,0:T(8,128)(2,1)} %get-tuple-element.60.hidden_ref, bf16[1024,1152]{1,0:T(8,128)(2,1)} %get-tuple-element.61.grad_ref), custom_call_target="tpu_custom_call" | custom-call | flops 10871635968 | bytes 24772608 | tf_op jit(solution)/shard_map/pallas_call | solution.py:442
  522.3 8.5 shard_map.302.grad_ref
  530.8 46.6 %shard_map.303 = (bf16[16,1024,128]{2,1,0:T(8,128)(2,1)}, bf16[16,1024,128]{2,1,0:T(8,128)(2,1)}, bf16[16,1024,128]{2,1,0:T(8,128)(2,1)}) custom-call(bf16[3,16,1024,128]{3,2,1,0:T(8,128)(2,1)} %shard_map.298.query_ref.key_ref.value_ref, bf16[3,16,1024,128]{3,2,1,0:T(8,128)(2,1)} %shard_map.298.query_ref.key_ref.value_ref, ...), custom_call_target="tpu_custom_call" | custom-call | flops 42949672960 | bytes 33554432 | tf_op jit(solution)/shard_map/pallas_call | solution.py:235
  577.4 30.0 %shard_map.304 = (bf16[3,1024,1152]{2,1,0:T(8,128)(2,1)}, bf16[1024,1152]{1,0:T(8,128)(2,1)}, bf16[768,1152]{1,0:T(8,128)(2,1)}, f32[8,1152]{1,0:T(8,128)}) custom-call(s32[1]{0:T(128)} %bitcast.core_ref, s32[1]{0:T(128)S(6)} %copy.83.count_ref, s32[1,768]{1,0:T(1,128)} %index_row_ref.1, s32[768,1]{1,0:T(8,128)} %copy.56.index_ref, ...), custom_call_target="tpu_custom_call" | custom-call | flops 10871635968 | bytes 30670848 | tf_op jit(solution)/shard_map/pallas_call | solution.py:586
  607.4 12.6 %shard_map.306 = bf16[2,1152,1152]{2,1,0:T(8,128)(2,1)} custom-call(s32[2]{0:T(128)} %iota_add_fusion.block_ref, bf16[1024,1152]{1,0:T(8,128)(2,1)} %get-tuple-element.39.norm_ref, bf16[1024,1152]{1,0:T(8,128)(2,1)} %get-tuple-element.57.joined_ref, bf16[3,1024,1152]{2,1,0:T(8,128)(2,1)} %get-tuple-element.58.projected_ref, ...), custom_call_target="tpu_custom_call" | custom-call | flops 5435817984 | bytes 17104896 | tf_op jit(solution)/shard_map/pallas_call | solution.py:473
  624.3 6.7 collective-permute-done.4
  633.7 12.8 %shard_map.305 = bf16[2,1152,1152]{2,1,0:T(8,128)(2,1)} custom-call(s32[2]{0:T(128)} %iota_add_fusion.1.block_ref, bf16[1024,1152]{1,0:T(8,128)(2,1)} %get-tuple-element.39.norm_ref, bf16[1024,1152]{1,0:T(8,128)(2,1)} %get-tuple-element.57.joined_ref, bf16[3,1024,1152]{2,1,0:T(8,128)(2,1)} %get-tuple-element.58.projected_ref, ...), custom_call_target="tpu_custom_call" | custom-call | flops 5435817984 | bytes 17104896 | tf_op jit(solution)/shard_map/pallas_call | solution.py:473
  646.5 7.8 add_convert_fusion.1
  654.4 18.6 %shard_map.307 = bf16[4,1152,1152]{2,1,0:T(8,128)(2,1)} custom-call(bf16[1024,1152]{1,0:T(8,128)(2,1)} %get-tuple-element.42.norm_ref, bf16[4,1024,1152]{2,1,0:T(8,128)(2,1)} %get-tuple-element.59.pre_ref, bf16[4,1024,1152]{2,1,0:T(8,128)(2,1)} %get-tuple-element.60.hidden_ref, bf16[1024,1152]{1,0:T(8,128)(2,1)} %get-tuple-element.61.grad_ref), custom_call_target="tpu_custom_call" | custom-call | flops 10871635968 | bytes 24772608 | tf_op jit(solution)/shard_map/pallas_call | solution.py:442
  673.0 13.2 %add_convert_fusion = bf16[4,1152,1152]{2,1,0:T(8,128)(2,1)} fusion(bf16[4,1152,1152]{2,1,0:T(8,128)(2,1)} %collective-permute-done.10, bf16[4,1152,1152]{2,1,0:T(8,128)(2,1)} %shard_map.307), kind=kLoop, calls=%fused_computation | loop fusion | flops 21233664 | bytes 31850496 | tf_op jit(solution)/shard_map/convert_element_type | solution.py:637
  687.7 9.6 all_to_all.53
  708.8 11.6 %reduce.15 = bf16[768,1152]{1,0:T(8,128)(2,1)} reduce(bf16[768,1,1152]{2,1,0:T(2,128)(2,1)S(1)} %bitcast.79, bf16[]{:T(256)} %broadcast.45), dimensions={1}, to_apply=%bitcast.75.reduce_sub_computation | reduce | bytes 3538946
  720.4 5.7 reshape.328
  726.1 6.0 all-to-all-start.2
  732.2 5.3 all_gather.26
  748.3 77.0 %reduce-scatter.7.cloned.1.call-done = bf16[2,144,1152]{2,1,0:T(8,128)(2,1)} async-done(((bf16[2,1152,1152]{2,1,0:T(8,128)(2,1)}), bf16[2,144,1152]{2,1,0:T(8,128)(2,1)}) %reduce-scatter.7.cloned.1.call-update) | async-done | bytes 663568 | tf_op jit(solution)/shard_map/reduce_scatter | solution.py:646
  835.6 5.8 collective-permute-done.8
  842.7 165.3 %reduce-scatter.9.cloned.1.call-done = bf16[4,144,1152]{2,1,0:T(8,128)(2,1)} async-done(((bf16[4,1152,1152]{2,1,0:T(8,128)(2,1)}), bf16[4,144,1152]{2,1,0:T(8,128)(2,1)}) %reduce-scatter.9.cloned.1.call-update) | async-done | bytes 1327120 | tf_op jit(solution)/shard_map/reduce_scatter | solution.py:646
  1012.8 26.3 %collective-permute-done.11 = bf16[4,144,1152]{2,1,0:T(8,128)(2,1)S(1)} collective-permute-done((bf16[4,144,1152]{2,1,0:T(8,128)(2,1)}, bf16[4,144,1152]{2,1,0:T(8,128)(2,1)S(1)}, u32[]{:S(2)}, u32[]{:S(2)}) %collective-permute-start.11) | collective-permute-done | bytes 1327136 | tf_op jit(solution)/shard_map/ppermute | solution.py:649
  1049.3 7.5 copy.63
  1056.8 7.4 reshape.301
  (200 shorter events, 102.6 us)
Async XLA Ops:
  7.2 93.5 %all-gather.8.cloned.1.call-start = ((), (), s32[]{:S(2)}) async-start(), calls=%async_computation.8 | async-start | bytes 5971968 | tf_op jit(solution)/shard_map/all_gather | solution.py:641
  10.2 133.6 %all-gather.14.cloned.1.call-start = ((), (), s32[]{:S(2)}) async-start(), calls=%async_computation.13 | async-start | bytes 1492992 | tf_op jit(solution)/shard_map/all_gather | solution.py:641
  12.7 254.2 %all-gather.10.cloned.1.call-start = ((), (), s32[]{:S(2)}) async-start(), calls=%async_computation.9 | async-start | bytes 5971968 | tf_op jit(solution)/shard_map/all_gather | solution.py:641
  21.5 79.2 %copy-start.15 = (f32[1,1152]{1,0:T(1,128)S(1)}, f32[1,1152]{1,0:T(1,128)}, u32[]{:S(2)}) copy-start(f32[1,1152]{1,0:T(1,128)} %param.21) | copy-start | bytes 13828
  21.5 335.2 %all-gather.12.cloned.1.call-start = ((), (), s32[]{:S(2)}) async-start(), calls=%async_computation.10 | async-start | bytes 5971968 | tf_op jit(solution)/shard_map/all_gather | solution.py:641
  24.5 159.0 %copy-start.3 = (f32[8,96,1152]{2,1,0:T(8,128)S(1)}, f32[8,96,1152]{2,1,0:T(8,128)}, u32[]{:S(2)}) copy-start(f32[8,96,1152]{2,1,0:T(8,128)} %param.18) | copy-start | bytes 10616836
  100.7 271.0 %collective-permute-start.1 = (bf16[2,1152,1152]{2,1,0:T(8,128)(2,1)}, bf16[2,1152,1152]{2,1,0:T(8,128)(2,1)}, u32[]{:S(2)}, u32[]{:S(2)}) collective-permute-start(bf16[2,1152,1152]{2,1,0:T(8,128)(2,1)} %all-gather.8.cloned.1.call-done.mine_ref), channel_id=1, source_target_pairs={{0,8},{8,0},{16,24},{24,16},{1,9},{9,1},{17,25},{25,17},{2,10},{10... | collective-permute-start | bytes 15925256 | tf_op jit(solution)/shard_map/ppermute | solution.py:630
  143.8 212.9 %collective-permute-start = (bf16[8,72,1152]{2,1,0:T(8,128)(2,1)}, bf16[8,72,1152]{2,1,0:T(8,128)(2,1)}, u32[]{:S(2)}, u32[]{:S(2)}) collective-permute-start(bf16[8,72,1152]{2,1,0:T(8,128)(2,1)} %bitcast.88), channel_id=1, source_target_pairs={{0,8},{8,0},{16,24},{24,16},{1,9},{9,1},{17,25},{25,17},{2,10},{10... | collective-permute-start | bytes 3981320 | tf_op jit(solution)/shard_map/ppermute | solution.py:630
  179.6 11.1 %all-to-all-start.1 = ((f32[8,1,864]{2,1,0:T(1,128)}), f32[8,1,864]{2,1,0:T(1,128)}, u32[]{:S(2)}, u32[]{:S(2)}) async-start(f32[8,1,864]{2,1,0:T(1,128)} %copy.53), calls=%async_computation.1 | async-start | bytes 57344 | tf_op jit(solution)/shard_map/all_to_all | solution.py:690
  190.7 172.5 %all-to-all-start = ((bf16[8,96,1152]{2,1,0:T(8,128)(2,1)}), bf16[8,96,1152]{2,1,0:T(8,128)(2,1)}, u32[]{:S(2)}, u32[]{:S(2)}) async-start(bf16[8,96,1152]{2,1,0:T(8,128)(2,1)} %convert_element_type.203), calls=%async_computation | async-start | bytes 3538944 | tf_op jit(solution)/shard_map/all_to_all | solution.py:693
  195.0 551.7 %reduce-scatter.11.cloned.1.call-start = ((), (), s32[]{:S(2)}) async-start(), calls=%async_computation.14 | async-start | bytes 1492992
  266.9 163.1 %collective-permute-start.2 = (bf16[2,1152,1152]{2,1,0:T(8,128)(2,1)}, bf16[2,1152,1152]{2,1,0:T(8,128)(2,1)}, u32[]{:S(2)}, u32[]{:S(2)}) collective-permute-start(bf16[2,1152,1152]{2,1,0:T(8,128)(2,1)} %all-gather.10.cloned.1.call-done.up_mine), channel_id=1, source_target_pairs={{0,8},{8,0},{16,24},{24,16},{1,9},{9,1},{17,25},{25,17},{2,10},{10... | collective-permute-start | bytes 15925256 | tf_op jit(solution)/shard_map/ppermute | solution.py:630
  356.7 73.3 %collective-permute-start.3 = (bf16[2,1152,1152]{2,1,0:T(8,128)(2,1)}, bf16[2,1152,1152]{2,1,0:T(8,128)(2,1)}, u32[]{:S(2)}, u32[]{:S(2)}) collective-permute-start(bf16[2,1152,1152]{2,1,0:T(8,128)(2,1)} %all-gather.12.cloned.1.call-done.down_mine), channel_id=1, source_target_pairs={{0,8},{8,0},{16,24},{24,16},{1,9},{9,1},{17,25},{25,17},{2,10},{10... | collective-permute-start | bytes 15925256 | tf_op jit(solution)/shard_map/ppermute | solution.py:630
  521.7 151.3 %collective-permute-start.10 = (bf16[4,1152,1152]{2,1,0:T(8,128)(2,1)}, bf16[4,1152,1152]{2,1,0:T(8,128)(2,1)}, u32[]{:S(2)}, u32[]{:S(2)}) collective-permute-start(bf16[4,1152,1152]{2,1,0:T(8,128)(2,1)} %shard_map.308), channel_id=1, source_target_pairs={{0,8},{8,0},{16,24},{24,16},{1,9},{9,1},{17,25},{25,17},{2,10},{10... | collective-permute-start | bytes 31850504 | tf_op jit(solution)/shard_map/ppermute | solution.py:630
  607.4 12.7 %copy-start.12 = (f32[8,1152]{1,0:T(8,128)S(1)}, f32[8,1152]{1,0:T(8,128)}, u32[]{:S(2)}) copy-start(f32[8,1152]{1,0:T(8,128)} %get-tuple-element.54) | copy-start | bytes 110596
  607.4 12.8 %copy-start.14 = (f32[4,1,1152]{2,1,0:T(1,128)S(1)}, f32[4,1,1152]{2,1,0:T(1,128)}, u32[]{:S(2)}) copy-start(f32[4,1,1152]{2,1,0:T(1,128)} %get-tuple-element.56) | copy-start | bytes 55300
  607.4 13.8 %copy-start = (bf16[1024,1152]{1,0:T(8,128)(2,1)S(1)}, bf16[1024,1152]{1,0:T(8,128)(2,1)}, u32[]{:S(2)}) copy-start(bf16[1024,1152]{1,0:T(8,128)(2,1)} %get-tuple-element.55) | copy-start | bytes 7077892
  620.1 26.5 %collective-permute-start.7 = (bf16[2,1152,1152]{2,1,0:T(8,128)(2,1)}, bf16[2,1152,1152]{2,1,0:T(8,128)(2,1)}, u32[]{:S(2)}, u32[]{:S(2)}) collective-permute-start(bf16[2,1152,1152]{2,1,0:T(8,128)(2,1)} %shard_map.306), channel_id=1, source_target_pairs={{0,8},{8,0},{16,24},{24,16},{1,9},{9,1},{17,25},{25,17},{2,10},{10... | collective-permute-start | bytes 15925256 | tf_op jit(solution)/shard_map/ppermute | solution.py:630
  623.3 7.7 collective-permute-start.4
  633.7 191.7 %reduce-scatter.7.cloned.1.call-start = ((), (), s32[]{:S(2)}) async-start(), calls=%async_computation.11 | async-start | bytes 5971968 | tf_op jit(solution)/shard_map/reduce_scatter | solution.py:646
  654.4 353.6 %reduce-scatter.9.cloned.1.call-start = ((), (), s32[]{:S(2)}) async-start(), calls=%async_computation.12 | async-start | bytes 11943936 | tf_op jit(solution)/shard_map/reduce_scatter | solution.py:646
  700.6 25.5 %all-to-all-start.4 = ((f32[8,1,1152]{2,1,0:T(1,128)}), f32[8,1,1152]{2,1,0:T(1,128)}, u32[]{:S(2)}, u32[]{:S(2)}) async-start(f32[8,1,1152]{2,1,0:T(1,128)} %copy.59), calls=%async_computation.4 | async-start | bytes 73728 | tf_op jit(solution)/shard_map/all_to_all | solution.py:846
  726.1 101.3 %all-to-all-start.2 = ((bf16[8,2,55296]{2,1,0:T(2,128)(2,1)}), bf16[8,2,55296]{2,1,0:T(2,128)(2,1)}, u32[]{:S(2)}, u32[]{:S(2)}) async-start(bf16[8,2,55296]{2,1,0:T(2,128)(2,1)} %reshape.328), calls=%async_computation.2 | async-start | bytes 3538944 | tf_op jit(solution)/shard_map/all_to_all | solution.py:779
  732.1 94.7 %copy-start.16 = (f32[1,1152]{1,0:T(1,128)S(1)}, f32[1,1152]{1,0:T(1,128)}, u32[]{:S(2)}) copy-start(f32[1,1152]{1,0:T(1,128)} %param.21) | copy-start | bytes 13828
  732.1 94.6 %copy-start.17 = (f32[1,1152]{1,0:T(1,128)S(1)}, f32[1,1152]{1,0:T(1,128)}, u32[]{:S(2)}) copy-start(f32[1,1152]{1,0:T(1,128)} %get-tuple-element.68) | copy-start | bytes 13828
  746.8 87.7 %collective-permute-start.5 = (bf16[1,72,1152]{2,1,0:T(8,128)(2,1)}, bf16[1,72,1152]{2,1,0:T(8,128)(2,1)}, u32[]{:S(2)}, u32[]{:S(2)}) collective-permute-start(bf16[1,72,1152]{2,1,0:T(8,128)(2,1)} %reduce-scatter.11.cloned.1.call-done), channel_id=1, source_target_pairs={{0,16},{8,24},{16,0},{24,8},{1,17},{9,25},{17,1},{25,9},{2,18},{10... | collective-permute-start | bytes 497672 | tf_op jit(solution)/shard_map/ppermute | solution.py:649
  825.3 16.1 %collective-permute-start.8 = (bf16[2,144,1152]{2,1,0:T(8,128)(2,1)}, bf16[2,144,1152]{2,1,0:T(8,128)(2,1)}, u32[]{:S(2)}, u32[]{:S(2)}) collective-permute-start(bf16[2,144,1152]{2,1,0:T(8,128)(2,1)} %reduce-scatter.7.cloned.1.call-done), channel_id=1, source_target_pairs={{0,16},{8,24},{16,0},{24,8},{1,17},{9,25},{17,1},{25,9},{2,18},{10... | collective-permute-start | bytes 1990664 | tf_op jit(solution)/shard_map/ppermute | solution.py:649
  835.5 174.0 %collective-permute-start.6 = (bf16[72,1152]{1,0:T(8,128)(2,1)S(1)}, bf16[72,1152]{1,0:T(8,128)(2,1)}, u32[]{:S(2)}, u32[]{:S(2)}) collective-permute-start(bf16[72,1152]{1,0:T(8,128)(2,1)S(1)} %fusion.4), channel_id=1, source_target_pairs={{0,8},{8,0},{16,24},{24,16},{1,9},{9,1},{17,25},{25,17},{2,10},{10... | collective-permute-start | bytes 497672 | tf_op jit(solution)/shard_map/ppermute | solution.py:630
  842.6 170.0 %collective-permute-start.9 = (bf16[2,144,1152]{2,1,0:T(8,128)(2,1)S(1)}, bf16[2,144,1152]{2,1,0:T(8,128)(2,1)S(1)}, u32[]{:S(2)}, u32[]{:S(2)}) collective-permute-start(bf16[2,144,1152]{2,1,0:T(8,128)(2,1)S(1)} %add_convert_fusion.3), channel_id=1, source_target_pairs={{0,8},{8,0},{16,24},{24,16},{1,9},{9,1},{17,25},{25,17},{2,10},{10... | collective-permute-start | bytes 1990664 | tf_op jit(solution)/shard_map/ppermute | solution.py:630
  1008.0 31.1 %collective-permute-start.11 = (bf16[4,144,1152]{2,1,0:T(8,128)(2,1)}, bf16[4,144,1152]{2,1,0:T(8,128)(2,1)S(1)}, u32[]{:S(2)}, u32[]{:S(2)}) collective-permute-start(bf16[4,144,1152]{2,1,0:T(8,128)(2,1)} %reduce-scatter.9.cloned.1.call-done), channel_id=1, source_target_pairs={{0,16},{8,24},{16,0},{24,8},{1,17},{9,25},{17,1},{25,9},{2,18},{10... | collective-permute-start | bytes 3981320 | tf_op jit(solution)/shard_map/ppermute | solution.py:649
  1011.8 27.3 %copy-start.5 = (bf16[4,144,1152]{2,1,0:T(8,128)(2,1)S(1)}, bf16[4,144,1152]{2,1,0:T(8,128)(2,1)}, u32[]{:S(2)}) copy-start(bf16[4,144,1152]{2,1,0:T(8,128)(2,1)} %reduce-scatter.9.cloned.1.call-done) | copy-start | bytes 3981316
  1039.4 3.1 collective-permute-start.12
  (15 other events, 67.8 us)
Sparse Core Ops, SparseCore 0:
  10.8 89.7 all-gather.7
  103.4 40.3 all-gather.13
  146.7 120.1 all-gather.9
  269.6 87.0 all-gather.11
  633.8 60.8 reduce-scatter.10
  698.2 127.0 reduce-scatter.6
  828.9 179.0 reduce-scatter.8

commit v3 on v2

v3 whole, which is shorter than its diff:
```python
import functools
import math

import jax
import jax.numpy as jnp
from jax import lax
from jax.experimental import pallas as pl
from jax.experimental.pallas import tpu as pltpu
from jax.sharding import PartitionSpec as P

H = 16
HD = 72
LANES = 128

epsilon = 1e-06
f32 = jnp.float32
bf16 = jnp.bfloat16
plain = (((1,), (0,)), ((), ()))
right_turned = (((1,), (1,)), ((), ()))
left_turned = (((0,), (0,)), ((), ()))
vmem_limit = 60 << 20


def product(left, right, dims=plain):
    return lax.dot_general(left, right, dims, preferred_element_type=f32)


def whole_block(array):
    zeros = (0,) * array.ndim
    return pl.BlockSpec(array.shape, lambda *_: zeros)


def row_block(rows, *rest):
    return pl.BlockSpec((rows,) + rest, lambda i: (i,) + (0,) * len(rest))


smem = pl.BlockSpec(memory_space=pltpu.SMEM)
anywhere = pl.BlockSpec(memory_space=pl.ANY)


def params():
    return pltpu.CompilerParams(vmem_limit_bytes=vmem_limit)


def cost(flops, moved, exps=0):
    return pl.CostEstimate(flops=int(flops), bytes_accessed=int(moved), transcendentals=int(exps))


def column_sum(values):
    return jnp.sum(values, axis=0, keepdims=True)


def normalize(values):
    center = values - jnp.mean(values, axis=-1, keepdims=True)
    spread = jnp.mean(center * center, axis=-1, keepdims=True)
    inverse = lax.rsqrt(spread + epsilon)
    return center * inverse, inverse


def normalize_back(grad, unit, inverse, scale):
    scaled = grad * (1.0 + scale)
    first = jnp.mean(scaled, axis=-1, keepdims=True)
    second = jnp.mean(scaled * unit, axis=-1, keepdims=True)
    return (scaled - first - unit * second) * inverse


def start_kernel(core_ref, places_ref, count_ref, index_ref, kept_ref, mask_ref, mod_ref, *rest, chunks, row, share):
    refs, (start_ref, norm_ref, table, sems) = rest[: len(chunks.arrays)], rest[len(chunks.arrays) :]
    rows, slots = start_ref.shape[0], kept_ref.shape[0]
    step = pl.program_id(0)
    low, high = table.at[:, :share], table.at[:, share:]

    @pl.when(step == 0)
    def _():
        @pl.when(core_ref[0] == 0)
        def _():
            chunks.load(refs, places_ref, True, row, low, sems.at[0])
            chunks.load(refs, places_ref, False, row, high, sems.at[1])

        @pl.when(core_ref[0] != 0)
        def _():
            chunks.load(refs, places_ref, False, row, low, sems.at[0])
            chunks.load(refs, places_ref, True, row, high, sems.at[1])

        wait_block(low, sems.at[0])
        wait_block(high, sems.at[1])

    base = step * rows
    here = lax.broadcasted_iota(jnp.int32, (rows, slots), 0) + base
    slot = lax.broadcasted_iota(jnp.int32, (rows, slots), 1)
    chosen = jnp.where((index_ref[...] == here) & (slot < count_ref[0]), 1.0, 0.0)
    filled = product(chosen.astype(bf16), kept_ref[...])
    empty = 1.0 - jnp.sum(chosen, axis=1, keepdims=True)
    groups_here = rows // table.shape[1]
    position = table[pl.ds(step * groups_here, groups_here)].reshape(rows, -1)
    start = filled + empty * mask_ref[...] + position.astype(f32)
    start_ref[...] = start
    unit, _ = normalize(start)
    norm_ref[...] = (unit * (1.0 + mod_ref[1:2]) + mod_ref[0:1]).astype(bf16)


def start_call(core, places, count, index, kept, mask, mod, chunks, row, share, seq_len):
    width = kept.shape[1]
    rows = seq_len // 4
    return pl.pallas_call(
        functools.partial(start_kernel, chunks=chunks, row=row, share=share),
        grid=(4,),
        in_specs=[
            smem,
            smem,
            smem,
            whole_block(index),
            whole_block(kept),
            whole_block(mask),
            whole_block(mod),
        ]
        + chunks.specs,
        out_specs=[row_block(rows, width)] * 2,
        out_shape=[
            jax.ShapeDtypeStruct((seq_len, width), f32),
            jax.ShapeDtypeStruct((seq_len, width), bf16),
        ],
        scratch_shapes=[
            pltpu.VMEM((8, seq_len // 8, width), bf16),
            pltpu.SemaphoreType.DMA((2,)),
        ],
        compiler_params=params(),
        cost_estimate=cost(2 * seq_len * width * kept.shape[0], 14 * seq_len * width),
    )(core, places, count, index, kept, mask, mod, *chunks.arrays)


class Chunks:
    def __init__(self, mine, other):
        self.arrays = list(mine) + list(other)
        self.counts = [array.shape[0] for array in mine]
        self.specs = [anywhere] * len(self.arrays)

    def load(self, refs, places_ref, from_mine, row, target, sem):
        count = len(self.counts)
        rows = pl.ds(row, target.shape[1])
        place = 0
        for ref, size in zip(refs[:count] if from_mine else refs[count:], self.counts):
            for index in range(size):
                pltpu.make_async_copy(
                    ref.at[index, rows], target.at[places_ref[place]], sem
                ).start()
                place += 1

    def load_block(self, refs, places_ref, core_ref, block, target, sem, first=0):
        owner, row = block // 2, (first + block % 2) * target.shape[1]

        @pl.when(core_ref[0] == owner)
        def _():
            self.load(refs, places_ref, True, row, target, sem)

        @pl.when(core_ref[0] != owner)
        def _():
            self.load(refs, places_ref, False, row, target, sem)


def wait_block(target, sem):
    pltpu.make_async_copy(target, target, sem).wait()


def square(weight):
    return weight.reshape(-1, weight.shape[-1])


def split_heads(values, store):
    rows = values.shape[0]
    blank = jnp.zeros((rows, LANES - HD), values.dtype)
    for head in range(H):
        store(head, jnp.concatenate([values[:, head * HD : (head + 1) * HD], blank], axis=1))


def project_kernel(core_ref, places_ref, norm_ref, bias_ref, *rest, chunks):
    refs, (out_ref, weight, sems) = rest[: len(chunks.arrays)], rest[len(chunks.arrays) :]
    step = pl.program_id(0)

    @pl.when(step == 0)
    def _():
        for block in range(3):
            chunks.load_block(refs, places_ref, core_ref, block, weight.at[block], sems.at[block])

    wait_block(weight.at[step], sems.at[step])
    half = norm_ref.shape[0] // 2
    for part in range(2):
        rows = slice(part * half, (part + 1) * half)
        result = product(norm_ref[rows], square(weight[step])) + bias_ref[0]

        def store(head, value):
            out_ref[0, head, rows] = value

        split_heads(result.astype(bf16), store)


def project_call(core, places, norm, bias, chunks):
    seq_len, width = norm.shape
    return pl.pallas_call(
        functools.partial(project_kernel, chunks=chunks),
        grid=(3,),
        in_specs=[
            smem,
            smem,
            whole_block(norm),
            pl.BlockSpec((1, 1, width), lambda i: (i, 0, 0)),
        ]
        + chunks.specs,
        out_specs=pl.BlockSpec((1, H, seq_len, LANES), lambda i: (i, 0, 0, 0)),
        out_shape=jax.ShapeDtypeStruct((3, H, seq_len, LANES), bf16),
        scratch_shapes=[
            pltpu.VMEM((3, 8, width // 8, width), bf16),
            pltpu.SemaphoreType.DMA((3,)),
        ],
        compiler_params=params(),
        cost_estimate=cost(6 * seq_len * width * width, 12 * seq_len * width + 6 * width * width),
    )(core, places, norm, bias, *chunks.arrays)


def attend_kernel(query_ref, key_ref, value_ref, mix_ref, log_ref, *, size, factor):
    turned_value = value_ref[0, 0].T
    for part in range(query_ref.shape[2] // size):
        rows = slice(part * size, (part + 1) * size)
        scores = product(key_ref[0, 0], query_ref[0, 0, rows], right_turned)
        top = jnp.max(scores, axis=0, keepdims=True)
        weights = jnp.exp2((scores - top) * factor)
        total = jnp.sum(weights, axis=0, keepdims=True)
        mix = product(turned_value, weights.astype(bf16))
        mix_ref[0, rows] = (mix / total).T.astype(bf16)
        log_ref[0, :, rows] = top * factor + jnp.log2(total)


groups = 4


def head_block(place, seq_len, group):
    first = group * (H // groups)
    return pl.BlockSpec((1, 1, seq_len, LANES), lambda h: (place, first + h, 0, 0))


def attend_call(projected, group):
    seq_len = projected.shape[2]
    heads = H // groups
    flat = pl.BlockSpec((1, seq_len, LANES), lambda h: (h, 0, 0))
    return pl.pallas_call(
        functools.partial(
            attend_kernel, size=seq_len, factor=math.log2(math.e) / math.sqrt(HD)
        ),
        grid=(heads,),
        in_specs=[head_block(place, seq_len, group) for place in range(3)],
        out_specs=[flat, pl.BlockSpec((1, 1, seq_len), lambda h: (h, 0, 0))],
        out_shape=[
            jax.ShapeDtypeStruct((heads, seq_len, LANES), bf16),
            jax.ShapeDtypeStruct((heads, 1, seq_len), f32),
        ],
        compiler_params=params(),
        cost_estimate=cost(4 * heads * seq_len * seq_len * 256, 8 * heads * seq_len * LANES, heads * seq_len * seq_len),
    )(projected, projected, projected)


def attend_back_kernel(
    query_ref, key_ref, value_ref, mix_ref, log_ref, grad_ref, query_grad_ref, key_grad_ref,
    value_grad_ref, key_sum, value_sum, *, size, factor
):
    key, value = key_ref[0, 0], value_ref[0, 0]
    turned_key = key.T
    base_two = factor * math.log2(math.e)
    for part in range(query_ref.shape[2] // size):
        rows = slice(part * size, (part + 1) * size)
        query, grad = query_ref[0, 0, rows], grad_ref[0, rows]
        scores = product(key, query, right_turned)
        weights = jnp.exp2(scores * base_two - log_ref[0, :, rows])
        value_part = product(weights.astype(bf16), grad)
        weight_grad = product(value, grad, right_turned)
        inner = column_sum((grad.astype(f32) * mix_ref[0, rows].astype(f32)).T)
        score_grad = (weights * (weight_grad - inner)).astype(bf16)
        key_part = product(score_grad, query)
        query_grad_ref[0, rows] = (product(turned_key, score_grad) * factor).T.astype(bf16)
        if part == 0:
            key_sum[...] = key_part
            value_sum[...] = value_part
        else:
            key_sum[...] += key_part
            value_sum[...] += value_part
    key_grad_ref[0] = (key_sum[...] * factor).astype(bf16)
    value_grad_ref[0] = value_sum[...].astype(bf16)


def attend_back_call(projected, mix, logs, grad, group):
    seq_len = projected.shape[2]
    heads = H // groups
    first = group * heads
    flat = pl.BlockSpec((1, seq_len, LANES), lambda h: (h, 0, 0))
    return pl.pallas_call(
        functools.partial(attend_back_kernel, size=seq_len // 2, factor=1.0 / math.sqrt(HD)),
        grid=(heads,),
        in_specs=[head_block(place, seq_len, group) for place in range(3)]
        + [
            flat,
            pl.BlockSpec((1, 1, seq_len), lambda h: (h, 0, 0)),
            pl.BlockSpec((1, seq_len, LANES), lambda h: (first + h, 0, 0)),
        ],
        out_specs=[flat] * 3,
        out_shape=[jax.ShapeDtypeStruct((heads, seq_len, LANES), bf16)] * 3,
        scratch_shapes=[pltpu.VMEM((seq_len, LANES), f32)] * 2,
        compiler_params=params(),
        cost_estimate=cost(10 * heads * seq_len * seq_len * 256, 16 * heads * seq_len * LANES, heads * seq_len * seq_len),
    )(projected, projected, projected, mix, logs, grad)


def join_heads(refs):
    return jnp.concatenate(
        [ref[head][:, :HD] for ref in refs for head in range(ref.shape[0])], axis=1
    )


def mix_kernel(core_ref, places_ref, start_ref, bias_ref, mod_ref, *rest, chunks):
    mix_refs, rest = rest[:groups], rest[groups:]
    refs, rest = rest[: len(chunks.arrays)], rest[len(chunks.arrays) :]
    joined_ref, branch_ref, middle_ref, norm_ref, weight, sem = rest

    @pl.when(pl.program_id(0) == 0)
    def _():
        chunks.load_block(refs, places_ref, core_ref, 3, weight, sem)
        wait_block(weight, sem)

    joined = join_heads(mix_refs)
    joined_ref[...] = joined
    branch = product(joined, square(weight[...])) + bias_ref[...]
    branch_ref[...] = branch
    middle = start_ref[...] + mod_ref[2:3] * branch
    middle_ref[...] = middle
    unit, _ = normalize(middle)
    norm_ref[...] = (unit * (1.0 + mod_ref[4:5]) + mod_ref[3:4]).astype(bf16)


def mix_call(core, places, mix, start, bias, mod, chunks):
    seq_len, width = start.shape
    rows = seq_len // 4
    block = row_block(rows, width)
    return pl.pallas_call(
        functools.partial(mix_kernel, chunks=chunks),
        grid=(4,),
        in_specs=[smem, smem, block, whole_block(bias), whole_block(mod)]
        + [pl.BlockSpec((H // groups, rows, LANES), lambda i: (0, i, 0))] * groups
        + chunks.specs,
        out_specs=[block] * 4,
        out_shape=[
            jax.ShapeDtypeStruct((seq_len, width), kind) for kind in (bf16, f32, f32, bf16)
        ],
        scratch_shapes=[pltpu.VMEM((8, width // 8, width), bf16), pltpu.SemaphoreType.DMA],
        compiler_params=params(),
        cost_estimate=cost(2 * seq_len * width * width, 18 * seq_len * width),
    )(core, places, start, bias, mod, *mix, *chunks.arrays)


def gelu_parts(values):
    inner = 0.7978845608028654 * (values + 0.044715 * values * values * values)
    turned = jnp.tanh(inner)
    half = 0.5 * (1.0 + turned)
    slope = half + 0.5 * values * (1.0 - turned * turned) * (
        0.7978845608028654 * (1.0 + 0.134145 * values * values)
    )
    return values * half, slope


def feed_kernel(
    core_ref, places_ref, norm_ref, middle_ref, cot_ref, branch_ref, mod_ref, up_bias_ref, down_bias_ref,
    *rest, source
):
    refs, rest = rest[: len(source.arrays)], rest[len(source.arrays) :]
    (
        out_ref, hidden_ref, pre_ref, grad_two_ref, middle_grad_ref, grad_one_ref, sums_ref,
        up_sums_ref, up, down, slopes, sems,
    ) = rest
    step = pl.program_id(0)
    chunks = 4

    @pl.when(step == 0)
    def _():
        for chunk in range(chunks):
            for side, target in enumerate((up, down)):
                source.load_block(
                    refs, places_ref, core_ref, chunk, target.at[chunk], sems.at[side, chunk], 2 * side
                )
        sums_ref[...] = jnp.zeros_like(sums_ref)
        up_sums_ref[...] = jnp.zeros_like(up_sums_ref)

    norm = norm_ref[...]
    total = None
    for chunk in range(chunks):

        @pl.when(step == 0)
        def _():
            wait_block(up.at[chunk], sems.at[0, chunk])
            wait_block(down.at[chunk], sems.at[1, chunk])

        before = product(norm, square(up[chunk])) + up_bias_ref[chunk]
        hidden, slope = gelu_parts(before)
        hidden = hidden.astype(bf16)
        hidden_ref[chunk] = hidden
        slopes[chunk] = slope.astype(slopes.dtype)
        part = product(hidden, square(down[chunk]))
        total = part if total is None else total + part
    branch_two = total + down_bias_ref[...]
    middle, cot = middle_ref[...], cot_ref[...]
    gate_two = mod_ref[5:6]
    out_ref[...] = middle + gate_two * branch_two
    grad_two = (gate_two * cot).astype(bf16)
    grad_two_ref[...] = grad_two
    sums_ref[0:1] += column_sum(cot * branch_two)
    sums_ref[1:2] += column_sum(grad_two.astype(f32))
    total = None
    for chunk in range(chunks):
        pre = (product(grad_two, square(down[chunk]), right_turned) * slopes[chunk].astype(f32)).astype(bf16)
        pre_ref[chunk] = pre
        up_sums_ref[chunk] += column_sum(pre.astype(f32))
        part = product(pre, square(up[chunk]), right_turned)
        total = part if total is None else total + part
    unit, inverse = normalize(middle)
    sums_ref[2:3] += column_sum(total * unit)
    sums_ref[3:4] += column_sum(total)
    middle_grad = cot + normalize_back(total, unit, inverse, mod_ref[4:5])
    middle_grad_ref[...] = middle_grad
    sums_ref[4:5] += column_sum(middle_grad * branch_ref[...])
    grad_one = (mod_ref[2:3] * middle_grad).astype(bf16)
    grad_one_ref[...] = grad_one
    sums_ref[5:6] += column_sum(grad_one.astype(f32))


def feed_call(core, places, norm, middle, cot, branch, mod, up_bias, down_bias, source):
    seq_len, width = middle.shape
    steps = 4
    rows = seq_len // steps
    block = row_block(rows, width)
    chunked = pl.BlockSpec((4, rows, width), lambda i: (0, i, 0))
    wide = jax.ShapeDtypeStruct((4, seq_len, width), bf16)
    return pl.pallas_call(
        functools.partial(feed_kernel, source=source),
        grid=(steps,),
        in_specs=[
            smem,
            smem,
            block,
            block,
            block,
            block,
            whole_block(mod),
            whole_block(up_bias),
            whole_block(down_bias),
        ]
        + source.specs,
        out_specs=[
            block,
            chunked,
            chunked,
            block,
            block,
            block,
            pl.BlockSpec((8, width), lambda i: (0, 0)),
            pl.BlockSpec((4, 1, width), lambda i: (0, 0, 0)),
        ],
        out_shape=[
            jax.ShapeDtypeStruct((seq_len, width), f32),
            wide,
            wide,
            jax.ShapeDtypeStruct((seq_len, width), bf16),
            jax.ShapeDtypeStruct((seq_len, width), f32),
            jax.ShapeDtypeStruct((seq_len, width), bf16),
            jax.ShapeDtypeStruct((8, width), f32),
            jax.ShapeDtypeStruct((4, 1, width), f32),
        ],
        scratch_shapes=[
            pltpu.VMEM((4, 8, width // 8, width), bf16),
            pltpu.VMEM((4, 8, width // 8, width), bf16),
            pltpu.VMEM((4, rows, width), f32),
            pltpu.SemaphoreType.DMA((2, 4)),
        ],
        compiler_params=params(),
        cost_estimate=cost(32 * seq_len * width * width, 60 * seq_len * width, 4 * seq_len * width),
    )(core, places, norm, middle, cot, branch, mod, up_bias, down_bias, *source.arrays)


def feed_weight_kernel(first_ref, norm_ref, pre_ref, hidden_ref, grad_ref, out_ref):
    step = pl.program_id(0)

    @pl.when(step < 2)
    def _():
        result = product(norm_ref[...], pre_ref[0], left_turned)
        out_ref[...] = result.astype(bf16).reshape(out_ref.shape)

    @pl.when(step >= 2)
    def _():
        result = product(hidden_ref[0], grad_ref[...], left_turned)
        out_ref[...] = result.astype(bf16).reshape(out_ref.shape)


def feed_weight_call(first, norm, pre, hidden, grad):
    seq_len, width = norm.shape
    block = (1, seq_len, width)
    full = pl.BlockSpec((seq_len, width), lambda i, f: (0, 0))
    return pl.pallas_call(
        feed_weight_kernel,
        grid_spec=pltpu.PrefetchScalarGridSpec(
            num_scalar_prefetch=1,
            grid=(4,),
            in_specs=[
                full,
                pl.BlockSpec(block, lambda i, f: (f[0] + jnp.minimum(i, 1), 0, 0)),
                pl.BlockSpec(block, lambda i, f: (f[0] + jnp.maximum(i - 2, 0), 0, 0)),
                full,
            ],
            out_specs=pl.BlockSpec((8, width // 8, width), lambda i, f: (0, i, 0)),
        ),
        out_shape=jax.ShapeDtypeStruct((8, width // 2, width), bf16),
        compiler_params=params(),
        cost_estimate=cost(8 * seq_len * width * width, 12 * seq_len * width + 8 * width * width),
    )(first, norm, pre, hidden, grad)


def attention_weight_kernel(owner_ref, norm_ref, joined_ref, grad_ref, *rest):
    head_refs = [rest[block * groups : (block + 1) * groups] for block in range(3)]
    out_ref, left, heads, right, sems = rest[3 * groups :]
    step = pl.program_id(0)
    size = heads.shape[1] // groups

    def copies(block, slot):
        if block == 3:
            return [(joined_ref, left.at[slot]), (grad_ref, right.at[slot])]
        return [(norm_ref, left.at[slot])] + [
            (ref, heads.at[slot, pl.ds(group * size, size)])
            for group, ref in enumerate(head_refs[block])
        ]

    @pl.when(step == 0)
    def _():
        for block in range(4):

            @pl.when(owner_ref[0] == block // 2)
            def _():
                for source, target in copies(block, block % 2):
                    pltpu.make_async_copy(source, target, sems.at[block % 2]).start()

    for block in range(4):

        @pl.when((owner_ref[0] == block // 2) & (step == block % 2))
        def _():
            slot = block % 2
            wait_block(left.at[slot], sems.at[slot])
            if block == 3:
                wait_block(right.at[slot], sems.at[slot])
            else:
                wait_block(heads.at[slot], sems.at[slot])
                right[slot] = jnp.concatenate(
                    [heads[slot, head][:, :HD] for head in range(H)], axis=1
                )

    result = product(left[step], right[step], left_turned)
    out_ref[...] = result.astype(bf16).reshape(out_ref.shape)


def attention_weight_call(owner, norm, joined, grad_one, grads):
    seq_len, width = norm.shape
    return pl.pallas_call(
        attention_weight_kernel,
        grid=(2,),
        in_specs=[smem] + [anywhere] * (3 + 3 * groups),
        out_specs=pl.BlockSpec((8, width // 8, width), lambda i: (0, i, 0)),
        out_shape=jax.ShapeDtypeStruct((8, width // 4, width), bf16),
        scratch_shapes=[
            pltpu.VMEM((2, seq_len, width), bf16),
            pltpu.VMEM((2, H, seq_len, LANES), bf16),
            pltpu.VMEM((2, seq_len, width), bf16),
            pltpu.SemaphoreType.DMA((2,)),
        ],
        compiler_params=params(),
        cost_estimate=cost(4 * seq_len * width * width, 10 * seq_len * width + 4 * width * width),
    )(owner, norm, joined, grad_one, *grads)


def mix_grad_kernel(core_ref, places_ref, grad_ref, *rest, chunks):
    refs, (out_ref, weight, sem) = rest[: len(chunks.arrays)], rest[len(chunks.arrays) :]

    @pl.when(pl.program_id(0) == 0)
    def _():
        chunks.load_block(refs, places_ref, core_ref, 3, weight, sem)
        wait_block(weight, sem)

    def store(head, value):
        out_ref[head] = value

    split_heads(product(grad_ref[...], square(weight[...]), right_turned).astype(bf16), store)


def mix_grad_call(core, places, grad_one, chunks):
    seq_len, width = grad_one.shape
    rows = seq_len // 2
    return pl.pallas_call(
        functools.partial(mix_grad_kernel, chunks=chunks),
        grid=(2,),
        in_specs=[smem, smem, row_block(rows, width)] + chunks.specs,
        out_specs=pl.BlockSpec((H, rows, LANES), lambda i: (0, i, 0)),
        out_shape=jax.ShapeDtypeStruct((H, seq_len, LANES), bf16),
        scratch_shapes=[pltpu.VMEM((8, width // 8, width), bf16), pltpu.SemaphoreType.DMA],
        compiler_params=params(),
        cost_estimate=cost(2 * seq_len * width * width, 8 * seq_len * width),
    )(core, places, grad_one, *chunks.arrays)


def start_back_kernel(
    core_ref, places_ref, count_ref, index_row_ref, index_ref, middle_grad_ref, start_ref, mod_ref,
    *rest, chunks, first
):
    grad_refs = [rest[block * groups : (block + 1) * groups] for block in range(3)]
    rest = rest[3 * groups :]
    refs, rest = rest[: len(chunks.arrays)], rest[len(chunks.arrays) :]
    row_grad_ref, slot_ref, sums_ref, weight, slots, sems = rest
    step = pl.program_id(0)
    rows, width = start_ref.shape
    slot_count = slots.shape[0]

    @pl.when(step == 0)
    def _():
        for block in range(3):
            chunks.load_block(refs, places_ref, core_ref, block, weight.at[block], sems.at[block])
        sums_ref[...] = jnp.zeros_like(sums_ref)

    total = None
    for block, refs in enumerate(grad_refs):
        joined = join_heads(refs)
        if block != 1:
            place = block // 2
            sums_ref[place : place + 1] += column_sum(joined.astype(f32))

        @pl.when(step == 0)
        def _():
            wait_block(weight.at[block], sems.at[block])

        part = product(joined, square(weight[block]), right_turned)
        total = part if total is None else total + part
    unit, inverse = normalize(start_ref[...])
    sums_ref[2:3] += column_sum(total * unit)
    sums_ref[3:4] += column_sum(total)
    row_grad = middle_grad_ref[...] + normalize_back(total, unit, inverse, mod_ref[1:2])
    row_low = row_grad.astype(bf16)
    row_grad_ref[...] = row_low
    base = (first + step) * rows
    place = lax.broadcasted_iota(jnp.int32, (slot_count, rows), 1) + base
    slot = lax.broadcasted_iota(jnp.int32, (slot_count, rows), 0)
    chosen = jnp.where((index_ref[...] == place) & (slot < count_ref[0]), 1.0, 0.0)
    part = product(chosen.astype(bf16), row_low)

    @pl.when(step == 0)
    def _():
        slots[...] = part

    @pl.when(step > 0)
    def _():
        slots[...] += part

    here = lax.broadcasted_iota(jnp.int32, (rows, slot_count), 0) + base
    lane = lax.broadcasted_iota(jnp.int32, (rows, slot_count), 1)
    taken = jnp.where((index_row_ref[...] == here) & (lane < count_ref[0]), 1.0, 0.0)
    empty = 1.0 - jnp.sum(taken, axis=1, keepdims=True)
    sums_ref[4:5] += column_sum(row_grad * empty)

    @pl.when(step == pl.num_programs(0) - 1)
    def _():
        slot_ref[...] = slots[...].astype(bf16)


def start_back_call(half, core, places, count, index, grads, middle_grad, start, mod, chunks):
    seq_len, width = start.shape
    slot_count = index.shape[1]
    steps = 2
    rows = seq_len // 4
    first = half * steps
    heads = pl.BlockSpec((H // groups, rows, LANES), lambda i: (0, first + i, 0))
    block = pl.BlockSpec((rows, width), lambda i: (first + i, 0))
    column = index.reshape(slot_count, 1)
    return pl.pallas_call(
        functools.partial(start_back_kernel, chunks=chunks, first=first),
        grid=(steps,),
        in_specs=[
            smem,
            smem,
            smem,
            whole_block(index),
            whole_block(column),
            block,
            block,
            whole_block(mod),
        ]
        + [heads] * (3 * groups)
        + chunks.specs,
        out_specs=[
            row_block(rows, width),
            pl.BlockSpec((slot_count, width), lambda i: (0, 0)),
            pl.BlockSpec((8, width), lambda i: (0, 0)),
        ],
        out_shape=[
            jax.ShapeDtypeStruct((seq_len // 2, width), bf16),
            jax.ShapeDtypeStruct((slot_count, width), bf16),
            jax.ShapeDtypeStruct((8, width), f32),
        ],
        scratch_shapes=[
            pltpu.VMEM((3, 8, width // 8, width), bf16),
            pltpu.VMEM((slot_count, width), f32),
            pltpu.SemaphoreType.DMA((3,)),
        ],
        compiler_params=params(),
        cost_estimate=cost(4 * seq_len * width * width, 13 * seq_len * width),
    )(core, places, count, index, column, middle_grad, start, mod, *grads, *chunks.arrays)


def swap_pairs(size, bit):
    return [(place, place ^ bit) for place in range(size)]


def swap_core(values):
    return lax.ppermute(values, "grp", swap_pairs(lax.axis_size("grp"), 1))


def add_low(*parts):
    total = parts[0].astype(f32)
    for part in parts[1:]:
        total = total + part.astype(f32)
    return total.astype(bf16)


def swap_x(values):
    return lax.ppermute(values, "grp", swap_pairs(lax.axis_size("grp"), 2))


class Ring:
    def __init__(self):
        size = lax.axis_size("tok")
        self.size = size
        order = list(range(0, size, 2)) + list(range(1, size, 2))[::-1]
        self.ahead = [(order[i], order[(i + 1) % size]) for i in range(size)]
        self.behind = [(after, before) for before, after in self.ahead]
        tok = lax.axis_index("tok")
        self.place = jnp.where(tok % 2 == 0, tok // 2, size - 1 - tok // 2)
        self.x_bit = (lax.axis_index("grp") // 2) % 2

    def tok_at(self, distance):
        place = (self.place + distance) % self.size
        return jnp.where(place < self.size // 2, 2 * place, 2 * (self.size - 1 - place) + 1)

    def forward(self, values):
        return lax.ppermute(values, "tok", self.ahead)

    def backward(self, values):
        return lax.ppermute(values, "tok", self.behind)


def sync(*values):
    return lax.optimization_barrier(values)


class Gather:
    def __init__(self, ring, mine, other, part, middle):
        self.ring, self.part, self.middle = ring, part, middle
        self.mine, self.other = [mine[None]], [other[None]]
        payload = lax.dynamic_slice_in_dim(mine, part * ring.x_bit, part + middle, 0)
        self.pieces = [payload, payload]
        self.distance = 0
        self.arrived = self.whole = None

    def issue(self):
        ring, flight = self.ring, {}
        bit, half = ring.x_bit, self.ring.size // 2
        if self.distance < half:
            self.distance += 1
            ahead, behind = self.pieces
            if self.distance == half:
                split = ahead.shape[0] // 2
                ahead, behind = ahead[:split], behind[split:]
            flight["ring"] = [ring.forward(ahead), ring.backward(behind)]
        if self.arrived is not None:
            own = lax.dynamic_slice_in_dim(self.arrived, self.middle * bit, self.part, 1)
            flight["x"] = swap_x(own)
        if self.whole is not None:
            flight["core"] = swap_core(self.whole)
        return flight

    def land(self, flight):
        bit, waiting = self.ring.x_bit, self.arrived
        self.arrived = self.whole = None
        if "ring" in flight:
            self.pieces = flight["ring"]
            if self.distance == self.ring.size // 2:
                self.arrived = jnp.concatenate(self.pieces)[None]
            else:
                self.arrived = jnp.stack(self.pieces)
        if "x" in flight:
            got = flight["x"]
            self.whole = jnp.where(
                bit == 0,
                jnp.concatenate([waiting, got], axis=1),
                jnp.concatenate([got, waiting], axis=1),
            )
            self.mine.append(self.whole)
        if "core" in flight:
            self.other.append(flight["core"])


class Scatter:
    def __init__(self, ring, mine, got):
        self.ring, self.values = ring, (mine, got)
        self.distance = ring.size // 2
        self.split = mine.shape[1] // 2

    def piece(self, place, row, count):
        tok, width = self.ring.tok_at(place), self.values[0].shape[2]
        mine, got = (
            lax.dynamic_slice(values, (tok, row, 0), (1, count, width))[0].astype(f32)
            for values in self.values
        )
        return mine + got

    def hop(self):
        ring, distance, split = self.ring, self.distance, self.split
        rows = self.values[0].shape[1]
        if distance == ring.size // 2:
            ahead = self.piece(distance, 0, split)
            behind = self.piece(distance, split, rows - split)
        else:
            ahead, behind = self.ahead.astype(f32), self.behind.astype(f32)
            if distance == ring.size // 2 - 1:
                ahead = jnp.pad(ahead, ((0, rows - split), (0, 0)))
                behind = jnp.pad(behind, ((split, 0), (0, 0)))
            ahead = self.piece(distance, 0, rows) + ahead
            behind = self.piece(-distance, 0, rows) + behind
        self.distance -= 1
        return ring.forward(ahead.astype(bf16)), ring.backward(behind.astype(bf16))

    def land(self, flight):
        self.ahead, self.behind = flight

    def total(self):
        rows = self.values[0].shape[1]
        total = self.piece(0, 0, rows) + self.ahead.astype(f32) + self.behind.astype(f32)
        return total.astype(bf16)


def gather_plain(shard, share):
    size, width = lax.axis_size("tok"), shard.shape[1]
    full = lax.all_gather(shard, "tok", axis=0)
    blocks = [
        full[:, row : row + share].reshape(8, -1, width) for row in range(0, shard.shape[0], share)
    ]
    return jnp.concatenate(blocks, axis=1)


def by_tok(values, share):
    size = lax.axis_size("tok")
    if size == 8:
        return values
    rows = share * size // 8
    blocks = [
        values[:, row : row + rows].reshape(size, share, -1)
        for row in range(0, values.shape[1], rows)
    ]
    return jnp.concatenate(blocks, axis=1)


def scatter_plain(chip):
    return lax.psum_scatter(chip, "tok", scatter_dimension=0, tiled=True)[0]


def add_x(shard):
    step = 2
    while step < lax.axis_size("grp"):
        shard = add_low(shard, lax.ppermute(shard, "grp", swap_pairs(lax.axis_size("grp"), step)))
        step *= 2
    return shard


def spread_kernel(weight_ref, out_ref, *, count):
    share = weight_ref.shape[0]
    for block in range(4):
        pieces = [
            weight_ref[:, (4 * tok + block) * share : (4 * tok + block + 1) * share]
            for tok in range(count)
        ]
        out_ref[block] = jnp.concatenate(pieces, axis=1).astype(bf16)


def spread_call(weight, count):
    share = weight.shape[0]
    return pl.pallas_call(
        functools.partial(spread_kernel, count=count),
        out_shape=jax.ShapeDtypeStruct((4, share, weight.shape[1] // 4), bf16),
        compiler_params=params(),
    )(weight)


def unspread_kernel(core_ref, mine_ref, other_ref, out_ref, *, count):
    share = mine_ref.shape[1]

    def write(refs):
        pieces = [
            refs[block // 2][block % 2, :, tok * share : (tok + 1) * share].astype(f32)
            for tok in range(count)
            for block in range(4)
        ]
        out_ref[...] = jnp.concatenate(pieces, axis=1)

    @pl.when(core_ref[0] == 0)
    def _():
        write((mine_ref, other_ref))

    @pl.when(core_ref[0] != 0)
    def _():
        write((other_ref, mine_ref))


def unspread_call(core, mine, other, count):
    share, width = mine.shape[1:]
    return pl.pallas_call(
        functools.partial(unspread_kernel, count=count),
        in_specs=[smem, whole_block(mine), whole_block(other)],
        out_shape=jax.ShapeDtypeStruct((share, 4 * width), f32),
        compiler_params=params(),
    )(core, mine, other)


def on_device(
    kept_tokens,
    kept_index,
    kept_count,
    condition,
    mask_token,
    position_table,
    modulation_weight,
    modulation_bias,
    input_weight,
    query_bias,
    value_bias,
    output_weight,
    output_bias,
    up_weight,
    up_bias,
    down_weight,
    down_bias,
    cotangent,
):
    _, seq_len, width = cotangent.shape
    tok_count = lax.axis_size("tok")
    core = lax.axis_index("grp") % 2
    core_row = core.reshape(1)
    share = input_weight.shape[0]
    position_rows = position_table.shape[0]

    def by_core(first, second):
        return jnp.where(core == 0, first, second)

    def exchange(values):
        return lax.all_to_all(values, "tok", split_axis=0, concat_axis=0, tiled=True)

    ring = Ring()

    condition_low = jax.nn.silu(condition).astype(bf16)
    slots_here = kept_tokens.shape[1]
    condition_rows = jnp.broadcast_to(condition_low, (tok_count, 8, width))
    arrived = exchange(jnp.concatenate([kept_tokens.astype(bf16), condition_rows], axis=1))
    routed = arrived[:, :slots_here].reshape(-1, width)
    condition_group = arrived[:, slots_here]

    modulation_low = modulation_weight.astype(bf16)

    def modulate_all(conditions):
        modulation_part = jnp.dot(
            conditions, modulation_low, preferred_element_type=f32
        ) + modulation_bias.astype(bf16).astype(f32)
        return exchange(modulation_part).reshape(6, width)

    condition_all = lax.all_gather(condition_group, "grp", axis=0, tiled=True)

    ringed = share % 16 == 0 and lax.axis_size("grp") == 4
    small_parts = [mask_token, query_bias, value_bias, output_bias, down_bias, up_bias]
    small_widths = [part.shape[0] for part in small_parts]
    cuts = [sum(small_widths[:number]) for number in range(len(small_widths) + 1)]
    small_rows = position_rows // 8
    table_rows = position_rows * 5 // 8
    tail_rows = position_rows - table_rows

    def as_rows(parts):
        flat = jnp.concatenate(parts, axis=-1)
        lead = flat.shape[:-1]
        flat = jnp.pad(flat, [(0, 0)] * len(lead) + [(0, small_rows * width - flat.shape[-1])])
        return flat.reshape(lead + (small_rows, width))

    def table_parts(table, small):
        lead = table.shape[:-2]
        blank = jnp.zeros(lead + (table_rows - tail_rows - small_rows, width), table.dtype)
        return table[..., :table_rows, :], jnp.concatenate(
            [table[..., table_rows:, :], small, blank], axis=-2
        )

    input_low = input_weight.astype(bf16)
    input_blocks = [input_low[:, number * width : (number + 1) * width] for number in range(3)]
    table_low = table_parts(position_table.astype(bf16), as_rows(small_parts).astype(bf16))
    attention_low = (
        jnp.concatenate(input_blocks[:2] + [table_low[0]]),
        jnp.concatenate([input_blocks[2], output_weight.astype(bf16), table_low[1]]),
    )
    up_low = spread_call(up_weight, tok_count)
    down_low = down_weight.astype(bf16).reshape(4, share, width)
    feed_low = tuple(
        jnp.concatenate([up_low[half : half + 2], down_low[half : half + 2]]).reshape(-1, width)
        for half in (0, 2)
    )

    attention_cut, feed_cut = (8 * share // 9, 7 * share // 9), (4 * share // 3, 4 * share // 3)
    if ringed:
        mine, other = by_core(*attention_low), by_core(*attention_low[::-1])
        gather = Gather(ring, mine, other, *attention_cut)
        mine, other = by_core(*feed_low), by_core(*feed_low[::-1])
        feed_gather = Gather(ring, mine, other, *feed_cut)
        for _ in range(2):
            (flight,) = sync(gather.issue())
            gather.land(flight)
        flight, condition_group, routed = sync(gather.issue(), condition_group, routed)
        gather.land(flight)
    mod = modulate_all(condition_group)
    if ringed:
        flight, mod = sync(gather.issue(), mod)
        gather.land(flight)
        feed_gather.pieces, gather.arrived = sync(feed_gather.pieces, gather.arrived)
        feed_flight = feed_gather.issue()
        (flight,) = sync(gather.issue())
        gather.land(flight)
        flight, feed_flight = sync(gather.issue(), feed_flight)
        gather.land(flight)
        feed_gather.land(feed_flight)
        attention_chunks = Chunks(gather.mine, gather.other)
        distances = [0]
        for distance in range(1, ring.size // 2):
            distances += [-distance, distance]
        places = ring.tok_at(jnp.array(distances + [ring.size // 2], jnp.int32))
        small_rel = jnp.concatenate(
            [
                by_core(other, mine)[:, 2 * share + tail_rows : 2 * share + tail_rows + small_rows]
                for mine, other in zip(gather.mine, gather.other)
            ]
        )
        small = jnp.zeros_like(small_rel).at[places].set(small_rel).reshape(tok_count, -1)
    else:
        places = jnp.arange(8, dtype=jnp.int32)
        mine = gather_plain(by_core(*attention_low)[: 2 * share], share)
        attention_chunks = Chunks([mine], [swap_core(mine)])
        mine = gather_plain(by_core(*feed_low), share)
        feed_chunks = Chunks([mine], [swap_core(mine)])
        table = lax.all_gather(
            jnp.concatenate([position_table.astype(bf16), as_rows(small_parts).astype(bf16)]), "tok"
        )
        small = table[:, position_rows:].reshape(tok_count, -1)
        table = table[:, :position_rows].reshape(8, -1, width)
    mask_full, query_bias_full, value_bias_full, output_bias_full, down_bias_full = (
        small[:, cuts[number] : cuts[number + 1]].reshape(1, width).astype(f32)
        for number in range(5)
    )
    up_bias_full = (
        small[:, cuts[5] : cuts[6]].reshape(tok_count, 4, share).transpose(1, 0, 2).reshape(4, 1, width)
    ).astype(f32)

    if ringed:
        table_chunks, table_row, table_share = attention_chunks, 2 * share, table_rows
    else:
        table_share = table.shape[1] // 2
        halves = table[:, :table_share], table[:, table_share:]
        table_chunks, table_row = Chunks([by_core(*halves)], [by_core(*halves[::-1])]), 0
    start, norm_one = start_call(
        core_row, places, kept_count, kept_index, routed, mask_full, mod, table_chunks, table_row,
        table_share, seq_len,
    )
    blank = jnp.zeros_like(query_bias_full)
    projected_bias = jnp.stack([query_bias_full, blank, value_bias_full])
    projected = project_call(core_row, places, norm_one, projected_bias, attention_chunks)
    if ringed:
        flight, projected, start = sync(feed_gather.issue(), projected, start)
        feed_gather.land(flight)
    attended = []
    for group in range(groups):
        attended.append(attend_call(projected, group))
        if ringed and group % 2:
            flight, attended, projected = sync(feed_gather.issue(), attended, projected)
            feed_gather.land(flight)
    joined, branch_one, middle, norm_two = mix_call(
        core_row, places, [pair[0] for pair in attended], start, output_bias_full, mod, attention_chunks
    )
    if ringed:
        flight, norm_two = sync(feed_gather.issue(), norm_two)
        feed_gather.land(flight)
        (flight,) = sync(feed_gather.issue())
        feed_gather.land(flight)
        feed_chunks = Chunks(feed_gather.mine, feed_gather.other)
    (
        block_output,
        hidden,
        pre_grad,
        grad_two,
        middle_grad,
        grad_one,
        feed_sums,
        up_bias_sum,
    ) = feed_call(
        core_row, places, norm_two, middle, cotangent[0], branch_one, mod, up_bias_full, down_bias_full,
        feed_chunks,
    )
    feed_other = feed_weight_call(2 - 2 * core_row, norm_two, pre_grad, hidden, grad_two)
    feed_other, norm_two, grad_one = sync(feed_other, norm_two, grad_one)
    feed_mine = feed_weight_call(2 * core_row, norm_two, pre_grad, hidden, grad_two)
    feed_got, feed_mine, grad_one = sync(swap_core(feed_other), feed_mine, grad_one)
    mix_grad = mix_grad_call(core_row, places, grad_one, attention_chunks)
    if ringed:
        feed_scatter = Scatter(ring, feed_mine, feed_got)
    grads = []
    for group in range(groups):
        grads.append(attend_back_call(projected, *attended[group], mix_grad, group))
        if ringed and group in (0, 2):
            flight, grads, mix_grad = sync(feed_scatter.hop(), grads, mix_grad)
            feed_scatter.land(flight)
    grads = [triple[block] for block in range(3) for triple in grads]

    def attention_weights(owner, norm):
        return attention_weight_call(owner, norm, joined, grad_one, grads)

    def start_back(half, grads):
        return start_back_call(
            half, core_row, places, kept_count, kept_index, grads, middle_grad, start, mod, attention_chunks
        )

    attention_other = attention_weights(1 - core_row, norm_one)
    if ringed:
        flight, attention_other, norm_one, grads = sync(
            feed_scatter.hop(), attention_other, norm_one, grads
        )
        feed_scatter.land(flight)
    attention_mine = attention_weights(core_row, norm_one)
    attention_got = swap_core(attention_other)
    first_half = start_back(0, grads)
    if ringed:
        flight, attention_mine, attention_got, first_half, grads = sync(
            feed_scatter.hop(), attention_mine, attention_got, first_half, grads
        )
        feed_scatter.land(flight)
        feed_shard = feed_scatter.total()
        scatter = Scatter(ring, attention_mine, attention_got)
        second_half = start_back(1, grads)
        flight, second_half = sync(scatter.hop(), second_half)
        scatter.land(flight)
    else:
        second_half = start_back(1, grads)
    row_grad = jnp.concatenate([first_half[0], second_half[0]])
    slot_grad = first_half[1] + second_half[1]
    start_sums = first_half[2] + second_half[2]
    kept_grad = exchange(slot_grad.reshape(tok_count, -1, width)).astype(f32)

    up_sums = up_bias_sum.reshape(4, tok_count, share).transpose(1, 0, 2).reshape(tok_count, -1)
    rows_of = lambda row: row.reshape(tok_count, -1)
    small_grads = as_rows(
        [
            rows_of(start_sums[4]),
            rows_of(start_sums[0]),
            rows_of(start_sums[1]),
            rows_of(feed_sums[5]),
            rows_of(feed_sums[1]),
            up_sums,
        ]
    ).astype(bf16)
    position_grad = row_grad.reshape(tok_count, position_rows, width)
    tables = table_parts(position_grad, small_grads)
    table_got = swap_core(by_core(tables[1], tables[0]))
    table_chip = add_low(by_core(tables[0], tables[1]), table_got)
    table_shard = jnp.sum(exchange(table_chip).astype(f32), axis=0).astype(bf16)
    table_shard = add_x(table_shard)
    table_far = swap_core(table_shard)
    first, second = by_core(table_shard, table_far), by_core(table_far, table_shard)
    position_total = jnp.concatenate([first, second[:tail_rows]]).astype(f32)
    small_total = second[tail_rows : tail_rows + small_rows].astype(f32).reshape(-1)
    if ringed:
        while scatter.distance > 0:
            (flight,) = sync(scatter.hop())
            scatter.land(flight)
        attention_shard = add_x(scatter.total())
    else:
        attention_chip = by_tok(add_low(attention_mine, attention_got), share)
        attention_shard = add_x(scatter_plain(attention_chip))
        feed_shard = scatter_plain(by_tok(add_low(feed_mine, feed_got), share))
    feed_shard = add_x(feed_shard)

    (
        mask_total,
        query_bias_total,
        value_bias_total,
        output_bias_total,
        down_bias_total,
        up_bias_total,
    ) = (small_total[cuts[number] : cuts[number + 1]] for number in range(6))
    far = swap_core(attention_shard)
    first, second = by_core(attention_shard, far).astype(f32), by_core(far, attention_shard).astype(f32)
    input_total = jnp.concatenate([first[:share], first[share:], second[:share]], axis=1)
    output_total = second[share:]
    feed_shard = feed_shard.reshape(4, share, width)
    feed_far = swap_core(feed_shard)
    up_total = unspread_call(core_row, feed_shard[:2], feed_far[:2], tok_count)
    down_total = jnp.concatenate(
        [by_core(feed_shard[2:], feed_far[2:]), by_core(feed_far[2:], feed_shard[2:])]
    ).reshape(-1, width).astype(f32)

    modulation_grad = jnp.concatenate(
        [start_sums[3], start_sums[2], feed_sums[4], feed_sums[3], feed_sums[2], feed_sums[0]]
    ).astype(bf16)
    modulation_grad_group = exchange(modulation_grad.reshape(tok_count, -1))
    modulation_grad_all = lax.all_gather(modulation_grad_group, "grp", axis=0, tiled=True)
    modulation_total = jnp.einsum(
        "id,ie->de", condition_all, modulation_grad_all, preferred_element_type=f32
    )
    modulation_bias_total = jnp.sum(modulation_grad_all.astype(f32), axis=0)
    condition_part = jnp.einsum(
        "ie,de->id", modulation_grad_group, modulation_low, preferred_element_type=f32
    )
    condition_low_grad = jnp.sum(exchange(condition_part), axis=0, keepdims=True)
    _, silu_back = jax.vjp(jax.nn.silu, condition)
    condition_grad = silu_back(condition_low_grad)[0]
    return (
        block_output[None],
        kept_grad,
        condition_grad,
        mask_total,
        position_total,
        modulation_total,
        modulation_bias_total,
        input_total,
        query_bias_total,
        value_bias_total,
        output_total,
        output_bias_total,
        up_total,
        up_bias_total,
        down_total,
        down_bias_total,
    )


def solution(mesh):
    return jax.shard_map(
        on_device,
        mesh=mesh,
        in_specs=(
            P("grp", "tok", None),
            P(("grp", "tok"), None),
            P(("grp", "tok")),
            P(("grp", "tok"), None),
            P("tok"),
            P("tok", None),
            P(None, "tok"),
            P("tok"),
            P("tok", None),
            P("tok"),
            P("tok"),
            P("tok", None),
            P("tok"),
            P("tok", None),
            P("tok"),
            P("tok", None),
            P("tok"),
            P(("grp", "tok"), None, None),
        ),
        out_specs=(
            P(("grp", "tok"), None, None),
            P("grp", "tok", None),
            P(("grp", "tok"), None),
            P("tok"),
            P("tok", None),
            P(None, "tok"),
            P("tok"),
            P("tok", None),
            P("tok"),
            P("tok"),
            P("tok", None),
            P("tok"),
            P("tok", None),
            P("tok"),
            P("tok", None),
            P("tok"),
        ),
        check_vma=False,
    )
```

time: 1080 us -> 751 us (0.70)
  waiting for transfers between devices: 564 us -> 141 us
  starting transfers between devices: 24.4 us -> 99.6 us
  other arithmetic: 67.3 us -> 114 us
  blocking collectives: 51.2 us -> 11 us
  Pallas kernels: 286 us -> 313 us
  between operations: 15.7 us -> 2.53 us
    all_gather x4 -> x0, waiting for transfers between devices: 276 us -> none  [gather_blocks(): return lax.all_gather(shard, 'tok', axis=1, tiled=True)]
    reduce_scatter x2 -> x0, waiting for transfers between devices: 242 us -> none  [scatter_blocks(): shard = lax.psum_scatter(chip, 'tok', scatter_dimension=1, tiled=True)]
    ppermute x3 -> x43, waiting for transfers between devices: 32.1 us -> 115 us  [the longest x16 90.2 us: forward(): return lax.ppermute(values, 'tok', self.ahead)]
    ppermute x3 -> x43, starting transfers between devices: 4.47 us -> 61.7 us  [the longest x16 36 us: forward(): return lax.ppermute(values, 'tok', self.ahead)]
    convert_element_type x6 -> x19, other arithmetic: 5.44 us -> 44.2 us  [the longest x8 26.7 us: hop(): behind.astype(bf16)]
    all_gather x1 -> x0, blocking collectives: 31 us -> none  [on_device(): condition_group = lax.all_gather(condition_low, 'tok', axis=0, tiled=True)]
    select_n x0 -> x9, other arithmetic: none -> 24.9 us  [the longest x8 24.3 us: land(): jnp.where(bit == 0, jnp.concatenate([waiting, got], axis=1), jnp.concaten...]
    all_to_all x4 -> x6, waiting for transfers between devices: 5.74 us -> 26 us  [exchange(): lax.all_to_all(values, 'tok', split_axis=0, concat_axis=0, tiled=True)]
  transfers between devices with their start and end apart: 24 -> 63, of which waited for: 11 -> 28; matrix products, arithmetic and copies ran while one was open for 10% -> 16% of each run, Pallas kernels for 18% -> 29%
where the time goes in v3:
time: 751 us; the launch traced here: 741 us
  Pallas kernels  313 us (42%)
  waiting for transfers between devices  141 us (19%)
  other arithmetic  114 us (15%)
  starting transfers between devices  99.6 us (13%)
  local copies, waits for them, and re-layouts  53.9 us (7%)
  blocking collectives  11 us (1%)
    ppermute x16, waiting for transfers between devices, forward(): return lax.ppermute(values, 'tok', self.ahead)  90.2 us
    pallas_call x1, Pallas kernels, feed_call(): pl.pallas_call(functools.partial(feed_kernel, source=source), grid=(steps...  73.2 us
    pallas_call x4, Pallas kernels, attend_back_call(): pl.pallas_call(functools.partial(attend_back_kernel, size=seq_len // 2, f...  53.2 us
    pallas_call x2, Pallas kernels, feed_weight_call(): pl.pallas_call(feed_weight_kernel, grid_spec=pltpu.PrefetchScalarGridSpec...  37 us
    all_to_all x6, starting transfers between devices, exchange(): lax.all_to_all(values, 'tok', split_axis=0, concat_axis=0, tiled=True)  37 us
    pallas_call x2, Pallas kernels, start_back_call(): pl.pallas_call(functools.partial(start_back_kernel, chunks=chunks, first=...  36.1 us
    ppermute x16, starting transfers between devices, forward(): return lax.ppermute(values, 'tok', self.ahead)  36 us
    pallas_call x4, Pallas kernels, attend_call(): pl.pallas_call(functools.partial(attend_kernel, size=seq_len, factor=math...  34.8 us
  transfers between devices with their start and end apart: 63, of which 28 were waited for; matrix products, arithmetic and copies ran while one was open for 16% of the time, Pallas kernels for 29%

profile of v3, /device:TPU:0, one launch (start us, length us, event | category | flops | bytes accessed | tf_op | source)
XLA Modules:
  0.0 741.5 jit_solution(15726543378993645167)
XLA Ops:
  13.6 6.3 all-to-all-start
  32.7 32.5 %collective-permute-done.2 = bf16[240,1152]{1,0:T(8,128)(2,1)} collective-permute-done((bf16[240,1152]{1,0:T(8,128)(2,1)S(1)}, bf16[240,1152]{1,0:T(8,128)(2,1)}, u32[]{:S(2)}, u32[]{:S(2)}) %collective-permute-start.2) | collective-permute-done | bytes 552992 | tf_op jit(solution)/shard_map/ppermute | solution.py:751
  72.1 12.9 %collective-permute-start.6 = (bf16[240,1152]{1,0:T(8,128)(2,1)}, bf16[240,1152]{1,0:T(8,128)(2,1)}, u32[]{:S(2)}, u32[]{:S(2)}) collective-permute-start(bf16[240,1152]{1,0:T(8,128)(2,1)} %collective-permute-done.2), channel_id=1, source_target_pairs={{0,2},{2,4},{4,6},{6,7},{7,5},{5,3},{3,1},{1,0},{8,10},{10,12},{12... | collective-permute-start | bytes 1658888 | tf_op jit(solution)/shard_map/ppermute | solution.py:751
  150.9 12.3 %collective-permute-done.16 = bf16[384,1152]{1,0:T(8,128)(2,1)S(1)} collective-permute-done((bf16[384,1152]{1,0:T(8,128)(2,1)S(1)}, bf16[384,1152]{1,0:T(8,128)(2,1)S(1)}, u32[]{:S(2)}, u32[]{:S(2)}) %collective-permute-start.16) | collective-permute-done | bytes 884768 | tf_op jit(solution)/shard_map/ppermute | solution.py:751
  176.6 8.3 %shard_map.307 = (f32[1024,1152]{1,0:T(8,128)}, bf16[1024,1152]{1,0:T(8,128)(2,1)}) custom-call(s32[1]{0:T(128)} %bitcast.core_ref.owner_ref, s32[8]{0:T(128)} %get-tuple-element.356.places_ref, s32[1]{0:T(128)S(6)} %copy.83.count_ref, s32[1,768]{1,0:T(1,128)} %index_row_ref.3, bf16[768,1152]{1,0:T(8,128)(2,1)} %bitcast.145, f32[1,1152]{1,0:T(1,128)} %reshape.685.mask_ref, ...), custom_call_target="tpu_custom_call" | custom-call | flops 1811939328 | bytes 16515072 | tf_op jit(solution)/shard_map/pallas_call | solution.py:105
  184.8 16.6 %shard_map.308.query_ref.key_ref.value_ref = bf16[3,16,1024,128]{3,2,1,0:T(8,128)(2,1)} custom-call(s32[1]{0:T(128)} %bitcast.core_ref.owner_ref, s32[8]{0:T(128)} %get-tuple-element.356.places_ref, bf16[1024,1152]{1,0:T(8,128)(2,1)} %get-tuple-element.291.norm_ref, f32[3,1,1152]{2,1,0:T(1,128)} %pad_maximum_fusion.8.bias_ref, ...), custom_call_target="tpu_custom_call" | custom-call | flops 8153726976 | bytes 22118400 | tf_op jit(solution)/shard_map/pallas_call | solution.py:199
  201.5 5.5 maximum_select_fusion.rest_1_
  211.8 8.7 %shard_map.309 = (bf16[4,1024,128]{2,1,0:T(8,128)(2,1)}, f32[4,1,1024]{2,1,0:T(1,128)}) custom-call(bf16[3,16,1024,128]{3,2,1,0:T(8,128)(2,1)} %shard_map.308.query_ref.key_ref.value_ref, bf16[3,16,1024,128]{3,2,1,0:T(8,128)(2,1)} %shard_map.308.query_ref.key_ref.value_ref, bf16[3,16,1024,128]{3,2,1,0:T(8,128)(2,1)} %shard_map.308.query_ref.key_ref.value_ref), custom_call_target="tpu_custom_call" | custom-call | flops 4294967296 | bytes 4194304 | tf_op jit(solution)/shard_map/pallas_call | solution.py:245
  220.4 8.7 %shard_map.310 = (bf16[4,1024,128]{2,1,0:T(8,128)(2,1)}, f32[4,1,1024]{2,1,0:T(1,128)}) custom-call(bf16[3,16,1024,128]{3,2,1,0:T(8,128)(2,1)} %shard_map.308.query_ref.key_ref.value_ref, bf16[3,16,1024,128]{3,2,1,0:T(8,128)(2,1)} %shard_map.308.query_ref.key_ref.value_ref, bf16[3,16,1024,128]{3,2,1,0:T(8,128)(2,1)} %shard_map.308.query_ref.key_ref.value_ref), custom_call_target="tpu_custom_call" | custom-call | flops 4294967296 | bytes 4194304 | tf_op jit(solution)/shard_map/pallas_call | solution.py:245
  232.4 5.9 maximum_select_fusion.1.rest_2_
  243.0 8.7 %shard_map.311 = (bf16[4,1024,128]{2,1,0:T(8,128)(2,1)}, f32[4,1,1024]{2,1,0:T(1,128)}) custom-call(bf16[3,16,1024,128]{3,2,1,0:T(8,128)(2,1)} %shard_map.308.query_ref.key_ref.value_ref, bf16[3,16,1024,128]{3,2,1,0:T(8,128)(2,1)} %shard_map.308.query_ref.key_ref.value_ref, bf16[3,16,1024,128]{3,2,1,0:T(8,128)(2,1)} %shard_map.308.query_ref.key_ref.value_ref), custom_call_target="tpu_custom_call" | custom-call | flops 4294967296 | bytes 4194304 | tf_op jit(solution)/shard_map/pallas_call | solution.py:245
  251.7 8.7 %shard_map.312 = (bf16[4,1024,128]{2,1,0:T(8,128)(2,1)}, f32[4,1,1024]{2,1,0:T(1,128)}) custom-call(bf16[3,16,1024,128]{3,2,1,0:T(8,128)(2,1)} %shard_map.308.query_ref.key_ref.value_ref, bf16[3,16,1024,128]{3,2,1,0:T(8,128)(2,1)} %shard_map.308.query_ref.key_ref.value_ref, bf16[3,16,1024,128]{3,2,1,0:T(8,128)(2,1)} %shard_map.308.query_ref.key_ref.value_ref), custom_call_target="tpu_custom_call" | custom-call | flops 4294967296 | bytes 4194304 | tf_op jit(solution)/shard_map/pallas_call | solution.py:245
  268.5 12.5 %shard_map.313 = (bf16[1024,1152]{1,0:T(8,128)(2,1)}, f32[1024,1152]{1,0:T(8,128)}, f32[1024,1152]{1,0:T(8,128)}, bf16[1024,1152]{1,0:T(8,128)(2,1)}) custom-call(s32[1]{0:T(128)} %bitcast.core_ref.owner_ref, s32[8]{0:T(128)} %get-tuple-element.356.places_ref, f32[1024,1152]{1,0:T(8,128)} %get-tuple-element.229.start_ref, f32[1,1152]{1,0:T(1,128)} %reshape.688.bias_ref, ...), custom_call_target="tpu_custom_call" | custom-call | flops 2717908992 | bytes 21233664 | tf_op jit(solution)/shard_map/pallas_call | solution.py:341
  284.8 73.2 %shard_map.314 = (f32[1024,1152]{1,0:T(8,128)}, bf16[4,1024,1152]{2,1,0:T(8,128)(2,1)}, bf16[4,1024,1152]{2,1,0:T(8,128)(2,1)}, bf16[1024,1152]{1,0:T(8,128)(2,1...) custom-call(s32[1]{0:T(128)} %bitcast.core_ref.owner_ref, ...), custom_call_target="tpu_custom_call" | custom-call | flops 43486543872 | bytes 70778880 | tf_op jit(solution)/shard_map/pallas_call | solution.py:438
  357.9 18.5 %shard_map.315 = bf16[8,576,1152]{2,1,0:T(8,128)(2,1)} custom-call(s32[1]{0:T(128)S(6)} %sub.62.first_ref, bf16[1024,1152]{1,0:T(8,128)(2,1)} %get-tuple-element.248.norm_ref, bf16[4,1024,1152]{2,1,0:T(8,128)(2,1)} %get-tuple-element.243.pre_ref, bf16[4,1024,1152]{2,1,0:T(8,128)(2,1)} %get-tuple-element.244.hidden_ref, ...), custom_call_target="tpu_custom_call" | custom-call | flops 10871635968 | bytes 24772608 | tf_op jit(solution)/shard_map/pallas_call | solution.py:502
  376.7 18.5 %shard_map.316 = bf16[8,576,1152]{2,1,0:T(8,128)(2,1)} custom-call(s32[1]{0:T(128)S(6)} %mul.116.first_ref, bf16[1024,1152]{1,0:T(8,128)(2,1)} %get-tuple-element.248.norm_ref, bf16[4,1024,1152]{2,1,0:T(8,128)(2,1)} %get-tuple-element.243.pre_ref, bf16[4,1024,1152]{2,1,0:T(8,128)(2,1)} %get-tuple-element.244.hidden_ref, ...), custom_call_target="tpu_custom_call" | custom-call | flops 10871635968 | bytes 24772608 | tf_op jit(solution)/shard_map/pallas_call | solution.py:502
  395.2 8.5 %shard_map.317.grad_ref = bf16[16,1024,128]{2,1,0:T(8,128)(2,1)} custom-call(s32[1]{0:T(128)} %bitcast.core_ref.owner_ref, s32[8]{0:T(128)} %get-tuple-element.356.places_ref, bf16[1024,1152]{1,0:T(8,128)(2,1)} %get-tuple-element.254.grad_ref, bf16[1,368,1152]{2,1,0:T(8,128)(2,1)} %get-tuple-element.380.rest_0_.rest_4_.rest_12_, ...), custom_call_target="tpu_custom_call" | custom-call | flops 2717908992 | bytes 9437184 | tf_op jit(solution)/shard_map/pallas_call | solution.py:598
  407.8 13.4 %shard_map.318 = (bf16[4,1024,128]{2,1,0:T(8,128)(2,1)}, bf16[4,1024,128]{2,1,0:T(8,128)(2,1)}, bf16[4,1024,128]{2,1,0:T(8,128)(2,1)}) custom-call(bf16[3,16,1024,128]{3,2,1,0:T(8,128)(2,1)} %shard_map.308.query_ref.key_ref.value_ref, bf16[3,16,1024,128]{3,2,1,0:T(8,128)(2,1)} %shard_map.308.query_ref.key_ref.value_ref, ...), custom_call_target="tpu_custom_call" | custom-call | flops 10737418240 | bytes 8388608 | tf_op jit(solution)/shard_map/pallas_call | solution.py:294
  428.6 13.2 %shard_map.320 = (bf16[4,1024,128]{2,1,0:T(8,128)(2,1)}, bf16[4,1024,128]{2,1,0:T(8,128)(2,1)}, bf16[4,1024,128]{2,1,0:T(8,128)(2,1)}) custom-call(bf16[3,16,1024,128]{3,2,1,0:T(8,128)(2,1)} %shard_map.308.query_ref.key_ref.value_ref, bf16[3,16,1024,128]{3,2,1,0:T(8,128)(2,1)} %shard_map.308.query_ref.key_ref.value_ref, ...), custom_call_target="tpu_custom_call" | custom-call | flops 10737418240 | bytes 8388608 | tf_op jit(solution)/shard_map/pallas_call | solution.py:294
  441.9 13.2 %shard_map.319 = (bf16[4,1024,128]{2,1,0:T(8,128)(2,1)}, bf16[4,1024,128]{2,1,0:T(8,128)(2,1)}, bf16[4,1024,128]{2,1,0:T(8,128)(2,1)}) custom-call(bf16[3,16,1024,128]{3,2,1,0:T(8,128)(2,1)} %shard_map.308.query_ref.key_ref.value_ref, bf16[3,16,1024,128]{3,2,1,0:T(8,128)(2,1)} %shard_map.308.query_ref.key_ref.value_ref, ...), custom_call_target="tpu_custom_call" | custom-call | flops 10737418240 | bytes 8388608 | tf_op jit(solution)/shard_map/pallas_call | solution.py:294
  457.3 5.4 fusion.3
  464.7 13.4 %shard_map.321 = (bf16[4,1024,128]{2,1,0:T(8,128)(2,1)}, bf16[4,1024,128]{2,1,0:T(8,128)(2,1)}, bf16[4,1024,128]{2,1,0:T(8,128)(2,1)}) custom-call(bf16[3,16,1024,128]{3,2,1,0:T(8,128)(2,1)} %shard_map.308.query_ref.key_ref.value_ref, bf16[3,16,1024,128]{3,2,1,0:T(8,128)(2,1)} %shard_map.308.query_ref.key_ref.value_ref, ...), custom_call_target="tpu_custom_call" | custom-call | flops 10737418240 | bytes 8388608 | tf_op jit(solution)/shard_map/pallas_call | solution.py:294
  478.1 12.1 %shard_map.322 = bf16[8,288,1152]{2,1,0:T(8,128)(2,1)} custom-call(s32[1]{0:T(128)S(6)} %sub.69.owner_ref, bf16[1024,1152]{1,0:T(8,128)(2,1)} %get-tuple-element.291.norm_ref, bf16[1024,1152]{1,0:T(8,128)(2,1)} %get-tuple-element.274.joined_ref, bf16[1024,1152]{1,0:T(8,128)(2,1)} %get-tuple-element.254.grad_ref, ...), custom_call_target="tpu_custom_call" | custom-call | flops 5435817984 | bytes 17104896 | tf_op jit(solution)/shard_map/pallas_call | solution.py:564
  501.3 5.7 all-gather
  507.5 13.6 %shard_map.323 = bf16[8,288,1152]{2,1,0:T(8,128)(2,1)} custom-call(s32[1]{0:T(128)} %bitcast.core_ref.owner_ref, bf16[1024,1152]{1,0:T(8,128)(2,1)} %get-tuple-element.291.norm_ref, bf16[1024,1152]{1,0:T(8,128)(2,1)} %get-tuple-element.274.joined_ref, bf16[1024,1152]{1,0:T(8,128)(2,1)} %get-tuple-element.254.grad_ref, ...), custom_call_target="tpu_custom_call" | custom-call | flops 5435817984 | bytes 17104896 | tf_op jit(solution)/shard_map/pallas_call | solution.py:564
  521.2 18.0 %shard_map.324 = (bf16[512,1152]{1,0:T(8,128)(2,1)}, bf16[768,1152]{1,0:T(8,128)(2,1)}, f32[8,1152]{1,0:T(8,128)}) custom-call(s32[1]{0:T(128)} %bitcast.core_ref.owner_ref, s32[8]{0:T(128)} %get-tuple-element.356.places_ref, s32[1]{0:T(128)S(6)} %copy.83.count_ref, s32[1,768]{1,0:T(1,128)} %index_row_ref.3, s32[768,1]{1,0:T(8,128)} %copy.46.index_ref, ...), custom_call_target="tpu_custom_call" | custom-call | flops 5435817984 | bytes 15335424 | tf_op jit(solution)/shard_map/pallas_call | solution.py:681
  546.7 18.1 %shard_map.325 = (bf16[512,1152]{1,0:T(8,128)(2,1)}, bf16[768,1152]{1,0:T(8,128)(2,1)}, f32[8,1152]{1,0:T(8,128)}) custom-call(s32[1]{0:T(128)} %bitcast.core_ref.owner_ref, s32[8]{0:T(128)} %get-tuple-element.356.places_ref, s32[1]{0:T(128)S(6)} %copy.83.count_ref, s32[1,768]{1,0:T(1,128)} %index_row_ref.3, s32[768,1]{1,0:T(8,128)} %copy.46.index_ref, ...), custom_call_target="tpu_custom_call" | custom-call | flops 5435817984 | bytes 15335424 | tf_op jit(solution)/shard_map/pallas_call | solution.py:681
  604.7 5.3 all-gather.1
  618.9 6.0 all-to-all-start.2
  642.7 31.6 %collective-permute-done.51 = bf16[288,1152]{1,0:T(8,128)(2,1)S(1)} collective-permute-done((bf16[288,1152]{1,0:T(8,128)(2,1)S(1)}, bf16[288,1152]{1,0:T(8,128)(2,1)S(1)}, u32[]{:S(2)}, u32[]{:S(2)}) %collective-permute-start.51) | collective-permute-done | bytes 663584 | tf_op jit(solution)/shard_map/ppermute | solution.py:751
  683.4 13.2 %all-to-all-start.5 = ((bf16[8,80,1152]{2,1,0:T(8,128)(2,1)}), bf16[8,80,1152]{2,1,0:T(8,128)(2,1)S(1)}, u32[]{:S(2)}, u32[]{:S(2)}) async-start(bf16[8,80,1152]{2,1,0:T(8,128)(2,1)} %add_convert_fusion), calls=%async_computation.5 | async-start | bytes 2949120 | tf_op jit(solution)/shard_map/all_to_all | solution.py:960
  710.2 20.6 %all-to-all-done.5 = bf16[8,80,1152]{2,1,0:T(8,128)(2,1)S(1)} async-done(((bf16[8,80,1152]{2,1,0:T(8,128)(2,1)}), bf16[8,80,1152]{2,1,0:T(8,128)(2,1)S(1)}, u32[]{:S(2)}, u32[]{:S(2)}) %all-to-all-start.5) | async-done | bytes 1474592 | tf_op jit(solution)/shard_map/all_to_all | solution.py:960
  (362 shorter events, 270.0 us)
Async XLA Ops:
  13.6 81.3 %all-to-all-start = ((bf16[8,104,1152]{2,1,0:T(8,128)(2,1)}), bf16[8,104,1152]{2,1,0:T(8,128)(2,1)}, u32[]{:S(2)}, u32[]{:S(2)}) async-start(bf16[8,104,1152]{2,1,0:T(8,128)(2,1)} %pad_maximum_fusion.2), calls=%async_computation | async-start | bytes 3833856 | tf_op jit(solution)/shard_map/all_to_all | solution.py:960
  25.0 40.2 %collective-permute-start.2 = (bf16[240,1152]{1,0:T(8,128)(2,1)S(1)}, bf16[240,1152]{1,0:T(8,128)(2,1)}, u32[]{:S(2)}, u32[]{:S(2)}) collective-permute-start(bf16[240,1152]{1,0:T(8,128)(2,1)S(1)} %collective-permute-done), channel_id=1, source_target_pairs={{0,2},{2,4},{4,6},{6,7},{7,5},{5,3},{3,1},{1,0},{8,10},{10,12},{12... | collective-permute-start | bytes 1658888 | tf_op jit(solution)/shard_map/ppermute | solution.py:751
  28.9 36.5 %collective-permute-start.3 = (bf16[240,1152]{1,0:T(8,128)(2,1)S(1)}, bf16[240,1152]{1,0:T(8,128)(2,1)}, u32[]{:S(2)}, u32[]{:S(2)}) collective-permute-start(bf16[240,1152]{1,0:T(8,128)(2,1)S(1)} %collective-permute-done.1), channel_id=1, source_target_pairs={{2,0},{4,2},{6,4},{7,6},{5,7},{3,5},{1,3},{0,1},{10,8},{12,10},{14... | collective-permute-start | bytes 1658888 | tf_op jit(solution)/shard_map/ppermute | solution.py:754
  28.9 36.5 %collective-permute-start.4 = (bf16[2,128,1152]{2,1,0:T(8,128)(2,1)S(1)}, bf16[2,128,1152]{2,1,0:T(8,128)(2,1)}, u32[]{:S(2)}, u32[]{:S(2)}) collective-permute-start(bf16[2,128,1152]{2,1,0:T(8,128)(2,1)S(1)} %fusion.26), channel_id=1, source_target_pairs={{0,16},{8,24},{16,0},{24,8},{1,17},{9,25},{17,1},{25,9},{2,18},{10... | collective-permute-start | bytes 1769480 | tf_op jit(solution)/shard_map/ppermute | solution.py:732
  67.2 35.3 %collective-permute-start.5 = (bf16[2,368,1152]{2,1,0:T(8,128)(2,1)S(1)}, bf16[2,368,1152]{2,1,0:T(8,128)(2,1)S(1)}, u32[]{:S(2)}, u32[]{:S(2)}) collective-permute-start(bf16[2,368,1152]{2,1,0:T(8,128)(2,1)S(1)} %maximum_select_fusion.3.rest_1_.rest_5_.rest_13_), channel_id=1, source_target_pairs={{0,8},{8,0},{16,24},{24,16},{1,9},{9,1},{17,25},{25,17},{2,10},{10... | collective-permute-start | bytes 5087240 | tf_op jit(solution)/shard_map/ppermute | solution.py:721
  72.1 27.2 %collective-permute-start.6 = (bf16[240,1152]{1,0:T(8,128)(2,1)}, bf16[240,1152]{1,0:T(8,128)(2,1)}, u32[]{:S(2)}, u32[]{:S(2)}) collective-permute-start(bf16[240,1152]{1,0:T(8,128)(2,1)} %collective-permute-done.2), channel_id=1, source_target_pairs={{0,2},{2,4},{4,6},{6,7},{7,5},{5,3},{3,1},{1,0},{8,10},{10,12},{12... | collective-permute-start | bytes 1658888 | tf_op jit(solution)/shard_map/ppermute | solution.py:751
  106.0 25.0 %collective-permute-start.9 = (bf16[2,368,1152]{2,1,0:T(8,128)(2,1)S(1)}, bf16[2,368,1152]{2,1,0:T(8,128)(2,1)}, u32[]{:S(2)}, u32[]{:S(2)}) collective-permute-start(bf16[2,368,1152]{2,1,0:T(8,128)(2,1)S(1)} %maximum_select_fusion.4.rest_2_.rest_6_.rest_14_), channel_id=1, source_target_pairs={{0,8},{8,0},{16,24},{24,16},{1,9},{9,1},{17,25},{25,17},{2,10},{10... | collective-permute-start | bytes 5087240 | tf_op jit(solution)/shard_map/ppermute | solution.py:721
  141.4 21.8 %collective-permute-start.16 = (bf16[384,1152]{1,0:T(8,128)(2,1)S(1)}, bf16[384,1152]{1,0:T(8,128)(2,1)S(1)}, u32[]{:S(2)}, u32[]{:S(2)}) collective-permute-start(bf16[384,1152]{1,0:T(8,128)(2,1)S(1)} %constant_dynamic-slice_fusion.1), channel_id=1, source_target_pairs={{0,2},{2,4},{4,6},{6,7},{7,5},{5,3},{3,1},{1,0},{8,10},{10,12},{12... | collective-permute-start | bytes 2654216 | tf_op jit(solution)/shard_map/ppermute | solution.py:751
  172.2 29.3 %collective-permute-start.18 = (bf16[384,1152]{1,0:T(8,128)(2,1)S(1)}, bf16[384,1152]{1,0:T(8,128)(2,1)}, u32[]{:S(2)}, u32[]{:S(2)}) collective-permute-start(bf16[384,1152]{1,0:T(8,128)(2,1)S(1)} %copy-done.7), channel_id=1, source_target_pairs={{0,2},{2,4},{4,6},{6,7},{7,5},{5,3},{3,1},{1,0},{8,10},{10,12},{12... | collective-permute-start | bytes 2654216 | tf_op jit(solution)/shard_map/ppermute | solution.py:751
  173.2 28.3 %collective-permute-start.19 = (bf16[384,1152]{1,0:T(8,128)(2,1)S(1)}, bf16[384,1152]{1,0:T(8,128)(2,1)}, u32[]{:S(2)}, u32[]{:S(2)}) collective-permute-start(bf16[384,1152]{1,0:T(8,128)(2,1)S(1)} %copy-done.9), channel_id=1, source_target_pairs={{2,0},{4,2},{6,4},{7,6},{5,7},{3,5},{1,3},{0,1},{10,8},{12,10},{14... | collective-permute-start | bytes 2654216 | tf_op jit(solution)/shard_map/ppermute | solution.py:754
  175.4 26.1 %collective-permute-start.20 = (bf16[2,192,1152]{2,1,0:T(8,128)(2,1)}, bf16[2,192,1152]{2,1,0:T(8,128)(2,1)}, u32[]{:S(2)}, u32[]{:S(2)}) collective-permute-start(bf16[2,192,1152]{2,1,0:T(8,128)(2,1)} %fusion.21), channel_id=1, source_target_pairs={{0,16},{8,24},{16,0},{24,8},{1,17},{9,25},{17,1},{25,9},{2,18},{10... | collective-permute-start | bytes 2654216 | tf_op jit(solution)/shard_map/ppermute | solution.py:732
  207.0 25.5 %collective-permute-start.21 = (bf16[2,576,1152]{2,1,0:T(8,128)(2,1)}, bf16[2,576,1152]{2,1,0:T(8,128)(2,1)}, u32[]{:S(2)}, u32[]{:S(2)}) collective-permute-start(bf16[2,576,1152]{2,1,0:T(8,128)(2,1)} %maximum_select_fusion.rest_1_), channel_id=1, source_target_pairs={{0,8},{8,0},{16,24},{24,16},{1,9},{9,1},{17,25},{25,17},{2,10},{10... | collective-permute-start | bytes 7962632 | tf_op jit(solution)/shard_map/ppermute | solution.py:721
  208.2 22.1 %collective-permute-start.24 = (bf16[2,192,1152]{2,1,0:T(8,128)(2,1)S(1)}, bf16[2,192,1152]{2,1,0:T(8,128)(2,1)S(1)}, u32[]{:S(2)}, u32[]{:S(2)}) collective-permute-start(bf16[2,192,1152]{2,1,0:T(8,128)(2,1)S(1)} %fusion.20), channel_id=1, source_target_pairs={{0,16},{8,24},{16,0},{24,8},{1,17},{9,25},{17,1},{25,9},{2,18},{10... | collective-permute-start | bytes 2654216 | tf_op jit(solution)/shard_map/ppermute | solution.py:732
  209.7 22.0 %collective-permute-start.22 = (bf16[384,1152]{1,0:T(8,128)(2,1)}, bf16[384,1152]{1,0:T(8,128)(2,1)S(1)}, u32[]{:S(2)}, u32[]{:S(2)}) collective-permute-start(bf16[384,1152]{1,0:T(8,128)(2,1)} %collective-permute-done.18), channel_id=1, source_target_pairs={{0,2},{2,4},{4,6},{6,7},{7,5},{5,3},{3,1},{1,0},{8,10},{10,12},{12... | collective-permute-start | bytes 2654216 | tf_op jit(solution)/shard_map/ppermute | solution.py:751
  238.3 22.2 %collective-permute-start.25 = (bf16[2,576,1152]{2,1,0:T(8,128)(2,1)}, bf16[2,576,1152]{2,1,0:T(8,128)(2,1)}, u32[]{:S(2)}, u32[]{:S(2)}) collective-permute-start(bf16[2,576,1152]{2,1,0:T(8,128)(2,1)} %maximum_select_fusion.1.rest_2_), channel_id=1, source_target_pairs={{0,8},{8,0},{16,24},{24,16},{1,9},{9,1},{17,25},{25,17},{2,10},{10... | collective-permute-start | bytes 7962632 | tf_op jit(solution)/shard_map/ppermute | solution.py:721
  238.4 22.1 %collective-permute-start.28 = (bf16[2,192,1152]{2,1,0:T(8,128)(2,1)S(1)}, bf16[2,192,1152]{2,1,0:T(8,128)(2,1)S(1)}, u32[]{:S(2)}, u32[]{:S(2)}) collective-permute-start(bf16[2,192,1152]{2,1,0:T(8,128)(2,1)S(1)} %fusion.19), channel_id=1, source_target_pairs={{0,16},{8,24},{16,0},{24,8},{1,17},{9,25},{17,1},{25,9},{2,18},{10... | collective-permute-start | bytes 2654216 | tf_op jit(solution)/shard_map/ppermute | solution.py:732
  426.6 30.2 %collective-permute-start.35 = (bf16[576,1152]{1,0:T(8,128)(2,1)S(1)}, bf16[576,1152]{1,0:T(8,128)(2,1)S(1)}, u32[]{:S(2)}, u32[]{:S(2)}) collective-permute-start(bf16[576,1152]{1,0:T(8,128)(2,1)S(1)} %get-tuple-element.364), channel_id=1, source_target_pairs={{0,2},{2,4},{4,6},{6,7},{7,5},{5,3},{3,1},{1,0},{8,10},{10,12},{12... | collective-permute-start | bytes 3981320 | tf_op jit(solution)/shard_map/ppermute | solution.py:751
  427.3 30.0 %collective-permute-start.36 = (bf16[576,1152]{1,0:T(8,128)(2,1)S(1)}, bf16[576,1152]{1,0:T(8,128)(2,1)}, u32[]{:S(2)}, u32[]{:S(2)}) collective-permute-start(bf16[576,1152]{1,0:T(8,128)(2,1)S(1)} %get-tuple-element.363), channel_id=1, source_target_pairs={{2,0},{4,2},{6,4},{7,6},{5,7},{3,5},{1,3},{0,1},{10,8},{12,10},{14... | collective-permute-start | bytes 3981320 | tf_op jit(solution)/shard_map/ppermute | solution.py:754
  462.6 29.2 %collective-permute-start.37 = (bf16[576,1152]{1,0:T(8,128)(2,1)}, bf16[576,1152]{1,0:T(8,128)(2,1)S(1)}, u32[]{:S(2)}, u32[]{:S(2)}) collective-permute-start(bf16[576,1152]{1,0:T(8,128)(2,1)} %get-tuple-element.362), channel_id=1, source_target_pairs={{0,2},{2,4},{4,6},{6,7},{7,5},{5,3},{3,1},{1,0},{8,10},{10,12},{12... | collective-permute-start | bytes 3981320 | tf_op jit(solution)/shard_map/ppermute | solution.py:751
  464.4 28.9 %collective-permute-start.38 = (bf16[576,1152]{1,0:T(8,128)(2,1)}, bf16[576,1152]{1,0:T(8,128)(2,1)S(1)}, u32[]{:S(2)}, u32[]{:S(2)}) collective-permute-start(bf16[576,1152]{1,0:T(8,128)(2,1)} %get-tuple-element.361), channel_id=1, source_target_pairs={{2,0},{4,2},{6,4},{7,6},{5,7},{3,5},{1,3},{0,1},{10,8},{12,10},{14... | collective-permute-start | bytes 3981320 | tf_op jit(solution)/shard_map/ppermute | solution.py:754
  493.3 45.9 %collective-permute-start.41 = (bf16[8,288,1152]{2,1,0:T(8,128)(2,1)}, bf16[8,288,1152]{2,1,0:T(8,128)(2,1)}, u32[]{:S(2)}, u32[]{:S(2)}) collective-permute-start(bf16[8,288,1152]{2,1,0:T(8,128)(2,1)} %shard_map.322), channel_id=1, source_target_pairs={{0,8},{8,0},{16,24},{24,16},{1,9},{9,1},{17,25},{25,17},{2,10},{10... | collective-permute-start | bytes 15925256 | tf_op jit(solution)/shard_map/ppermute | solution.py:721
  498.3 40.9 %collective-permute-start.39 = (bf16[576,1152]{1,0:T(8,128)(2,1)}, bf16[576,1152]{1,0:T(8,128)(2,1)S(1)}, u32[]{:S(2)}, u32[]{:S(2)}) collective-permute-start(bf16[576,1152]{1,0:T(8,128)(2,1)} %get-tuple-element.360), channel_id=1, source_target_pairs={{0,2},{2,4},{4,6},{6,7},{7,5},{5,3},{3,1},{1,0},{8,10},{10,12},{12... | collective-permute-start | bytes 3981320 | tf_op jit(solution)/shard_map/ppermute | solution.py:751
  498.9 40.2 %collective-permute-start.40 = (bf16[576,1152]{1,0:T(8,128)(2,1)}, bf16[576,1152]{1,0:T(8,128)(2,1)S(1)}, u32[]{:S(2)}, u32[]{:S(2)}) collective-permute-start(bf16[576,1152]{1,0:T(8,128)(2,1)} %get-tuple-element.359), channel_id=1, source_target_pairs={{2,0},{4,2},{6,4},{7,6},{5,7},{3,5},{1,3},{0,1},{10,8},{12,10},{14... | collective-permute-start | bytes 3981320 | tf_op jit(solution)/shard_map/ppermute | solution.py:754
  542.6 96.9 %collective-permute-start.55 = (bf16[576,1152]{1,0:T(8,128)(2,1)}, bf16[576,1152]{1,0:T(8,128)(2,1)}, u32[]{:S(2)}, u32[]{:S(2)}) collective-permute-start(bf16[576,1152]{1,0:T(8,128)(2,1)} %fusion.1), channel_id=1, source_target_pairs={{0,16},{8,24},{16,0},{24,8},{1,17},{9,25},{17,1},{25,9},{2,18},{10... | collective-permute-start | bytes 3981320 | tf_op jit(solution)/shard_map/ppermute | solution.py:875
  568.1 41.8 %collective-permute-start.47 = (bf16[288,1152]{1,0:T(8,128)(2,1)}, bf16[288,1152]{1,0:T(8,128)(2,1)}, u32[]{:S(2)}, u32[]{:S(2)}) collective-permute-start(bf16[288,1152]{1,0:T(8,128)(2,1)} %get-tuple-element.372), channel_id=1, source_target_pairs={{0,2},{2,4},{4,6},{6,7},{7,5},{5,3},{3,1},{1,0},{8,10},{10,12},{12... | collective-permute-start | bytes 1990664 | tf_op jit(solution)/shard_map/ppermute | solution.py:751
  568.7 41.2 %collective-permute-start.48 = (bf16[288,1152]{1,0:T(8,128)(2,1)}, bf16[288,1152]{1,0:T(8,128)(2,1)}, u32[]{:S(2)}, u32[]{:S(2)}) collective-permute-start(bf16[288,1152]{1,0:T(8,128)(2,1)} %get-tuple-element.371), channel_id=1, source_target_pairs={{2,0},{4,2},{6,4},{7,6},{5,7},{3,5},{1,3},{0,1},{10,8},{12,10},{14... | collective-permute-start | bytes 1990664 | tf_op jit(solution)/shard_map/ppermute | solution.py:754
  591.1 88.1 %collective-permute-start.44 = (bf16[8,80,1152]{2,1,0:T(8,128)(2,1)}, bf16[8,80,1152]{2,1,0:T(8,128)(2,1)}, u32[]{:S(2)}, u32[]{:S(2)}) collective-permute-start(bf16[8,80,1152]{2,1,0:T(8,128)(2,1)} %broadcast_select_fusion), channel_id=1, source_target_pairs={{0,8},{8,0},{16,24},{24,16},{1,9},{9,1},{17,25},{25,17},{2,10},{10... | collective-permute-start | bytes 4423688 | tf_op jit(solution)/shard_map/ppermute | solution.py:721
  618.9 64.5 %all-to-all-start.2 = ((bf16[8,96,1152]{2,1,0:T(8,128)(2,1)}), bf16[8,96,1152]{2,1,0:T(8,128)(2,1)}, u32[]{:S(2)}, u32[]{:S(2)}) async-start(bf16[8,96,1152]{2,1,0:T(8,128)(2,1)} %bitcast.144), calls=%async_computation.2 | async-start | bytes 3538944 | tf_op jit(solution)/shard_map/all_to_all | solution.py:960
  636.2 38.1 %collective-permute-start.51 = (bf16[288,1152]{1,0:T(8,128)(2,1)S(1)}, bf16[288,1152]{1,0:T(8,128)(2,1)S(1)}, u32[]{:S(2)}, u32[]{:S(2)}) collective-permute-start(bf16[288,1152]{1,0:T(8,128)(2,1)S(1)} %get-tuple-element.368), channel_id=1, source_target_pairs={{0,2},{2,4},{4,6},{6,7},{7,5},{5,3},{3,1},{1,0},{8,10},{10,12},{12... | collective-permute-start | bytes 1990664 | tf_op jit(solution)/shard_map/ppermute | solution.py:751
  639.4 35.9 %collective-permute-start.52 = (bf16[288,1152]{1,0:T(8,128)(2,1)S(1)}, bf16[288,1152]{1,0:T(8,128)(2,1)S(1)}, u32[]{:S(2)}, u32[]{:S(2)}) collective-permute-start(bf16[288,1152]{1,0:T(8,128)(2,1)S(1)} %get-tuple-element.367), channel_id=1, source_target_pairs={{2,0},{4,2},{6,4},{7,6},{5,7},{3,5},{1,3},{0,1},{10,8},{12,10},{14... | collective-permute-start | bytes 1990664 | tf_op jit(solution)/shard_map/ppermute | solution.py:754
  641.6 40.6 %collective-permute-start.56 = (bf16[4,144,1152]{2,1,0:T(8,128)(2,1)S(1)}, bf16[4,144,1152]{2,1,0:T(8,128)(2,1)S(1)}, u32[]{:S(2)}, u32[]{:S(2)}) collective-permute-start(bf16[4,144,1152]{2,1,0:T(8,128)(2,1)S(1)} %bitcast.150), channel_id=1, source_target_pairs={{0,8},{8,0},{16,24},{24,16},{1,9},{9,1},{17,25},{25,17},{2,10},{10... | collective-permute-start | bytes 3981320 | tf_op jit(solution)/shard_map/ppermute | solution.py:721
  683.4 47.3 %all-to-all-start.5 = ((bf16[8,80,1152]{2,1,0:T(8,128)(2,1)}), bf16[8,80,1152]{2,1,0:T(8,128)(2,1)S(1)}, u32[]{:S(2)}, u32[]{:S(2)}) async-start(bf16[8,80,1152]{2,1,0:T(8,128)(2,1)} %add_convert_fusion), calls=%async_computation.5 | async-start | bytes 2949120 | tf_op jit(solution)/shard_map/all_to_all | solution.py:960
  (74 other events, 819.6 us)

commit v4 on v3

--- a/solution.py
+++ b/solution.py
@@ -64,7 +64,7 @@
     return (scaled - first - unit * second) * inverse
 
 
-def start_kernel(core_ref, places_ref, count_ref, index_ref, kept_ref, mask_ref, mod_ref, *rest, chunks, row, share):
+def start_kernel(core_ref, places_ref, count_ref, index_ref, kept_ref, small_ref, mod_ref, *rest, chunks, row, share):
     refs, (start_ref, norm_ref, table, sems) = rest[: len(chunks.arrays)], rest[len(chunks.arrays) :]
     rows, slots = start_ref.shape[0], kept_ref.shape[0]
     step = pl.program_id(0)
@@ -74,13 +74,13 @@
     def _():
         @pl.when(core_ref[0] == 0)
         def _():
-            chunks.load(refs, places_ref, True, row, low, sems.at[0])
-            chunks.load(refs, places_ref, False, row, high, sems.at[1])
+            chunks.load(refs, places_ref, core_ref, True, row, low, sems.at[0])
+            chunks.load(refs, places_ref, core_ref, False, row, high, sems.at[1])
 
         @pl.when(core_ref[0] != 0)
         def _():
-            chunks.load(refs, places_ref, False, row, low, sems.at[0])
-            chunks.load(refs, places_ref, True, row, high, sems.at[1])
+            chunks.load(refs, places_ref, core_ref, False, row, low, sems.at[0])
+            chunks.load(refs, places_ref, core_ref, True, row, high, sems.at[1])
 
         wait_block(low, sems.at[0])
         wait_block(high, sems.at[1])
@@ -93,13 +93,13 @@
     empty = 1.0 - jnp.sum(chosen, axis=1, keepdims=True)
     groups_here = rows // table.shape[1]
     position = table[pl.ds(step * groups_here, groups_here)].reshape(rows, -1)
-    start = filled + empty * mask_ref[...] + position.astype(f32)
+    start = filled + empty * small_ref[0:1] + position.astype(f32)
     start_ref[...] = start
     unit, _ = normalize(start)
     norm_ref[...] = (unit * (1.0 + mod_ref[1:2]) + mod_ref[0:1]).astype(bf16)
 
 
-def start_call(core, places, count, index, kept, mask, mod, chunks, row, share, seq_len):
+def start_call(core, places, count, index, kept, small, mod, chunks, row, share, seq_len):
     width = kept.shape[1]
     rows = seq_len // 4
     return pl.pallas_call(
@@ -111,7 +111,7 @@
             smem,
             whole_block(index),
             whole_block(kept),
-            whole_block(mask),
+            whole_block(small),
             whole_block(mod),
         ]
         + chunks.specs,
@@ -126,36 +126,68 @@
         ],
         compiler_params=params(),
         cost_estimate=cost(2 * seq_len * width * kept.shape[0], 14 * seq_len * width),
-    )(core, places, count, index, kept, mask, mod, *chunks.arrays)
+    )(core, places, count, index, kept, small, mod, *chunks.arrays)
 
 
 class Chunks:
-    def __init__(self, mine, other):
-        self.arrays = list(mine) + list(other)
-        self.counts = [array.shape[0] for array in mine]
+    def __init__(self, mine, other, part=0, middle=0):
+        self.sources = list(mine), list(other)
+        self.part, self.middle = part, middle
+        self.arrays = [entry[0] for source in self.sources for entry in source]
         self.specs = [anywhere] * len(self.arrays)
 
-    def load(self, refs, places_ref, from_mine, row, target, sem):
-        count = len(self.counts)
-        rows = pl.ds(row, target.shape[1])
-        place = 0
-        for ref, size in zip(refs[:count] if from_mine else refs[count:], self.counts):
-            for index in range(size):
-                pltpu.make_async_copy(
-                    ref.at[index, rows], target.at[places_ref[place]], sem
-                ).start()
-                place += 1
-
-    def load_block(self, refs, places_ref, core_ref, block, target, sem, first=0):
+    def span(self, kind, bit):
+        part, middle = self.part, self.middle
+        start = part * bit
+        return {
+            "piece": (start, start + part + middle),
+            "first": (start, start + middle),
+            "second": (start + middle, start + part + middle),
+            "got": ((0, part) if bit else (part + middle, 2 * part + middle)),
+            "all": (0, 1 << 20),
+        }[kind]
+
+    def spans(self, kind, bit):
+        if kind == "pair":
+            return [self.span("piece", bit) + (0,), self.span("got", bit) + (self.part + self.middle,)]
+        return [self.span(kind, bit) + (0,)]
+
+    def load(self, refs, places_ref, spot_ref, from_mine, row, target, sem):
+        source = self.sources[0 if from_mine else 1]
+        refs = refs[: len(source)] if from_mine else refs[len(self.sources[0]) :]
+
+        def start(ref, kind, places, bit):
+            for low, high, base in self.spans(kind, bit):
+                begin, end = max(row, low), min(row + target.shape[1], high)
+                for index, place in enumerate(places if begin < end else []):
+                    pltpu.make_async_copy(
+                        ref.at[index, pl.ds(base + begin - low, end - begin)],
+                        target.at[places_ref[place], pl.ds(begin - row, end - begin)],
+                        sem,
+                    ).start()
+
+        for ref, (_, kind, places) in zip(refs, source):
+            if kind == "all":
+                start(ref, kind, places, 0)
+        if any(kind != "all" for _, kind, _ in source):
+            for bit in (0, 1):
+
+                @pl.when(spot_ref[1] == bit)
+                def _():
+                    for ref, (_, kind, places) in zip(refs, source):
+                        if kind != "all":
+                            start(ref, kind, places, bit)
+
+    def load_block(self, refs, places_ref, spot_ref, block, target, sem, first=0):
         owner, row = block // 2, (first + block % 2) * target.shape[1]
 
-        @pl.when(core_ref[0] == owner)
+        @pl.when(spot_ref[0] == owner)
         def _():
-            self.load(refs, places_ref, True, row, target, sem)
-
-        @pl.when(core_ref[0] != owner)
+            self.load(refs, places_ref, spot_ref, True, row, target, sem)
+
+        @pl.when(spot_ref[0] != owner)
         def _():
-            self.load(refs, places_ref, False, row, target, sem)
+            self.load(refs, places_ref, spot_ref, False, row, target, sem)
 
 
 def wait_block(target, sem):
@@ -173,7 +205,7 @@
         store(head, jnp.concatenate([values[:, head * HD : (head + 1) * HD], blank], axis=1))
 
 
-def project_kernel(core_ref, places_ref, norm_ref, bias_ref, *rest, chunks):
+def project_kernel(core_ref, places_ref, norm_ref, small_ref, *rest, chunks):
     refs, (out_ref, weight, sems) = rest[: len(chunks.arrays)], rest[len(chunks.arrays) :]
     step = pl.program_id(0)
 
@@ -183,10 +215,12 @@
             chunks.load_block(refs, places_ref, core_ref, block, weight.at[block], sems.at[block])
 
     wait_block(weight.at[step], sems.at[step])
+    key_free = jnp.where(step == 1, 0.0, 1.0)
+    bias = jnp.where(step == 0, small_ref[1:2], small_ref[2:3]) * key_free
     half = norm_ref.shape[0] // 2
     for part in range(2):
         rows = slice(part * half, (part + 1) * half)
-        result = product(norm_ref[rows], square(weight[step])) + bias_ref[0]
+        result = product(norm_ref[rows], square(weight[step])) + bias
 
         def store(head, value):
             out_ref[0, head, rows] = value
@@ -194,7 +228,7 @@
         split_heads(result.astype(bf16), store)
 
 
-def project_call(core, places, norm, bias, chunks):
+def project_call(core, places, norm, small, chunks):
     seq_len, width = norm.shape
     return pl.pallas_call(
         functools.partial(project_kernel, chunks=chunks),
@@ -203,7 +237,7 @@
             smem,
             smem,
             whole_block(norm),
-            pl.BlockSpec((1, 1, width), lambda i: (i, 0, 0)),
+            whole_block(small),
         ]
         + chunks.specs,
         out_specs=pl.BlockSpec((1, H, seq_len, LANES), lambda i: (i, 0, 0, 0)),
@@ -214,7 +248,7 @@
         ],
         compiler_params=params(),
         cost_estimate=cost(6 * seq_len * width * width, 12 * seq_len * width + 6 * width * width),
-    )(core, places, norm, bias, *chunks.arrays)
+    )(core, places, norm, small, *chunks.arrays)
 
 
 def attend_kernel(query_ref, key_ref, value_ref, mix_ref, log_ref, *, size, factor):
@@ -314,7 +348,7 @@
     )
 
 
-def mix_kernel(core_ref, places_ref, start_ref, bias_ref, mod_ref, *rest, chunks):
+def mix_kernel(core_ref, places_ref, start_ref, small_ref, mod_ref, *rest, chunks):
     mix_refs, rest = rest[:groups], rest[groups:]
     refs, rest = rest[: len(chunks.arrays)], rest[len(chunks.arrays) :]
     joined_ref, branch_ref, middle_ref, norm_ref, weight, sem = rest
@@ -326,7 +360,7 @@
 
     joined = join_heads(mix_refs)
     joined_ref[...] = joined
-    branch = product(joined, square(weight[...])) + bias_ref[...]
+    branch = product(joined, square(weight[...])) + small_ref[3:4]
     branch_ref[...] = branch
     middle = start_ref[...] + mod_ref[2:3] * branch
     middle_ref[...] = middle
@@ -334,14 +368,14 @@
     norm_ref[...] = (unit * (1.0 + mod_ref[4:5]) + mod_ref[3:4]).astype(bf16)
 
 
-def mix_call(core, places, mix, start, bias, mod, chunks):
+def mix_call(core, places, mix, start, small, mod, chunks):
     seq_len, width = start.shape
     rows = seq_len // 4
     block = row_block(rows, width)
     return pl.pallas_call(
         functools.partial(mix_kernel, chunks=chunks),
         grid=(4,),
-        in_specs=[smem, smem, block, whole_block(bias), whole_block(mod)]
+        in_specs=[smem, smem, block, whole_block(small), whole_block(mod)]
         + [pl.BlockSpec((H // groups, rows, LANES), lambda i: (0, i, 0))] * groups
         + chunks.specs,
         out_specs=[block] * 4,
@@ -351,7 +385,7 @@
         scratch_shapes=[pltpu.VMEM((8, width // 8, width), bf16), pltpu.SemaphoreType.DMA],
         compiler_params=params(),
         cost_estimate=cost(2 * seq_len * width * width, 18 * seq_len * width),
-    )(core, places, start, bias, mod, *mix, *chunks.arrays)
+    )(core, places, start, small, mod, *mix, *chunks.arrays)
 
 
 def gelu_parts(values):
@@ -365,8 +399,7 @@
 
 
 def feed_kernel(
-    core_ref, places_ref, norm_ref, middle_ref, cot_ref, branch_ref, mod_ref, up_bias_ref, down_bias_ref,
-    *rest, source
+    core_ref, places_ref, norm_ref, middle_ref, cot_ref, branch_ref, mod_ref, small_ref, *rest, source
 ):
     refs, rest = rest[: len(source.arrays)], rest[len(source.arrays) :]
     (
@@ -395,14 +428,14 @@
             wait_block(up.at[chunk], sems.at[0, chunk])
             wait_block(down.at[chunk], sems.at[1, chunk])
 
-        before = product(norm, square(up[chunk])) + up_bias_ref[chunk]
+        before = product(norm, square(up[chunk])) + small_ref[5 + chunk : 6 + chunk]
         hidden, slope = gelu_parts(before)
         hidden = hidden.astype(bf16)
         hidden_ref[chunk] = hidden
         slopes[chunk] = slope.astype(slopes.dtype)
         part = product(hidden, square(down[chunk]))
         total = part if total is None else total + part
-    branch_two = total + down_bias_ref[...]
+    branch_two = total + small_ref[4:5]
     middle, cot = middle_ref[...], cot_ref[...]
     gate_two = mod_ref[5:6]
     out_ref[...] = middle + gate_two * branch_two
@@ -428,7 +461,7 @@
     sums_ref[5:6] += column_sum(grad_one.astype(f32))
 
 
-def feed_call(core, places, norm, middle, cot, branch, mod, up_bias, down_bias, source):
+def feed_call(core, places, norm, middle, cot, branch, mod, small, source):
     seq_len, width = middle.shape
     steps = 4
     rows = seq_len // steps
@@ -446,8 +479,7 @@
             block,
             block,
             whole_block(mod),
-            whole_block(up_bias),
-            whole_block(down_bias),
+            whole_block(small),
         ]
         + source.specs,
         out_specs=[
@@ -478,7 +510,7 @@
         ],
         compiler_params=params(),
         cost_estimate=cost(32 * seq_len * width * width, 60 * seq_len * width, 4 * seq_len * width),
-    )(core, places, norm, middle, cot, branch, mod, up_bias, down_bias, *source.arrays)
+    )(core, places, norm, middle, cot, branch, mod, small, *source.arrays)
 
 
 def feed_weight_kernel(first_ref, norm_ref, pre_ref, hidden_ref, grad_ref, out_ref):
@@ -713,6 +745,33 @@
     )(core, places, count, index, column, middle_grad, start, mod, *grads, *chunks.arrays)
 
 
+def collect_kernel(first_ref, second_ref, feed_ref, up_ref, mod_ref, small_ref):
+    start = first_ref[...] + second_ref[...]
+    feed = feed_ref[...]
+    row = lambda values, number: values[number : number + 1]
+    blank = jnp.zeros((7, start.shape[1]), f32)
+    mod_ref[...] = jnp.concatenate(
+        [row(start, 3), row(start, 2), row(feed, 4), row(feed, 3), row(feed, 2), row(feed, 0)]
+    ).astype(bf16)
+    small_ref[...] = jnp.concatenate(
+        [row(start, 4), row(start, 0), row(start, 1), row(feed, 5), row(feed, 1)]
+        + [up_ref[block] for block in range(4)]
+        + [blank]
+    ).astype(bf16)
+
+
+def collect_call(first, second, feed, up):
+    width = first.shape[1]
+    return pl.pallas_call(
+        collect_kernel,
+        out_shape=[
+            jax.ShapeDtypeStruct((6, width), bf16),
+            jax.ShapeDtypeStruct((16, width), bf16),
+        ],
+        compiler_params=params(),
+    )(first, second, feed, up)
+
+
 def swap_pairs(size, bit):
     return [(place, place ^ bit) for place in range(size)]
 
@@ -761,48 +820,60 @@
 class Gather:
     def __init__(self, ring, mine, other, part, middle):
         self.ring, self.part, self.middle = ring, part, middle
-        self.mine, self.other = [mine[None]], [other[None]]
+        self.mine, self.other = [(mine[None], "all", [0])], [(other[None], "all", [0])]
         payload = lax.dynamic_slice_in_dim(mine, part * ring.x_bit, part + middle, 0)
         self.pieces = [payload, payload]
         self.distance = 0
-        self.arrived = self.whole = None
+        self.own = self.pair = None
 
     def issue(self):
         ring, flight = self.ring, {}
-        bit, half = ring.x_bit, self.ring.size // 2
+        middle, half = self.middle, ring.size // 2
         if self.distance < half:
             self.distance += 1
             ahead, behind = self.pieces
             if self.distance == half:
-                split = ahead.shape[0] // 2
-                ahead, behind = ahead[:split], behind[split:]
+                ahead, behind = ahead[:middle], behind[middle:]
             flight["ring"] = [ring.forward(ahead), ring.backward(behind)]
-        if self.arrived is not None:
-            own = lax.dynamic_slice_in_dim(self.arrived, self.middle * bit, self.part, 1)
-            flight["x"] = swap_x(own)
-        if self.whole is not None:
-            flight["core"] = swap_core(self.whole)
+        if self.own is not None:
+            flight["x"] = swap_x(self.own)
+        if self.pair is not None:
+            flight["core"] = swap_core(self.pair)
         return flight
 
     def land(self, flight):
-        bit, waiting = self.ring.x_bit, self.arrived
-        self.arrived = self.whole = None
-        if "ring" in flight:
-            self.pieces = flight["ring"]
-            if self.distance == self.ring.size // 2:
-                self.arrived = jnp.concatenate(self.pieces)[None]
-            else:
-                self.arrived = jnp.stack(self.pieces)
+        bit, part, middle = self.ring.x_bit, self.part, self.middle
+        if "core" in flight:
+            self.other.append((flight["core"], "pair", self.pair_places))
+        self.pair = self.own = None
         if "x" in flight:
             got = flight["x"]
-            self.whole = jnp.where(
-                bit == 0,
-                jnp.concatenate([waiting, got], axis=1),
-                jnp.concatenate([got, waiting], axis=1),
-            )
-            self.mine.append(self.whole)
-        if "core" in flight:
-            self.other.append(flight["core"])
+            self.mine.append((got, "got", self.places))
+            if len(self.places) == 1:
+                ahead, behind = self.pieces
+                self.pair = jnp.concatenate([ahead, behind, got[0]])[None]
+            else:
+                self.pair = jnp.concatenate([jnp.stack(self.pieces), got], axis=1)
+            self.pair_places = self.places
+        if "ring" in flight:
+            ahead, behind = self.pieces = flight["ring"]
+            place = 2 * self.distance - 1
+            if self.distance == self.ring.size // 2:
+                self.places = [place]
+                self.mine += [(ahead[None], "first", [place]), (behind[None], "second", [place])]
+                self.own = jnp.where(bit == 0, ahead[:part], behind)[None]
+            else:
+                self.places = [place, place + 1]
+                self.mine += [(ahead[None], "piece", [place]), (behind[None], "piece", [place + 1])]
+                self.own = jnp.stack(
+                    [
+                        lax.dynamic_slice_in_dim(piece, middle * bit, part, 0)
+                        for piece in self.pieces
+                    ]
+                )
+
+    def chunks(self):
+        return Chunks(self.mine, self.other, self.part, self.middle)
 
 
 class Scatter:
@@ -867,6 +938,15 @@
 
 def scatter_plain(chip):
     return lax.psum_scatter(chip, "tok", scatter_dimension=0, tiled=True)[0]
+
+
+def gather_grp(values):
+    step = 1
+    while step < lax.axis_size("grp"):
+        got = lax.ppermute(values, "grp", swap_pairs(lax.axis_size("grp"), step))
+        values = jnp.concatenate([values, got])
+        step *= 2
+    return values
 
 
 def add_x(shard):
@@ -949,7 +1029,6 @@
     _, seq_len, width = cotangent.shape
     tok_count = lax.axis_size("tok")
     core = lax.axis_index("grp") % 2
-    core_row = core.reshape(1)
     share = input_weight.shape[0]
     position_rows = position_table.shape[0]
 
@@ -961,50 +1040,47 @@
 
     ring = Ring()
 
+    core_row = jnp.stack([core, ring.x_bit])
     condition_low = jax.nn.silu(condition).astype(bf16)
     slots_here = kept_tokens.shape[1]
-    condition_rows = jnp.broadcast_to(condition_low, (tok_count, 8, width))
-    arrived = exchange(jnp.concatenate([kept_tokens.astype(bf16), condition_rows], axis=1))
+    small_here = jnp.concatenate(
+        [
+            jnp.stack([mask_token, query_bias, value_bias, output_bias, down_bias]),
+            up_bias.reshape(4, share),
+        ]
+    ).astype(bf16)
+    extra = lax.dynamic_update_slice(
+        jnp.zeros((16, width), bf16), small_here, (0, share * lax.axis_index("tok"))
+    )
+    extra = jnp.concatenate([extra[:9], condition_low, extra[10:]])
+    arrived = exchange(
+        jnp.concatenate(
+            [kept_tokens.astype(bf16), jnp.broadcast_to(extra, (tok_count, 16, width))], axis=1
+        )
+    )
     routed = arrived[:, :slots_here].reshape(-1, width)
-    condition_group = arrived[:, slots_here]
+    condition_group = arrived[:, slots_here + 9]
+    small = jnp.sum(arrived[:, slots_here:].astype(f32), axis=0)
 
     modulation_low = modulation_weight.astype(bf16)
 
-    def modulate_all(conditions):
+    def modulate_all(conditions, weight):
         modulation_part = jnp.dot(
-            conditions, modulation_low, preferred_element_type=f32
+            conditions, weight, preferred_element_type=f32
         ) + modulation_bias.astype(bf16).astype(f32)
         return exchange(modulation_part).reshape(6, width)
 
-    condition_all = lax.all_gather(condition_group, "grp", axis=0, tiled=True)
+    condition_all = gather_grp(condition_group)
 
     ringed = share % 16 == 0 and lax.axis_size("grp") == 4
-    small_parts = [mask_token, query_bias, value_bias, output_bias, down_bias, up_bias]
-    small_widths = [part.shape[0] for part in small_parts]
-    cuts = [sum(small_widths[:number]) for number in range(len(small_widths) + 1)]
-    small_rows = position_rows // 8
-    table_rows = position_rows * 5 // 8
-    tail_rows = position_rows - table_rows
-
-    def as_rows(parts):
-        flat = jnp.concatenate(parts, axis=-1)
-        lead = flat.shape[:-1]
-        flat = jnp.pad(flat, [(0, 0)] * len(lead) + [(0, small_rows * width - flat.shape[-1])])
-        return flat.reshape(lead + (small_rows, width))
-
-    def table_parts(table, small):
-        lead = table.shape[:-2]
-        blank = jnp.zeros(lead + (table_rows - tail_rows - small_rows, width), table.dtype)
-        return table[..., :table_rows, :], jnp.concatenate(
-            [table[..., table_rows:, :], small, blank], axis=-2
-        )
+    table_rows = position_rows // 2
 
     input_low = input_weight.astype(bf16)
     input_blocks = [input_low[:, number * width : (number + 1) * width] for number in range(3)]
-    table_low = table_parts(position_table.astype(bf16), as_rows(small_parts).astype(bf16))
+    position_low = position_table.astype(bf16)
     attention_low = (
-        jnp.concatenate(input_blocks[:2] + [table_low[0]]),
-        jnp.concatenate([input_blocks[2], output_weight.astype(bf16), table_low[1]]),
+        jnp.concatenate(input_blocks[:2] + [position_low[:table_rows]]),
+        jnp.concatenate([input_blocks[2], output_weight.astype(bf16), position_low[table_rows:]]),
     )
     up_low = spread_call(up_weight, tok_count)
     down_low = down_weight.astype(bf16).reshape(4, share, width)
@@ -1013,72 +1089,64 @@
         for half in (0, 2)
     )
 
-    attention_cut, feed_cut = (8 * share // 9, 7 * share // 9), (4 * share // 3, 4 * share // 3)
+    attention_cut, feed_cut = (7 * share // 9, 8 * share // 9), (4 * share // 3, 4 * share // 3)
     if ringed:
         mine, other = by_core(*attention_low), by_core(*attention_low[::-1])
         gather = Gather(ring, mine, other, *attention_cut)
+        (flight,) = sync(gather.issue())
+        gather.land(flight)
         mine, other = by_core(*feed_low), by_core(*feed_low[::-1])
+        flight, mine, other, modulation_low = sync(gather.issue(), mine, other, modulation_low)
+        gather.land(flight)
         feed_gather = Gather(ring, mine, other, *feed_cut)
-        for _ in range(2):
-            (flight,) = sync(gather.issue())
-            gather.land(flight)
-        flight, condition_group, routed = sync(gather.issue(), condition_group, routed)
+        flight, condition_group, routed, small = sync(
+            gather.issue(), condition_group, routed, small
+        )
         gather.land(flight)
-    mod = modulate_all(condition_group)
+    mod = modulate_all(condition_group, modulation_low)
     if ringed:
+        (flight,) = sync(gather.issue())
+        gather.land(flight)
+        feed_flight = feed_gather.issue()
         flight, mod = sync(gather.issue(), mod)
         gather.land(flight)
-        feed_gather.pieces, gather.arrived = sync(feed_gather.pieces, gather.arrived)
-        feed_flight = feed_gather.issue()
         (flight,) = sync(gather.issue())
         gather.land(flight)
-        flight, feed_flight = sync(gather.issue(), feed_flight)
-        gather.land(flight)
-        feed_gather.land(feed_flight)
-        attention_chunks = Chunks(gather.mine, gather.other)
+        attention_chunks = gather.chunks()
         distances = [0]
         for distance in range(1, ring.size // 2):
             distances += [-distance, distance]
         places = ring.tok_at(jnp.array(distances + [ring.size // 2], jnp.int32))
-        small_rel = jnp.concatenate(
-            [
-                by_core(other, mine)[:, 2 * share + tail_rows : 2 * share + tail_rows + small_rows]
-                for mine, other in zip(gather.mine, gather.other)
-            ]
-        )
-        small = jnp.zeros_like(small_rel).at[places].set(small_rel).reshape(tok_count, -1)
     else:
         places = jnp.arange(8, dtype=jnp.int32)
         mine = gather_plain(by_core(*attention_low)[: 2 * share], share)
-        attention_chunks = Chunks([mine], [swap_core(mine)])
-        mine = gather_plain(by_core(*feed_low), share)
-        feed_chunks = Chunks([mine], [swap_core(mine)])
-        table = lax.all_gather(
-            jnp.concatenate([position_table.astype(bf16), as_rows(small_parts).astype(bf16)]), "tok"
+        everywhere = list(range(8))
+        plain_chunks = lambda mine: Chunks(
+            [(mine, "all", everywhere)], [(swap_core(mine), "all", everywhere)]
         )
-        small = table[:, position_rows:].reshape(tok_count, -1)
-        table = table[:, :position_rows].reshape(8, -1, width)
-    mask_full, query_bias_full, value_bias_full, output_bias_full, down_bias_full = (
-        small[:, cuts[number] : cuts[number + 1]].reshape(1, width).astype(f32)
-        for number in range(5)
-    )
-    up_bias_full = (
-        small[:, cuts[5] : cuts[6]].reshape(tok_count, 4, share).transpose(1, 0, 2).reshape(4, 1, width)
-    ).astype(f32)
+        attention_chunks = plain_chunks(mine)
+        feed_chunks = plain_chunks(gather_plain(by_core(*feed_low), share))
+        table = lax.all_gather(position_low, "tok").reshape(8, -1, width)
 
     if ringed:
         table_chunks, table_row, table_share = attention_chunks, 2 * share, table_rows
     else:
         table_share = table.shape[1] // 2
         halves = table[:, :table_share], table[:, table_share:]
-        table_chunks, table_row = Chunks([by_core(*halves)], [by_core(*halves[::-1])]), 0
+        table_chunks, table_row = (
+            Chunks(
+                [(by_core(*halves), "all", everywhere)], [(by_core(*halves[::-1]), "all", everywhere)]
+            ),
+            0,
+        )
     start, norm_one = start_call(
-        core_row, places, kept_count, kept_index, routed, mask_full, mod, table_chunks, table_row,
+        core_row, places, kept_count, kept_index, routed, small, mod, table_chunks, table_row,
         table_share, seq_len,
     )
-    blank = jnp.zeros_like(query_bias_full)
-    projected_bias = jnp.stack([query_bias_full, blank, value_bias_full])
-    projected = project_call(core_row, places, norm_one, projected_bias, attention_chunks)
+    if ringed:
+        feed_flight, start, norm_one = sync(feed_flight, start, norm_one)
+        feed_gather.land(feed_flight)
+    projected = project_call(core_row, places, norm_one, small, attention_chunks)
     if ringed:
         flight, projected, start = sync(feed_gather.issue(), projected, start)
         feed_gather.land(flight)
@@ -1089,14 +1157,14 @@
             flight, attended, projected = sync(feed_gather.issue(), attended, projected)
             feed_gather.land(flight)
     joined, branch_one, middle, norm_two = mix_call(
-        core_row, places, [pair[0] for pair in attended], start, output_bias_full, mod, attention_chunks
+        core_row, places, [pair[0] for pair in attended], start, small, mod, attention_chunks
     )
     if ringed:
         flight, norm_two = sync(feed_gather.issue(), norm_two)
         feed_gather.land(flight)
         (flight,) = sync(feed_gather.issue())
         feed_gather.land(flight)
-        feed_chunks = Chunks(feed_gather.mine, feed_gather.other)
+        feed_chunks = feed_gather.chunks()
     (
         block_output,
         hidden,
@@ -1107,12 +1175,11 @@
         feed_sums,
         up_bias_sum,
     ) = feed_call(
-        core_row, places, norm_two, middle, cotangent[0], branch_one, mod, up_bias_full, down_bias_full,
-        feed_chunks,
-    )
-    feed_other = feed_weight_call(2 - 2 * core_row, norm_two, pre_grad, hidden, grad_two)
+        core_row, places, norm_two, middle, cotangent[0], branch_one, mod, small, feed_chunks
+    )
+    feed_other = feed_weight_call(2 - 2 * core_row[:1], norm_two, pre_grad, hidden, grad_two)
     feed_other, norm_two, grad_one = sync(feed_other, norm_two, grad_one)
-    feed_mine = feed_weight_call(2 * core_row, norm_two, pre_grad, hidden, grad_two)
+    feed_mine = feed_weight_call(2 * core_row[:1], norm_two, pre_grad, hidden, grad_two)
     feed_got, feed_mine, grad_one = sync(swap_core(feed_other), feed_mine, grad_one)
     mix_grad = mix_grad_call(core_row, places, grad_one, attention_chunks)
     if ringed:
@@ -1133,73 +1200,95 @@
             half, core_row, places, kept_count, kept_index, grads, middle_grad, start, mod, attention_chunks
         )
 
-    attention_other = attention_weights(1 - core_row, norm_one)
+    attention_other = attention_weights(1 - core_row[:1], norm_one)
     if ringed:
         flight, attention_other, norm_one, grads = sync(
             feed_scatter.hop(), attention_other, norm_one, grads
         )
         feed_scatter.land(flight)
-    attention_mine = attention_weights(core_row, norm_one)
+        feed_flight = feed_scatter.hop()
+    attention_mine = attention_weights(core_row[:1], norm_one)
     attention_got = swap_core(attention_other)
+    if ringed:
+        attention_mine, attention_got, grads = sync(attention_mine, attention_got, grads)
+        scatter = Scatter(ring, attention_mine, attention_got)
+        flight = scatter.hop()
     first_half = start_back(0, grads)
     if ringed:
-        flight, attention_mine, attention_got, first_half, grads = sync(
-            feed_scatter.hop(), attention_mine, attention_got, first_half, grads
-        )
-        feed_scatter.land(flight)
+        flight, feed_flight, first_half, grads = sync(flight, feed_flight, first_half, grads)
+        scatter.land(flight)
+        feed_scatter.land(feed_flight)
         feed_shard = feed_scatter.total()
-        scatter = Scatter(ring, attention_mine, attention_got)
+        feed_cross = swap_x(feed_shard)
         second_half = start_back(1, grads)
-        flight, second_half = sync(scatter.hop(), second_half)
+        flight, second_half, feed_cross = sync(scatter.hop(), second_half, feed_cross)
         scatter.land(flight)
     else:
         second_half = start_back(1, grads)
     row_grad = jnp.concatenate([first_half[0], second_half[0]])
     slot_grad = first_half[1] + second_half[1]
-    start_sums = first_half[2] + second_half[2]
-    kept_grad = exchange(slot_grad.reshape(tok_count, -1, width)).astype(f32)
-
-    up_sums = up_bias_sum.reshape(4, tok_count, share).transpose(1, 0, 2).reshape(tok_count, -1)
-    rows_of = lambda row: row.reshape(tok_count, -1)
-    small_grads = as_rows(
-        [
-            rows_of(start_sums[4]),
-            rows_of(start_sums[0]),
-            rows_of(start_sums[1]),
-            rows_of(feed_sums[5]),
-            rows_of(feed_sums[1]),
-            up_sums,
-        ]
-    ).astype(bf16)
+    modulation_grad, small_grad = collect_call(
+        first_half[2], second_half[2], feed_sums, up_bias_sum
+    )
+
     position_grad = row_grad.reshape(tok_count, position_rows, width)
-    tables = table_parts(position_grad, small_grads)
-    table_got = swap_core(by_core(tables[1], tables[0]))
-    table_chip = add_low(by_core(tables[0], tables[1]), table_got)
-    table_shard = jnp.sum(exchange(table_chip).astype(f32), axis=0).astype(bf16)
-    table_shard = add_x(table_shard)
-    table_far = swap_core(table_shard)
-    first, second = by_core(table_shard, table_far), by_core(table_far, table_shard)
-    position_total = jnp.concatenate([first, second[:tail_rows]]).astype(f32)
-    small_total = second[tail_rows : tail_rows + small_rows].astype(f32).reshape(-1)
+    halves = [
+        half.reshape(-1, width)
+        for half in (position_grad[:, :table_rows], position_grad[:, table_rows:])
+    ]
+    table_got = swap_core(jnp.concatenate([by_core(halves[1], halves[0]), small_grad]))
+    modulation_grad_group = exchange(modulation_grad.reshape(tok_count, -1))
     if ringed:
-        while scatter.distance > 0:
-            (flight,) = sync(scatter.hop())
-            scatter.land(flight)
+        flight, table_got, modulation_grad_group = sync(
+            scatter.hop(), table_got, modulation_grad_group
+        )
+        scatter.land(flight)
+    table_chip = add_low(jnp.concatenate([by_core(halves[0], halves[1]), small_grad]), table_got)
+    arrived = exchange(
+        jnp.concatenate(
+            [
+                slot_grad.reshape(tok_count, -1, width),
+                table_chip[:-16].reshape(tok_count, table_rows, width),
+                jnp.broadcast_to(table_chip[-16:], (tok_count, 16, width)),
+            ],
+            axis=1,
+        )
+    )
+    modulation_grad_all = gather_grp(modulation_grad_group)
+    condition_part = jnp.einsum(
+        "ie,de->id", modulation_grad_group, modulation_low, preferred_element_type=f32
+    )
+    modulation_total = jnp.einsum(
+        "id,ie->de", condition_all, modulation_grad_all, preferred_element_type=f32
+    )
+    modulation_bias_total = jnp.sum(modulation_grad_all.astype(f32), axis=0)
+    if ringed:
+        flight, condition_part, modulation_total, modulation_bias_total = sync(
+            scatter.hop(), condition_part, modulation_total, modulation_bias_total
+        )
+        scatter.land(flight)
+    condition_part, arrived = sync(condition_part, arrived)
+    condition_parts = exchange(condition_part)
+    kept_low = arrived[:, :slots_here]
+    table_shard = add_x(jnp.sum(arrived[:, slots_here:].astype(f32), axis=0).astype(bf16))
+    if ringed:
         attention_shard = add_x(scatter.total())
+        feed_shard = add_low(feed_shard, feed_cross)
     else:
         attention_chip = by_tok(add_low(attention_mine, attention_got), share)
         attention_shard = add_x(scatter_plain(attention_chip))
-        feed_shard = scatter_plain(by_tok(add_low(feed_mine, feed_got), share))
-    feed_shard = add_x(feed_shard)
-
-    (
-        mask_total,
-        query_bias_total,
-        value_bias_total,
-        output_bias_total,
-        down_bias_total,
-        up_bias_total,
-    ) = (small_total[cuts[number] : cuts[number + 1]] for number in range(6))
+        feed_shard = add_x(scatter_plain(by_tok(add_low(feed_mine, feed_got), share)))
+    table_far = swap_core(table_shard[:table_rows])
+    first, second = by_core(table_shard[:table_rows], table_far), by_core(table_far, table_shard[:table_rows])
+    position_total = jnp.concatenate([first, second]).astype(f32)
+    small_total = lax.dynamic_slice_in_dim(
+        table_shard[table_rows:], share * lax.axis_index("tok"), share, 1
+    ).astype(f32)
+    mask_total, query_bias_total, value_bias_total, output_bias_total, down_bias_total = (
+        small_total[number] for number in range(5)
+    )
+    up_bias_total = small_total[5:9].reshape(-1)
+    kept_grad = kept_low.astype(f32)
     far = swap_core(attention_shard)
     first, second = by_core(attention_shard, far).astype(f32), by_core(far, attention_shard).astype(f32)
     input_total = jnp.concatenate([first[:share], first[share:], second[:share]], axis=1)
@@ -1211,19 +1300,7 @@
         [by_core(feed_shard[2:], feed_far[2:]), by_core(feed_far[2:], feed_shard[2:])]
     ).reshape(-1, width).astype(f32)
 
-    modulation_grad = jnp.concatenate(
-        [start_sums[3], start_sums[2], feed_sums[4], feed_sums[3], feed_sums[2], feed_sums[0]]
-    ).astype(bf16)
-    modulation_grad_group = exchange(modulation_grad.reshape(tok_count, -1))
-    modulation_grad_all = lax.all_gather(modulation_grad_group, "grp", axis=0, tiled=True)
-    modulation_total = jnp.einsum(
-        "id,ie->de", condition_all, modulation_grad_all, preferred_element_type=f32
-    )
-    modulation_bias_total = jnp.sum(modulation_grad_all.astype(f32), axis=0)
-    condition_part = jnp.einsum(
-        "ie,de->id", modulation_grad_group, modulation_low, preferred_element_type=f32
-    )
-    condition_low_grad = jnp.sum(exchange(condition_part), axis=0, keepdims=True)
+    condition_low_grad = jnp.sum(condition_parts, axis=0, keepdims=True)
     _, silu_back = jax.vjp(jax.nn.silu, condition)
     condition_grad = silu_back(condition_low_grad)[0]
     return (

time: 751 us -> 703 us (0.936)
  local copies, waits for them, and re-layouts: 53.9 us -> 28.7 us
  other arithmetic: 114 us -> 96.5 us
  waiting for transfers between devices: 141 us -> 154 us
  starting transfers between devices: 99.6 us -> 86.8 us
  Pallas kernels: 313 us -> 324 us
  blocking collectives: 11 us -> 0 us
    ppermute x16, waiting for transfers between devices: 90.2 us -> 44.1 us  [forward(): return lax.ppermute(values, 'tok', self.ahead)]
    all_to_all x6 -> x5, waiting for transfers between devices: 26 us -> 52.9 us  [exchange(): lax.all_to_all(values, 'tok', split_axis=0, concat_axis=0, tiled=True)]
    select_n x9 -> x1, other arithmetic: 24.9 us -> 0.52 us  [tok_at(): jnp.where(place < self.size // 2, 2 * place, 2 * (self.size - 1 - place)...]
    ppermute x8 -> x9, waiting for transfers between devices: 9.06 us -> 27.7 us  [swap_x(): return lax.ppermute(values, 'grp', swap_pairs(lax.axis_size('grp'), 2))]
    concatenate x2 -> x13, other arithmetic: 1.43 us -> 19.9 us  [the longest x6 13.6 us: land(): self.pair = jnp.concatenate([jnp.stack(self.pieces), got], axis=1)]
    all_to_all x6 -> x5, starting transfers between devices: 37 us -> 21.7 us  [exchange(): lax.all_to_all(values, 'tok', split_axis=0, concat_axis=0, tiled=True)]
    unnamed x103 -> x124, local copies, waits for them, and re-layouts: 19.1 us -> 6.26 us
    all_gather x2 -> x0, blocking collectives: 11 us -> none  [the longest x1 5.71 us: on_device(): condition_all = lax.all_gather(condition_group, 'grp', axis=0, tiled=True)]
  transfers between devices with their start and end apart: 63 -> 66, of which waited for: 28 -> 31; matrix products, arithmetic and copies ran while one was open for 16% -> 13% of each run, Pallas kernels for 29% -> 31%
where the time goes in v4:
time: 703 us; the launch traced here: 699 us
  Pallas kernels  324 us (46%)
  waiting for transfers between devices  154 us (22%)
  other arithmetic  96.5 us (14%)
  starting transfers between devices  86.8 us (12%)
  local copies, waits for them, and re-layouts  28.7 us (4%)
    pallas_call x1, Pallas kernels, feed_call(): pl.pallas_call(functools.partial(feed_kernel, source=source), grid=(steps...  83.2 us
    pallas_call x4, Pallas kernels, attend_back_call(): pl.pallas_call(functools.partial(attend_back_kernel, size=seq_len // 2, f...  53.2 us
    all_to_all x5, waiting for transfers between devices, exchange(): lax.all_to_all(values, 'tok', split_axis=0, concat_axis=0, tiled=True)  52.9 us
    ppermute x16, waiting for transfers between devices, forward(): return lax.ppermute(values, 'tok', self.ahead)  44.1 us
    pallas_call x2, Pallas kernels, feed_weight_call(): pl.pallas_call(feed_weight_kernel, grid_spec=pltpu.PrefetchScalarGridSpec...  37 us
    pallas_call x2, Pallas kernels, start_back_call(): pl.pallas_call(functools.partial(start_back_kernel, chunks=chunks, first=...  36 us
    pallas_call x4, Pallas kernels, attend_call(): pl.pallas_call(functools.partial(attend_kernel, size=seq_len, factor=math...  34.9 us
    ppermute x16, starting transfers between devices, forward(): return lax.ppermute(values, 'tok', self.ahead)  32.7 us
  transfers between devices with their start and end apart: 66, of which 31 were waited for; matrix products, arithmetic and copies ran while one was open for 13% of the time, Pallas kernels for 31%

profile of v4, /device:TPU:0, one launch (start us, length us, event | category | flops | bytes accessed | tf_op | source)
XLA Modules:
  0.0 698.5 jit_solution(15678039209041086615)
XLA Ops:
  13.9 6.5 all-to-all-start
  33.5 6.8 collective-permute-done.4.rest_3_.rest_7_.rest_15_
  40.3 26.4 %collective-permute-done.2 = bf16[240,1152]{1,0:T(8,128)(2,1)S(1)} collective-permute-done((bf16[240,1152]{1,0:T(8,128)(2,1)S(1)}, bf16[240,1152]{1,0:T(8,128)(2,1)S(1)}, u32[]{:S(2)}, u32[]{:S(2)}) %collective-permute-start.2) | collective-permute-done | bytes 552992 | tf_op jit(solution)/shard_map/ppermute | solution.py:810
  68.0 13.8 %collective-permute-start.8 = (bf16[240,1152]{1,0:T(8,128)(2,1)S(1)}, bf16[240,1152]{1,0:T(8,128)(2,1)S(1)}, u32[]{:S(2)}, u32[]{:S(2)}) collective-permute-start(bf16[240,1152]{1,0:T(8,128)(2,1)S(1)} %collective-permute-done.2), channel_id=1, source_target_pairs={{0,2},{2,4},{4,6},{6,7},{7,5},{5,3},{3,1},{1,0},{8,10},{10,12},{12... | collective-permute-start | bytes 1658888 | tf_op jit(solution)/shard_map/ppermute | solution.py:810
  91.2 6.7 collective-permute-done.10.rest_6_.rest_10_.rest_18_
  106.3 7.7 %collective-permute-done.13 = bf16[112,1152]{1,0:T(8,128)(2,1)S(1)} collective-permute-done((bf16[112,1152]{1,0:T(8,128)(2,1)S(1)}, bf16[112,1152]{1,0:T(8,128)(2,1)S(1)}, u32[]{:S(2)}, u32[]{:S(2)}) %collective-permute-start.13) | collective-permute-done | bytes 258080 | tf_op jit(solution)/shard_map/ppermute | solution.py:813
  129.9 5.4 all-to-all-done.1
  145.4 8.3 %shard_map.307 = (f32[1024,1152]{1,0:T(8,128)}, bf16[1024,1152]{1,0:T(8,128)(2,1)}) custom-call(s32[2]{0:T(128)} %pad_add_fusion.core_ref, s32[8]{0:T(128)} %compare_select_fusion.2.places_ref, s32[1]{0:T(128)S(6)} %copy.60.count_ref, s32[1,768]{1,0:T(1,128)} %index_row_ref.3, bf16[768,1152]{1,0:T(8,128)(2,1)} %bitcast.222, ...), custom_call_target="tpu_custom_call" | custom-call | flops 1811939328 | bytes 16515072 | tf_op jit(solution)/shard_map/pallas_call | solution.py:105
  153.7 8.3 %collective-permute-done.5 = bf16[384,1152]{1,0:T(8,128)(2,1)S(1)} collective-permute-done((bf16[384,1152]{1,0:T(8,128)(2,1)}, bf16[384,1152]{1,0:T(8,128)(2,1)S(1)}, u32[]{:S(2)}, u32[]{:S(2)}) %collective-permute-start.5) | collective-permute-done | bytes 884768 | tf_op jit(solution)/shard_map/ppermute | solution.py:810
  165.9 16.5 %shard_map.308.query_ref.key_ref.value_ref = bf16[3,16,1024,128]{3,2,1,0:T(8,128)(2,1)} custom-call(s32[2]{0:T(128)} %pad_add_fusion.core_ref, s32[8]{0:T(128)} %compare_select_fusion.2.places_ref, bf16[1024,1152]{1,0:T(8,128)(2,1)} %get-tuple-element.315.norm_ref, f32[16,1152]{1,0:T(8,128)} %convert_reduce_fusion.small_ref, ...), custom_call_target="tpu_custom_call" | custom-call | flops 8153726976 | bytes 22118400 | tf_op jit(solution)/shard_map/pallas_call | solution.py:233
  193.8 8.7 %shard_map.309 = (bf16[4,1024,128]{2,1,0:T(8,128)(2,1)}, f32[4,1,1024]{2,1,0:T(1,128)}) custom-call(bf16[3,16,1024,128]{3,2,1,0:T(8,128)(2,1)} %shard_map.308.query_ref.key_ref.value_ref, bf16[3,16,1024,128]{3,2,1,0:T(8,128)(2,1)} %shard_map.308.query_ref.key_ref.value_ref, bf16[3,16,1024,128]{3,2,1,0:T(8,128)(2,1)} %shard_map.308.query_ref.key_ref.value_ref), custom_call_target="tpu_custom_call" | custom-call | flops 4294967296 | bytes 4194304 | tf_op jit(solution)/shard_map/pallas_call | solution.py:279
  202.5 8.7 %shard_map.310 = (bf16[4,1024,128]{2,1,0:T(8,128)(2,1)}, f32[4,1,1024]{2,1,0:T(1,128)}) custom-call(bf16[3,16,1024,128]{3,2,1,0:T(8,128)(2,1)} %shard_map.308.query_ref.key_ref.value_ref, bf16[3,16,1024,128]{3,2,1,0:T(8,128)(2,1)} %shard_map.308.query_ref.key_ref.value_ref, bf16[3,16,1024,128]{3,2,1,0:T(8,128)(2,1)} %shard_map.308.query_ref.key_ref.value_ref), custom_call_target="tpu_custom_call" | custom-call | flops 4294967296 | bytes 4194304 | tf_op jit(solution)/shard_map/pallas_call | solution.py:279
  220.8 8.7 %shard_map.311 = (bf16[4,1024,128]{2,1,0:T(8,128)(2,1)}, f32[4,1,1024]{2,1,0:T(1,128)}) custom-call(bf16[3,16,1024,128]{3,2,1,0:T(8,128)(2,1)} %shard_map.308.query_ref.key_ref.value_ref, bf16[3,16,1024,128]{3,2,1,0:T(8,128)(2,1)} %shard_map.308.query_ref.key_ref.value_ref, bf16[3,16,1024,128]{3,2,1,0:T(8,128)(2,1)} %shard_map.308.query_ref.key_ref.value_ref), custom_call_target="tpu_custom_call" | custom-call | flops 4294967296 | bytes 4194304 | tf_op jit(solution)/shard_map/pallas_call | solution.py:279
  229.5 8.7 %shard_map.312 = (bf16[4,1024,128]{2,1,0:T(8,128)(2,1)}, f32[4,1,1024]{2,1,0:T(1,128)}) custom-call(bf16[3,16,1024,128]{3,2,1,0:T(8,128)(2,1)} %shard_map.308.query_ref.key_ref.value_ref, bf16[3,16,1024,128]{3,2,1,0:T(8,128)(2,1)} %shard_map.308.query_ref.key_ref.value_ref, bf16[3,16,1024,128]{3,2,1,0:T(8,128)(2,1)} %shard_map.308.query_ref.key_ref.value_ref), custom_call_target="tpu_custom_call" | custom-call | flops 4294967296 | bytes 4194304 | tf_op jit(solution)/shard_map/pallas_call | solution.py:279
  243.9 12.3 %shard_map.313 = (bf16[1024,1152]{1,0:T(8,128)(2,1)}, f32[1024,1152]{1,0:T(8,128)}, f32[1024,1152]{1,0:T(8,128)}, bf16[1024,1152]{1,0:T(8,128)(2,1)}) custom-call(s32[2]{0:T(128)} %pad_add_fusion.core_ref, s32[8]{0:T(128)} %compare_select_fusion.2.places_ref, f32[1024,1152]{1,0:T(8,128)} %get-tuple-element.254.start_ref, ...), custom_call_target="tpu_custom_call" | custom-call | flops 2717908992 | bytes 21233664 | tf_op jit(solution)/shard_map/pallas_call | solution.py:375
  260.6 83.2 %shard_map.314 = (f32[1024,1152]{1,0:T(8,128)}, bf16[4,1024,1152]{2,1,0:T(8,128)(2,1)}, bf16[4,1024,1152]{2,1,0:T(8,128)(2,1)}, bf16[1024,1152]{1,0:T(8,128)(2,1...) custom-call(s32[2]{0:T(128)} %pad_add_fusion.core_ref, ...), custom_call_target="tpu_custom_call" | custom-call | flops 43486543872 | bytes 70778880 | tf_op jit(solution)/shard_map/pallas_call | solution.py:471
  343.8 18.5 %shard_map.315 = bf16[8,576,1152]{2,1,0:T(8,128)(2,1)} custom-call(s32[1]{0:T(128)S(6)} %sub.62.first_ref, bf16[1024,1152]{1,0:T(8,128)(2,1)} %get-tuple-element.274.norm_ref, bf16[4,1024,1152]{2,1,0:T(8,128)(2,1)} %get-tuple-element.269.pre_ref, bf16[4,1024,1152]{2,1,0:T(8,128)(2,1)} %get-tuple-element.270.hidden_ref, ...), custom_call_target="tpu_custom_call" | custom-call | flops 10871635968 | bytes 24772608 | tf_op jit(solution)/shard_map/pallas_call | solution.py:534
  362.6 18.4 %shard_map.316 = bf16[8,576,1152]{2,1,0:T(8,128)(2,1)} custom-call(s32[1]{0:T(128)S(6)} %mul.125.first_ref, bf16[1024,1152]{1,0:T(8,128)(2,1)} %get-tuple-element.274.norm_ref, bf16[4,1024,1152]{2,1,0:T(8,128)(2,1)} %get-tuple-element.269.pre_ref, bf16[4,1024,1152]{2,1,0:T(8,128)(2,1)} %get-tuple-element.270.hidden_ref, ...), custom_call_target="tpu_custom_call" | custom-call | flops 10871635968 | bytes 24772608 | tf_op jit(solution)/shard_map/pallas_call | solution.py:534
  381.0 8.6 %shard_map.317.grad_ref = bf16[16,1024,128]{2,1,0:T(8,128)(2,1)} custom-call(s32[2]{0:T(128)} %pad_add_fusion.core_ref, s32[8]{0:T(128)} %compare_select_fusion.2.places_ref, bf16[1024,1152]{1,0:T(8,128)(2,1)} %get-tuple-element.280.grad_ref, bf16[1,352,1152]{2,1,0:T(8,128)(2,1)} %get-tuple-element.417.rest_0_.rest_4_.rest_12_, ...), custom_call_target="tpu_custom_call" | custom-call | flops 2717908992 | bytes 9437184 | tf_op jit(solution)/shard_map/pallas_call | solution.py:630
  393.7 13.4 %shard_map.318 = (bf16[4,1024,128]{2,1,0:T(8,128)(2,1)}, bf16[4,1024,128]{2,1,0:T(8,128)(2,1)}, bf16[4,1024,128]{2,1,0:T(8,128)(2,1)}) custom-call(bf16[3,16,1024,128]{3,2,1,0:T(8,128)(2,1)} %shard_map.308.query_ref.key_ref.value_ref, bf16[3,16,1024,128]{3,2,1,0:T(8,128)(2,1)} %shard_map.308.query_ref.key_ref.value_ref, ...), custom_call_target="tpu_custom_call" | custom-call | flops 10737418240 | bytes 8388608 | tf_op jit(solution)/shard_map/pallas_call | solution.py:328
  414.6 13.2 %shard_map.320 = (bf16[4,1024,128]{2,1,0:T(8,128)(2,1)}, bf16[4,1024,128]{2,1,0:T(8,128)(2,1)}, bf16[4,1024,128]{2,1,0:T(8,128)(2,1)}) custom-call(bf16[3,16,1024,128]{3,2,1,0:T(8,128)(2,1)} %shard_map.308.query_ref.key_ref.value_ref, bf16[3,16,1024,128]{3,2,1,0:T(8,128)(2,1)} %shard_map.308.query_ref.key_ref.value_ref, ...), custom_call_target="tpu_custom_call" | custom-call | flops 10737418240 | bytes 8388608 | tf_op jit(solution)/shard_map/pallas_call | solution.py:328
  427.8 13.3 %shard_map.319 = (bf16[4,1024,128]{2,1,0:T(8,128)(2,1)}, bf16[4,1024,128]{2,1,0:T(8,128)(2,1)}, bf16[4,1024,128]{2,1,0:T(8,128)(2,1)}) custom-call(bf16[3,16,1024,128]{3,2,1,0:T(8,128)(2,1)} %shard_map.308.query_ref.key_ref.value_ref, bf16[3,16,1024,128]{3,2,1,0:T(8,128)(2,1)} %shard_map.308.query_ref.key_ref.value_ref, ...), custom_call_target="tpu_custom_call" | custom-call | flops 10737418240 | bytes 8388608 | tf_op jit(solution)/shard_map/pallas_call | solution.py:328
  443.3 5.4 fusion.4
  450.7 13.4 %shard_map.321 = (bf16[4,1024,128]{2,1,0:T(8,128)(2,1)}, bf16[4,1024,128]{2,1,0:T(8,128)(2,1)}, bf16[4,1024,128]{2,1,0:T(8,128)(2,1)}) custom-call(bf16[3,16,1024,128]{3,2,1,0:T(8,128)(2,1)} %shard_map.308.query_ref.key_ref.value_ref, bf16[3,16,1024,128]{3,2,1,0:T(8,128)(2,1)} %shard_map.308.query_ref.key_ref.value_ref, ...), custom_call_target="tpu_custom_call" | custom-call | flops 10737418240 | bytes 8388608 | tf_op jit(solution)/shard_map/pallas_call | solution.py:328
  464.1 12.0 %shard_map.322 = bf16[8,288,1152]{2,1,0:T(8,128)(2,1)} custom-call(s32[1]{0:T(128)S(6)} %sub.68.owner_ref, bf16[1024,1152]{1,0:T(8,128)(2,1)} %get-tuple-element.315.norm_ref, bf16[1024,1152]{1,0:T(8,128)(2,1)} %get-tuple-element.300.joined_ref, bf16[1024,1152]{1,0:T(8,128)(2,1)} %get-tuple-element.280.grad_ref, ...), custom_call_target="tpu_custom_call" | custom-call | flops 5435817984 | bytes 17104896 | tf_op jit(solution)/shard_map/pallas_call | solution.py:596
  487.1 13.6 %shard_map.323 = bf16[8,288,1152]{2,1,0:T(8,128)(2,1)} custom-call(s32[1]{0:T(128)} %bitcast.owner_ref, bf16[1024,1152]{1,0:T(8,128)(2,1)} %get-tuple-element.315.norm_ref, bf16[1024,1152]{1,0:T(8,128)(2,1)} %get-tuple-element.300.joined_ref, bf16[1024,1152]{1,0:T(8,128)(2,1)} %get-tuple-element.280.grad_ref, ...), custom_call_target="tpu_custom_call" | custom-call | flops 5435817984 | bytes 17104896 | tf_op jit(solution)/shard_map/pallas_call | solution.py:596
  504.9 17.9 %shard_map.324 = (bf16[512,1152]{1,0:T(8,128)(2,1)}, bf16[768,1152]{1,0:T(8,128)(2,1)}, f32[8,1152]{1,0:T(8,128)}) custom-call(s32[2]{0:T(128)} %pad_add_fusion.core_ref, s32[8]{0:T(128)} %compare_select_fusion.2.places_ref, s32[1]{0:T(128)S(6)} %copy.60.count_ref, s32[1,768]{1,0:T(1,128)} %index_row_ref.3, s32[768,1]{1,0:T(8,128)} %copy.47.index_ref, ...), custom_call_target="tpu_custom_call" | custom-call | flops 5435817984 | bytes 15335424 | tf_op jit(solution)/shard_map/pallas_call | solution.py:713
  533.8 18.1 %shard_map.325 = (bf16[512,1152]{1,0:T(8,128)(2,1)}, bf16[768,1152]{1,0:T(8,128)(2,1)}, f32[8,1152]{1,0:T(8,128)}) custom-call(s32[2]{0:T(128)} %pad_add_fusion.core_ref, s32[8]{0:T(128)} %compare_select_fusion.2.places_ref, s32[1]{0:T(128)S(6)} %copy.60.count_ref, s32[1,768]{1,0:T(1,128)} %index_row_ref.3, s32[768,1]{1,0:T(8,128)} %copy.47.index_ref, ...), custom_call_target="tpu_custom_call" | custom-call | flops 5435817984 | bytes 15335424 | tf_op jit(solution)/shard_map/pallas_call | solution.py:713
  552.0 5.5 collective-permute-done.46
  581.6 6.2 all-to-all-done.2
  611.9 7.7 %collective-permute-done.51 = bf16[288,1152]{1,0:T(8,128)(2,1)} collective-permute-done((bf16[288,1152]{1,0:T(8,128)(2,1)}, bf16[288,1152]{1,0:T(8,128)(2,1)}, u32[]{:S(2)}, u32[]{:S(2)}) %collective-permute-start.51) | collective-permute-done | bytes 663584 | tf_op jit(solution)/shard_map/ppermute | solution.py:813
  645.1 36.3 %all-to-all-done.3 = bf16[8,176,1152]{2,1,0:T(8,128)(2,1)S(1)} async-done(((bf16[8,176,1152]{2,1,0:T(8,128)(2,1)}), bf16[8,176,1152]{2,1,0:T(8,128)(2,1)S(1)}, u32[]{:S(2)}, u32[]{:S(2)}) %all-to-all-start.3) | async-done | bytes 3244064 | tf_op jit(solution)/shard_map/all_to_all | solution.py:1039
  (372 shorter events, 237.4 us)
Async XLA Ops:
  5.5 20.3 %collective-permute-start = (bf16[240,1152]{1,0:T(8,128)(2,1)S(1)}, bf16[240,1152]{1,0:T(8,128)(2,1)S(1)}, u32[]{:S(2)}, u32[]{:S(2)}) collective-permute-start(bf16[240,1152]{1,0:T(8,128)(2,1)S(1)} %fusion.21), channel_id=1, source_target_pairs={{0,2},{2,4},{4,6},{6,7},{7,5},{5,3},{3,1},{1,0},{8,10},{10,12},{12... | collective-permute-start | bytes 1658888 | tf_op jit(solution)/shard_map/ppermute | solution.py:810
  13.9 71.3 %all-to-all-start = ((bf16[8,112,1152]{2,1,0:T(8,128)(2,1)}), bf16[8,112,1152]{2,1,0:T(8,128)(2,1)}, u32[]{:S(2)}, u32[]{:S(2)}) async-start(bf16[8,112,1152]{2,1,0:T(8,128)(2,1)} %pad_maximum_fusion.5), calls=%async_computation | async-start | bytes 4128768 | tf_op jit(solution)/shard_map/all_to_all | solution.py:1039
  25.9 40.8 %collective-permute-start.2 = (bf16[240,1152]{1,0:T(8,128)(2,1)S(1)}, bf16[240,1152]{1,0:T(8,128)(2,1)S(1)}, u32[]{:S(2)}, u32[]{:S(2)}) collective-permute-start(bf16[240,1152]{1,0:T(8,128)(2,1)S(1)} %collective-permute-done), channel_id=1, source_target_pairs={{0,2},{2,4},{4,6},{6,7},{7,5},{5,3},{3,1},{1,0},{8,10},{10,12},{12... | collective-permute-start | bytes 1658888 | tf_op jit(solution)/shard_map/ppermute | solution.py:810
  28.0 38.7 %collective-permute-start.3 = (bf16[240,1152]{1,0:T(8,128)(2,1)S(1)}, bf16[240,1152]{1,0:T(8,128)(2,1)}, u32[]{:S(2)}, u32[]{:S(2)}) collective-permute-start(bf16[240,1152]{1,0:T(8,128)(2,1)S(1)} %collective-permute-done.1), channel_id=1, source_target_pairs={{2,0},{4,2},{6,4},{7,6},{5,7},{3,5},{1,3},{0,1},{10,8},{12,10},{14... | collective-permute-start | bytes 1658888 | tf_op jit(solution)/shard_map/ppermute | solution.py:813
  68.0 29.9 %collective-permute-start.7 = (bf16[2,352,1152]{2,1,0:T(8,128)(2,1)}, bf16[2,352,1152]{2,1,0:T(8,128)(2,1)S(1)}, u32[]{:S(2)}, u32[]{:S(2)}) collective-permute-start(bf16[2,352,1152]{2,1,0:T(8,128)(2,1)} %pad_maximum_fusion.9), channel_id=1, source_target_pairs={{0,8},{8,0},{16,24},{24,16},{1,9},{9,1},{17,25},{25,17},{2,10},{10... | collective-permute-start | bytes 4866056 | tf_op jit(solution)/shard_map/ppermute | solution.py:780
  68.0 29.9 %collective-permute-start.8 = (bf16[240,1152]{1,0:T(8,128)(2,1)S(1)}, bf16[240,1152]{1,0:T(8,128)(2,1)S(1)}, u32[]{:S(2)}, u32[]{:S(2)}) collective-permute-start(bf16[240,1152]{1,0:T(8,128)(2,1)S(1)} %collective-permute-done.2), channel_id=1, source_target_pairs={{0,2},{2,4},{4,6},{6,7},{7,5},{5,3},{3,1},{1,0},{8,10},{10,12},{12... | collective-permute-start | bytes 1658888 | tf_op jit(solution)/shard_map/ppermute | solution.py:810
  139.8 22.2 %collective-permute-start.5 = (bf16[384,1152]{1,0:T(8,128)(2,1)}, bf16[384,1152]{1,0:T(8,128)(2,1)S(1)}, u32[]{:S(2)}, u32[]{:S(2)}) collective-permute-start(bf16[384,1152]{1,0:T(8,128)(2,1)} %constant_dynamic-slice_fusion.1), channel_id=1, source_target_pairs={{0,2},{2,4},{4,6},{6,7},{7,5},{5,3},{3,1},{1,0},{8,10},{10,12},{12... | collective-permute-start | bytes 2654216 | tf_op jit(solution)/shard_map/ppermute | solution.py:810
  140.2 22.0 %collective-permute-start.6 = (bf16[384,1152]{1,0:T(8,128)(2,1)}, bf16[384,1152]{1,0:T(8,128)(2,1)}, u32[]{:S(2)}, u32[]{:S(2)}) collective-permute-start(bf16[384,1152]{1,0:T(8,128)(2,1)} %constant_dynamic-slice_fusion.1), channel_id=1, source_target_pairs={{2,0},{4,2},{6,4},{7,6},{5,7},{3,5},{1,3},{0,1},{10,8},{12,10},{14... | collective-permute-start | bytes 2654216 | tf_op jit(solution)/shard_map/ppermute | solution.py:813
  163.5 21.5 %collective-permute-start.20 = (bf16[2,192,1152]{2,1,0:T(8,128)(2,1)S(1)}, bf16[2,192,1152]{2,1,0:T(8,128)(2,1)}, u32[]{:S(2)}, u32[]{:S(2)}) collective-permute-start(bf16[2,192,1152]{2,1,0:T(8,128)(2,1)S(1)} %pad_maximum_fusion.15), channel_id=1, source_target_pairs={{0,16},{8,24},{16,0},{24,8},{1,17},{9,25},{17,1},{25,9},{2,18},{10... | collective-permute-start | bytes 2654216 | tf_op jit(solution)/shard_map/ppermute | solution.py:791
  163.6 21.4 %collective-permute-start.18 = (bf16[384,1152]{1,0:T(8,128)(2,1)S(1)}, bf16[384,1152]{1,0:T(8,128)(2,1)S(1)}, u32[]{:S(2)}, u32[]{:S(2)}) collective-permute-start(bf16[384,1152]{1,0:T(8,128)(2,1)S(1)} %collective-permute-done.5), channel_id=1, source_target_pairs={{0,2},{2,4},{4,6},{6,7},{7,5},{5,3},{3,1},{1,0},{8,10},{10,12},{12... | collective-permute-start | bytes 2654216 | tf_op jit(solution)/shard_map/ppermute | solution.py:810
  164.2 21.3 %collective-permute-start.19 = (bf16[384,1152]{1,0:T(8,128)(2,1)}, bf16[384,1152]{1,0:T(8,128)(2,1)S(1)}, u32[]{:S(2)}, u32[]{:S(2)}) collective-permute-start(bf16[384,1152]{1,0:T(8,128)(2,1)} %collective-permute-done.6), channel_id=1, source_target_pairs={{2,0},{4,2},{6,4},{7,6},{5,7},{3,5},{1,3},{0,1},{10,8},{12,10},{14... | collective-permute-start | bytes 2654216 | tf_op jit(solution)/shard_map/ppermute | solution.py:813
  189.0 25.0 %collective-permute-start.21 = (bf16[2,576,1152]{2,1,0:T(8,128)(2,1)}, bf16[2,576,1152]{2,1,0:T(8,128)(2,1)}, u32[]{:S(2)}, u32[]{:S(2)}) collective-permute-start(bf16[2,576,1152]{2,1,0:T(8,128)(2,1)} %pad_maximum_fusion.1), channel_id=1, source_target_pairs={{0,8},{8,0},{16,24},{24,16},{1,9},{9,1},{17,25},{25,17},{2,10},{10... | collective-permute-start | bytes 7962632 | tf_op jit(solution)/shard_map/ppermute | solution.py:780
  190.1 22.4 %collective-permute-start.24 = (bf16[2,192,1152]{2,1,0:T(8,128)(2,1)}, bf16[2,192,1152]{2,1,0:T(8,128)(2,1)}, u32[]{:S(2)}, u32[]{:S(2)}) collective-permute-start(bf16[2,192,1152]{2,1,0:T(8,128)(2,1)} %pad_maximum_fusion.16), channel_id=1, source_target_pairs={{0,16},{8,24},{16,0},{24,8},{1,17},{9,25},{17,1},{25,9},{2,18},{10... | collective-permute-start | bytes 2654216 | tf_op jit(solution)/shard_map/ppermute | solution.py:791
  191.8 21.8 %collective-permute-start.22 = (bf16[384,1152]{1,0:T(8,128)(2,1)S(1)}, bf16[384,1152]{1,0:T(8,128)(2,1)S(1)}, u32[]{:S(2)}, u32[]{:S(2)}) collective-permute-start(bf16[384,1152]{1,0:T(8,128)(2,1)S(1)} %collective-permute-done.18), channel_id=1, source_target_pairs={{0,2},{2,4},{4,6},{6,7},{7,5},{5,3},{3,1},{1,0},{8,10},{10,12},{12... | collective-permute-start | bytes 2654216 | tf_op jit(solution)/shard_map/ppermute | solution.py:810
  192.4 21.5 %collective-permute-start.23 = (bf16[384,1152]{1,0:T(8,128)(2,1)S(1)}, bf16[384,1152]{1,0:T(8,128)(2,1)S(1)}, u32[]{:S(2)}, u32[]{:S(2)}) collective-permute-start(bf16[384,1152]{1,0:T(8,128)(2,1)S(1)} %copy-done.27), channel_id=1, source_target_pairs={{2,0},{4,2},{6,4},{7,6},{5,7},{3,5},{1,3},{0,1},{10,8},{12,10},{14... | collective-permute-start | bytes 2654216 | tf_op jit(solution)/shard_map/ppermute | solution.py:813
  217.1 23.2 %collective-permute-start.25 = (bf16[2,576,1152]{2,1,0:T(8,128)(2,1)}, bf16[2,576,1152]{2,1,0:T(8,128)(2,1)}, u32[]{:S(2)}, u32[]{:S(2)}) collective-permute-start(bf16[2,576,1152]{2,1,0:T(8,128)(2,1)} %pad_maximum_fusion.2), channel_id=1, source_target_pairs={{0,8},{8,0},{16,24},{24,16},{1,9},{9,1},{17,25},{25,17},{2,10},{10... | collective-permute-start | bytes 7962632 | tf_op jit(solution)/shard_map/ppermute | solution.py:780
  218.1 22.2 %collective-permute-start.28 = (bf16[2,192,1152]{2,1,0:T(8,128)(2,1)S(1)}, bf16[2,192,1152]{2,1,0:T(8,128)(2,1)}, u32[]{:S(2)}, u32[]{:S(2)}) collective-permute-start(bf16[2,192,1152]{2,1,0:T(8,128)(2,1)S(1)} %pad_maximum_fusion.17), channel_id=1, source_target_pairs={{0,16},{8,24},{16,0},{24,8},{1,17},{9,25},{17,1},{25,9},{2,18},{10... | collective-permute-start | bytes 2654216 | tf_op jit(solution)/shard_map/ppermute | solution.py:791
  412.5 30.2 %collective-permute-start.35 = (bf16[576,1152]{1,0:T(8,128)(2,1)S(1)}, bf16[576,1152]{1,0:T(8,128)(2,1)S(1)}, u32[]{:S(2)}, u32[]{:S(2)}) collective-permute-start(bf16[576,1152]{1,0:T(8,128)(2,1)S(1)} %get-tuple-element.399), channel_id=1, source_target_pairs={{0,2},{2,4},{4,6},{6,7},{7,5},{5,3},{3,1},{1,0},{8,10},{10,12},{12... | collective-permute-start | bytes 3981320 | tf_op jit(solution)/shard_map/ppermute | solution.py:810
  413.3 30.0 %collective-permute-start.36 = (bf16[576,1152]{1,0:T(8,128)(2,1)S(1)}, bf16[576,1152]{1,0:T(8,128)(2,1)}, u32[]{:S(2)}, u32[]{:S(2)}) collective-permute-start(bf16[576,1152]{1,0:T(8,128)(2,1)S(1)} %get-tuple-element.398), channel_id=1, source_target_pairs={{2,0},{4,2},{6,4},{7,6},{5,7},{3,5},{1,3},{0,1},{10,8},{12,10},{14... | collective-permute-start | bytes 3981320 | tf_op jit(solution)/shard_map/ppermute | solution.py:813
  448.7 29.2 %collective-permute-start.37 = (bf16[576,1152]{1,0:T(8,128)(2,1)}, bf16[576,1152]{1,0:T(8,128)(2,1)S(1)}, u32[]{:S(2)}, u32[]{:S(2)}) collective-permute-start(bf16[576,1152]{1,0:T(8,128)(2,1)} %get-tuple-element.397), channel_id=1, source_target_pairs={{0,2},{2,4},{4,6},{6,7},{7,5},{5,3},{3,1},{1,0},{8,10},{10,12},{12... | collective-permute-start | bytes 3981320 | tf_op jit(solution)/shard_map/ppermute | solution.py:810
  450.3 28.9 %collective-permute-start.38 = (bf16[576,1152]{1,0:T(8,128)(2,1)}, bf16[576,1152]{1,0:T(8,128)(2,1)S(1)}, u32[]{:S(2)}, u32[]{:S(2)}) collective-permute-start(bf16[576,1152]{1,0:T(8,128)(2,1)} %get-tuple-element.396), channel_id=1, source_target_pairs={{2,0},{4,2},{6,4},{7,6},{5,7},{3,5},{1,3},{0,1},{10,8},{12,10},{14... | collective-permute-start | bytes 3981320 | tf_op jit(solution)/shard_map/ppermute | solution.py:813
  479.1 21.6 %collective-permute-start.39 = (bf16[8,288,1152]{2,1,0:T(8,128)(2,1)}, bf16[8,288,1152]{2,1,0:T(8,128)(2,1)}, u32[]{:S(2)}, u32[]{:S(2)}) collective-permute-start(bf16[8,288,1152]{2,1,0:T(8,128)(2,1)} %shard_map.322), channel_id=1, source_target_pairs={{0,8},{8,0},{16,24},{24,16},{1,9},{9,1},{17,25},{25,17},{2,10},{10... | collective-permute-start | bytes 15925256 | tf_op jit(solution)/shard_map/ppermute | solution.py:780
  484.1 38.7 %collective-permute-start.42 = (bf16[576,1152]{1,0:T(8,128)(2,1)}, bf16[576,1152]{1,0:T(8,128)(2,1)S(1)}, u32[]{:S(2)}, u32[]{:S(2)}) collective-permute-start(bf16[576,1152]{1,0:T(8,128)(2,1)} %get-tuple-element.395), channel_id=1, source_target_pairs={{0,2},{2,4},{4,6},{6,7},{7,5},{5,3},{3,1},{1,0},{8,10},{10,12},{12... | collective-permute-start | bytes 3981320 | tf_op jit(solution)/shard_map/ppermute | solution.py:810
  485.5 37.4 %collective-permute-start.43 = (bf16[576,1152]{1,0:T(8,128)(2,1)}, bf16[576,1152]{1,0:T(8,128)(2,1)S(1)}, u32[]{:S(2)}, u32[]{:S(2)}) collective-permute-start(bf16[576,1152]{1,0:T(8,128)(2,1)} %get-tuple-element.394), channel_id=1, source_target_pairs={{2,0},{4,2},{6,4},{7,6},{5,7},{3,5},{1,3},{0,1},{10,8},{12,10},{14... | collective-permute-start | bytes 3981320 | tf_op jit(solution)/shard_map/ppermute | solution.py:813
  527.0 30.5 %collective-permute-start.46 = (bf16[576,1152]{1,0:T(8,128)(2,1)S(1)}, bf16[576,1152]{1,0:T(8,128)(2,1)S(1)}, u32[]{:S(2)}, u32[]{:S(2)}) collective-permute-start(bf16[576,1152]{1,0:T(8,128)(2,1)S(1)} %fusion.1), channel_id=1, source_target_pairs={{0,16},{8,24},{16,0},{24,8},{1,17},{9,25},{17,1},{25,9},{2,18},{10... | collective-permute-start | bytes 3981320 | tf_op jit(solution)/shard_map/ppermute | solution.py:791
  531.8 20.1 %collective-permute-start.44 = (bf16[288,1152]{1,0:T(8,128)(2,1)}, bf16[288,1152]{1,0:T(8,128)(2,1)}, u32[]{:S(2)}, u32[]{:S(2)}) collective-permute-start(bf16[288,1152]{1,0:T(8,128)(2,1)} %get-tuple-element.407), channel_id=1, source_target_pairs={{0,2},{2,4},{4,6},{6,7},{7,5},{5,3},{3,1},{1,0},{8,10},{10,12},{12... | collective-permute-start | bytes 1990664 | tf_op jit(solution)/shard_map/ppermute | solution.py:810
  533.8 36.4 %collective-permute-start.52 = (bf16[8,1152]{1,0:T(8,128)(2,1)S(1)}, bf16[8,1152]{1,0:T(8,128)(2,1)S(1)}, u32[]{:S(2)}, u32[]{:S(2)}) collective-permute-start(bf16[8,1152]{1,0:T(8,128)(2,1)S(1)} %bitcast.247), channel_id=1, source_target_pairs={{0,8},{8,0},{16,24},{24,16},{1,9},{9,1},{17,25},{25,17},{2,10},{10... | collective-permute-start | bytes 55304 | tf_op jit(solution)/shard_map/ppermute | solution.py:946
  564.4 23.5 %collective-permute-start.49 = (bf16[528,1152]{1,0:T(8,128)(2,1)}, bf16[528,1152]{1,0:T(8,128)(2,1)}, u32[]{:S(2)}, u32[]{:S(2)}) collective-permute-start(bf16[528,1152]{1,0:T(8,128)(2,1)} %pad_maximum_fusion.8), channel_id=1, source_target_pairs={{0,8},{8,0},{16,24},{24,16},{1,9},{9,1},{17,25},{25,17},{2,10},{10... | collective-permute-start | bytes 3649544 | tf_op jit(solution)/shard_map/ppermute | solution.py:780
  570.2 35.8 %collective-permute-start.53 = (bf16[16,1152]{1,0:T(8,128)(2,1)S(1)}, bf16[16,1152]{1,0:T(8,128)(2,1)S(1)}, u32[]{:S(2)}, u32[]{:S(2)}) collective-permute-start(bf16[16,1152]{1,0:T(8,128)(2,1)S(1)} %pad_maximum_fusion.24), channel_id=1, source_target_pairs={{0,16},{8,24},{16,0},{24,8},{1,17},{9,25},{17,1},{25,9},{2,18},{10... | collective-permute-start | bytes 110600 | tf_op jit(solution)/shard_map/ppermute | solution.py:946
  578.8 46.6 %collective-permute-start.60 = (bf16[4,144,1152]{2,1,0:T(8,128)(2,1)}, bf16[4,144,1152]{2,1,0:T(8,128)(2,1)}, u32[]{:S(2)}, u32[]{:S(2)}) collective-permute-start(bf16[4,144,1152]{2,1,0:T(8,128)(2,1)} %bitcast.83), channel_id=1, source_target_pairs={{0,8},{8,0},{16,24},{24,16},{1,9},{9,1},{17,25},{25,17},{2,10},{10... | collective-permute-start | bytes 3981320 | tf_op jit(solution)/shard_map/ppermute | solution.py:780
  594.5 25.1 %collective-permute-start.51 = (bf16[288,1152]{1,0:T(8,128)(2,1)}, bf16[288,1152]{1,0:T(8,128)(2,1)}, u32[]{:S(2)}, u32[]{:S(2)}) collective-permute-start(bf16[288,1152]{1,0:T(8,128)(2,1)} %get-tuple-element.402), channel_id=1, source_target_pairs={{2,0},{4,2},{6,4},{7,6},{5,7},{3,5},{1,3},{0,1},{10,8},{12,10},{14... | collective-permute-start | bytes 1990664 | tf_op jit(solution)/shard_map/ppermute | solution.py:813
  597.8 83.6 %all-to-all-start.3 = ((bf16[8,176,1152]{2,1,0:T(8,128)(2,1)}), bf16[8,176,1152]{2,1,0:T(8,128)(2,1)S(1)}, u32[]{:S(2)}, u32[]{:S(2)}) async-start(bf16[8,176,1152]{2,1,0:T(8,128)(2,1)} %pad_maximum_fusion), calls=%async_computation.3 | async-start | bytes 6488064 | tf_op jit(solution)/shard_map/all_to_all | solution.py:1039
  (93 other events, 1027.1 us)

commit v5 on v4

--- a/solution.py
+++ b/solution.py
@@ -66,7 +66,7 @@
 
 def start_kernel(core_ref, places_ref, count_ref, index_ref, kept_ref, small_ref, mod_ref, *rest, chunks, row, share):
     refs, (start_ref, norm_ref, table, sems) = rest[: len(chunks.arrays)], rest[len(chunks.arrays) :]
-    rows, slots = start_ref.shape[0], kept_ref.shape[0]
+    rows, slots = start_ref.shape[0], index_ref.shape[1]
     step = pl.program_id(0)
     low, high = table.at[:, :share], table.at[:, share:]
 
@@ -89,7 +89,8 @@
     here = lax.broadcasted_iota(jnp.int32, (rows, slots), 0) + base
     slot = lax.broadcasted_iota(jnp.int32, (rows, slots), 1)
     chosen = jnp.where((index_ref[...] == here) & (slot < count_ref[0]), 1.0, 0.0)
-    filled = product(chosen.astype(bf16), kept_ref[...])
+    kept = kept_ref[:, : slots // kept_ref.shape[0]].reshape(slots, -1)
+    filled = product(chosen.astype(bf16), kept)
     empty = 1.0 - jnp.sum(chosen, axis=1, keepdims=True)
     groups_here = rows // table.shape[1]
     position = table[pl.ds(step * groups_here, groups_here)].reshape(rows, -1)
@@ -100,7 +101,7 @@
 
 
 def start_call(core, places, count, index, kept, small, mod, chunks, row, share, seq_len):
-    width = kept.shape[1]
+    width = kept.shape[2]
     rows = seq_len // 4
     return pl.pallas_call(
         functools.partial(start_kernel, chunks=chunks, row=row, share=share),
@@ -125,14 +126,14 @@
             pltpu.SemaphoreType.DMA((2,)),
         ],
         compiler_params=params(),
-        cost_estimate=cost(2 * seq_len * width * kept.shape[0], 14 * seq_len * width),
+        cost_estimate=cost(2 * seq_len * width * index.shape[1], 14 * seq_len * width),
     )(core, places, count, index, kept, small, mod, *chunks.arrays)
 
 
 class Chunks:
-    def __init__(self, mine, other, part=0, middle=0):
+    def __init__(self, mine, other, part=0, middle=0, stride=0):
         self.sources = list(mine), list(other)
-        self.part, self.middle = part, middle
+        self.part, self.middle, self.stride = part, middle, stride
         self.arrays = [entry[0] for source in self.sources for entry in source]
         self.specs = [anywhere] * len(self.arrays)
 
@@ -179,7 +180,8 @@
                             start(ref, kind, places, bit)
 
     def load_block(self, refs, places_ref, spot_ref, block, target, sem, first=0):
-        owner, row = block // 2, (first + block % 2) * target.shape[1]
+        rows = target.shape[1]
+        owner, row = block // 2, first * rows + (block % 2) * (self.stride or rows)
 
         @pl.when(spot_ref[0] == owner)
         def _():
@@ -251,7 +253,8 @@
     )(core, places, norm, small, *chunks.arrays)
 
 
-def attend_kernel(query_ref, key_ref, value_ref, mix_ref, log_ref, *, size, factor):
+def attend_kernel(query_ref, key_ref, value_ref, *rest, size, factor):
+    mix_ref, log_ref = rest[-2:]
     turned_value = value_ref[0, 0].T
     for part in range(query_ref.shape[2] // size):
         rows = slice(part * size, (part + 1) * size)
@@ -264,32 +267,36 @@
         log_ref[0, :, rows] = top * factor + jnp.log2(total)
 
 
-groups = 4
-
-
-def head_block(place, seq_len, group):
-    first = group * (H // groups)
+forward_groups = ((0, 8), (8, 8))
+back_groups = ((0, 4), (4, 8), (12, 4))
+groups = len(back_groups)
+
+
+def head_block(place, seq_len, first):
     return pl.BlockSpec((1, 1, seq_len, LANES), lambda h: (place, first + h, 0, 0))
 
 
-def attend_call(projected, group):
+def attend_call(projected, first, heads, earlier=None):
     seq_len = projected.shape[2]
-    heads = H // groups
-    flat = pl.BlockSpec((1, seq_len, LANES), lambda h: (h, 0, 0))
+    kept = [] if earlier is None else list(earlier)
     return pl.pallas_call(
         functools.partial(
             attend_kernel, size=seq_len, factor=math.log2(math.e) / math.sqrt(HD)
         ),
         grid=(heads,),
-        in_specs=[head_block(place, seq_len, group) for place in range(3)],
-        out_specs=[flat, pl.BlockSpec((1, 1, seq_len), lambda h: (h, 0, 0))],
+        in_specs=[head_block(place, seq_len, first) for place in range(3)] + [anywhere] * len(kept),
+        out_specs=[
+            pl.BlockSpec((1, seq_len, LANES), lambda h: (first + h, 0, 0)),
+            pl.BlockSpec((1, 1, seq_len), lambda h: (first + h, 0, 0)),
+        ],
         out_shape=[
-            jax.ShapeDtypeStruct((heads, seq_len, LANES), bf16),
-            jax.ShapeDtypeStruct((heads, 1, seq_len), f32),
-        ],
+            jax.ShapeDtypeStruct((H, seq_len, LANES), bf16),
+            jax.ShapeDtypeStruct((H, 1, seq_len), f32),
+        ],
+        input_output_aliases={3: 0, 4: 1} if kept else {},
         compiler_params=params(),
         cost_estimate=cost(4 * heads * seq_len * seq_len * 256, 8 * heads * seq_len * LANES, heads * seq_len * seq_len),
-    )(projected, projected, projected)
+    )(projected, projected, projected, *kept)
 
 
 def attend_back_kernel(
@@ -320,18 +327,17 @@
     value_grad_ref[0] = value_sum[...].astype(bf16)
 
 
-def attend_back_call(projected, mix, logs, grad, group):
+def attend_back_call(projected, attended, grad, first, heads):
     seq_len = projected.shape[2]
-    heads = H // groups
-    first = group * heads
+    mix, logs = attended
     flat = pl.BlockSpec((1, seq_len, LANES), lambda h: (h, 0, 0))
     return pl.pallas_call(
         functools.partial(attend_back_kernel, size=seq_len // 2, factor=1.0 / math.sqrt(HD)),
         grid=(heads,),
-        in_specs=[head_block(place, seq_len, group) for place in range(3)]
+        in_specs=[head_block(place, seq_len, first) for place in range(3)]
         + [
-            flat,
-            pl.BlockSpec((1, 1, seq_len), lambda h: (h, 0, 0)),
+            pl.BlockSpec((1, seq_len, LANES), lambda h: (first + h, 0, 0)),
+            pl.BlockSpec((1, 1, seq_len), lambda h: (first + h, 0, 0)),
             pl.BlockSpec((1, seq_len, LANES), lambda h: (first + h, 0, 0)),
         ],
         out_specs=[flat] * 3,
@@ -349,7 +355,7 @@
 
 
 def mix_kernel(core_ref, places_ref, start_ref, small_ref, mod_ref, *rest, chunks):
-    mix_refs, rest = rest[:groups], rest[groups:]
+    mix_refs, rest = rest[:1], rest[1:]
     refs, rest = rest[: len(chunks.arrays)], rest[len(chunks.arrays) :]
     joined_ref, branch_ref, middle_ref, norm_ref, weight, sem = rest
 
@@ -376,7 +382,7 @@
         functools.partial(mix_kernel, chunks=chunks),
         grid=(4,),
         in_specs=[smem, smem, block, whole_block(small), whole_block(mod)]
-        + [pl.BlockSpec((H // groups, rows, LANES), lambda i: (0, i, 0))] * groups
+        + [pl.BlockSpec((H, rows, LANES), lambda i: (0, i, 0))]
         + chunks.specs,
         out_specs=[block] * 4,
         out_shape=[
@@ -385,7 +391,7 @@
         scratch_shapes=[pltpu.VMEM((8, width // 8, width), bf16), pltpu.SemaphoreType.DMA],
         compiler_params=params(),
         cost_estimate=cost(2 * seq_len * width * width, 18 * seq_len * width),
-    )(core, places, start, small, mod, *mix, *chunks.arrays)
+    )(core, places, start, small, mod, mix, *chunks.arrays)
 
 
 def gelu_parts(values):
@@ -513,55 +519,58 @@
     )(core, places, norm, middle, cot, branch, mod, small, *source.arrays)
 
 
-def feed_weight_kernel(first_ref, norm_ref, pre_ref, hidden_ref, grad_ref, out_ref):
-    step = pl.program_id(0)
-
-    @pl.when(step < 2)
-    def _():
-        result = product(norm_ref[...], pre_ref[0], left_turned)
-        out_ref[...] = result.astype(bf16).reshape(out_ref.shape)
-
-    @pl.when(step >= 2)
-    def _():
-        result = product(hidden_ref[0], grad_ref[...], left_turned)
-        out_ref[...] = result.astype(bf16).reshape(out_ref.shape)
-
-
-def feed_weight_call(first, norm, pre, hidden, grad):
-    seq_len, width = norm.shape
-    block = (1, seq_len, width)
-    full = pl.BlockSpec((seq_len, width), lambda i, f: (0, 0))
+def feed_weight_kernel(first_ref, left_ref, right_ref, *rest):
+    out_ref = rest[-1]
+    left = left_ref[0] if left_ref.ndim == 3 else left_ref[...]
+    right = right_ref[0] if right_ref.ndim == 3 else right_ref[...]
+    result = product(left, right, left_turned).reshape(out_ref.shape)
+    if len(rest) > 1:
+        result = result + rest[0][...].astype(f32)
+    out_ref[...] = result.astype(bf16)
+
+
+def feed_weight_call(first, left, right, got=None, base=None, row=0, rows=2):
+    width = left.shape[-1]
+    seq_len = left.shape[-2]
+    out_block = (8, width // 8, width)
+
+    def spec(array):
+        if array.ndim == 2:
+            return pl.BlockSpec(array.shape, lambda i, f: (0, 0))
+        return pl.BlockSpec((1, seq_len, width), lambda i, f: (f[0] + i, 0, 0))
+
+    more, specs, aliases = [], [], {}
+    if got is not None:
+        more, specs = [got], [pl.BlockSpec(out_block, lambda i, f: (0, i, 0))]
+    if base is not None:
+        aliases = {3 + len(more): 0}
+        more, specs = more + [base], specs + [anywhere]
     return pl.pallas_call(
         feed_weight_kernel,
         grid_spec=pltpu.PrefetchScalarGridSpec(
             num_scalar_prefetch=1,
-            grid=(4,),
-            in_specs=[
-                full,
-                pl.BlockSpec(block, lambda i, f: (f[0] + jnp.minimum(i, 1), 0, 0)),
-                pl.BlockSpec(block, lambda i, f: (f[0] + jnp.maximum(i - 2, 0), 0, 0)),
-                full,
-            ],
-            out_specs=pl.BlockSpec((8, width // 8, width), lambda i, f: (0, i, 0)),
+            grid=(2,),
+            in_specs=[spec(left), spec(right)] + specs,
+            out_specs=pl.BlockSpec(out_block, lambda i, f: (0, row + i, 0)),
         ),
-        out_shape=jax.ShapeDtypeStruct((8, width // 2, width), bf16),
+        out_shape=jax.ShapeDtypeStruct((8, rows * width // 8, width), bf16),
+        input_output_aliases=aliases,
         compiler_params=params(),
-        cost_estimate=cost(8 * seq_len * width * width, 12 * seq_len * width + 8 * width * width),
-    )(first, norm, pre, hidden, grad)
+        cost_estimate=cost(4 * seq_len * width * width, 8 * seq_len * width + 4 * width * width),
+    )(first, left, right, *more)
 
 
 def attention_weight_kernel(owner_ref, norm_ref, joined_ref, grad_ref, *rest):
     head_refs = [rest[block * groups : (block + 1) * groups] for block in range(3)]
     out_ref, left, heads, right, sems = rest[3 * groups :]
     step = pl.program_id(0)
-    size = heads.shape[1] // groups
 
     def copies(block, slot):
         if block == 3:
             return [(joined_ref, left.at[slot]), (grad_ref, right.at[slot])]
         return [(norm_ref, left.at[slot])] + [
-            (ref, heads.at[slot, pl.ds(group * size, size)])
-            for group, ref in enumerate(head_refs[block])
+            (ref, heads.at[slot, pl.ds(first, count)])
+            for (first, count), ref in zip(back_groups, head_refs[block])
         ]
 
     @pl.when(step == 0)
@@ -646,73 +655,63 @@
     grad_refs = [rest[block * groups : (block + 1) * groups] for block in range(3)]
     rest = rest[3 * groups :]
     refs, rest = rest[: len(chunks.arrays)], rest[len(chunks.arrays) :]
-    row_grad_ref, slot_ref, sums_ref, weight, slots, sems = rest
-    step = pl.program_id(0)
+    row_grad_ref, slot_ref, sums_ref, weight, sems = rest[-5:]
+    earlier = rest[:-5]
     rows, width = start_ref.shape
-    slot_count = slots.shape[0]
-
-    @pl.when(step == 0)
-    def _():
-        for block in range(3):
-            chunks.load_block(refs, places_ref, core_ref, block, weight.at[block], sems.at[block])
-        sums_ref[...] = jnp.zeros_like(sums_ref)
-
+    toks, per_tok = slot_ref.shape[0], index_ref.shape[0] // slot_ref.shape[0]
+    slot_count = index_ref.shape[0]
+
+    for block in range(3):
+        chunks.load_block(refs, places_ref, core_ref, block, weight.at[block], sems.at[block])
+    sums = {}
     total = None
     for block, refs in enumerate(grad_refs):
         joined = join_heads(refs)
         if block != 1:
-            place = block // 2
-            sums_ref[place : place + 1] += column_sum(joined.astype(f32))
-
-        @pl.when(step == 0)
-        def _():
-            wait_block(weight.at[block], sems.at[block])
-
+            sums[block // 2] = column_sum(joined.astype(f32))
+        wait_block(weight.at[block], sems.at[block])
         part = product(joined, square(weight[block]), right_turned)
         total = part if total is None else total + part
     unit, inverse = normalize(start_ref[...])
-    sums_ref[2:3] += column_sum(total * unit)
-    sums_ref[3:4] += column_sum(total)
+    sums[2] = column_sum(total * unit)
+    sums[3] = column_sum(total)
     row_grad = middle_grad_ref[...] + normalize_back(total, unit, inverse, mod_ref[1:2])
     row_low = row_grad.astype(bf16)
     row_grad_ref[...] = row_low
-    base = (first + step) * rows
+    base = first * rows
     place = lax.broadcasted_iota(jnp.int32, (slot_count, rows), 1) + base
     slot = lax.broadcasted_iota(jnp.int32, (slot_count, rows), 0)
     chosen = jnp.where((index_ref[...] == place) & (slot < count_ref[0]), 1.0, 0.0)
     part = product(chosen.astype(bf16), row_low)
 
-    @pl.when(step == 0)
-    def _():
-        slots[...] = part
-
-    @pl.when(step > 0)
-    def _():
-        slots[...] += part
-
+    part = part.astype(bf16).reshape(toks, per_tok, width)
+    if earlier:
+        part = part + earlier[0][:, :per_tok]
+    slot_ref[:, :per_tok] = part
     here = lax.broadcasted_iota(jnp.int32, (rows, slot_count), 0) + base
     lane = lax.broadcasted_iota(jnp.int32, (rows, slot_count), 1)
     taken = jnp.where((index_row_ref[...] == here) & (lane < count_ref[0]), 1.0, 0.0)
     empty = 1.0 - jnp.sum(taken, axis=1, keepdims=True)
-    sums_ref[4:5] += column_sum(row_grad * empty)
-
-    @pl.when(step == pl.num_programs(0) - 1)
-    def _():
-        slot_ref[...] = slots[...].astype(bf16)
-
-
-def start_back_call(half, core, places, count, index, grads, middle_grad, start, mod, chunks):
+    sums[4] = column_sum(row_grad * empty)
+    sums_ref[...] = jnp.concatenate(
+        [sums[number] for number in range(5)] + [jnp.zeros((3, width), f32)]
+    )
+
+
+def start_back_call(quarter, earlier, core, places, count, index, grads, middle_grad, start, mod, chunks):
     seq_len, width = start.shape
     slot_count = index.shape[1]
-    steps = 2
+    toks = lax.axis_size("tok")
     rows = seq_len // 4
-    first = half * steps
-    heads = pl.BlockSpec((H // groups, rows, LANES), lambda i: (0, first + i, 0))
-    block = pl.BlockSpec((rows, width), lambda i: (first + i, 0))
+    heads = [
+        pl.BlockSpec((array.shape[0], rows, LANES), lambda i: (0, quarter, 0)) for array in grads
+    ]
+    block = pl.BlockSpec((rows, width), lambda i: (quarter, 0))
+    kept = [] if earlier is None else [earlier]
     column = index.reshape(slot_count, 1)
     return pl.pallas_call(
-        functools.partial(start_back_kernel, chunks=chunks, first=first),
-        grid=(steps,),
+        functools.partial(start_back_kernel, chunks=chunks, first=quarter),
+        grid=(1,),
         in_specs=[
             smem,
             smem,
@@ -723,36 +722,49 @@
             block,
             whole_block(mod),
         ]
-        + [heads] * (3 * groups)
-        + chunks.specs,
+        + heads
+        + chunks.specs
+        + [whole_block(array) for array in kept],
         out_specs=[
             row_block(rows, width),
-            pl.BlockSpec((slot_count, width), lambda i: (0, 0)),
+            pl.BlockSpec((toks, slot_count // toks + 8, width), lambda i: (0, 0, 0)),
             pl.BlockSpec((8, width), lambda i: (0, 0)),
         ],
         out_shape=[
-            jax.ShapeDtypeStruct((seq_len // 2, width), bf16),
-            jax.ShapeDtypeStruct((slot_count, width), bf16),
+            jax.ShapeDtypeStruct((rows, width), bf16),
+            jax.ShapeDtypeStruct((toks, slot_count // toks + 8, width), bf16),
             jax.ShapeDtypeStruct((8, width), f32),
         ],
         scratch_shapes=[
             pltpu.VMEM((3, 8, width // 8, width), bf16),
-            pltpu.VMEM((slot_count, width), f32),
             pltpu.SemaphoreType.DMA((3,)),
         ],
         compiler_params=params(),
-        cost_estimate=cost(4 * seq_len * width * width, 13 * seq_len * width),
-    )(core, places, count, index, column, middle_grad, start, mod, *grads, *chunks.arrays)
-
-
-def collect_kernel(first_ref, second_ref, feed_ref, up_ref, mod_ref, small_ref):
-    start = first_ref[...] + second_ref[...]
+        cost_estimate=cost(2 * seq_len * width * width, 7 * seq_len * width),
+    )(core, places, count, index, column, middle_grad, start, mod, *grads, *chunks.arrays, *kept)
+
+
+def collect_kernel(feed_ref, up_ref, *rest):
+    *start_refs, _, mod_ref, small_ref = rest
+    start = start_refs[0][...]
+    for ref in start_refs[1:]:
+        start = start + ref[...]
     feed = feed_ref[...]
     row = lambda values, number: values[number : number + 1]
     blank = jnp.zeros((7, start.shape[1]), f32)
-    mod_ref[...] = jnp.concatenate(
-        [row(start, 3), row(start, 2), row(feed, 4), row(feed, 3), row(feed, 2), row(feed, 0)]
-    ).astype(bf16)
+    width = start.shape[1]
+    rows = [row(start, 3), row(start, 2), row(feed, 4), row(feed, 3), row(feed, 2), row(feed, 0)]
+    share = 6 * width // mod_ref.shape[0]
+    for tok in range(mod_ref.shape[0]):
+        place, left, pieces = tok * share, share, []
+        while left:
+            within = place % width
+            count = min(left, width - within)
+            pieces.append(rows[place // width][:, within : within + count])
+            place, left = place + count, left - count
+        pieces.append(jnp.zeros((1, width - share), f32))
+        line = jnp.concatenate(pieces, axis=1)
+        mod_ref[tok] = jnp.broadcast_to(line, (8, width)).astype(bf16)
     small_ref[...] = jnp.concatenate(
         [row(start, 4), row(start, 0), row(start, 1), row(feed, 5), row(feed, 1)]
         + [up_ref[block] for block in range(4)]
@@ -760,16 +772,25 @@
     ).astype(bf16)
 
 
-def collect_call(first, second, feed, up):
-    width = first.shape[1]
+def collect_call(feed, up, slots, *starts):
+    toks, rows, width = slots.shape
     return pl.pallas_call(
         collect_kernel,
+        grid=(1,),
+        in_specs=[whole_block(feed), whole_block(up)]
+        + [whole_block(start) for start in starts]
+        + [anywhere],
+        out_specs=[
+            pl.BlockSpec((toks, 8, width), lambda i: (0, rows // 8 - 1, 0)),
+            pl.BlockSpec((16, width), lambda i: (0, 0)),
+        ],
         out_shape=[
-            jax.ShapeDtypeStruct((6, width), bf16),
+            jax.ShapeDtypeStruct(slots.shape, bf16),
             jax.ShapeDtypeStruct((16, width), bf16),
         ],
+        input_output_aliases={2 + len(starts): 0},
         compiler_params=params(),
-    )(first, second, feed, up)
+    )(feed, up, *starts, slots)
 
 
 def swap_pairs(size, bit):
@@ -824,11 +845,19 @@
         payload = lax.dynamic_slice_in_dim(mine, part * ring.x_bit, part + middle, 0)
         self.pieces = [payload, payload]
         self.distance = 0
-        self.own = self.pair = None
+        self.own = None
+        self.making, self.ready = [], []
 
     def issue(self):
         ring, flight = self.ring, {}
         middle, half = self.middle, ring.size // 2
+        if self.distance == half:
+            self.ready, self.making = self.ready + self.making, []
+        flight["pair"] = [array for array, _ in self.making]
+        self.made = [places for _, places in self.making]
+        self.making = []
+        flight["core"] = [swap_core(array) for array, _ in self.ready]
+        self.sent = [places for _, places in self.ready]
         if self.distance < half:
             self.distance += 1
             ahead, behind = self.pieces
@@ -837,24 +866,22 @@
             flight["ring"] = [ring.forward(ahead), ring.backward(behind)]
         if self.own is not None:
             flight["x"] = swap_x(self.own)
-        if self.pair is not None:
-            flight["core"] = swap_core(self.pair)
         return flight
 
     def land(self, flight):
         bit, part, middle = self.ring.x_bit, self.part, self.middle
-        if "core" in flight:
-            self.other.append((flight["core"], "pair", self.pair_places))
-        self.pair = self.own = None
+        self.other += [(array, "pair", places) for array, places in zip(flight["core"], self.sent)]
+        self.ready = list(zip(flight["pair"], self.made))
+        self.own = None
         if "x" in flight:
             got = flight["x"]
             self.mine.append((got, "got", self.places))
             if len(self.places) == 1:
                 ahead, behind = self.pieces
-                self.pair = jnp.concatenate([ahead, behind, got[0]])[None]
+                pair = jnp.concatenate([ahead, behind, got[0]])[None]
             else:
-                self.pair = jnp.concatenate([jnp.stack(self.pieces), got], axis=1)
-            self.pair_places = self.places
+                pair = jnp.concatenate([jnp.stack(self.pieces), got], axis=1)
+            self.making = [(pair, self.places)]
         if "ring" in flight:
             ahead, behind = self.pieces = flight["ring"]
             place = 2 * self.distance - 1
@@ -872,23 +899,33 @@
                     ]
                 )
 
-    def chunks(self):
-        return Chunks(self.mine, self.other, self.part, self.middle)
+    def chunks(self, stride=0):
+        return Chunks(self.mine, self.other, self.part, self.middle, stride)
+
+    def rows(self, first, count):
+        bit, part, middle = self.ring.x_bit, self.part, self.middle
+        low = first - part
+        ahead, behind = self.pieces
+        parts = [self.mine[0][0][0, first : first + count]]
+        for array, kind, _ in self.mine:
+            if kind == "piece":
+                parts.append(lax.dynamic_slice_in_dim(array[0], first - part * bit, count, 0))
+        parts.append(jnp.where(bit == 0, behind[first - middle :][:count], ahead[low:][:count]))
+        return jnp.stack(parts)
 
 
 class Scatter:
-    def __init__(self, ring, mine, got):
-        self.ring, self.values = ring, (mine, got)
+    def __init__(self, ring, *values):
+        self.ring, self.values = ring, values
         self.distance = ring.size // 2
-        self.split = mine.shape[1] // 2
+        self.split = values[0].shape[1] // 2
 
     def piece(self, place, row, count):
         tok, width = self.ring.tok_at(place), self.values[0].shape[2]
-        mine, got = (
+        return sum(
             lax.dynamic_slice(values, (tok, row, 0), (1, count, width))[0].astype(f32)
             for values in self.values
         )
-        return mine + got
 
     def hop(self):
         ring, distance, split = self.ring, self.distance, self.split
@@ -1035,6 +1072,9 @@
     def by_core(first, second):
         return jnp.where(core == 0, first, second)
 
+    def by_core_pair(pairs):
+        return [by_core(first, second) for first, second in zip(*pairs)]
+
     def exchange(values):
         return lax.all_to_all(values, "tok", split_axis=0, concat_axis=0, tiled=True)
 
@@ -1058,11 +1098,8 @@
             [kept_tokens.astype(bf16), jnp.broadcast_to(extra, (tok_count, 16, width))], axis=1
         )
     )
-    routed = arrived[:, :slots_here].reshape(-1, width)
     condition_group = arrived[:, slots_here + 9]
     small = jnp.sum(arrived[:, slots_here:].astype(f32), axis=0)
-
-    modulation_low = modulation_weight.astype(bf16)
 
     def modulate_all(conditions, weight):
         modulation_part = jnp.dot(
@@ -1078,48 +1115,53 @@
     input_low = input_weight.astype(bf16)
     input_blocks = [input_low[:, number * width : (number + 1) * width] for number in range(3)]
     position_low = position_table.astype(bf16)
-    attention_low = (
-        jnp.concatenate(input_blocks[:2] + [position_low[:table_rows]]),
-        jnp.concatenate([input_blocks[2], output_weight.astype(bf16), position_low[table_rows:]]),
-    )
+    attention_pairs = input_blocks[:2], [input_blocks[2], output_weight.astype(bf16)]
+    attention_low = tuple(
+        jnp.concatenate([pair[0], position_low[half * table_rows : (half + 1) * table_rows], pair[1]])
+        for half, pair in enumerate(attention_pairs)
+    )
+    attention_cut, feed_cut = (7 * share // 9, 8 * share // 9), (4 * share // 3, 4 * share // 3)
+    if ringed:
+        mine, other = by_core(*attention_low), by_core(*attention_low[::-1])
+        gather = Gather(ring, mine, other, *attention_cut)
+        flight, up_weight, down_weight, modulation_weight = sync(
+            gather.issue(), up_weight, down_weight, modulation_weight
+        )
+        gather.land(flight)
+        (flight,) = sync(gather.issue())
+        gather.land(flight)
+    modulation_low = modulation_weight.astype(bf16)
     up_low = spread_call(up_weight, tok_count)
     down_low = down_weight.astype(bf16).reshape(4, share, width)
     feed_low = tuple(
         jnp.concatenate([up_low[half : half + 2], down_low[half : half + 2]]).reshape(-1, width)
         for half in (0, 2)
     )
-
-    attention_cut, feed_cut = (7 * share // 9, 8 * share // 9), (4 * share // 3, 4 * share // 3)
     if ringed:
-        mine, other = by_core(*attention_low), by_core(*attention_low[::-1])
-        gather = Gather(ring, mine, other, *attention_cut)
-        (flight,) = sync(gather.issue())
-        gather.land(flight)
         mine, other = by_core(*feed_low), by_core(*feed_low[::-1])
-        flight, mine, other, modulation_low = sync(gather.issue(), mine, other, modulation_low)
+        flight, condition_group, arrived, small, mine, other, modulation_low = sync(
+            gather.issue(), condition_group, arrived, small, mine, other, modulation_low
+        )
         gather.land(flight)
         feed_gather = Gather(ring, mine, other, *feed_cut)
-        flight, condition_group, routed, small = sync(
-            gather.issue(), condition_group, routed, small
-        )
+        flight, condition_group = sync(gather.issue(), condition_group)
         gather.land(flight)
     mod = modulate_all(condition_group, modulation_low)
     if ringed:
-        (flight,) = sync(gather.issue())
+        table_mine = gather.rows(share, table_rows)
+        feed_flight = feed_gather.issue()
+        flight, table_mine, table_other, mod = sync(
+            gather.issue(), table_mine, swap_core(table_mine), mod
+        )
         gather.land(flight)
-        feed_flight = feed_gather.issue()
-        flight, mod = sync(gather.issue(), mod)
-        gather.land(flight)
-        (flight,) = sync(gather.issue())
-        gather.land(flight)
-        attention_chunks = gather.chunks()
+        flight = gather.issue()
         distances = [0]
         for distance in range(1, ring.size // 2):
             distances += [-distance, distance]
         places = ring.tok_at(jnp.array(distances + [ring.size // 2], jnp.int32))
     else:
         places = jnp.arange(8, dtype=jnp.int32)
-        mine = gather_plain(by_core(*attention_low)[: 2 * share], share)
+        mine = gather_plain(jnp.concatenate(by_core_pair(attention_pairs)), share)
         everywhere = list(range(8))
         plain_chunks = lambda mine: Chunks(
             [(mine, "all", everywhere)], [(swap_core(mine), "all", everywhere)]
@@ -1128,36 +1170,32 @@
         feed_chunks = plain_chunks(gather_plain(by_core(*feed_low), share))
         table = lax.all_gather(position_low, "tok").reshape(8, -1, width)
 
+        halves = jnp.split(table, 2, axis=1)
+        table_mine, table_other = by_core(*halves), by_core(*halves[::-1])
+    table_chunks = Chunks(
+        [(table_mine, "all", list(range(8)))], [(table_other, "all", list(range(8)))]
+    )
+    start, norm_one = start_call(
+        core_row, places, kept_count, kept_index, arrived, small, mod, table_chunks, 0,
+        table_mine.shape[1], seq_len,
+    )
     if ringed:
-        table_chunks, table_row, table_share = attention_chunks, 2 * share, table_rows
-    else:
-        table_share = table.shape[1] // 2
-        halves = table[:, :table_share], table[:, table_share:]
-        table_chunks, table_row = (
-            Chunks(
-                [(by_core(*halves), "all", everywhere)], [(by_core(*halves[::-1]), "all", everywhere)]
-            ),
-            0,
-        )
-    start, norm_one = start_call(
-        core_row, places, kept_count, kept_index, routed, small, mod, table_chunks, table_row,
-        table_share, seq_len,
-    )
-    if ringed:
-        feed_flight, start, norm_one = sync(feed_flight, start, norm_one)
+        flight, feed_flight, start, norm_one = sync(flight, feed_flight, start, norm_one)
+        gather.land(flight)
+        attention_chunks = gather.chunks(share + table_rows)
         feed_gather.land(feed_flight)
     projected = project_call(core_row, places, norm_one, small, attention_chunks)
     if ringed:
         flight, projected, start = sync(feed_gather.issue(), projected, start)
         feed_gather.land(flight)
-    attended = []
-    for group in range(groups):
-        attended.append(attend_call(projected, group))
-        if ringed and group % 2:
+    attended = None
+    for first, heads in forward_groups:
+        attended = attend_call(projected, first, heads, attended)
+        if ringed:
             flight, attended, projected = sync(feed_gather.issue(), attended, projected)
             feed_gather.land(flight)
     joined, branch_one, middle, norm_two = mix_call(
-        core_row, places, [pair[0] for pair in attended], start, small, mod, attention_chunks
+        core_row, places, attended[0], start, small, mod, attention_chunks
     )
     if ringed:
         flight, norm_two = sync(feed_gather.issue(), norm_two)
@@ -1177,17 +1215,22 @@
     ) = feed_call(
         core_row, places, norm_two, middle, cotangent[0], branch_one, mod, small, feed_chunks
     )
-    feed_other = feed_weight_call(2 - 2 * core_row[:1], norm_two, pre_grad, hidden, grad_two)
-    feed_other, norm_two, grad_one = sync(feed_other, norm_two, grad_one)
-    feed_mine = feed_weight_call(2 * core_row[:1], norm_two, pre_grad, hidden, grad_two)
-    feed_got, feed_mine, grad_one = sync(swap_core(feed_other), feed_mine, grad_one)
+    far, near = 2 - 2 * core_row[:1], 2 * core_row[:1]
+    other_up = feed_weight_call(far, norm_two, pre_grad)
+    other_up, hidden, grad_one = sync(other_up, hidden, grad_one)
+    other_down = feed_weight_call(far, hidden, grad_two)
+    got_up, other_down, norm_two = sync(swap_core(other_up), other_down, norm_two)
+    feed_chip = feed_weight_call(near, norm_two, pre_grad, got_up, rows=4)
+    got_down, feed_chip, hidden = sync(swap_core(other_down), feed_chip, hidden)
+    feed_chip = feed_weight_call(near, hidden, grad_two, got_down, feed_chip, 2, 4)
+    feed_chip, grad_one = sync(feed_chip, grad_one)
     mix_grad = mix_grad_call(core_row, places, grad_one, attention_chunks)
     if ringed:
-        feed_scatter = Scatter(ring, feed_mine, feed_got)
+        feed_scatter = Scatter(ring, feed_chip)
     grads = []
-    for group in range(groups):
-        grads.append(attend_back_call(projected, *attended[group], mix_grad, group))
-        if ringed and group in (0, 2):
+    for group, (first, heads) in enumerate(back_groups):
+        grads.append(attend_back_call(projected, attended, mix_grad, first, heads))
+        if ringed and group < 2:
             flight, grads, mix_grad = sync(feed_scatter.hop(), grads, mix_grad)
             feed_scatter.land(flight)
     grads = [triple[block] for block in range(3) for triple in grads]
@@ -1195,9 +1238,10 @@
     def attention_weights(owner, norm):
         return attention_weight_call(owner, norm, joined, grad_one, grads)
 
-    def start_back(half, grads):
+    def start_back(quarter, earlier, grads):
         return start_back_call(
-            half, core_row, places, kept_count, kept_index, grads, middle_grad, start, mod, attention_chunks
+            quarter, earlier, core_row, places, kept_count, kept_index, grads, middle_grad, start, mod,
+            attention_chunks,
         )
 
     attention_other = attention_weights(1 - core_row[:1], norm_one)
@@ -1212,23 +1256,27 @@
     if ringed:
         attention_mine, attention_got, grads = sync(attention_mine, attention_got, grads)
         scatter = Scatter(ring, attention_mine, attention_got)
-        flight = scatter.hop()
-    first_half = start_back(0, grads)
-    if ringed:
-        flight, feed_flight, first_half, grads = sync(flight, feed_flight, first_half, grads)
-        scatter.land(flight)
-        feed_scatter.land(feed_flight)
-        feed_shard = feed_scatter.total()
-        feed_cross = swap_x(feed_shard)
-        second_half = start_back(1, grads)
-        flight, second_half, feed_cross = sync(scatter.hop(), second_half, feed_cross)
-        scatter.land(flight)
-    else:
-        second_half = start_back(1, grads)
-    row_grad = jnp.concatenate([first_half[0], second_half[0]])
-    slot_grad = first_half[1] + second_half[1]
-    modulation_grad, small_grad = collect_call(
-        first_half[2], second_half[2], feed_sums, up_bias_sum
+    quarters = []
+    slot_grad = None
+    for quarter in range(4):
+        part = start_back(quarter, slot_grad, grads)
+        if ringed:
+            if quarter in (0, 3):
+                flight, part, grads, feed_flight = sync(scatter.hop(), part, grads, feed_flight)
+            else:
+                flight, part, grads = sync(scatter.hop(), part, grads)
+            scatter.land(flight)
+            if quarter == 0:
+                feed_scatter.land(feed_flight)
+                feed_shard = feed_scatter.total()
+                feed_flight = feed_cross = swap_x(feed_shard)
+            else:
+                feed_cross = feed_flight
+        quarters.append(part)
+        slot_grad = part[1]
+    row_grad = jnp.concatenate([part[0] for part in quarters])
+    slot_grad, small_grad = collect_call(
+        feed_sums, up_bias_sum, slot_grad, *[part[2] for part in quarters]
     )
 
     position_grad = row_grad.reshape(tok_count, position_rows, width)
@@ -1237,52 +1285,78 @@
         for half in (position_grad[:, :table_rows], position_grad[:, table_rows:])
     ]
     table_got = swap_core(jnp.concatenate([by_core(halves[1], halves[0]), small_grad]))
-    modulation_grad_group = exchange(modulation_grad.reshape(tok_count, -1))
-    if ringed:
-        flight, table_got, modulation_grad_group = sync(
-            scatter.hop(), table_got, modulation_grad_group
-        )
-        scatter.land(flight)
+    arrived = exchange(slot_grad)
     table_chip = add_low(jnp.concatenate([by_core(halves[0], halves[1]), small_grad]), table_got)
-    arrived = exchange(
+    small_chip = table_chip[-16:]
+    table_chip = table_chip[:-16].reshape(tok_count, table_rows, width)
+    half_rows = table_rows // 2
+    table_near, table_away = (
         jnp.concatenate(
             [
-                slot_grad.reshape(tok_count, -1, width),
-                table_chip[:-16].reshape(tok_count, table_rows, width),
-                jnp.broadcast_to(table_chip[-16:], (tok_count, 16, width)),
+                lax.dynamic_slice_in_dim(table_chip, half_rows * place, half_rows, 1).reshape(-1, width),
+                small_chip,
+            ]
+        )
+        for place in (ring.x_bit, 1 - ring.x_bit)
+    )
+    table_got = swap_x(table_away)
+    if ringed:
+        attention_shard = scatter.total()
+        attention_cross = swap_x(attention_shard)
+    table_pair = add_low(table_near, table_got)
+    table_pair, small_grad, arrived = sync(table_pair[:-16], table_pair[-16:], arrived)
+    kept_low = arrived[:, :slots_here]
+    modulation_grad_group = arrived[:, slots_here, : modulation_bias.shape[0]]
+    condition_part = jnp.einsum(
+        "ie,de->id", modulation_grad_group, modulation_low, preferred_element_type=f32
+    )
+    condition_high = condition_part.astype(bf16)
+    condition_rest = (condition_part - condition_high.astype(f32)).astype(bf16)
+    table_parts = exchange(
+        jnp.concatenate(
+            [
+                table_pair.reshape(tok_count, half_rows, width),
+                jnp.broadcast_to(small_grad[:14], (tok_count, 14, width)),
+                condition_high[:, None],
+                condition_rest[:, None],
             ],
             axis=1,
         )
     )
     modulation_grad_all = gather_grp(modulation_grad_group)
-    condition_part = jnp.einsum(
-        "ie,de->id", modulation_grad_group, modulation_low, preferred_element_type=f32
-    )
     modulation_total = jnp.einsum(
         "id,ie->de", condition_all, modulation_grad_all, preferred_element_type=f32
     )
     modulation_bias_total = jnp.sum(modulation_grad_all.astype(f32), axis=0)
+    table_sum = jnp.sum(table_parts.astype(f32), axis=0)
+    table_shard = table_sum.astype(bf16)
+    condition_low_grad = table_sum[-2:-1] + table_sum[-1:]
+    step = 4
+    while step < lax.axis_size("grp"):
+        table_shard = add_low(
+            table_shard, lax.ppermute(table_shard, "grp", swap_pairs(lax.axis_size("grp"), step))
+        )
+        step *= 2
+    table_cross = swap_x(table_shard[:half_rows])
+    table_half = jnp.concatenate(
+        [
+            jnp.where(ring.x_bit == 0, table_shard[:half_rows], table_cross),
+            jnp.where(ring.x_bit == 0, table_cross, table_shard[:half_rows]),
+        ]
+    )
     if ringed:
-        flight, condition_part, modulation_total, modulation_bias_total = sync(
-            scatter.hop(), condition_part, modulation_total, modulation_bias_total
-        )
-        scatter.land(flight)
-    condition_part, arrived = sync(condition_part, arrived)
-    condition_parts = exchange(condition_part)
-    kept_low = arrived[:, :slots_here]
-    table_shard = add_x(jnp.sum(arrived[:, slots_here:].astype(f32), axis=0).astype(bf16))
-    if ringed:
-        attention_shard = add_x(scatter.total())
+        attention_shard = add_low(attention_shard, attention_cross)
         feed_shard = add_low(feed_shard, feed_cross)
     else:
         attention_chip = by_tok(add_low(attention_mine, attention_got), share)
         attention_shard = add_x(scatter_plain(attention_chip))
-        feed_shard = add_x(scatter_plain(by_tok(add_low(feed_mine, feed_got), share)))
-    table_far = swap_core(table_shard[:table_rows])
-    first, second = by_core(table_shard[:table_rows], table_far), by_core(table_far, table_shard[:table_rows])
-    position_total = jnp.concatenate([first, second]).astype(f32)
+        feed_shard = add_x(scatter_plain(by_tok(feed_chip, share)))
+    table_far = swap_core(table_half)
+    position_total = jnp.concatenate(
+        [by_core(table_half, table_far), by_core(table_far, table_half)]
+    ).astype(f32)
     small_total = lax.dynamic_slice_in_dim(
-        table_shard[table_rows:], share * lax.axis_index("tok"), share, 1
+        table_shard[half_rows:], share * lax.axis_index("tok"), share, 1
     ).astype(f32)
     mask_total, query_bias_total, value_bias_total, output_bias_total, down_bias_total = (
         small_total[number] for number in range(5)
@@ -1300,7 +1374,6 @@
         [by_core(feed_shard[2:], feed_far[2:]), by_core(feed_far[2:], feed_shard[2:])]
     ).reshape(-1, width).astype(f32)
 
-    condition_low_grad = jnp.sum(condition_parts, axis=0, keepdims=True)
     _, silu_back = jax.vjp(jax.nn.silu, condition)
     condition_grad = silu_back(condition_low_grad)[0]
     return (

time: 703 us -> 673 us (0.957)
  waiting for transfers between devices: 154 us -> 117 us
    all_to_all x5 -> x4, waiting for transfers between devices: 52.9 us -> 26.1 us  [exchange(): lax.all_to_all(values, 'tok', split_axis=0, concat_axis=0, tiled=True)]
    pallas_call x1, Pallas kernels: 83.2 us -> 73.2 us  [feed_call(): pl.pallas_call(functools.partial(feed_kernel, source=source), grid=(steps...]
    pallas_call x2 -> x4, Pallas kernels: 36 us -> 45.2 us  [start_back_call(): pl.pallas_call(functools.partial(start_back_kernel, chunks=chunks, first=...]
    unnamed x124 -> x117, local copies, waits for them, and re-layouts: 6.26 us -> 14.5 us
    pallas_call x2 -> x4, Pallas kernels: 37 us -> 43.5 us  [feed_weight_call(): pl.pallas_call(feed_weight_kernel, grid_spec=pltpu.PrefetchScalarGridSpec...]
    convert_element_type x8 -> x7, other arithmetic: 28.5 us -> 23.1 us  [hop(): behind.astype(bf16)]
    ppermute x9 -> x12, starting transfers between devices: 11.8 us -> 15.7 us  [swap_x(): return lax.ppermute(values, 'grp', swap_pairs(lax.axis_size('grp'), 2))]
    pallas_call x4 -> x2, Pallas kernels: 34.9 us -> 31.1 us  [attend_call(): pl.pallas_call(functools.partial(attend_kernel, size=seq_len, factor=math...]
  transfers between devices with their start and end apart: 66 -> 68, of which waited for: 31 -> 33; matrix products, arithmetic and copies ran while one was open for 13% -> 14% of each run, Pallas kernels for 31% -> 33%
where the time goes in v5:
time: 673 us; the launch traced here: 663 us
  Pallas kernels  324 us (48%)
  waiting for transfers between devices  117 us (17%)
  other arithmetic  91.3 us (14%)
  starting transfers between devices  89.9 us (13%)
  local copies, waits for them, and re-layouts  34.8 us (5%)
    pallas_call x1, Pallas kernels, feed_call(): pl.pallas_call(functools.partial(feed_kernel, source=source), grid=(steps...  73.2 us
    pallas_call x3, Pallas kernels, attend_back_call(): pl.pallas_call(functools.partial(attend_back_kernel, size=seq_len // 2, f...  51.1 us
    ppermute x16, waiting for transfers between devices, forward(): return lax.ppermute(values, 'tok', self.ahead)  45.3 us
    pallas_call x4, Pallas kernels, start_back_call(): pl.pallas_call(functools.partial(start_back_kernel, chunks=chunks, first=...  45.2 us
    pallas_call x4, Pallas kernels, feed_weight_call(): pl.pallas_call(feed_weight_kernel, grid_spec=pltpu.PrefetchScalarGridSpec...  43.5 us
    ppermute x16, starting transfers between devices, forward(): return lax.ppermute(values, 'tok', self.ahead)  34.3 us
    pallas_call x2, Pallas kernels, attend_call(): pl.pallas_call(functools.partial(attend_kernel, size=seq_len, factor=math...  31.1 us
    ppermute x12, waiting for transfers between devices, swap_x(): return lax.ppermute(values, 'grp', swap_pairs(lax.axis_size('grp'), 2))  26.9 us
  transfers between devices with their start and end apart: 68, of which 33 were waited for; matrix products, arithmetic and copies ran while one was open for 14% of the time, Pallas kernels for 33%

profile of v5, /device:TPU:0, one launch (start us, length us, event | category | flops | bytes accessed | tf_op | source)
XLA Modules:
  0.0 663.4 jit_solution(11808018117958242245)
XLA Ops:
  18.2 6.5 all-to-all-start
  46.4 23.4 %collective-permute-done.2 = bf16[240,1152]{1,0:T(8,128)(2,1)} collective-permute-done((bf16[240,1152]{1,0:T(8,128)(2,1)S(1)}, bf16[240,1152]{1,0:T(8,128)(2,1)}, u32[]{:S(2)}, u32[]{:S(2)}) %collective-permute-start.2) | collective-permute-done | bytes 552992 | tf_op jit(solution)/shard_map/ppermute | solution.py:831
  69.8 14.4 %collective-permute-start.5 = (bf16[240,1152]{1,0:T(8,128)(2,1)}, bf16[240,1152]{1,0:T(8,128)(2,1)S(1)}, u32[]{:S(2)}, u32[]{:S(2)}) collective-permute-start(bf16[240,1152]{1,0:T(8,128)(2,1)} %collective-permute-done.2), channel_id=1, source_target_pairs={{0,2},{2,4},{4,6},{6,7},{7,5},{5,3},{3,1},{1,0},{8,10},{10,12},{12... | collective-permute-start | bytes 1658888 | tf_op jit(solution)/shard_map/ppermute | solution.py:831
  117.9 5.6 all-to-all-start.1
  139.7 8.4 %shard_map.307 = (f32[1024,1152]{1,0:T(8,128)}, bf16[1024,1152]{1,0:T(8,128)(2,1)}) custom-call(s32[2]{0:T(128)} %pad_add_fusion.core_ref, s32[8]{0:T(128)} %compare_select_fusion.2.places_ref, s32[1]{0:T(128)S(6)} %copy.72.count_ref, s32[1,768]{1,0:T(1,128)} %index_row_ref.7, bf16[8,112,1152]{2,1,0:T(8,128)(2,1)} %all-to-all-done.kept_ref, ...), custom_call_target="tpu_custom_call" | custom-call | flops 1811939328 | bytes 16515072 | tf_op jit(solution)/shard_map/pallas_call | solution.py:106
  150.6 4.5 collective-permute-done.18
  161.0 16.5 %shard_map.308.query_ref.key_ref.value_ref = bf16[3,16,1024,128]{3,2,1,0:T(8,128)(2,1)} custom-call(s32[2]{0:T(128)} %pad_add_fusion.core_ref, s32[8]{0:T(128)} %compare_select_fusion.2.places_ref, bf16[1024,1152]{1,0:T(8,128)(2,1)} %get-tuple-element.328.norm_ref, f32[16,1152]{1,0:T(8,128)} %convert_reduce_fusion.1.small_ref, ...), custom_call_target="tpu_custom_call" | custom-call | flops 8153726976 | bytes 22118400 | tf_op jit(solution)/shard_map/pallas_call | solution.py:235
  187.1 15.5 %shard_map.309 = (bf16[16,1024,128]{2,1,0:T(8,128)(2,1)}, f32[16,1,1024]{2,1,0:T(1,128)}) custom-call(bf16[3,16,1024,128]{3,2,1,0:T(8,128)(2,1)} %shard_map.308.query_ref.key_ref.value_ref, bf16[3,16,1024,128]{3,2,1,0:T(8,128)(2,1)} %shard_map.308.query_ref.key_ref.value_ref, bf16[3,16,1024,128]{3,2,1,0:T(8,128)(2,1)} %shard_map.308.query_ref.key_ref.value_ref), custom_call_target="tpu_custom_call" | custom-call | flops 8589934592 | bytes 8388608 | tf_op jit(solution)/shard_map/pallas_call | solution.py:282
  208.8 15.5 %shard_map.310 = (bf16[16,1024,128]{2,1,0:T(8,128)(2,1)}, f32[16,1,1024]{2,1,0:T(1,128)}) custom-call(bf16[3,16,1024,128]{3,2,1,0:T(8,128)(2,1)} %shard_map.308.query_ref.key_ref.value_ref, bf16[3,16,1024,128]{3,2,1,0:T(8,128)(2,1)} %shard_map.308.query_ref.key_ref.value_ref, ...), custom_call_target="tpu_custom_call", output_to_operand_aliasing={{0}: (3, {}), {1}: (4, {})} | custom-call | flops 8589934592 | bytes 8388608 | tf_op jit(solution)/shard_map/pallas_call | solution.py:282
  233.4 12.4 %shard_map.311 = (bf16[1024,1152]{1,0:T(8,128)(2,1)}, f32[1024,1152]{1,0:T(8,128)}, f32[1024,1152]{1,0:T(8,128)}, bf16[1024,1152]{1,0:T(8,128)(2,1)}) custom-call(s32[2]{0:T(128)} %pad_add_fusion.core_ref, s32[8]{0:T(128)} %compare_select_fusion.2.places_ref, f32[1024,1152]{1,0:T(8,128)} %get-tuple-element.274.start_ref, ...), custom_call_target="tpu_custom_call" | custom-call | flops 2717908992 | bytes 21233664 | tf_op jit(solution)/shard_map/pallas_call | solution.py:381
  251.5 73.2 %shard_map.312 = (f32[1024,1152]{1,0:T(8,128)}, bf16[4,1024,1152]{2,1,0:T(8,128)(2,1)}, bf16[4,1024,1152]{2,1,0:T(8,128)(2,1)}, bf16[1024,1152]{1,0:T(8,128)(2,1...) custom-call(s32[2]{0:T(128)} %pad_add_fusion.core_ref, ...), custom_call_target="tpu_custom_call" | custom-call | flops 43486543872 | bytes 70778880 | tf_op jit(solution)/shard_map/pallas_call | solution.py:477
  324.7 10.5 %shard_map.313 = bf16[8,288,1152]{2,1,0:T(8,128)(2,1)} custom-call(s32[1]{0:T(128)S(6)} %sub.77.first_ref, bf16[1024,1152]{1,0:T(8,128)(2,1)} %get-tuple-element.293.norm_ref.left_ref, bf16[4,1024,1152]{2,1,0:T(8,128)(2,1)} %get-tuple-element.286.right_ref), custom_call_target="tpu_custom_call" | custom-call | flops 5435817984 | bytes 14745600 | tf_op jit(solution)/shard_map/pallas_call | solution.py:548
  335.3 10.5 %shard_map.314 = bf16[8,288,1152]{2,1,0:T(8,128)(2,1)} custom-call(s32[1]{0:T(128)S(6)} %sub.77.first_ref, bf16[4,1024,1152]{2,1,0:T(8,128)(2,1)} %get-tuple-element.295.left_ref, bf16[1024,1152]{1,0:T(8,128)(2,1)} %get-tuple-element.291.right_ref), custom_call_target="tpu_custom_call" | custom-call | flops 5435817984 | bytes 14745600 | tf_op jit(solution)/shard_map/pallas_call | solution.py:548
  346.2 11.3 %shard_map.315.rest_1_ = bf16[8,576,1152]{2,1,0:T(8,128)(2,1)} custom-call(s32[1]{0:T(128)S(6)} %mul.141.first_ref, bf16[1024,1152]{1,0:T(8,128)(2,1)} %get-tuple-element.293.norm_ref.left_ref, bf16[4,1024,1152]{2,1,0:T(8,128)(2,1)} %get-tuple-element.286.right_ref, bf16[8,288,1152]{2,1,0:T(8,128)(2,1)} %collective-permute-done.33.rest_0_), custom_call_target="tpu_custom_call" | custom-call | flops 5435817984 | bytes 14745600 | tf_op jit(solution)/shard_map/pallas_call | solution.py:548
  357.5 11.3 %shard_map.316 = bf16[8,576,1152]{2,1,0:T(8,128)(2,1)} custom-call(s32[1]{0:T(128)S(6)} %mul.141.first_ref, bf16[4,1024,1152]{2,1,0:T(8,128)(2,1)} %get-tuple-element.295.left_ref, bf16[1024,1152]{1,0:T(8,128)(2,1)} %get-tuple-element.291.right_ref, bf16[8,288,1152]{2,1,0:T(8,128)(2,1)} %collective-permute-done.34.rest_0_, ...), custom_call_target="tpu_custom_call", output_to_operand_aliasing={{}: (4, {})} | custom-call | flops 5435817984 | bytes 14745600 | tf_op jit(solution)/shard_map/pallas_call | solution.py:548
  368.7 8.7 %shard_map.317.grad_ref = bf16[16,1024,128]{2,1,0:T(8,128)(2,1)} custom-call(s32[2]{0:T(128)} %pad_add_fusion.core_ref, s32[8]{0:T(128)} %compare_select_fusion.2.places_ref, bf16[1024,1152]{1,0:T(8,128)(2,1)} %get-tuple-element.302.grad_ref, bf16[1,352,1152]{2,1,0:T(8,128)(2,1)} %copy-done.3, bf16[1,240,1152]{2,1,0:T(8,128)(2,1)} %bitcast.201, ...), custom_call_target="tpu_custom_call" | custom-call | flops 2717908992 | bytes 9437184 | tf_op jit(solution)/shard_map/pallas_call | solution.py:639
  380.9 13.2 %shard_map.318 = (bf16[4,1024,128]{2,1,0:T(8,128)(2,1)}, bf16[4,1024,128]{2,1,0:T(8,128)(2,1)}, bf16[4,1024,128]{2,1,0:T(8,128)(2,1)}) custom-call(bf16[3,16,1024,128]{3,2,1,0:T(8,128)(2,1)} %shard_map.308.query_ref.key_ref.value_ref, bf16[3,16,1024,128]{3,2,1,0:T(8,128)(2,1)} %shard_map.308.query_ref.key_ref.value_ref, ...), custom_call_target="tpu_custom_call" | custom-call | flops 10737418240 | bytes 8388608 | tf_op jit(solution)/shard_map/pallas_call | solution.py:334
  402.3 24.3 %shard_map.319 = (bf16[8,1024,128]{2,1,0:T(8,128)(2,1)}, bf16[8,1024,128]{2,1,0:T(8,128)(2,1)}, bf16[8,1024,128]{2,1,0:T(8,128)(2,1)}) custom-call(bf16[3,16,1024,128]{3,2,1,0:T(8,128)(2,1)} %shard_map.308.query_ref.key_ref.value_ref, bf16[3,16,1024,128]{3,2,1,0:T(8,128)(2,1)} %shard_map.308.query_ref.key_ref.value_ref, ...), custom_call_target="tpu_custom_call" | custom-call | flops 21474836480 | bytes 16777216 | tf_op jit(solution)/shard_map/pallas_call | solution.py:334
  426.6 3.9 collective-permute-done.37
  437.3 13.6 %shard_map.320 = (bf16[4,1024,128]{2,1,0:T(8,128)(2,1)}, bf16[4,1024,128]{2,1,0:T(8,128)(2,1)}, bf16[4,1024,128]{2,1,0:T(8,128)(2,1)}) custom-call(bf16[3,16,1024,128]{3,2,1,0:T(8,128)(2,1)} %shard_map.308.query_ref.key_ref.value_ref, bf16[3,16,1024,128]{3,2,1,0:T(8,128)(2,1)} %shard_map.308.query_ref.key_ref.value_ref, ...), custom_call_target="tpu_custom_call" | custom-call | flops 10737418240 | bytes 8388608 | tf_op jit(solution)/shard_map/pallas_call | solution.py:334
  450.9 12.0 %shard_map.321 = bf16[8,288,1152]{2,1,0:T(8,128)(2,1)} custom-call(s32[1]{0:T(128)S(6)} %sub.83.owner_ref, bf16[1024,1152]{1,0:T(8,128)(2,1)} %get-tuple-element.328.norm_ref, bf16[1024,1152]{1,0:T(8,128)(2,1)} %get-tuple-element.317.joined_ref, bf16[1024,1152]{1,0:T(8,128)(2,1)} %get-tuple-element.302.grad_ref, ...), custom_call_target="tpu_custom_call" | custom-call | flops 5435817984 | bytes 17104896 | tf_op jit(solution)/shard_map/pallas_call | solution.py:605
  471.6 13.4 %shard_map.322 = bf16[8,288,1152]{2,1,0:T(8,128)(2,1)} custom-call(s32[1]{0:T(128)} %bitcast.owner_ref, bf16[1024,1152]{1,0:T(8,128)(2,1)} %get-tuple-element.328.norm_ref, bf16[1024,1152]{1,0:T(8,128)(2,1)} %get-tuple-element.317.joined_ref, bf16[1024,1152]{1,0:T(8,128)(2,1)} %get-tuple-element.302.grad_ref, ...), custom_call_target="tpu_custom_call" | custom-call | flops 5435817984 | bytes 17104896 | tf_op jit(solution)/shard_map/pallas_call | solution.py:605
  490.2 10.8 %shard_map.323 = (bf16[256,1152]{1,0:T(8,128)(2,1)}, bf16[8,104,1152]{2,1,0:T(8,128)(2,1)}, f32[8,1152]{1,0:T(8,128)}) custom-call(s32[2]{0:T(128)} %pad_add_fusion.core_ref, s32[8]{0:T(128)} %compare_select_fusion.2.places_ref, s32[1]{0:T(128)S(6)} %copy.72.count_ref, s32[1,768]{1,0:T(1,128)} %index_row_ref.7, s32[768,1]{1,0:T(8,128)} %copy.48.index_ref, ...), custom_call_target="tpu_custom_call" | custom-call | flops 2717908992 | bytes 8257536 | tf_op jit(solution)/shard_map/pallas_call | solution.py:712
  502.5 5.9 collective-permute-done.42
  514.8 11.5 %shard_map.324 = (bf16[256,1152]{1,0:T(8,128)(2,1)}, bf16[8,104,1152]{2,1,0:T(8,128)(2,1)}, f32[8,1152]{1,0:T(8,128)}) custom-call(s32[2]{0:T(128)} %pad_add_fusion.core_ref, s32[8]{0:T(128)} %compare_select_fusion.2.places_ref, s32[1]{0:T(128)S(6)} %copy.72.count_ref, s32[1,768]{1,0:T(1,128)} %index_row_ref.7, s32[768,1]{1,0:T(8,128)} %copy.48.index_ref, ...), custom_call_target="tpu_custom_call" | custom-call | flops 2717908992 | bytes 8257536 | tf_op jit(solution)/shard_map/pallas_call | solution.py:712
  536.8 11.5 %shard_map.325 = (bf16[256,1152]{1,0:T(8,128)(2,1)}, bf16[8,104,1152]{2,1,0:T(8,128)(2,1)}, f32[8,1152]{1,0:T(8,128)}) custom-call(s32[2]{0:T(128)} %pad_add_fusion.core_ref, s32[8]{0:T(128)} %compare_select_fusion.2.places_ref, s32[1]{0:T(128)S(6)} %copy.72.count_ref, s32[1,768]{1,0:T(1,128)} %index_row_ref.7, s32[768,1]{1,0:T(8,128)} %copy.48.index_ref, ...), custom_call_target="tpu_custom_call" | custom-call | flops 2717908992 | bytes 8257536 | tf_op jit(solution)/shard_map/pallas_call | solution.py:712
  557.1 11.5 %shard_map.326 = (bf16[256,1152]{1,0:T(8,128)(2,1)}, bf16[8,104,1152]{2,1,0:T(8,128)(2,1)}, f32[8,1152]{1,0:T(8,128)}) custom-call(s32[2]{0:T(128)} %pad_add_fusion.core_ref, s32[8]{0:T(128)} %compare_select_fusion.2.places_ref, s32[1]{0:T(128)S(6)} %copy.72.count_ref, s32[1,768]{1,0:T(1,128)} %index_row_ref.7, s32[768,1]{1,0:T(8,128)} %copy.48.index_ref, ...), custom_call_target="tpu_custom_call" | custom-call | flops 2717908992 | bytes 8257536 | tf_op jit(solution)/shard_map/pallas_call | solution.py:712
  578.1 4.3 all-to-all-start.2
  583.4 5.1 collective-permute-done.61
  596.6 11.8 %collective-permute-done.54 = bf16[272,1152]{1,0:T(8,128)(2,1)S(1)} collective-permute-done((bf16[272,1152]{1,0:T(8,128)(2,1)S(1)}, bf16[272,1152]{1,0:T(8,128)(2,1)S(1)}, u32[]{:S(2)}, u32[]{:S(2)}) %collective-permute-start.54) | collective-permute-done | bytes 626720 | tf_op jit(solution)/shard_map/ppermute | solution.py:812
  609.3 18.0 %all-to-all-done.2 = bf16[8,104,1152]{2,1,0:T(8,128)(2,1)} async-done(((bf16[8,104,1152]{2,1,0:T(8,128)(2,1)}), bf16[8,104,1152]{2,1,0:T(8,128)(2,1)}, u32[]{:S(2)}, u32[]{:S(2)}) %all-to-all-start.2) | async-done | bytes 1916960 | tf_op jit(solution)/shard_map/all_to_all | solution.py:1079
  647.9 8.1 %all-to-all-done.3 = bf16[8,48,1152]{2,1,0:T(8,128)(2,1)S(1)} async-done(((bf16[8,48,1152]{2,1,0:T(8,128)(2,1)}), bf16[8,48,1152]{2,1,0:T(8,128)(2,1)S(1)}, u32[]{:S(2)}, u32[]{:S(2)}) %all-to-all-start.3) | async-done | bytes 884768 | tf_op jit(solution)/shard_map/all_to_all | solution.py:1079
  (375 shorter events, 233.7 us)
Async XLA Ops:
  7.2 19.4 %collective-permute-start = (bf16[240,1152]{1,0:T(8,128)(2,1)}, bf16[240,1152]{1,0:T(8,128)(2,1)S(1)}, u32[]{:S(2)}, u32[]{:S(2)}) collective-permute-start(bf16[240,1152]{1,0:T(8,128)(2,1)} %fusion.19), channel_id=1, source_target_pairs={{0,2},{2,4},{4,6},{6,7},{7,5},{5,3},{3,1},{1,0},{8,10},{10,12},{12... | collective-permute-start | bytes 1658888 | tf_op jit(solution)/shard_map/ppermute | solution.py:831
  18.2 74.1 %all-to-all-start = ((bf16[8,112,1152]{2,1,0:T(8,128)(2,1)}), bf16[8,112,1152]{2,1,0:T(8,128)(2,1)}, u32[]{:S(2)}, u32[]{:S(2)}) async-start(bf16[8,112,1152]{2,1,0:T(8,128)(2,1)} %pad_maximum_fusion.4), calls=%async_computation | async-start | bytes 4128768 | tf_op jit(solution)/shard_map/all_to_all | solution.py:1079
  26.6 43.1 %collective-permute-start.2 = (bf16[240,1152]{1,0:T(8,128)(2,1)S(1)}, bf16[240,1152]{1,0:T(8,128)(2,1)}, u32[]{:S(2)}, u32[]{:S(2)}) collective-permute-start(bf16[240,1152]{1,0:T(8,128)(2,1)S(1)} %collective-permute-done), channel_id=1, source_target_pairs={{0,2},{2,4},{4,6},{6,7},{7,5},{5,3},{3,1},{1,0},{8,10},{10,12},{12... | collective-permute-start | bytes 1658888 | tf_op jit(solution)/shard_map/ppermute | solution.py:831
  28.7 41.0 %collective-permute-start.3 = (bf16[240,1152]{1,0:T(8,128)(2,1)S(1)}, bf16[240,1152]{1,0:T(8,128)(2,1)}, u32[]{:S(2)}, u32[]{:S(2)}) collective-permute-start(bf16[240,1152]{1,0:T(8,128)(2,1)S(1)} %collective-permute-done.1), channel_id=1, source_target_pairs={{2,0},{4,2},{6,4},{7,6},{5,7},{3,5},{1,3},{0,1},{10,8},{12,10},{14... | collective-permute-start | bytes 1658888 | tf_op jit(solution)/shard_map/ppermute | solution.py:834
  69.8 28.3 %collective-permute-start.5 = (bf16[240,1152]{1,0:T(8,128)(2,1)}, bf16[240,1152]{1,0:T(8,128)(2,1)S(1)}, u32[]{:S(2)}, u32[]{:S(2)}) collective-permute-start(bf16[240,1152]{1,0:T(8,128)(2,1)} %collective-permute-done.2), channel_id=1, source_target_pairs={{0,2},{2,4},{4,6},{6,7},{7,5},{5,3},{3,1},{1,0},{8,10},{10,12},{12... | collective-permute-start | bytes 1658888 | tf_op jit(solution)/shard_map/ppermute | solution.py:831
  115.3 19.9 %collective-permute-start.13 = (bf16[2,352,1152]{2,1,0:T(8,128)(2,1)}, bf16[2,352,1152]{2,1,0:T(8,128)(2,1)S(1)}, u32[]{:S(2)}, u32[]{:S(2)}) collective-permute-start(bf16[2,352,1152]{2,1,0:T(8,128)(2,1)} %pad_maximum_fusion.10), channel_id=1, source_target_pairs={{0,8},{8,0},{16,24},{24,16},{1,9},{9,1},{17,25},{25,17},{2,10},{10... | collective-permute-start | bytes 4866056 | tf_op jit(solution)/shard_map/ppermute | solution.py:801
  115.3 19.9 %collective-permute-start.12 = (bf16[2,352,1152]{2,1,0:T(8,128)(2,1)}, bf16[2,352,1152]{2,1,0:T(8,128)(2,1)S(1)}, u32[]{:S(2)}, u32[]{:S(2)}) collective-permute-start(bf16[2,352,1152]{2,1,0:T(8,128)(2,1)} %pad_maximum_fusion.9), channel_id=1, source_target_pairs={{0,8},{8,0},{16,24},{24,16},{1,9},{9,1},{17,25},{25,17},{2,10},{10... | collective-permute-start | bytes 4866056 | tf_op jit(solution)/shard_map/ppermute | solution.py:801
  128.7 21.8 %collective-permute-start.17 = (bf16[384,1152]{1,0:T(8,128)(2,1)}, bf16[384,1152]{1,0:T(8,128)(2,1)}, u32[]{:S(2)}, u32[]{:S(2)}) collective-permute-start(bf16[384,1152]{1,0:T(8,128)(2,1)} %constant_dynamic-slice_fusion.3), channel_id=1, source_target_pairs={{0,2},{2,4},{4,6},{6,7},{7,5},{5,3},{3,1},{1,0},{8,10},{10,12},{12... | collective-permute-start | bytes 2654216 | tf_op jit(solution)/shard_map/ppermute | solution.py:831
  133.6 21.5 %collective-permute-start.18 = (bf16[384,1152]{1,0:T(8,128)(2,1)}, bf16[384,1152]{1,0:T(8,128)(2,1)}, u32[]{:S(2)}, u32[]{:S(2)}) collective-permute-start(bf16[384,1152]{1,0:T(8,128)(2,1)} %constant_dynamic-slice_fusion.3), channel_id=1, source_target_pairs={{2,0},{4,2},{6,4},{7,6},{5,7},{3,5},{1,3},{0,1},{10,8},{12,10},{14... | collective-permute-start | bytes 2654216 | tf_op jit(solution)/shard_map/ppermute | solution.py:834
  157.3 20.3 %collective-permute-start.21 = (bf16[2,192,1152]{2,1,0:T(8,128)(2,1)S(1)}, bf16[2,192,1152]{2,1,0:T(8,128)(2,1)S(1)}, u32[]{:S(2)}, u32[]{:S(2)}) collective-permute-start(bf16[2,192,1152]{2,1,0:T(8,128)(2,1)S(1)} %pad_maximum_fusion.14), channel_id=1, source_target_pairs={{0,16},{8,24},{16,0},{24,8},{1,17},{9,25},{17,1},{25,9},{2,18},{10... | collective-permute-start | bytes 2654216 | tf_op jit(solution)/shard_map/ppermute | solution.py:812
  158.8 20.0 %collective-permute-start.19 = (bf16[384,1152]{1,0:T(8,128)(2,1)}, bf16[384,1152]{1,0:T(8,128)(2,1)S(1)}, u32[]{:S(2)}, u32[]{:S(2)}) collective-permute-start(bf16[384,1152]{1,0:T(8,128)(2,1)} %collective-permute-done.17), channel_id=1, source_target_pairs={{0,2},{2,4},{4,6},{6,7},{7,5},{5,3},{3,1},{1,0},{8,10},{10,12},{12... | collective-permute-start | bytes 2654216 | tf_op jit(solution)/shard_map/ppermute | solution.py:831
  160.2 19.6 %collective-permute-start.20 = (bf16[384,1152]{1,0:T(8,128)(2,1)}, bf16[384,1152]{1,0:T(8,128)(2,1)S(1)}, u32[]{:S(2)}, u32[]{:S(2)}) collective-permute-start(bf16[384,1152]{1,0:T(8,128)(2,1)} %collective-permute-done.18), channel_id=1, source_target_pairs={{2,0},{4,2},{6,4},{7,6},{5,7},{3,5},{1,3},{0,1},{10,8},{12,10},{14... | collective-permute-start | bytes 2654216 | tf_op jit(solution)/shard_map/ppermute | solution.py:834
  179.8 22.8 %collective-permute-start.22 = (bf16[384,1152]{1,0:T(8,128)(2,1)S(1)}, bf16[384,1152]{1,0:T(8,128)(2,1)S(1)}, u32[]{:S(2)}, u32[]{:S(2)}) collective-permute-start(bf16[384,1152]{1,0:T(8,128)(2,1)S(1)} %collective-permute-done.19), channel_id=1, source_target_pairs={{0,2},{2,4},{4,6},{6,7},{7,5},{5,3},{3,1},{1,0},{8,10},{10,12},{12... | collective-permute-start | bytes 2654216 | tf_op jit(solution)/shard_map/ppermute | solution.py:831
  181.4 21.2 %collective-permute-start.23 = (bf16[384,1152]{1,0:T(8,128)(2,1)S(1)}, bf16[384,1152]{1,0:T(8,128)(2,1)S(1)}, u32[]{:S(2)}, u32[]{:S(2)}) collective-permute-start(bf16[384,1152]{1,0:T(8,128)(2,1)S(1)} %collective-permute-done.20), channel_id=1, source_target_pairs={{2,0},{4,2},{6,4},{7,6},{5,7},{3,5},{1,3},{0,1},{10,8},{12,10},{14... | collective-permute-start | bytes 2654216 | tf_op jit(solution)/shard_map/ppermute | solution.py:834
  183.0 19.6 %collective-permute-start.24 = (bf16[2,192,1152]{2,1,0:T(8,128)(2,1)}, bf16[2,192,1152]{2,1,0:T(8,128)(2,1)}, u32[]{:S(2)}, u32[]{:S(2)}) collective-permute-start(bf16[2,192,1152]{2,1,0:T(8,128)(2,1)} %pad_maximum_fusion.15), channel_id=1, source_target_pairs={{0,16},{8,24},{16,0},{24,8},{1,17},{9,25},{17,1},{25,9},{2,18},{10... | collective-permute-start | bytes 2654216 | tf_op jit(solution)/shard_map/ppermute | solution.py:812
  202.6 25.1 %collective-permute-start.25 = (bf16[2,576,1152]{2,1,0:T(8,128)(2,1)}, bf16[2,576,1152]{2,1,0:T(8,128)(2,1)}, u32[]{:S(2)}, u32[]{:S(2)}) collective-permute-start(bf16[2,576,1152]{2,1,0:T(8,128)(2,1)} %pad_maximum_fusion), channel_id=1, source_target_pairs={{0,8},{8,0},{16,24},{24,16},{1,9},{9,1},{17,25},{25,17},{2,10},{10... | collective-permute-start | bytes 7962632 | tf_op jit(solution)/shard_map/ppermute | solution.py:801
  205.6 22.2 %collective-permute-start.28 = (bf16[2,192,1152]{2,1,0:T(8,128)(2,1)}, bf16[2,192,1152]{2,1,0:T(8,128)(2,1)}, u32[]{:S(2)}, u32[]{:S(2)}) collective-permute-start(bf16[2,192,1152]{2,1,0:T(8,128)(2,1)} %pad_maximum_fusion.16), channel_id=1, source_target_pairs={{0,16},{8,24},{16,0},{24,8},{1,17},{9,25},{17,1},{25,9},{2,18},{10... | collective-permute-start | bytes 2654216 | tf_op jit(solution)/shard_map/ppermute | solution.py:812
  206.7 20.5 %collective-permute-start.26 = (bf16[192,1152]{1,0:T(8,128)(2,1)}, bf16[192,1152]{1,0:T(8,128)(2,1)S(1)}, u32[]{:S(2)}, u32[]{:S(2)}) collective-permute-start(bf16[192,1152]{1,0:T(8,128)(2,1)} %get-tuple-element.470), channel_id=1, source_target_pairs={{0,2},{2,4},{4,6},{6,7},{7,5},{5,3},{3,1},{1,0},{8,10},{10,12},{12... | collective-permute-start | bytes 1327112 | tf_op jit(solution)/shard_map/ppermute | solution.py:831
  208.2 19.0 %collective-permute-start.27 = (bf16[192,1152]{1,0:T(8,128)(2,1)}, bf16[192,1152]{1,0:T(8,128)(2,1)}, u32[]{:S(2)}, u32[]{:S(2)}) collective-permute-start(bf16[192,1152]{1,0:T(8,128)(2,1)} %get-tuple-element.472), channel_id=1, source_target_pairs={{2,0},{4,2},{6,4},{7,6},{5,7},{3,5},{1,3},{0,1},{10,8},{12,10},{14... | collective-permute-start | bytes 1327112 | tf_op jit(solution)/shard_map/ppermute | solution.py:834
  400.2 30.3 %collective-permute-start.37 = (bf16[576,1152]{1,0:T(8,128)(2,1)}, bf16[576,1152]{1,0:T(8,128)(2,1)S(1)}, u32[]{:S(2)}, u32[]{:S(2)}) collective-permute-start(bf16[576,1152]{1,0:T(8,128)(2,1)} %get-tuple-element.437), channel_id=1, source_target_pairs={{0,2},{2,4},{4,6},{6,7},{7,5},{5,3},{3,1},{1,0},{8,10},{10,12},{12... | collective-permute-start | bytes 3981320 | tf_op jit(solution)/shard_map/ppermute | solution.py:831
  401.7 29.8 %collective-permute-start.38 = (bf16[576,1152]{1,0:T(8,128)(2,1)S(1)}, bf16[576,1152]{1,0:T(8,128)(2,1)S(1)}, u32[]{:S(2)}, u32[]{:S(2)}) collective-permute-start(bf16[576,1152]{1,0:T(8,128)(2,1)S(1)} %get-tuple-element.436), channel_id=1, source_target_pairs={{2,0},{4,2},{6,4},{7,6},{5,7},{3,5},{1,3},{0,1},{10,8},{12,10},{14... | collective-permute-start | bytes 3981320 | tf_op jit(solution)/shard_map/ppermute | solution.py:834
  435.3 29.0 %collective-permute-start.39 = (bf16[576,1152]{1,0:T(8,128)(2,1)}, bf16[576,1152]{1,0:T(8,128)(2,1)S(1)}, u32[]{:S(2)}, u32[]{:S(2)}) collective-permute-start(bf16[576,1152]{1,0:T(8,128)(2,1)} %get-tuple-element.435), channel_id=1, source_target_pairs={{0,2},{2,4},{4,6},{6,7},{7,5},{5,3},{3,1},{1,0},{8,10},{10,12},{12... | collective-permute-start | bytes 3981320 | tf_op jit(solution)/shard_map/ppermute | solution.py:831
  436.9 28.8 %collective-permute-start.40 = (bf16[576,1152]{1,0:T(8,128)(2,1)}, bf16[576,1152]{1,0:T(8,128)(2,1)S(1)}, u32[]{:S(2)}, u32[]{:S(2)}) collective-permute-start(bf16[576,1152]{1,0:T(8,128)(2,1)} %get-tuple-element.434), channel_id=1, source_target_pairs={{2,0},{4,2},{6,4},{7,6},{5,7},{3,5},{1,3},{0,1},{10,8},{12,10},{14... | collective-permute-start | bytes 3981320 | tf_op jit(solution)/shard_map/ppermute | solution.py:834
  465.7 19.3 %collective-permute-start.41 = (bf16[8,288,1152]{2,1,0:T(8,128)(2,1)}, bf16[8,288,1152]{2,1,0:T(8,128)(2,1)}, u32[]{:S(2)}, u32[]{:S(2)}) collective-permute-start(bf16[8,288,1152]{2,1,0:T(8,128)(2,1)} %shard_map.321), channel_id=1, source_target_pairs={{0,8},{8,0},{16,24},{24,16},{1,9},{9,1},{17,25},{25,17},{2,10},{10... | collective-permute-start | bytes 15925256 | tf_op jit(solution)/shard_map/ppermute | solution.py:801
  469.6 32.1 %collective-permute-start.44 = (bf16[576,1152]{1,0:T(8,128)(2,1)}, bf16[576,1152]{1,0:T(8,128)(2,1)S(1)}, u32[]{:S(2)}, u32[]{:S(2)}) collective-permute-start(bf16[576,1152]{1,0:T(8,128)(2,1)} %get-tuple-element.431), channel_id=1, source_target_pairs={{0,2},{2,4},{4,6},{6,7},{7,5},{5,3},{3,1},{1,0},{8,10},{10,12},{12... | collective-permute-start | bytes 3981320 | tf_op jit(solution)/shard_map/ppermute | solution.py:831
  470.3 32.2 %collective-permute-start.45 = (bf16[576,1152]{1,0:T(8,128)(2,1)}, bf16[576,1152]{1,0:T(8,128)(2,1)S(1)}, u32[]{:S(2)}, u32[]{:S(2)}) collective-permute-start(bf16[576,1152]{1,0:T(8,128)(2,1)} %get-tuple-element.430), channel_id=1, source_target_pairs={{2,0},{4,2},{6,4},{7,6},{5,7},{3,5},{1,3},{0,1},{10,8},{12,10},{14... | collective-permute-start | bytes 3981320 | tf_op jit(solution)/shard_map/ppermute | solution.py:834
  487.2 21.2 %collective-permute-start.42 = (bf16[144,1152]{1,0:T(8,128)(2,1)}, bf16[144,1152]{1,0:T(8,128)(2,1)S(1)}, u32[]{:S(2)}, u32[]{:S(2)}) collective-permute-start(bf16[144,1152]{1,0:T(8,128)(2,1)} %get-tuple-element.433), channel_id=1, source_target_pairs={{0,2},{2,4},{4,6},{6,7},{7,5},{5,3},{3,1},{1,0},{8,10},{10,12},{12... | collective-permute-start | bytes 995336 | tf_op jit(solution)/shard_map/ppermute | solution.py:831
  488.0 20.9 %collective-permute-start.43 = (bf16[144,1152]{1,0:T(8,128)(2,1)}, bf16[144,1152]{1,0:T(8,128)(2,1)S(1)}, u32[]{:S(2)}, u32[]{:S(2)}) collective-permute-start(bf16[144,1152]{1,0:T(8,128)(2,1)} %get-tuple-element.432), channel_id=1, source_target_pairs={{2,0},{4,2},{6,4},{7,6},{5,7},{3,5},{1,3},{0,1},{10,8},{12,10},{14... | collective-permute-start | bytes 995336 | tf_op jit(solution)/shard_map/ppermute | solution.py:834
  536.7 31.8 %collective-permute-start.52 = (bf16[576,1152]{1,0:T(8,128)(2,1)S(1)}, bf16[576,1152]{1,0:T(8,128)(2,1)S(1)}, u32[]{:S(2)}, u32[]{:S(2)}) collective-permute-start(bf16[576,1152]{1,0:T(8,128)(2,1)S(1)} %fusion.1), channel_id=1, source_target_pairs={{0,16},{8,24},{16,0},{24,8},{1,17},{9,25},{17,1},{25,9},{2,18},{10... | collective-permute-start | bytes 3981320 | tf_op jit(solution)/shard_map/ppermute | solution.py:812
  555.4 89.8 %collective-permute-start.58 = (bf16[16,1152]{1,0:T(8,128)(2,1)S(1)}, bf16[16,1152]{1,0:T(8,128)(2,1)S(1)}, u32[]{:S(2)}, u32[]{:S(2)}) collective-permute-start(bf16[16,1152]{1,0:T(8,128)(2,1)S(1)} %pad_maximum_fusion.28), channel_id=1, source_target_pairs={{0,16},{8,24},{16,0},{24,8},{1,17},{9,25},{17,1},{25,9},{2,18},{10... | collective-permute-start | bytes 110600 | tf_op jit(solution)/shard_map/ppermute | solution.py:983
  578.1 49.2 %all-to-all-start.2 = ((bf16[8,104,1152]{2,1,0:T(8,128)(2,1)}), bf16[8,104,1152]{2,1,0:T(8,128)(2,1)}, u32[]{:S(2)}, u32[]{:S(2)}) async-start(bf16[8,104,1152]{2,1,0:T(8,128)(2,1)} %get-tuple-element.415), calls=%async_computation.2 | async-start | bytes 3833856 | tf_op jit(solution)/shard_map/all_to_all | solution.py:1079
  629.9 26.1 %all-to-all-start.3 = ((bf16[8,48,1152]{2,1,0:T(8,128)(2,1)}), bf16[8,48,1152]{2,1,0:T(8,128)(2,1)S(1)}, u32[]{:S(2)}, u32[]{:S(2)}) async-start(bf16[8,48,1152]{2,1,0:T(8,128)(2,1)} %pad_maximum_fusion.17), calls=%async_computation.3 | async-start | bytes 1769472 | tf_op jit(solution)/shard_map/all_to_all | solution.py:1079
  (92 other events, 1091.8 us)

commit v6 on v5

--- a/solution.py
+++ b/solution.py
@@ -209,40 +209,40 @@
 
 def project_kernel(core_ref, places_ref, norm_ref, small_ref, *rest, chunks):
     refs, (out_ref, weight, sems) = rest[: len(chunks.arrays)], rest[len(chunks.arrays) :]
-    step = pl.program_id(0)
-
-    @pl.when(step == 0)
+    step, part = pl.program_id(0), pl.program_id(1)
+
+    @pl.when((step == 0) & (part == 0))
     def _():
         for block in range(3):
             chunks.load_block(refs, places_ref, core_ref, block, weight.at[block], sems.at[block])
 
-    wait_block(weight.at[step], sems.at[step])
+    @pl.when(part == 0)
+    def _():
+        wait_block(weight.at[step], sems.at[step])
+
     key_free = jnp.where(step == 1, 0.0, 1.0)
     bias = jnp.where(step == 0, small_ref[1:2], small_ref[2:3]) * key_free
-    half = norm_ref.shape[0] // 2
-    for part in range(2):
-        rows = slice(part * half, (part + 1) * half)
-        result = product(norm_ref[rows], square(weight[step])) + bias
-
-        def store(head, value):
-            out_ref[0, head, rows] = value
-
-        split_heads(result.astype(bf16), store)
+    result = product(norm_ref[...], square(weight[step])) + bias
+
+    def store(head, value):
+        out_ref[0, head] = value
+
+    split_heads(result.astype(bf16), store)
 
 
 def project_call(core, places, norm, small, chunks):
     seq_len, width = norm.shape
     return pl.pallas_call(
         functools.partial(project_kernel, chunks=chunks),
-        grid=(3,),
+        grid=(3, 2),
         in_specs=[
             smem,
             smem,
-            whole_block(norm),
+            pl.BlockSpec((seq_len // 2, width), lambda i, j: (j, 0)),
             whole_block(small),
         ]
         + chunks.specs,
-        out_specs=pl.BlockSpec((1, H, seq_len, LANES), lambda i: (i, 0, 0, 0)),
+        out_specs=pl.BlockSpec((1, H, seq_len // 2, LANES), lambda i, j: (i, 0, j, 0)),
         out_shape=jax.ShapeDtypeStruct((3, H, seq_len, LANES), bf16),
         scratch_shapes=[
             pltpu.VMEM((3, 8, width // 8, width), bf16),
@@ -253,27 +253,32 @@
     )(core, places, norm, small, *chunks.arrays)
 
 
-def attend_kernel(query_ref, key_ref, value_ref, *rest, size, factor):
+heads_a_step = 2
+forward_groups = ((0, 8), (8, 8))
+back_groups = ((0, 4), (4, 8), (12, 4))
+groups = len(back_groups)
+
+
+def attend_kernel(query_ref, key_ref, value_ref, *rest, factor):
     mix_ref, log_ref = rest[-2:]
-    turned_value = value_ref[0, 0].T
-    for part in range(query_ref.shape[2] // size):
-        rows = slice(part * size, (part + 1) * size)
-        scores = product(key_ref[0, 0], query_ref[0, 0, rows], right_turned)
+    for head in range(query_ref.shape[1]):
+        scores = product(key_ref[0, head], query_ref[0, head], right_turned)
         top = jnp.max(scores, axis=0, keepdims=True)
         weights = jnp.exp2((scores - top) * factor)
         total = jnp.sum(weights, axis=0, keepdims=True)
-        mix = product(turned_value, weights.astype(bf16))
-        mix_ref[0, rows] = (mix / total).T.astype(bf16)
-        log_ref[0, :, rows] = top * factor + jnp.log2(total)
-
-
-forward_groups = ((0, 8), (8, 8))
-back_groups = ((0, 4), (4, 8), (12, 4))
-groups = len(back_groups)
+        mix = product(value_ref[0, head].T, weights.astype(bf16))
+        mix_ref[head] = (mix / total).T.astype(bf16)
+        log_ref[head] = top * factor + jnp.log2(total)
 
 
 def head_block(place, seq_len, first):
-    return pl.BlockSpec((1, 1, seq_len, LANES), lambda h: (place, first + h, 0, 0))
+    first = first // heads_a_step
+    return pl.BlockSpec((1, heads_a_step, seq_len, LANES), lambda h: (place, first + h, 0, 0))
+
+
+def head_rows(first, *rest):
+    first = first // heads_a_step
+    return pl.BlockSpec((heads_a_step,) + rest, lambda h: (first + h, 0, 0))
 
 
 def attend_call(projected, first, heads, earlier=None):
@@ -281,13 +286,13 @@
     kept = [] if earlier is None else list(earlier)
     return pl.pallas_call(
         functools.partial(
-            attend_kernel, size=seq_len, factor=math.log2(math.e) / math.sqrt(HD)
+            attend_kernel, factor=math.log2(math.e) / math.sqrt(HD)
         ),
-        grid=(heads,),
+        grid=(heads // heads_a_step,),
         in_specs=[head_block(place, seq_len, first) for place in range(3)] + [anywhere] * len(kept),
         out_specs=[
-            pl.BlockSpec((1, seq_len, LANES), lambda h: (first + h, 0, 0)),
-            pl.BlockSpec((1, 1, seq_len), lambda h: (first + h, 0, 0)),
+            head_rows(first, seq_len, LANES),
+            head_rows(first, 1, seq_len),
         ],
         out_shape=[
             jax.ShapeDtypeStruct((H, seq_len, LANES), bf16),
@@ -301,48 +306,37 @@
 
 def attend_back_kernel(
     query_ref, key_ref, value_ref, mix_ref, log_ref, grad_ref, query_grad_ref, key_grad_ref,
-    value_grad_ref, key_sum, value_sum, *, size, factor
+    value_grad_ref, *, factor
 ):
-    key, value = key_ref[0, 0], value_ref[0, 0]
-    turned_key = key.T
     base_two = factor * math.log2(math.e)
-    for part in range(query_ref.shape[2] // size):
-        rows = slice(part * size, (part + 1) * size)
-        query, grad = query_ref[0, 0, rows], grad_ref[0, rows]
+    for head in range(query_ref.shape[1]):
+        query, key, value = query_ref[0, head], key_ref[0, head], value_ref[0, head]
+        grad = grad_ref[head]
         scores = product(key, query, right_turned)
-        weights = jnp.exp2(scores * base_two - log_ref[0, :, rows])
-        value_part = product(weights.astype(bf16), grad)
+        weights = jnp.exp2(scores * base_two - log_ref[head])
+        value_grad_ref[head] = product(weights.astype(bf16), grad).astype(bf16)
         weight_grad = product(value, grad, right_turned)
-        inner = column_sum((grad.astype(f32) * mix_ref[0, rows].astype(f32)).T)
+        inner = column_sum((grad.astype(f32) * mix_ref[head].astype(f32)).T)
         score_grad = (weights * (weight_grad - inner)).astype(bf16)
-        key_part = product(score_grad, query)
-        query_grad_ref[0, rows] = (product(turned_key, score_grad) * factor).T.astype(bf16)
-        if part == 0:
-            key_sum[...] = key_part
-            value_sum[...] = value_part
-        else:
-            key_sum[...] += key_part
-            value_sum[...] += value_part
-    key_grad_ref[0] = (key_sum[...] * factor).astype(bf16)
-    value_grad_ref[0] = value_sum[...].astype(bf16)
+        key_grad_ref[head] = (product(score_grad, query) * factor).astype(bf16)
+        query_grad_ref[head] = (product(key.T, score_grad) * factor).T.astype(bf16)
 
 
 def attend_back_call(projected, attended, grad, first, heads):
     seq_len = projected.shape[2]
     mix, logs = attended
-    flat = pl.BlockSpec((1, seq_len, LANES), lambda h: (h, 0, 0))
+    flat = head_rows(0, seq_len, LANES)
     return pl.pallas_call(
-        functools.partial(attend_back_kernel, size=seq_len // 2, factor=1.0 / math.sqrt(HD)),
-        grid=(heads,),
+        functools.partial(attend_back_kernel, factor=1.0 / math.sqrt(HD)),
+        grid=(heads // heads_a_step,),
         in_specs=[head_block(place, seq_len, first) for place in range(3)]
         + [
-            pl.BlockSpec((1, seq_len, LANES), lambda h: (first + h, 0, 0)),
-            pl.BlockSpec((1, 1, seq_len), lambda h: (first + h, 0, 0)),
-            pl.BlockSpec((1, seq_len, LANES), lambda h: (first + h, 0, 0)),
+            head_rows(first, seq_len, LANES),
+            head_rows(first, 1, seq_len),
+            head_rows(first, seq_len, LANES),
         ],
         out_specs=[flat] * 3,
         out_shape=[jax.ShapeDtypeStruct((heads, seq_len, LANES), bf16)] * 3,
-        scratch_shapes=[pltpu.VMEM((seq_len, LANES), f32)] * 2,
         compiler_params=params(),
         cost_estimate=cost(10 * heads * seq_len * seq_len * 256, 16 * heads * seq_len * LANES, heads * seq_len * seq_len),
     )(projected, projected, projected, mix, logs, grad)
@@ -367,7 +361,7 @@
     joined = join_heads(mix_refs)
     joined_ref[...] = joined
     branch = product(joined, square(weight[...])) + small_ref[3:4]
-    branch_ref[...] = branch
+    branch_ref[...] = branch.astype(bf16)
     middle = start_ref[...] + mod_ref[2:3] * branch
     middle_ref[...] = middle
     unit, _ = normalize(middle)
@@ -386,7 +380,7 @@
         + chunks.specs,
         out_specs=[block] * 4,
         out_shape=[
-            jax.ShapeDtypeStruct((seq_len, width), kind) for kind in (bf16, f32, f32, bf16)
+            jax.ShapeDtypeStruct((seq_len, width), kind) for kind in (bf16, bf16, f32, bf16)
         ],
         scratch_shapes=[pltpu.VMEM((8, width // 8, width), bf16), pltpu.SemaphoreType.DMA],
         compiler_params=params(),
@@ -461,7 +455,7 @@
     sums_ref[3:4] += column_sum(total)
     middle_grad = cot + normalize_back(total, unit, inverse, mod_ref[4:5])
     middle_grad_ref[...] = middle_grad
-    sums_ref[4:5] += column_sum(middle_grad * branch_ref[...])
+    sums_ref[4:5] += column_sum(middle_grad * branch_ref[...].astype(f32))
     grad_one = (mod_ref[2:3] * middle_grad).astype(bf16)
     grad_one_ref[...] = grad_one
     sums_ref[5:6] += column_sum(grad_one.astype(f32))
@@ -635,10 +629,10 @@
 
 def mix_grad_call(core, places, grad_one, chunks):
     seq_len, width = grad_one.shape
-    rows = seq_len // 2
+    rows = seq_len // 4
     return pl.pallas_call(
         functools.partial(mix_grad_kernel, chunks=chunks),
-        grid=(2,),
+        grid=(4,),
         in_specs=[smem, smem, row_block(rows, width)] + chunks.specs,
         out_specs=pl.BlockSpec((H, rows, LANES), lambda i: (0, i, 0)),
         out_shape=jax.ShapeDtypeStruct((H, seq_len, LANES), bf16),
@@ -952,6 +946,69 @@
         return total.astype(bf16)
 
 
+class CrossScatter:
+    def __init__(self, ring, part, middle, *values):
+        self.ring, self.values, self.part, self.middle = ring, values, part, middle
+        self.half = self.distance = ring.size // 2
+        self.split = (part + middle) // 2
+        self.extras = {}
+
+    def chip(self, place, row, count):
+        tok, width = self.ring.tok_at(place), self.values[0].shape[2]
+        return sum(
+            lax.dynamic_slice(values, (tok, row, 0), (1, count, width))[0].astype(f32)
+            for values in self.values
+        )
+
+    def cross(self, *distances):
+        row = (self.part + self.middle) * (1 - self.ring.x_bit)
+        places = [place for d in distances for place in ((d,) if d in (0, self.half) else (d, -d))]
+        sent = jnp.stack([self.chip(place, row, self.part).astype(bf16) for place in places])
+        return places, swap_x(sent)
+
+    def land_cross(self, places, got):
+        for number, place in enumerate(places):
+            self.extras[place] = got[number]
+
+    def piece(self, place):
+        part, bit = self.part, self.ring.x_bit
+        extra = self.extras[place].astype(f32)
+        blank = jnp.zeros((self.middle, extra.shape[1]), f32)
+        return self.chip(place, part * bit, part + self.middle) + jnp.where(
+            bit == 0, jnp.concatenate([extra, blank]), jnp.concatenate([blank, extra])
+        )
+
+    def hop(self):
+        ring, distance, split = self.ring, self.distance, self.split
+        if distance == self.half:
+            farthest = self.piece(distance)
+            ahead, behind = farthest[:split], farthest[split:]
+        else:
+            ahead, behind = self.ahead.astype(f32), self.behind.astype(f32)
+            if distance == self.half - 1:
+                rows = self.part + self.middle
+                ahead = jnp.pad(ahead, ((0, rows - split), (0, 0)))
+                behind = jnp.pad(behind, ((split, 0), (0, 0)))
+            ahead = self.piece(distance) + ahead
+            behind = self.piece(-distance) + behind
+        self.distance -= 1
+        return ring.forward(ahead.astype(bf16)), ring.backward(behind.astype(bf16))
+
+    def land(self, flight):
+        self.ahead, self.behind = flight
+
+    def total(self):
+        total = self.piece(0) + self.ahead.astype(f32) + self.behind.astype(f32)
+        return total.astype(bf16)
+
+    def join(self, total, far):
+        part, bit = self.part, self.ring.x_bit
+        low, high = jnp.where(bit == 0, total, far), jnp.where(bit == 0, far, total)
+        return jnp.concatenate(
+            [low[:part], add_low(low[part:], high[: self.middle]), high[self.middle :]]
+        )
+
+
 def gather_plain(shard, share):
     size, width = lax.axis_size("tok"), shard.shape[1]
     full = lax.all_gather(shard, "tok", axis=0)
@@ -1255,23 +1312,26 @@
     attention_got = swap_core(attention_other)
     if ringed:
         attention_mine, attention_got, grads = sync(attention_mine, attention_got, grads)
-        scatter = Scatter(ring, attention_mine, attention_got)
+        scatter = CrossScatter(ring, 2 * share // 3, 2 * share // 3, attention_mine, attention_got)
     quarters = []
     slot_grad = None
     for quarter in range(4):
         part = start_back(quarter, slot_grad, grads)
         if ringed:
-            if quarter in (0, 3):
-                flight, part, grads, feed_flight = sync(scatter.hop(), part, grads, feed_flight)
-            else:
-                flight, part, grads = sync(scatter.hop(), part, grads)
-            scatter.land(flight)
             if quarter == 0:
+                places_crossed, crossed = scatter.cross(scatter.half, scatter.half - 1)
+                crossed, part, grads, feed_flight = sync(crossed, part, grads, feed_flight)
                 feed_scatter.land(feed_flight)
                 feed_shard = feed_scatter.total()
-                feed_flight = feed_cross = swap_x(feed_shard)
+                feed_cross = swap_x(feed_shard)
             else:
-                feed_cross = feed_flight
+                following = (scatter.half - 1 - quarter,)
+                if quarter == 3:
+                    following = tuple(range(scatter.half - 4, -1, -1))
+                places_crossed, crossed = scatter.cross(*following)
+                flight, crossed, part, grads = sync(scatter.hop(), crossed, part, grads)
+                scatter.land(flight)
+            scatter.land_cross(places_crossed, crossed)
         quarters.append(part)
         slot_grad = part[1]
     row_grad = jnp.concatenate([part[0] for part in quarters])
@@ -1301,6 +1361,8 @@
     )
     table_got = swap_x(table_away)
     if ringed:
+        while scatter.distance > 0:
+            scatter.land(scatter.hop())
         attention_shard = scatter.total()
         attention_cross = swap_x(attention_shard)
     table_pair = add_low(table_near, table_got)
@@ -1345,7 +1407,7 @@
         ]
     )
     if ringed:
-        attention_shard = add_low(attention_shard, attention_cross)
+        attention_shard = scatter.join(attention_shard, attention_cross)
         feed_shard = add_low(feed_shard, feed_cross)
     else:
         attention_chip = by_tok(add_low(attention_mine, attention_got), share)

time: 673 us -> 673 us (level)
  waiting for transfers between devices: 117 us -> 107 us
  starting transfers between devices: 89.9 us -> 98.2 us
  Pallas kernels: 324 us -> 332 us
    convert_element_type x0 -> x6, other arithmetic: none -> 10.5 us  [the longest x4 4.41 us: piece(): extra = self.extras[place].astype(f32)]
    pallas_call x1, Pallas kernels: 73.2 us -> 83.2 us  [feed_call(): pl.pallas_call(functools.partial(feed_kernel, source=source), grid=(steps...]
    ppermute x12 -> x16, starting transfers between devices: 15.7 us -> 24.2 us  [swap_x(): return lax.ppermute(values, 'grp', swap_pairs(lax.axis_size('grp'), 2))]
    convert_element_type x7 -> x5, other arithmetic: 23.1 us -> 14.6 us  [hop(): behind.astype(bf16)]
    all_to_all x4, waiting for transfers between devices: 26.1 us -> 17.7 us  [exchange(): lax.all_to_all(values, 'tok', split_axis=0, concat_axis=0, tiled=True)]
    ppermute x16, waiting for transfers between devices: 45.3 us -> 38.2 us  [forward(): return lax.ppermute(values, 'tok', self.ahead)]
    ppermute x12 -> x16, waiting for transfers between devices: 26.9 us -> 32.2 us  [swap_x(): return lax.ppermute(values, 'grp', swap_pairs(lax.axis_size('grp'), 2))]
    unnamed x117 -> x113, local copies, waits for them, and re-layouts: 14.5 us -> 12.4 us
  transfers between devices with their start and end apart: 68 -> 72, of which waited for: 33 -> 28; matrix products, arithmetic and copies ran while one was open for 14% -> 15% of each run, Pallas kernels for 33% -> 33%
where the time goes in v6:
time: 673 us; the launch traced here: 668 us
  Pallas kernels  332 us (49%)
  waiting for transfers between devices  107 us (16%)
  starting transfers between devices  98.2 us (15%)
  other arithmetic  90.8 us (13%)
  local copies, waits for them, and re-layouts  32.8 us (5%)
    pallas_call x1, Pallas kernels, feed_call(): pl.pallas_call(functools.partial(feed_kernel, source=source), grid=(steps...  83.2 us
    pallas_call x3, Pallas kernels, attend_back_call(): pl.pallas_call(functools.partial(attend_back_kernel, factor=1.0 / math.sq...  50.1 us
    pallas_call x4, Pallas kernels, start_back_call(): pl.pallas_call(functools.partial(start_back_kernel, chunks=chunks, first=...  45.4 us
    pallas_call x4, Pallas kernels, feed_weight_call(): pl.pallas_call(feed_weight_kernel, grid_spec=pltpu.PrefetchScalarGridSpec...  43.6 us
    ppermute x16, waiting for transfers between devices, forward(): return lax.ppermute(values, 'tok', self.ahead)  38.2 us
    ppermute x16, starting transfers between devices, forward(): return lax.ppermute(values, 'tok', self.ahead)  36 us
    ppermute x16, waiting for transfers between devices, swap_x(): return lax.ppermute(values, 'grp', swap_pairs(lax.axis_size('grp'), 2))  32.2 us
    pallas_call x2, Pallas kernels, attend_call(): pl.pallas_call(functools.partial(attend_kernel, factor=math.log2(math.e)...  29.8 us
  transfers between devices with their start and end apart: 72, of which 28 were waited for; matrix products, arithmetic and copies ran while one was open for 15% of the time, Pallas kernels for 33%

profile of v6, /device:TPU:0, one launch (start us, length us, event | category | flops | bytes accessed | tf_op | source)
XLA Modules:
  0.0 668.2 jit_solution(2533710231391197555)
XLA Ops:
  17.8 6.5 all-to-all-start
  46.0 23.4 %collective-permute-done.2 = bf16[240,1152]{1,0:T(8,128)(2,1)} collective-permute-done((bf16[240,1152]{1,0:T(8,128)(2,1)S(1)}, bf16[240,1152]{1,0:T(8,128)(2,1)}, u32[]{:S(2)}, u32[]{:S(2)}) %collective-permute-start.2) | collective-permute-done | bytes 552992 | tf_op jit(solution)/shard_map/ppermute | solution.py:825
  69.4 14.4 %collective-permute-start.5 = (bf16[240,1152]{1,0:T(8,128)(2,1)}, bf16[240,1152]{1,0:T(8,128)(2,1)S(1)}, u32[]{:S(2)}, u32[]{:S(2)}) collective-permute-start(bf16[240,1152]{1,0:T(8,128)(2,1)} %collective-permute-done.2), channel_id=1, source_target_pairs={{0,2},{2,4},{4,6},{6,7},{7,5},{5,3},{3,1},{1,0},{8,10},{10,12},{12... | collective-permute-start | bytes 1658888 | tf_op jit(solution)/shard_map/ppermute | solution.py:825
  117.3 5.6 all-to-all-start.1
  135.5 8.4 %shard_map.307 = (f32[1024,1152]{1,0:T(8,128)}, bf16[1024,1152]{1,0:T(8,128)(2,1)}) custom-call(s32[2]{0:T(128)} %pad_add_fusion.core_ref, s32[8]{0:T(128)} %compare_select_fusion.2.places_ref, s32[1]{0:T(128)S(6)} %copy.72.count_ref, s32[1,768]{1,0:T(1,128)} %index_row_ref.7, bf16[8,112,1152]{2,1,0:T(8,128)(2,1)} %all-to-all-done.kept_ref, ...), custom_call_target="tpu_custom_call" | custom-call | flops 1811939328 | bytes 16515072 | tf_op jit(solution)/shard_map/pallas_call | solution.py:106
  143.9 4.1 collective-permute-done.17
  158.1 16.8 %shard_map.308.query_ref.key_ref.value_ref = bf16[3,16,1024,128]{3,2,1,0:T(8,128)(2,1)} custom-call(s32[2]{0:T(128)} %pad_add_fusion.core_ref, s32[8]{0:T(128)} %compare_select_fusion.2.places_ref, bf16[1024,1152]{1,0:T(8,128)(2,1)} %get-tuple-element.329.norm_ref, f32[16,1152]{1,0:T(8,128)} %convert_reduce_fusion.1.small_ref, ...), custom_call_target="tpu_custom_call" | custom-call | flops 8153726976 | bytes 22118400 | tf_op jit(solution)/shard_map/pallas_call | solution.py:235
  183.2 14.9 %shard_map.309 = (bf16[16,1024,128]{2,1,0:T(8,128)(2,1)}, f32[16,1,1024]{2,1,0:T(1,128)}) custom-call(bf16[3,16,1024,128]{3,2,1,0:T(8,128)(2,1)} %shard_map.308.query_ref.key_ref.value_ref, bf16[3,16,1024,128]{3,2,1,0:T(8,128)(2,1)} %shard_map.308.query_ref.key_ref.value_ref, bf16[3,16,1024,128]{3,2,1,0:T(8,128)(2,1)} %shard_map.308.query_ref.key_ref.value_ref), custom_call_target="tpu_custom_call" | custom-call | flops 8589934592 | bytes 8388608 | tf_op jit(solution)/shard_map/pallas_call | solution.py:287
  204.5 14.9 %shard_map.310 = (bf16[16,1024,128]{2,1,0:T(8,128)(2,1)}, f32[16,1,1024]{2,1,0:T(1,128)}) custom-call(bf16[3,16,1024,128]{3,2,1,0:T(8,128)(2,1)} %shard_map.308.query_ref.key_ref.value_ref, bf16[3,16,1024,128]{3,2,1,0:T(8,128)(2,1)} %shard_map.308.query_ref.key_ref.value_ref, ...), custom_call_target="tpu_custom_call", output_to_operand_aliasing={{0}: (3, {}), {1}: (4, {})} | custom-call | flops 8589934592 | bytes 8388608 | tf_op jit(solution)/shard_map/pallas_call | solution.py:287
  229.2 11.7 %shard_map.311 = (bf16[1024,1152]{1,0:T(8,128)(2,1)}, bf16[1024,1152]{1,0:T(8,128)(2,1)}, f32[1024,1152]{1,0:T(8,128)}, bf16[1024,1152]{1,0:T(8,128)(2,1)}) custom-call(s32[2]{0:T(128)} %pad_add_fusion.core_ref, s32[8]{0:T(128)} %compare_select_fusion.2.places_ref, f32[1024,1152]{1,0:T(8,128)} %get-tuple-element.275.start_ref, ...), custom_call_target="tpu_custom_call" | custom-call | flops 2717908992 | bytes 21233664 | tf_op jit(solution)/shard_map/pallas_call | solution.py:375
  246.7 83.2 %shard_map.312 = (f32[1024,1152]{1,0:T(8,128)}, bf16[4,1024,1152]{2,1,0:T(8,128)(2,1)}, bf16[4,1024,1152]{2,1,0:T(8,128)(2,1)}, bf16[1024,1152]{1,0:T(8,128)(2,1...) custom-call(s32[2]{0:T(128)} %pad_add_fusion.core_ref, ...), custom_call_target="tpu_custom_call" | custom-call | flops 43486543872 | bytes 70778880 | tf_op jit(solution)/shard_map/pallas_call | solution.py:471
  329.9 10.5 %shard_map.313 = bf16[8,288,1152]{2,1,0:T(8,128)(2,1)} custom-call(s32[1]{0:T(128)S(6)} %sub.88.first_ref, bf16[1024,1152]{1,0:T(8,128)(2,1)} %get-tuple-element.294.norm_ref.left_ref, bf16[4,1024,1152]{2,1,0:T(8,128)(2,1)} %get-tuple-element.287.right_ref), custom_call_target="tpu_custom_call" | custom-call | flops 5435817984 | bytes 14745600 | tf_op jit(solution)/shard_map/pallas_call | solution.py:542
  340.5 10.4 %shard_map.314 = bf16[8,288,1152]{2,1,0:T(8,128)(2,1)} custom-call(s32[1]{0:T(128)S(6)} %sub.88.first_ref, bf16[4,1024,1152]{2,1,0:T(8,128)(2,1)} %get-tuple-element.296.left_ref, bf16[1024,1152]{1,0:T(8,128)(2,1)} %get-tuple-element.292.right_ref), custom_call_target="tpu_custom_call" | custom-call | flops 5435817984 | bytes 14745600 | tf_op jit(solution)/shard_map/pallas_call | solution.py:542
  351.3 11.4 %shard_map.315.rest_1_ = bf16[8,576,1152]{2,1,0:T(8,128)(2,1)} custom-call(s32[1]{0:T(128)S(6)} %mul.77.first_ref, bf16[1024,1152]{1,0:T(8,128)(2,1)} %get-tuple-element.294.norm_ref.left_ref, bf16[4,1024,1152]{2,1,0:T(8,128)(2,1)} %get-tuple-element.287.right_ref, bf16[8,288,1152]{2,1,0:T(8,128)(2,1)} %collective-permute-done.33.rest_0_), custom_call_target="tpu_custom_call" | custom-call | flops 5435817984 | bytes 14745600 | tf_op jit(solution)/shard_map/pallas_call | solution.py:542
  362.7 11.3 %shard_map.316 = bf16[8,576,1152]{2,1,0:T(8,128)(2,1)} custom-call(s32[1]{0:T(128)S(6)} %mul.77.first_ref, bf16[4,1024,1152]{2,1,0:T(8,128)(2,1)} %get-tuple-element.296.left_ref, bf16[1024,1152]{1,0:T(8,128)(2,1)} %get-tuple-element.292.right_ref, bf16[8,288,1152]{2,1,0:T(8,128)(2,1)} %collective-permute-done.34.rest_0_, ...), custom_call_target="tpu_custom_call", output_to_operand_aliasing={{}: (4, {})} | custom-call | flops 5435817984 | bytes 14745600 | tf_op jit(solution)/shard_map/pallas_call | solution.py:542
  374.0 8.8 %shard_map.317.grad_ref = bf16[16,1024,128]{2,1,0:T(8,128)(2,1)} custom-call(s32[2]{0:T(128)} %pad_add_fusion.core_ref, s32[8]{0:T(128)} %compare_select_fusion.2.places_ref, bf16[1024,1152]{1,0:T(8,128)(2,1)} %get-tuple-element.303.grad_ref, bf16[1,352,1152]{2,1,0:T(8,128)(2,1)} %copy-done.2, bf16[1,240,1152]{2,1,0:T(8,128)(2,1)} %bitcast.239, ...), custom_call_target="tpu_custom_call" | custom-call | flops 2717908992 | bytes 9437184 | tf_op jit(solution)/shard_map/pallas_call | solution.py:633
  386.3 13.3 %shard_map.318 = (bf16[4,1024,128]{2,1,0:T(8,128)(2,1)}, bf16[4,1024,128]{2,1,0:T(8,128)(2,1)}, bf16[4,1024,128]{2,1,0:T(8,128)(2,1)}) custom-call(bf16[3,16,1024,128]{3,2,1,0:T(8,128)(2,1)} %shard_map.308.query_ref.key_ref.value_ref, bf16[3,16,1024,128]{3,2,1,0:T(8,128)(2,1)} %shard_map.308.query_ref.key_ref.value_ref, ...), custom_call_target="tpu_custom_call" | custom-call | flops 10737418240 | bytes 8388608 | tf_op jit(solution)/shard_map/pallas_call | solution.py:329
  407.6 23.5 %shard_map.319 = (bf16[8,1024,128]{2,1,0:T(8,128)(2,1)}, bf16[8,1024,128]{2,1,0:T(8,128)(2,1)}, bf16[8,1024,128]{2,1,0:T(8,128)(2,1)}) custom-call(bf16[3,16,1024,128]{3,2,1,0:T(8,128)(2,1)} %shard_map.308.query_ref.key_ref.value_ref, bf16[3,16,1024,128]{3,2,1,0:T(8,128)(2,1)} %shard_map.308.query_ref.key_ref.value_ref, ...), custom_call_target="tpu_custom_call" | custom-call | flops 21474836480 | bytes 16777216 | tf_op jit(solution)/shard_map/pallas_call | solution.py:329
  431.1 4.7 collective-permute-done.37
  443.2 13.3 %shard_map.320 = (bf16[4,1024,128]{2,1,0:T(8,128)(2,1)}, bf16[4,1024,128]{2,1,0:T(8,128)(2,1)}, bf16[4,1024,128]{2,1,0:T(8,128)(2,1)}) custom-call(bf16[3,16,1024,128]{3,2,1,0:T(8,128)(2,1)} %shard_map.308.query_ref.key_ref.value_ref, bf16[3,16,1024,128]{3,2,1,0:T(8,128)(2,1)} %shard_map.308.query_ref.key_ref.value_ref, ...), custom_call_target="tpu_custom_call" | custom-call | flops 10737418240 | bytes 8388608 | tf_op jit(solution)/shard_map/pallas_call | solution.py:329
  456.6 12.1 %shard_map.321 = bf16[8,288,1152]{2,1,0:T(8,128)(2,1)} custom-call(s32[1]{0:T(128)S(6)} %sub.94.owner_ref, bf16[1024,1152]{1,0:T(8,128)(2,1)} %get-tuple-element.329.norm_ref, bf16[1024,1152]{1,0:T(8,128)(2,1)} %get-tuple-element.318.joined_ref, bf16[1024,1152]{1,0:T(8,128)(2,1)} %get-tuple-element.303.grad_ref, ...), custom_call_target="tpu_custom_call" | custom-call | flops 5435817984 | bytes 17104896 | tf_op jit(solution)/shard_map/pallas_call | solution.py:599
  472.9 4.5 collective-permute-done.58
  484.2 13.6 %shard_map.322 = bf16[8,288,1152]{2,1,0:T(8,128)(2,1)} custom-call(s32[1]{0:T(128)} %bitcast.owner_ref, bf16[1024,1152]{1,0:T(8,128)(2,1)} %get-tuple-element.329.norm_ref, bf16[1024,1152]{1,0:T(8,128)(2,1)} %get-tuple-element.318.joined_ref, bf16[1024,1152]{1,0:T(8,128)(2,1)} %get-tuple-element.303.grad_ref, ...), custom_call_target="tpu_custom_call" | custom-call | flops 5435817984 | bytes 17104896 | tf_op jit(solution)/shard_map/pallas_call | solution.py:599
  504.1 10.8 %shard_map.323 = (bf16[256,1152]{1,0:T(8,128)(2,1)}, bf16[8,104,1152]{2,1,0:T(8,128)(2,1)}, f32[8,1152]{1,0:T(8,128)}) custom-call(s32[2]{0:T(128)} %pad_add_fusion.core_ref, s32[8]{0:T(128)} %compare_select_fusion.2.places_ref, s32[1]{0:T(128)S(6)} %copy.72.count_ref, s32[1,768]{1,0:T(1,128)} %index_row_ref.7, s32[768,1]{1,0:T(8,128)} %copy.48.index_ref, ...), custom_call_target="tpu_custom_call" | custom-call | flops 2717908992 | bytes 8257536 | tf_op jit(solution)/shard_map/pallas_call | solution.py:706
  526.7 11.5 %shard_map.324 = (bf16[256,1152]{1,0:T(8,128)(2,1)}, bf16[8,104,1152]{2,1,0:T(8,128)(2,1)}, f32[8,1152]{1,0:T(8,128)}) custom-call(s32[2]{0:T(128)} %pad_add_fusion.core_ref, s32[8]{0:T(128)} %compare_select_fusion.2.places_ref, s32[1]{0:T(128)S(6)} %copy.72.count_ref, s32[1,768]{1,0:T(1,128)} %index_row_ref.7, s32[768,1]{1,0:T(8,128)} %copy.48.index_ref, ...), custom_call_target="tpu_custom_call" | custom-call | flops 2717908992 | bytes 8257536 | tf_op jit(solution)/shard_map/pallas_call | solution.py:706
  544.2 11.5 %shard_map.325 = (bf16[256,1152]{1,0:T(8,128)(2,1)}, bf16[8,104,1152]{2,1,0:T(8,128)(2,1)}, f32[8,1152]{1,0:T(8,128)}) custom-call(s32[2]{0:T(128)} %pad_add_fusion.core_ref, s32[8]{0:T(128)} %compare_select_fusion.2.places_ref, s32[1]{0:T(128)S(6)} %copy.72.count_ref, s32[1,768]{1,0:T(1,128)} %index_row_ref.7, s32[768,1]{1,0:T(8,128)} %copy.48.index_ref, ...), custom_call_target="tpu_custom_call" | custom-call | flops 2717908992 | bytes 8257536 | tf_op jit(solution)/shard_map/pallas_call | solution.py:706
  562.2 11.5 %shard_map.326 = (bf16[256,1152]{1,0:T(8,128)(2,1)}, bf16[8,104,1152]{2,1,0:T(8,128)(2,1)}, f32[8,1152]{1,0:T(8,128)}) custom-call(s32[2]{0:T(128)} %pad_add_fusion.core_ref, s32[8]{0:T(128)} %compare_select_fusion.2.places_ref, s32[1]{0:T(128)S(6)} %copy.72.count_ref, s32[1,768]{1,0:T(1,128)} %index_row_ref.7, s32[768,1]{1,0:T(8,128)} %copy.48.index_ref, ...), custom_call_target="tpu_custom_call" | custom-call | flops 2717908992 | bytes 8257536 | tf_op jit(solution)/shard_map/pallas_call | solution.py:706
  582.0 4.4 all-to-all-start.2
  593.9 9.4 %collective-permute-done.64 = bf16[192,1152]{1,0:T(8,128)(2,1)S(1)} collective-permute-done((bf16[192,1152]{1,0:T(8,128)(2,1)S(1)}, bf16[192,1152]{1,0:T(8,128)(2,1)S(1)}, u32[]{:S(2)}, u32[]{:S(2)}) %collective-permute-start.64) | collective-permute-done | bytes 442400 | tf_op jit(solution)/shard_map/ppermute | solution.py:806
  612.2 10.0 %collective-permute-done.55 = bf16[272,1152]{1,0:T(8,128)(2,1)S(1)} collective-permute-done((bf16[272,1152]{1,0:T(8,128)(2,1)S(1)}, bf16[272,1152]{1,0:T(8,128)(2,1)S(1)}, u32[]{:S(2)}, u32[]{:S(2)}) %collective-permute-start.55) | collective-permute-done | bytes 626720 | tf_op jit(solution)/shard_map/ppermute | solution.py:806
  623.2 8.4 %all-to-all-done.2 = bf16[8,104,1152]{2,1,0:T(8,128)(2,1)} async-done(((bf16[8,104,1152]{2,1,0:T(8,128)(2,1)}), bf16[8,104,1152]{2,1,0:T(8,128)(2,1)}, u32[]{:S(2)}, u32[]{:S(2)}) %all-to-all-start.2) | async-done | bytes 1916960 | tf_op jit(solution)/shard_map/all_to_all | solution.py:1136
  652.7 8.3 %all-to-all-done.3 = bf16[8,48,1152]{2,1,0:T(8,128)(2,1)S(1)} async-done(((bf16[8,48,1152]{2,1,0:T(8,128)(2,1)}), bf16[8,48,1152]{2,1,0:T(8,128)(2,1)S(1)}, u32[]{:S(2)}, u32[]{:S(2)}) %all-to-all-start.3) | async-done | bytes 884768 | tf_op jit(solution)/shard_map/all_to_all | solution.py:1136
  (392 shorter events, 238.2 us)
Async XLA Ops:
  6.8 19.4 %collective-permute-start = (bf16[240,1152]{1,0:T(8,128)(2,1)}, bf16[240,1152]{1,0:T(8,128)(2,1)S(1)}, u32[]{:S(2)}, u32[]{:S(2)}) collective-permute-start(bf16[240,1152]{1,0:T(8,128)(2,1)} %fusion.27), channel_id=1, source_target_pairs={{0,2},{2,4},{4,6},{6,7},{7,5},{5,3},{3,1},{1,0},{8,10},{10,12},{12... | collective-permute-start | bytes 1658888 | tf_op jit(solution)/shard_map/ppermute | solution.py:825
  17.8 74.1 %all-to-all-start = ((bf16[8,112,1152]{2,1,0:T(8,128)(2,1)}), bf16[8,112,1152]{2,1,0:T(8,128)(2,1)}, u32[]{:S(2)}, u32[]{:S(2)}) async-start(bf16[8,112,1152]{2,1,0:T(8,128)(2,1)} %pad_maximum_fusion.4), calls=%async_computation | async-start | bytes 4128768 | tf_op jit(solution)/shard_map/all_to_all | solution.py:1136
  26.2 43.1 %collective-permute-start.2 = (bf16[240,1152]{1,0:T(8,128)(2,1)S(1)}, bf16[240,1152]{1,0:T(8,128)(2,1)}, u32[]{:S(2)}, u32[]{:S(2)}) collective-permute-start(bf16[240,1152]{1,0:T(8,128)(2,1)S(1)} %collective-permute-done), channel_id=1, source_target_pairs={{0,2},{2,4},{4,6},{6,7},{7,5},{5,3},{3,1},{1,0},{8,10},{10,12},{12... | collective-permute-start | bytes 1658888 | tf_op jit(solution)/shard_map/ppermute | solution.py:825
  28.3 41.1 %collective-permute-start.3 = (bf16[240,1152]{1,0:T(8,128)(2,1)S(1)}, bf16[240,1152]{1,0:T(8,128)(2,1)}, u32[]{:S(2)}, u32[]{:S(2)}) collective-permute-start(bf16[240,1152]{1,0:T(8,128)(2,1)S(1)} %collective-permute-done.1), channel_id=1, source_target_pairs={{2,0},{4,2},{6,4},{7,6},{5,7},{3,5},{1,3},{0,1},{10,8},{12,10},{14... | collective-permute-start | bytes 1658888 | tf_op jit(solution)/shard_map/ppermute | solution.py:828
  69.4 28.3 %collective-permute-start.5 = (bf16[240,1152]{1,0:T(8,128)(2,1)}, bf16[240,1152]{1,0:T(8,128)(2,1)S(1)}, u32[]{:S(2)}, u32[]{:S(2)}) collective-permute-start(bf16[240,1152]{1,0:T(8,128)(2,1)} %collective-permute-done.2), channel_id=1, source_target_pairs={{0,2},{2,4},{4,6},{6,7},{7,5},{5,3},{3,1},{1,0},{8,10},{10,12},{12... | collective-permute-start | bytes 1658888 | tf_op jit(solution)/shard_map/ppermute | solution.py:825
  126.6 21.4 %collective-permute-start.17 = (bf16[384,1152]{1,0:T(8,128)(2,1)}, bf16[384,1152]{1,0:T(8,128)(2,1)}, u32[]{:S(2)}, u32[]{:S(2)}) collective-permute-start(bf16[384,1152]{1,0:T(8,128)(2,1)} %constant_dynamic-slice_fusion.3), channel_id=1, source_target_pairs={{0,2},{2,4},{4,6},{6,7},{7,5},{5,3},{3,1},{1,0},{8,10},{10,12},{12... | collective-permute-start | bytes 2654216 | tf_op jit(solution)/shard_map/ppermute | solution.py:825
  130.9 20.8 %collective-permute-start.18 = (bf16[384,1152]{1,0:T(8,128)(2,1)}, bf16[384,1152]{1,0:T(8,128)(2,1)}, u32[]{:S(2)}, u32[]{:S(2)}) collective-permute-start(bf16[384,1152]{1,0:T(8,128)(2,1)} %constant_dynamic-slice_fusion.3), channel_id=1, source_target_pairs={{2,0},{4,2},{6,4},{7,6},{5,7},{3,5},{1,3},{0,1},{10,8},{12,10},{14... | collective-permute-start | bytes 2654216 | tf_op jit(solution)/shard_map/ppermute | solution.py:828
  154.2 20.7 %collective-permute-start.21 = (bf16[2,192,1152]{2,1,0:T(8,128)(2,1)S(1)}, bf16[2,192,1152]{2,1,0:T(8,128)(2,1)S(1)}, u32[]{:S(2)}, u32[]{:S(2)}) collective-permute-start(bf16[2,192,1152]{2,1,0:T(8,128)(2,1)S(1)} %pad_maximum_fusion.14), channel_id=1, source_target_pairs={{0,16},{8,24},{16,0},{24,8},{1,17},{9,25},{17,1},{25,9},{2,18},{10... | collective-permute-start | bytes 2654216 | tf_op jit(solution)/shard_map/ppermute | solution.py:806
  155.8 19.8 %collective-permute-start.19 = (bf16[384,1152]{1,0:T(8,128)(2,1)}, bf16[384,1152]{1,0:T(8,128)(2,1)S(1)}, u32[]{:S(2)}, u32[]{:S(2)}) collective-permute-start(bf16[384,1152]{1,0:T(8,128)(2,1)} %collective-permute-done.17), channel_id=1, source_target_pairs={{0,2},{2,4},{4,6},{6,7},{7,5},{5,3},{3,1},{1,0},{8,10},{10,12},{12... | collective-permute-start | bytes 2654216 | tf_op jit(solution)/shard_map/ppermute | solution.py:825
  157.2 19.1 %collective-permute-start.20 = (bf16[384,1152]{1,0:T(8,128)(2,1)}, bf16[384,1152]{1,0:T(8,128)(2,1)S(1)}, u32[]{:S(2)}, u32[]{:S(2)}) collective-permute-start(bf16[384,1152]{1,0:T(8,128)(2,1)} %collective-permute-done.18), channel_id=1, source_target_pairs={{2,0},{4,2},{6,4},{7,6},{5,7},{3,5},{1,3},{0,1},{10,8},{12,10},{14... | collective-permute-start | bytes 2654216 | tf_op jit(solution)/shard_map/ppermute | solution.py:828
  176.3 21.7 %collective-permute-start.22 = (bf16[384,1152]{1,0:T(8,128)(2,1)S(1)}, bf16[384,1152]{1,0:T(8,128)(2,1)S(1)}, u32[]{:S(2)}, u32[]{:S(2)}) collective-permute-start(bf16[384,1152]{1,0:T(8,128)(2,1)S(1)} %collective-permute-done.19), channel_id=1, source_target_pairs={{0,2},{2,4},{4,6},{6,7},{7,5},{5,3},{3,1},{1,0},{8,10},{10,12},{12... | collective-permute-start | bytes 2654216 | tf_op jit(solution)/shard_map/ppermute | solution.py:825
  177.9 20.2 %collective-permute-start.23 = (bf16[384,1152]{1,0:T(8,128)(2,1)S(1)}, bf16[384,1152]{1,0:T(8,128)(2,1)S(1)}, u32[]{:S(2)}, u32[]{:S(2)}) collective-permute-start(bf16[384,1152]{1,0:T(8,128)(2,1)S(1)} %collective-permute-done.20), channel_id=1, source_target_pairs={{2,0},{4,2},{6,4},{7,6},{5,7},{3,5},{1,3},{0,1},{10,8},{12,10},{14... | collective-permute-start | bytes 2654216 | tf_op jit(solution)/shard_map/ppermute | solution.py:828
  179.5 18.6 %collective-permute-start.24 = (bf16[2,192,1152]{2,1,0:T(8,128)(2,1)}, bf16[2,192,1152]{2,1,0:T(8,128)(2,1)}, u32[]{:S(2)}, u32[]{:S(2)}) collective-permute-start(bf16[2,192,1152]{2,1,0:T(8,128)(2,1)} %pad_maximum_fusion.15), channel_id=1, source_target_pairs={{0,16},{8,24},{16,0},{24,8},{1,17},{9,25},{17,1},{25,9},{2,18},{10... | collective-permute-start | bytes 2654216 | tf_op jit(solution)/shard_map/ppermute | solution.py:806
  198.1 25.1 %collective-permute-start.25 = (bf16[2,576,1152]{2,1,0:T(8,128)(2,1)}, bf16[2,576,1152]{2,1,0:T(8,128)(2,1)}, u32[]{:S(2)}, u32[]{:S(2)}) collective-permute-start(bf16[2,576,1152]{2,1,0:T(8,128)(2,1)} %pad_maximum_fusion), channel_id=1, source_target_pairs={{0,8},{8,0},{16,24},{24,16},{1,9},{9,1},{17,25},{25,17},{2,10},{10... | collective-permute-start | bytes 7962632 | tf_op jit(solution)/shard_map/ppermute | solution.py:795
  201.0 22.2 %collective-permute-start.28 = (bf16[2,192,1152]{2,1,0:T(8,128)(2,1)}, bf16[2,192,1152]{2,1,0:T(8,128)(2,1)}, u32[]{:S(2)}, u32[]{:S(2)}) collective-permute-start(bf16[2,192,1152]{2,1,0:T(8,128)(2,1)} %pad_maximum_fusion.16), channel_id=1, source_target_pairs={{0,16},{8,24},{16,0},{24,8},{1,17},{9,25},{17,1},{25,9},{2,18},{10... | collective-permute-start | bytes 2654216 | tf_op jit(solution)/shard_map/ppermute | solution.py:806
  202.5 19.8 %collective-permute-start.26 = (bf16[192,1152]{1,0:T(8,128)(2,1)}, bf16[192,1152]{1,0:T(8,128)(2,1)S(1)}, u32[]{:S(2)}, u32[]{:S(2)}) collective-permute-start(bf16[192,1152]{1,0:T(8,128)(2,1)} %get-tuple-element.480), channel_id=1, source_target_pairs={{0,2},{2,4},{4,6},{6,7},{7,5},{5,3},{3,1},{1,0},{8,10},{10,12},{12... | collective-permute-start | bytes 1327112 | tf_op jit(solution)/shard_map/ppermute | solution.py:825
  405.6 30.3 %collective-permute-start.37 = (bf16[576,1152]{1,0:T(8,128)(2,1)}, bf16[576,1152]{1,0:T(8,128)(2,1)S(1)}, u32[]{:S(2)}, u32[]{:S(2)}) collective-permute-start(bf16[576,1152]{1,0:T(8,128)(2,1)} %get-tuple-element.445), channel_id=1, source_target_pairs={{0,2},{2,4},{4,6},{6,7},{7,5},{5,3},{3,1},{1,0},{8,10},{10,12},{12... | collective-permute-start | bytes 3981320 | tf_op jit(solution)/shard_map/ppermute | solution.py:825
  407.3 30.1 %collective-permute-start.38 = (bf16[576,1152]{1,0:T(8,128)(2,1)S(1)}, bf16[576,1152]{1,0:T(8,128)(2,1)S(1)}, u32[]{:S(2)}, u32[]{:S(2)}) collective-permute-start(bf16[576,1152]{1,0:T(8,128)(2,1)S(1)} %get-tuple-element.444), channel_id=1, source_target_pairs={{2,0},{4,2},{6,4},{7,6},{5,7},{3,5},{1,3},{0,1},{10,8},{12,10},{14... | collective-permute-start | bytes 3981320 | tf_op jit(solution)/shard_map/ppermute | solution.py:828
  441.2 29.4 %collective-permute-start.39 = (bf16[576,1152]{1,0:T(8,128)(2,1)}, bf16[576,1152]{1,0:T(8,128)(2,1)S(1)}, u32[]{:S(2)}, u32[]{:S(2)}) collective-permute-start(bf16[576,1152]{1,0:T(8,128)(2,1)} %get-tuple-element.443), channel_id=1, source_target_pairs={{0,2},{2,4},{4,6},{6,7},{7,5},{5,3},{3,1},{1,0},{8,10},{10,12},{12... | collective-permute-start | bytes 3981320 | tf_op jit(solution)/shard_map/ppermute | solution.py:825
  442.7 28.8 %collective-permute-start.40 = (bf16[576,1152]{1,0:T(8,128)(2,1)}, bf16[576,1152]{1,0:T(8,128)(2,1)S(1)}, u32[]{:S(2)}, u32[]{:S(2)}) collective-permute-start(bf16[576,1152]{1,0:T(8,128)(2,1)} %get-tuple-element.442), channel_id=1, source_target_pairs={{2,0},{4,2},{6,4},{7,6},{5,7},{3,5},{1,3},{0,1},{10,8},{12,10},{14... | collective-permute-start | bytes 3981320 | tf_op jit(solution)/shard_map/ppermute | solution.py:828
  471.4 26.4 %collective-permute-start.41 = (bf16[8,288,1152]{2,1,0:T(8,128)(2,1)}, bf16[8,288,1152]{2,1,0:T(8,128)(2,1)}, u32[]{:S(2)}, u32[]{:S(2)}) collective-permute-start(bf16[8,288,1152]{2,1,0:T(8,128)(2,1)} %shard_map.321), channel_id=1, source_target_pairs={{0,8},{8,0},{16,24},{24,16},{1,9},{9,1},{17,25},{25,17},{2,10},{10... | collective-permute-start | bytes 15925256 | tf_op jit(solution)/shard_map/ppermute | solution.py:795
  478.0 171.3 %collective-permute-start.59 = (bf16[16,1152]{1,0:T(8,128)(2,1)}, bf16[16,1152]{1,0:T(8,128)(2,1)}, u32[]{:S(2)}, u32[]{:S(2)}) collective-permute-start(bf16[16,1152]{1,0:T(8,128)(2,1)} %pad_maximum_fusion.32), channel_id=1, source_target_pairs={{0,16},{8,24},{16,0},{24,8},{1,17},{9,25},{17,1},{25,9},{2,18},{10... | collective-permute-start | bytes 110600 | tf_op jit(solution)/shard_map/ppermute | solution.py:1040
  482.2 32.7 %collective-permute-start.43 = (bf16[576,1152]{1,0:T(8,128)(2,1)}, bf16[576,1152]{1,0:T(8,128)(2,1)S(1)}, u32[]{:S(2)}, u32[]{:S(2)}) collective-permute-start(bf16[576,1152]{1,0:T(8,128)(2,1)} %get-tuple-element.441), channel_id=1, source_target_pairs={{0,2},{2,4},{4,6},{6,7},{7,5},{5,3},{3,1},{1,0},{8,10},{10,12},{12... | collective-permute-start | bytes 3981320 | tf_op jit(solution)/shard_map/ppermute | solution.py:825
  483.2 33.6 %collective-permute-start.44 = (bf16[576,1152]{1,0:T(8,128)(2,1)}, bf16[576,1152]{1,0:T(8,128)(2,1)S(1)}, u32[]{:S(2)}, u32[]{:S(2)}) collective-permute-start(bf16[576,1152]{1,0:T(8,128)(2,1)} %get-tuple-element.440), channel_id=1, source_target_pairs={{2,0},{4,2},{6,4},{7,6},{5,7},{3,5},{1,3},{0,1},{10,8},{12,10},{14... | collective-permute-start | bytes 3981320 | tf_op jit(solution)/shard_map/ppermute | solution.py:828
  503.7 34.6 %collective-permute-start.47 = (bf16[2,96,1152]{2,1,0:T(8,128)(2,1)}, bf16[2,96,1152]{2,1,0:T(8,128)(2,1)}, u32[]{:S(2)}, u32[]{:S(2)}) collective-permute-start(bf16[2,96,1152]{2,1,0:T(8,128)(2,1)} %pad_maximum_fusion.27), channel_id=1, source_target_pairs={{0,16},{8,24},{16,0},{24,8},{1,17},{9,25},{17,1},{25,9},{2,18},{10... | collective-permute-start | bytes 1327112 | tf_op jit(solution)/shard_map/ppermute | solution.py:806
  514.9 41.8 %collective-permute-start.50 = (bf16[2,96,1152]{2,1,0:T(8,128)(2,1)S(1)}, bf16[2,96,1152]{2,1,0:T(8,128)(2,1)}, u32[]{:S(2)}, u32[]{:S(2)}) collective-permute-start(bf16[2,96,1152]{2,1,0:T(8,128)(2,1)S(1)} %pad_maximum_fusion.28), channel_id=1, source_target_pairs={{0,16},{8,24},{16,0},{24,8},{1,17},{9,25},{17,1},{25,9},{2,18},{10... | collective-permute-start | bytes 1327112 | tf_op jit(solution)/shard_map/ppermute | solution.py:806
  538.3 35.4 %collective-permute-start.53 = (bf16[1,96,1152]{2,1,0:T(8,128)(2,1)}, bf16[1,96,1152]{2,1,0:T(8,128)(2,1)}, u32[]{:S(2)}, u32[]{:S(2)}) collective-permute-start(bf16[1,96,1152]{2,1,0:T(8,128)(2,1)} %get-tuple-element.428), channel_id=1, source_target_pairs={{0,16},{8,24},{16,0},{24,8},{1,17},{9,25},{17,1},{25,9},{2,18},{10... | collective-permute-start | bytes 663560 | tf_op jit(solution)/shard_map/ppermute | solution.py:806
  556.8 30.6 %collective-permute-start.66 = (bf16[576,1152]{1,0:T(8,128)(2,1)S(1)}, bf16[576,1152]{1,0:T(8,128)(2,1)}, u32[]{:S(2)}, u32[]{:S(2)}) collective-permute-start(bf16[576,1152]{1,0:T(8,128)(2,1)S(1)} %fusion.1), channel_id=1, source_target_pairs={{0,16},{8,24},{16,0},{24,8},{1,17},{9,25},{17,1},{25,9},{2,18},{10... | collective-permute-start | bytes 3981320 | tf_op jit(solution)/shard_map/ppermute | solution.py:806
  581.9 21.8 %collective-permute-start.54 = (bf16[528,1152]{1,0:T(8,128)(2,1)S(1)}, bf16[528,1152]{1,0:T(8,128)(2,1)}, u32[]{:S(2)}, u32[]{:S(2)}) collective-permute-start(bf16[528,1152]{1,0:T(8,128)(2,1)S(1)} %pad_maximum_fusion.6), channel_id=1, source_target_pairs={{0,8},{8,0},{16,24},{24,16},{1,9},{9,1},{17,25},{25,17},{2,10},{10... | collective-permute-start | bytes 3649544 | tf_op jit(solution)/shard_map/ppermute | solution.py:795
  582.0 49.7 %all-to-all-start.2 = ((bf16[8,104,1152]{2,1,0:T(8,128)(2,1)}), bf16[8,104,1152]{2,1,0:T(8,128)(2,1)}, u32[]{:S(2)}, u32[]{:S(2)}) async-start(bf16[8,104,1152]{2,1,0:T(8,128)(2,1)} %get-tuple-element.414), calls=%async_computation.2 | async-start | bytes 3833856 | tf_op jit(solution)/shard_map/all_to_all | solution.py:1136
  589.0 22.1 %collective-permute-start.67 = (bf16[4,144,1152]{2,1,0:T(8,128)(2,1)S(1)}, bf16[4,144,1152]{2,1,0:T(8,128)(2,1)S(1)}, u32[]{:S(2)}, u32[]{:S(2)}) collective-permute-start(bf16[4,144,1152]{2,1,0:T(8,128)(2,1)S(1)} %bitcast.268), channel_id=1, source_target_pairs={{0,8},{8,0},{16,24},{24,16},{1,9},{9,1},{17,25},{25,17},{2,10},{10... | collective-permute-start | bytes 3981320 | tf_op jit(solution)/shard_map/ppermute | solution.py:795
  634.3 26.7 %all-to-all-start.3 = ((bf16[8,48,1152]{2,1,0:T(8,128)(2,1)}), bf16[8,48,1152]{2,1,0:T(8,128)(2,1)S(1)}, u32[]{:S(2)}, u32[]{:S(2)}) async-start(bf16[8,48,1152]{2,1,0:T(8,128)(2,1)} %pad_maximum_fusion.17), calls=%async_computation.3 | async-start | bytes 1769472 | tf_op jit(solution)/shard_map/all_to_all | solution.py:1136
  (94 other events, 1174.7 us)

commit v7 on v6

--- a/solution.py
+++ b/solution.py
@@ -833,8 +833,8 @@
 
 
 class Gather:
-    def __init__(self, ring, mine, other, part, middle):
-        self.ring, self.part, self.middle = ring, part, middle
+    def __init__(self, ring, mine, other, part, middle, early=False):
+        self.ring, self.part, self.middle, self.early = ring, part, middle, early
         self.mine, self.other = [(mine[None], "all", [0])], [(other[None], "all", [0])]
         payload = lax.dynamic_slice_in_dim(mine, part * ring.x_bit, part + middle, 0)
         self.pieces = [payload, payload]
@@ -847,11 +847,12 @@
         middle, half = self.middle, ring.size // 2
         if self.distance == half:
             self.ready, self.making = self.ready + self.making, []
-        flight["pair"] = [array for array, _ in self.making]
-        self.made = [places for _, places in self.making]
+        flight["pair"] = [entry[0] for entry in self.making]
+        self.made = [entry[1:] for entry in self.making]
         self.making = []
-        flight["core"] = [swap_core(array) for array, _ in self.ready]
-        self.sent = [places for _, places in self.ready]
+        flight["core"] = [swap_core(entry[0]) for entry in self.ready]
+        self.sent = [entry[1:] for entry in self.ready]
+        self.ready = []
         if self.distance < half:
             self.distance += 1
             ahead, behind = self.pieces
@@ -864,24 +865,29 @@
 
     def land(self, flight):
         bit, part, middle = self.ring.x_bit, self.part, self.middle
-        self.other += [(array, "pair", places) for array, places in zip(flight["core"], self.sent)]
-        self.ready = list(zip(flight["pair"], self.made))
+        self.other += [(array,) + entry for array, entry in zip(flight["core"], self.sent)]
+        self.ready = [(array,) + entry for array, entry in zip(flight["pair"], self.made)]
         self.own = None
         if "x" in flight:
             got = flight["x"]
             self.mine.append((got, "got", self.places))
             if len(self.places) == 1:
-                ahead, behind = self.pieces
-                pair = jnp.concatenate([ahead, behind, got[0]])[None]
+                if self.early:
+                    self.making = [(got, "got", self.places)]
+                else:
+                    pair = jnp.concatenate(self.pieces + [got[0]])[None]
+                    self.making = [(pair, "pair", self.places)]
             else:
                 pair = jnp.concatenate([jnp.stack(self.pieces), got], axis=1)
-            self.making = [(pair, self.places)]
+                self.making = [(pair, "pair", self.places)]
         if "ring" in flight:
             ahead, behind = self.pieces = flight["ring"]
             place = 2 * self.distance - 1
             if self.distance == self.ring.size // 2:
                 self.places = [place]
                 self.mine += [(ahead[None], "first", [place]), (behind[None], "second", [place])]
+                if self.early:
+                    self.ready.append((jnp.concatenate([ahead, behind])[None], "piece", [place]))
                 self.own = jnp.where(bit == 0, ahead[:part], behind)[None]
             else:
                 self.places = [place, place + 1]
@@ -1200,7 +1206,7 @@
             gather.issue(), condition_group, arrived, small, mine, other, modulation_low
         )
         gather.land(flight)
-        feed_gather = Gather(ring, mine, other, *feed_cut)
+        feed_gather = Gather(ring, mine, other, *feed_cut, early=True)
         flight, condition_group = sync(gather.issue(), condition_group)
         gather.land(flight)
     mod = modulate_all(condition_group, modulation_low)

time: 673 us -> 671 us (level)
  transfers between devices with their start and end apart: 72 -> 73, of which waited for: 28 -> 28; matrix products, arithmetic and copies ran while one was open for 15% -> 15% of each run, Pallas kernels for 33% -> 33%
where the time goes in v7:
time: 671 us; the launch traced here: 667 us
  Pallas kernels  332 us (49%)
  waiting for transfers between devices  108 us (16%)
  starting transfers between devices  97.1 us (14%)
  other arithmetic  90.5 us (13%)
  local copies, waits for them, and re-layouts  32.5 us (5%)
    pallas_call x1, Pallas kernels, feed_call(): pl.pallas_call(functools.partial(feed_kernel, source=source), grid=(steps...  83.2 us
    pallas_call x3, Pallas kernels, attend_back_call(): pl.pallas_call(functools.partial(attend_back_kernel, factor=1.0 / math.sq...  50.2 us
    pallas_call x4, Pallas kernels, start_back_call(): pl.pallas_call(functools.partial(start_back_kernel, chunks=chunks, first=...  45.4 us
    pallas_call x4, Pallas kernels, feed_weight_call(): pl.pallas_call(feed_weight_kernel, grid_spec=pltpu.PrefetchScalarGridSpec...  43.5 us
    ppermute x16, waiting for transfers between devices, forward(): return lax.ppermute(values, 'tok', self.ahead)  38.1 us
    ppermute x16, starting transfers between devices, forward(): return lax.ppermute(values, 'tok', self.ahead)  35.9 us
    ppermute x16, waiting for transfers between devices, swap_x(): return lax.ppermute(values, 'grp', swap_pairs(lax.axis_size('grp'), 2))  33.7 us
    pallas_call x2, Pallas kernels, attend_call(): pl.pallas_call(functools.partial(attend_kernel, factor=math.log2(math.e)...  29.8 us
  transfers between devices with their start and end apart: 73, of which 28 were waited for; matrix products, arithmetic and copies ran while one was open for 15% of the time, Pallas kernels for 33%

profile of v7, /device:TPU:0, one launch (start us, length us, event | category | flops | bytes accessed | tf_op | source)
XLA Modules:
  0.0 666.7 jit_solution(1001787459713913370)
XLA Ops:
  17.8 6.5 all-to-all-start
  46.0 23.3 %collective-permute-done.2 = bf16[240,1152]{1,0:T(8,128)(2,1)} collective-permute-done((bf16[240,1152]{1,0:T(8,128)(2,1)S(1)}, bf16[240,1152]{1,0:T(8,128)(2,1)}, u32[]{:S(2)}, u32[]{:S(2)}) %collective-permute-start.2) | collective-permute-done | bytes 552992 | tf_op jit(solution)/shard_map/ppermute | solution.py:825
  69.4 14.4 %collective-permute-start.5 = (bf16[240,1152]{1,0:T(8,128)(2,1)}, bf16[240,1152]{1,0:T(8,128)(2,1)S(1)}, u32[]{:S(2)}, u32[]{:S(2)}) collective-permute-start(bf16[240,1152]{1,0:T(8,128)(2,1)} %collective-permute-done.2), channel_id=1, source_target_pairs={{0,2},{2,4},{4,6},{6,7},{7,5},{5,3},{3,1},{1,0},{8,10},{10,12},{12... | collective-permute-start | bytes 1658888 | tf_op jit(solution)/shard_map/ppermute | solution.py:825
  117.2 5.6 all-to-all-start.1
  135.4 8.4 %shard_map.307 = (f32[1024,1152]{1,0:T(8,128)}, bf16[1024,1152]{1,0:T(8,128)(2,1)}) custom-call(s32[2]{0:T(128)} %pad_add_fusion.core_ref, s32[8]{0:T(128)} %compare_select_fusion.2.places_ref, s32[1]{0:T(128)S(6)} %copy.72.count_ref, s32[1,768]{1,0:T(1,128)} %index_row_ref.7, bf16[8,112,1152]{2,1,0:T(8,128)(2,1)} %all-to-all-done.kept_ref, ...), custom_call_target="tpu_custom_call" | custom-call | flops 1811939328 | bytes 16515072 | tf_op jit(solution)/shard_map/pallas_call | solution.py:106
  143.8 4.1 collective-permute-done.17
  158.1 16.8 %shard_map.308.query_ref.key_ref.value_ref = bf16[3,16,1024,128]{3,2,1,0:T(8,128)(2,1)} custom-call(s32[2]{0:T(128)} %pad_add_fusion.core_ref, s32[8]{0:T(128)} %compare_select_fusion.2.places_ref, bf16[1024,1152]{1,0:T(8,128)(2,1)} %get-tuple-element.331.norm_ref, f32[16,1152]{1,0:T(8,128)} %convert_reduce_fusion.1.small_ref, ...), custom_call_target="tpu_custom_call" | custom-call | flops 8153726976 | bytes 22118400 | tf_op jit(solution)/shard_map/pallas_call | solution.py:235
  183.1 14.9 %shard_map.309 = (bf16[16,1024,128]{2,1,0:T(8,128)(2,1)}, f32[16,1,1024]{2,1,0:T(1,128)}) custom-call(bf16[3,16,1024,128]{3,2,1,0:T(8,128)(2,1)} %shard_map.308.query_ref.key_ref.value_ref, bf16[3,16,1024,128]{3,2,1,0:T(8,128)(2,1)} %shard_map.308.query_ref.key_ref.value_ref, bf16[3,16,1024,128]{3,2,1,0:T(8,128)(2,1)} %shard_map.308.query_ref.key_ref.value_ref), custom_call_target="tpu_custom_call" | custom-call | flops 8589934592 | bytes 8388608 | tf_op jit(solution)/shard_map/pallas_call | solution.py:287
  204.5 14.9 %shard_map.310 = (bf16[16,1024,128]{2,1,0:T(8,128)(2,1)}, f32[16,1,1024]{2,1,0:T(1,128)}) custom-call(bf16[3,16,1024,128]{3,2,1,0:T(8,128)(2,1)} %shard_map.308.query_ref.key_ref.value_ref, bf16[3,16,1024,128]{3,2,1,0:T(8,128)(2,1)} %shard_map.308.query_ref.key_ref.value_ref, ...), custom_call_target="tpu_custom_call", output_to_operand_aliasing={{0}: (3, {}), {1}: (4, {})} | custom-call | flops 8589934592 | bytes 8388608 | tf_op jit(solution)/shard_map/pallas_call | solution.py:287
  230.4 11.7 %shard_map.311 = (bf16[1024,1152]{1,0:T(8,128)(2,1)}, bf16[1024,1152]{1,0:T(8,128)(2,1)}, f32[1024,1152]{1,0:T(8,128)}, bf16[1024,1152]{1,0:T(8,128)(2,1)}) custom-call(s32[2]{0:T(128)} %pad_add_fusion.core_ref, s32[8]{0:T(128)} %compare_select_fusion.2.places_ref, f32[1024,1152]{1,0:T(8,128)} %get-tuple-element.276.start_ref, ...), custom_call_target="tpu_custom_call" | custom-call | flops 2717908992 | bytes 21233664 | tf_op jit(solution)/shard_map/pallas_call | solution.py:375
  244.8 83.2 %shard_map.312 = (f32[1024,1152]{1,0:T(8,128)}, bf16[4,1024,1152]{2,1,0:T(8,128)(2,1)}, bf16[4,1024,1152]{2,1,0:T(8,128)(2,1)}, bf16[1024,1152]{1,0:T(8,128)(2,1...) custom-call(s32[2]{0:T(128)} %pad_add_fusion.core_ref, ...), custom_call_target="tpu_custom_call" | custom-call | flops 43486543872 | bytes 70778880 | tf_op jit(solution)/shard_map/pallas_call | solution.py:471
  328.0 10.4 %shard_map.313 = bf16[8,288,1152]{2,1,0:T(8,128)(2,1)} custom-call(s32[1]{0:T(128)S(6)} %sub.88.first_ref, bf16[1024,1152]{1,0:T(8,128)(2,1)} %get-tuple-element.296.norm_ref.left_ref, bf16[4,1024,1152]{2,1,0:T(8,128)(2,1)} %get-tuple-element.289.right_ref), custom_call_target="tpu_custom_call" | custom-call | flops 5435817984 | bytes 14745600 | tf_op jit(solution)/shard_map/pallas_call | solution.py:542
  338.7 10.4 %shard_map.314 = bf16[8,288,1152]{2,1,0:T(8,128)(2,1)} custom-call(s32[1]{0:T(128)S(6)} %sub.88.first_ref, bf16[4,1024,1152]{2,1,0:T(8,128)(2,1)} %get-tuple-element.298.left_ref, bf16[1024,1152]{1,0:T(8,128)(2,1)} %get-tuple-element.294.right_ref), custom_call_target="tpu_custom_call" | custom-call | flops 5435817984 | bytes 14745600 | tf_op jit(solution)/shard_map/pallas_call | solution.py:542
  349.4 11.3 %shard_map.315.rest_1_ = bf16[8,576,1152]{2,1,0:T(8,128)(2,1)} custom-call(s32[1]{0:T(128)S(6)} %mul.77.first_ref, bf16[1024,1152]{1,0:T(8,128)(2,1)} %get-tuple-element.296.norm_ref.left_ref, bf16[4,1024,1152]{2,1,0:T(8,128)(2,1)} %get-tuple-element.289.right_ref, bf16[8,288,1152]{2,1,0:T(8,128)(2,1)} %collective-permute-done.34.rest_0_), custom_call_target="tpu_custom_call" | custom-call | flops 5435817984 | bytes 14745600 | tf_op jit(solution)/shard_map/pallas_call | solution.py:542
  360.8 11.3 %shard_map.316 = bf16[8,576,1152]{2,1,0:T(8,128)(2,1)} custom-call(s32[1]{0:T(128)S(6)} %mul.77.first_ref, bf16[4,1024,1152]{2,1,0:T(8,128)(2,1)} %get-tuple-element.298.left_ref, bf16[1024,1152]{1,0:T(8,128)(2,1)} %get-tuple-element.294.right_ref, bf16[8,288,1152]{2,1,0:T(8,128)(2,1)} %collective-permute-done.35.rest_0_, ...), custom_call_target="tpu_custom_call", output_to_operand_aliasing={{}: (4, {})} | custom-call | flops 5435817984 | bytes 14745600 | tf_op jit(solution)/shard_map/pallas_call | solution.py:542
  372.1 8.7 %shard_map.317.grad_ref = bf16[16,1024,128]{2,1,0:T(8,128)(2,1)} custom-call(s32[2]{0:T(128)} %pad_add_fusion.core_ref, s32[8]{0:T(128)} %compare_select_fusion.2.places_ref, bf16[1024,1152]{1,0:T(8,128)(2,1)} %get-tuple-element.305.grad_ref, bf16[1,352,1152]{2,1,0:T(8,128)(2,1)} %copy-done.2, bf16[1,240,1152]{2,1,0:T(8,128)(2,1)} %bitcast.238, ...), custom_call_target="tpu_custom_call" | custom-call | flops 2717908992 | bytes 9437184 | tf_op jit(solution)/shard_map/pallas_call | solution.py:633
  384.3 13.4 %shard_map.318 = (bf16[4,1024,128]{2,1,0:T(8,128)(2,1)}, bf16[4,1024,128]{2,1,0:T(8,128)(2,1)}, bf16[4,1024,128]{2,1,0:T(8,128)(2,1)}) custom-call(bf16[3,16,1024,128]{3,2,1,0:T(8,128)(2,1)} %shard_map.308.query_ref.key_ref.value_ref, bf16[3,16,1024,128]{3,2,1,0:T(8,128)(2,1)} %shard_map.308.query_ref.key_ref.value_ref, ...), custom_call_target="tpu_custom_call" | custom-call | flops 10737418240 | bytes 8388608 | tf_op jit(solution)/shard_map/pallas_call | solution.py:329
  405.6 23.5 %shard_map.319 = (bf16[8,1024,128]{2,1,0:T(8,128)(2,1)}, bf16[8,1024,128]{2,1,0:T(8,128)(2,1)}, bf16[8,1024,128]{2,1,0:T(8,128)(2,1)}) custom-call(bf16[3,16,1024,128]{3,2,1,0:T(8,128)(2,1)} %shard_map.308.query_ref.key_ref.value_ref, bf16[3,16,1024,128]{3,2,1,0:T(8,128)(2,1)} %shard_map.308.query_ref.key_ref.value_ref, ...), custom_call_target="tpu_custom_call" | custom-call | flops 21474836480 | bytes 16777216 | tf_op jit(solution)/shard_map/pallas_call | solution.py:329
  429.1 4.8 collective-permute-done.38
  441.3 13.3 %shard_map.320 = (bf16[4,1024,128]{2,1,0:T(8,128)(2,1)}, bf16[4,1024,128]{2,1,0:T(8,128)(2,1)}, bf16[4,1024,128]{2,1,0:T(8,128)(2,1)}) custom-call(bf16[3,16,1024,128]{3,2,1,0:T(8,128)(2,1)} %shard_map.308.query_ref.key_ref.value_ref, bf16[3,16,1024,128]{3,2,1,0:T(8,128)(2,1)} %shard_map.308.query_ref.key_ref.value_ref, ...), custom_call_target="tpu_custom_call" | custom-call | flops 10737418240 | bytes 8388608 | tf_op jit(solution)/shard_map/pallas_call | solution.py:329
  454.6 12.1 %shard_map.321 = bf16[8,288,1152]{2,1,0:T(8,128)(2,1)} custom-call(s32[1]{0:T(128)S(6)} %sub.94.owner_ref, bf16[1024,1152]{1,0:T(8,128)(2,1)} %get-tuple-element.331.norm_ref, bf16[1024,1152]{1,0:T(8,128)(2,1)} %get-tuple-element.320.joined_ref, bf16[1024,1152]{1,0:T(8,128)(2,1)} %get-tuple-element.305.grad_ref, ...), custom_call_target="tpu_custom_call" | custom-call | flops 5435817984 | bytes 17104896 | tf_op jit(solution)/shard_map/pallas_call | solution.py:599
  471.0 4.5 collective-permute-done.59
  482.7 13.6 %shard_map.322 = bf16[8,288,1152]{2,1,0:T(8,128)(2,1)} custom-call(s32[1]{0:T(128)} %bitcast.owner_ref, bf16[1024,1152]{1,0:T(8,128)(2,1)} %get-tuple-element.331.norm_ref, bf16[1024,1152]{1,0:T(8,128)(2,1)} %get-tuple-element.320.joined_ref, bf16[1024,1152]{1,0:T(8,128)(2,1)} %get-tuple-element.305.grad_ref, ...), custom_call_target="tpu_custom_call" | custom-call | flops 5435817984 | bytes 17104896 | tf_op jit(solution)/shard_map/pallas_call | solution.py:599
  502.6 10.8 %shard_map.323 = (bf16[256,1152]{1,0:T(8,128)(2,1)}, bf16[8,104,1152]{2,1,0:T(8,128)(2,1)}, f32[8,1152]{1,0:T(8,128)}) custom-call(s32[2]{0:T(128)} %pad_add_fusion.core_ref, s32[8]{0:T(128)} %compare_select_fusion.2.places_ref, s32[1]{0:T(128)S(6)} %copy.72.count_ref, s32[1,768]{1,0:T(1,128)} %index_row_ref.7, s32[768,1]{1,0:T(8,128)} %copy.48.index_ref, ...), custom_call_target="tpu_custom_call" | custom-call | flops 2717908992 | bytes 8257536 | tf_op jit(solution)/shard_map/pallas_call | solution.py:706
  525.2 11.5 %shard_map.324 = (bf16[256,1152]{1,0:T(8,128)(2,1)}, bf16[8,104,1152]{2,1,0:T(8,128)(2,1)}, f32[8,1152]{1,0:T(8,128)}) custom-call(s32[2]{0:T(128)} %pad_add_fusion.core_ref, s32[8]{0:T(128)} %compare_select_fusion.2.places_ref, s32[1]{0:T(128)S(6)} %copy.72.count_ref, s32[1,768]{1,0:T(1,128)} %index_row_ref.7, s32[768,1]{1,0:T(8,128)} %copy.48.index_ref, ...), custom_call_target="tpu_custom_call" | custom-call | flops 2717908992 | bytes 8257536 | tf_op jit(solution)/shard_map/pallas_call | solution.py:706
  542.3 11.5 %shard_map.325 = (bf16[256,1152]{1,0:T(8,128)(2,1)}, bf16[8,104,1152]{2,1,0:T(8,128)(2,1)}, f32[8,1152]{1,0:T(8,128)}) custom-call(s32[2]{0:T(128)} %pad_add_fusion.core_ref, s32[8]{0:T(128)} %compare_select_fusion.2.places_ref, s32[1]{0:T(128)S(6)} %copy.72.count_ref, s32[1,768]{1,0:T(1,128)} %index_row_ref.7, s32[768,1]{1,0:T(8,128)} %copy.48.index_ref, ...), custom_call_target="tpu_custom_call" | custom-call | flops 2717908992 | bytes 8257536 | tf_op jit(solution)/shard_map/pallas_call | solution.py:706
  560.7 11.5 %shard_map.326 = (bf16[256,1152]{1,0:T(8,128)(2,1)}, bf16[8,104,1152]{2,1,0:T(8,128)(2,1)}, f32[8,1152]{1,0:T(8,128)}) custom-call(s32[2]{0:T(128)} %pad_add_fusion.core_ref, s32[8]{0:T(128)} %compare_select_fusion.2.places_ref, s32[1]{0:T(128)S(6)} %copy.72.count_ref, s32[1,768]{1,0:T(1,128)} %index_row_ref.7, s32[768,1]{1,0:T(8,128)} %copy.48.index_ref, ...), custom_call_target="tpu_custom_call" | custom-call | flops 2717908992 | bytes 8257536 | tf_op jit(solution)/shard_map/pallas_call | solution.py:706
  580.5 4.4 all-to-all-start.2
  592.1 9.7 %collective-permute-done.65 = bf16[192,1152]{1,0:T(8,128)(2,1)S(1)} collective-permute-done((bf16[192,1152]{1,0:T(8,128)(2,1)S(1)}, bf16[192,1152]{1,0:T(8,128)(2,1)S(1)}, u32[]{:S(2)}, u32[]{:S(2)}) %collective-permute-start.65) | collective-permute-done | bytes 442400 | tf_op jit(solution)/shard_map/ppermute | solution.py:806
  610.3 10.3 %collective-permute-done.56 = bf16[272,1152]{1,0:T(8,128)(2,1)S(1)} collective-permute-done((bf16[272,1152]{1,0:T(8,128)(2,1)S(1)}, bf16[272,1152]{1,0:T(8,128)(2,1)S(1)}, u32[]{:S(2)}, u32[]{:S(2)}) %collective-permute-start.56) | collective-permute-done | bytes 626720 | tf_op jit(solution)/shard_map/ppermute | solution.py:806
  621.7 8.5 %all-to-all-done.2 = bf16[8,104,1152]{2,1,0:T(8,128)(2,1)} async-done(((bf16[8,104,1152]{2,1,0:T(8,128)(2,1)}), bf16[8,104,1152]{2,1,0:T(8,128)(2,1)}, u32[]{:S(2)}, u32[]{:S(2)}) %all-to-all-start.2) | async-done | bytes 1916960 | tf_op jit(solution)/shard_map/all_to_all | solution.py:1142
  650.9 8.6 %all-to-all-done.3 = bf16[8,48,1152]{2,1,0:T(8,128)(2,1)S(1)} async-done(((bf16[8,48,1152]{2,1,0:T(8,128)(2,1)}), bf16[8,48,1152]{2,1,0:T(8,128)(2,1)S(1)}, u32[]{:S(2)}, u32[]{:S(2)}) %all-to-all-start.3) | async-done | bytes 884768 | tf_op jit(solution)/shard_map/all_to_all | solution.py:1142
  (394 shorter events, 235.8 us)
Async XLA Ops:
  6.8 19.4 %collective-permute-start = (bf16[240,1152]{1,0:T(8,128)(2,1)}, bf16[240,1152]{1,0:T(8,128)(2,1)S(1)}, u32[]{:S(2)}, u32[]{:S(2)}) collective-permute-start(bf16[240,1152]{1,0:T(8,128)(2,1)} %fusion.27), channel_id=1, source_target_pairs={{0,2},{2,4},{4,6},{6,7},{7,5},{5,3},{3,1},{1,0},{8,10},{10,12},{12... | collective-permute-start | bytes 1658888 | tf_op jit(solution)/shard_map/ppermute | solution.py:825
  17.8 74.1 %all-to-all-start = ((bf16[8,112,1152]{2,1,0:T(8,128)(2,1)}), bf16[8,112,1152]{2,1,0:T(8,128)(2,1)}, u32[]{:S(2)}, u32[]{:S(2)}) async-start(bf16[8,112,1152]{2,1,0:T(8,128)(2,1)} %pad_maximum_fusion.4), calls=%async_computation | async-start | bytes 4128768 | tf_op jit(solution)/shard_map/all_to_all | solution.py:1142
  26.3 43.1 %collective-permute-start.2 = (bf16[240,1152]{1,0:T(8,128)(2,1)S(1)}, bf16[240,1152]{1,0:T(8,128)(2,1)}, u32[]{:S(2)}, u32[]{:S(2)}) collective-permute-start(bf16[240,1152]{1,0:T(8,128)(2,1)S(1)} %collective-permute-done), channel_id=1, source_target_pairs={{0,2},{2,4},{4,6},{6,7},{7,5},{5,3},{3,1},{1,0},{8,10},{10,12},{12... | collective-permute-start | bytes 1658888 | tf_op jit(solution)/shard_map/ppermute | solution.py:825
  28.4 41.0 %collective-permute-start.3 = (bf16[240,1152]{1,0:T(8,128)(2,1)S(1)}, bf16[240,1152]{1,0:T(8,128)(2,1)}, u32[]{:S(2)}, u32[]{:S(2)}) collective-permute-start(bf16[240,1152]{1,0:T(8,128)(2,1)S(1)} %collective-permute-done.1), channel_id=1, source_target_pairs={{2,0},{4,2},{6,4},{7,6},{5,7},{3,5},{1,3},{0,1},{10,8},{12,10},{14... | collective-permute-start | bytes 1658888 | tf_op jit(solution)/shard_map/ppermute | solution.py:828
  69.4 28.3 %collective-permute-start.5 = (bf16[240,1152]{1,0:T(8,128)(2,1)}, bf16[240,1152]{1,0:T(8,128)(2,1)S(1)}, u32[]{:S(2)}, u32[]{:S(2)}) collective-permute-start(bf16[240,1152]{1,0:T(8,128)(2,1)} %collective-permute-done.2), channel_id=1, source_target_pairs={{0,2},{2,4},{4,6},{6,7},{7,5},{5,3},{3,1},{1,0},{8,10},{10,12},{12... | collective-permute-start | bytes 1658888 | tf_op jit(solution)/shard_map/ppermute | solution.py:825
  126.6 21.4 %collective-permute-start.17 = (bf16[384,1152]{1,0:T(8,128)(2,1)}, bf16[384,1152]{1,0:T(8,128)(2,1)}, u32[]{:S(2)}, u32[]{:S(2)}) collective-permute-start(bf16[384,1152]{1,0:T(8,128)(2,1)} %constant_dynamic-slice_fusion.3), channel_id=1, source_target_pairs={{0,2},{2,4},{4,6},{6,7},{7,5},{5,3},{3,1},{1,0},{8,10},{10,12},{12... | collective-permute-start | bytes 2654216 | tf_op jit(solution)/shard_map/ppermute | solution.py:825
  130.8 20.8 %collective-permute-start.18 = (bf16[384,1152]{1,0:T(8,128)(2,1)}, bf16[384,1152]{1,0:T(8,128)(2,1)}, u32[]{:S(2)}, u32[]{:S(2)}) collective-permute-start(bf16[384,1152]{1,0:T(8,128)(2,1)} %constant_dynamic-slice_fusion.3), channel_id=1, source_target_pairs={{2,0},{4,2},{6,4},{7,6},{5,7},{3,5},{1,3},{0,1},{10,8},{12,10},{14... | collective-permute-start | bytes 2654216 | tf_op jit(solution)/shard_map/ppermute | solution.py:828
  154.1 20.8 %collective-permute-start.21 = (bf16[2,192,1152]{2,1,0:T(8,128)(2,1)S(1)}, bf16[2,192,1152]{2,1,0:T(8,128)(2,1)S(1)}, u32[]{:S(2)}, u32[]{:S(2)}) collective-permute-start(bf16[2,192,1152]{2,1,0:T(8,128)(2,1)S(1)} %pad_maximum_fusion.14), channel_id=1, source_target_pairs={{0,16},{8,24},{16,0},{24,8},{1,17},{9,25},{17,1},{25,9},{2,18},{10... | collective-permute-start | bytes 2654216 | tf_op jit(solution)/shard_map/ppermute | solution.py:806
  155.8 19.8 %collective-permute-start.19 = (bf16[384,1152]{1,0:T(8,128)(2,1)}, bf16[384,1152]{1,0:T(8,128)(2,1)S(1)}, u32[]{:S(2)}, u32[]{:S(2)}) collective-permute-start(bf16[384,1152]{1,0:T(8,128)(2,1)} %collective-permute-done.17), channel_id=1, source_target_pairs={{0,2},{2,4},{4,6},{6,7},{7,5},{5,3},{3,1},{1,0},{8,10},{10,12},{12... | collective-permute-start | bytes 2654216 | tf_op jit(solution)/shard_map/ppermute | solution.py:825
  157.1 19.1 %collective-permute-start.20 = (bf16[384,1152]{1,0:T(8,128)(2,1)}, bf16[384,1152]{1,0:T(8,128)(2,1)S(1)}, u32[]{:S(2)}, u32[]{:S(2)}) collective-permute-start(bf16[384,1152]{1,0:T(8,128)(2,1)} %collective-permute-done.18), channel_id=1, source_target_pairs={{2,0},{4,2},{6,4},{7,6},{5,7},{3,5},{1,3},{0,1},{10,8},{12,10},{14... | collective-permute-start | bytes 2654216 | tf_op jit(solution)/shard_map/ppermute | solution.py:828
  176.3 21.7 %collective-permute-start.22 = (bf16[384,1152]{1,0:T(8,128)(2,1)S(1)}, bf16[384,1152]{1,0:T(8,128)(2,1)S(1)}, u32[]{:S(2)}, u32[]{:S(2)}) collective-permute-start(bf16[384,1152]{1,0:T(8,128)(2,1)S(1)} %collective-permute-done.19), channel_id=1, source_target_pairs={{0,2},{2,4},{4,6},{6,7},{7,5},{5,3},{3,1},{1,0},{8,10},{10,12},{12... | collective-permute-start | bytes 2654216 | tf_op jit(solution)/shard_map/ppermute | solution.py:825
  177.8 20.2 %collective-permute-start.23 = (bf16[384,1152]{1,0:T(8,128)(2,1)S(1)}, bf16[384,1152]{1,0:T(8,128)(2,1)S(1)}, u32[]{:S(2)}, u32[]{:S(2)}) collective-permute-start(bf16[384,1152]{1,0:T(8,128)(2,1)S(1)} %collective-permute-done.20), channel_id=1, source_target_pairs={{2,0},{4,2},{6,4},{7,6},{5,7},{3,5},{1,3},{0,1},{10,8},{12,10},{14... | collective-permute-start | bytes 2654216 | tf_op jit(solution)/shard_map/ppermute | solution.py:828
  179.5 18.6 %collective-permute-start.24 = (bf16[2,192,1152]{2,1,0:T(8,128)(2,1)}, bf16[2,192,1152]{2,1,0:T(8,128)(2,1)}, u32[]{:S(2)}, u32[]{:S(2)}) collective-permute-start(bf16[2,192,1152]{2,1,0:T(8,128)(2,1)} %pad_maximum_fusion.15), channel_id=1, source_target_pairs={{0,16},{8,24},{16,0},{24,8},{1,17},{9,25},{17,1},{25,9},{2,18},{10... | collective-permute-start | bytes 2654216 | tf_op jit(solution)/shard_map/ppermute | solution.py:806
  198.1 25.1 %collective-permute-start.25 = (bf16[2,576,1152]{2,1,0:T(8,128)(2,1)}, bf16[2,576,1152]{2,1,0:T(8,128)(2,1)}, u32[]{:S(2)}, u32[]{:S(2)}) collective-permute-start(bf16[2,576,1152]{2,1,0:T(8,128)(2,1)} %pad_maximum_fusion), channel_id=1, source_target_pairs={{0,8},{8,0},{16,24},{24,16},{1,9},{9,1},{17,25},{25,17},{2,10},{10... | collective-permute-start | bytes 7962632 | tf_op jit(solution)/shard_map/ppermute | solution.py:795
  201.0 22.2 %collective-permute-start.28 = (bf16[2,192,1152]{2,1,0:T(8,128)(2,1)}, bf16[2,192,1152]{2,1,0:T(8,128)(2,1)}, u32[]{:S(2)}, u32[]{:S(2)}) collective-permute-start(bf16[2,192,1152]{2,1,0:T(8,128)(2,1)} %pad_maximum_fusion.16), channel_id=1, source_target_pairs={{0,16},{8,24},{16,0},{24,8},{1,17},{9,25},{17,1},{25,9},{2,18},{10... | collective-permute-start | bytes 2654216 | tf_op jit(solution)/shard_map/ppermute | solution.py:806
  202.5 19.8 %collective-permute-start.26 = (bf16[192,1152]{1,0:T(8,128)(2,1)}, bf16[192,1152]{1,0:T(8,128)(2,1)S(1)}, u32[]{:S(2)}, u32[]{:S(2)}) collective-permute-start(bf16[192,1152]{1,0:T(8,128)(2,1)} %get-tuple-element.482), channel_id=1, source_target_pairs={{0,2},{2,4},{4,6},{6,7},{7,5},{5,3},{3,1},{1,0},{8,10},{10,12},{12... | collective-permute-start | bytes 1327112 | tf_op jit(solution)/shard_map/ppermute | solution.py:825
  403.6 30.3 %collective-permute-start.38 = (bf16[576,1152]{1,0:T(8,128)(2,1)}, bf16[576,1152]{1,0:T(8,128)(2,1)S(1)}, u32[]{:S(2)}, u32[]{:S(2)}) collective-permute-start(bf16[576,1152]{1,0:T(8,128)(2,1)} %get-tuple-element.447), channel_id=1, source_target_pairs={{0,2},{2,4},{4,6},{6,7},{7,5},{5,3},{3,1},{1,0},{8,10},{10,12},{12... | collective-permute-start | bytes 3981320 | tf_op jit(solution)/shard_map/ppermute | solution.py:825
  405.3 30.1 %collective-permute-start.39 = (bf16[576,1152]{1,0:T(8,128)(2,1)S(1)}, bf16[576,1152]{1,0:T(8,128)(2,1)S(1)}, u32[]{:S(2)}, u32[]{:S(2)}) collective-permute-start(bf16[576,1152]{1,0:T(8,128)(2,1)S(1)} %get-tuple-element.446), channel_id=1, source_target_pairs={{2,0},{4,2},{6,4},{7,6},{5,7},{3,5},{1,3},{0,1},{10,8},{12,10},{14... | collective-permute-start | bytes 3981320 | tf_op jit(solution)/shard_map/ppermute | solution.py:828
  439.3 29.4 %collective-permute-start.40 = (bf16[576,1152]{1,0:T(8,128)(2,1)}, bf16[576,1152]{1,0:T(8,128)(2,1)S(1)}, u32[]{:S(2)}, u32[]{:S(2)}) collective-permute-start(bf16[576,1152]{1,0:T(8,128)(2,1)} %get-tuple-element.445), channel_id=1, source_target_pairs={{0,2},{2,4},{4,6},{6,7},{7,5},{5,3},{3,1},{1,0},{8,10},{10,12},{12... | collective-permute-start | bytes 3981320 | tf_op jit(solution)/shard_map/ppermute | solution.py:825
  440.7 28.8 %collective-permute-start.41 = (bf16[576,1152]{1,0:T(8,128)(2,1)}, bf16[576,1152]{1,0:T(8,128)(2,1)S(1)}, u32[]{:S(2)}, u32[]{:S(2)}) collective-permute-start(bf16[576,1152]{1,0:T(8,128)(2,1)} %get-tuple-element.444), channel_id=1, source_target_pairs={{2,0},{4,2},{6,4},{7,6},{5,7},{3,5},{1,3},{0,1},{10,8},{12,10},{14... | collective-permute-start | bytes 3981320 | tf_op jit(solution)/shard_map/ppermute | solution.py:828
  469.5 26.8 %collective-permute-start.42 = (bf16[8,288,1152]{2,1,0:T(8,128)(2,1)}, bf16[8,288,1152]{2,1,0:T(8,128)(2,1)}, u32[]{:S(2)}, u32[]{:S(2)}) collective-permute-start(bf16[8,288,1152]{2,1,0:T(8,128)(2,1)} %shard_map.321), channel_id=1, source_target_pairs={{0,8},{8,0},{16,24},{24,16},{1,9},{9,1},{17,25},{25,17},{2,10},{10... | collective-permute-start | bytes 15925256 | tf_op jit(solution)/shard_map/ppermute | solution.py:795
  476.1 171.3 %collective-permute-start.60 = (bf16[16,1152]{1,0:T(8,128)(2,1)}, bf16[16,1152]{1,0:T(8,128)(2,1)}, u32[]{:S(2)}, u32[]{:S(2)}) collective-permute-start(bf16[16,1152]{1,0:T(8,128)(2,1)} %pad_maximum_fusion.32), channel_id=1, source_target_pairs={{0,16},{8,24},{16,0},{24,8},{1,17},{9,25},{17,1},{25,9},{2,18},{10... | collective-permute-start | bytes 110600 | tf_op jit(solution)/shard_map/ppermute | solution.py:1046
  480.6 32.8 %collective-permute-start.44 = (bf16[576,1152]{1,0:T(8,128)(2,1)}, bf16[576,1152]{1,0:T(8,128)(2,1)S(1)}, u32[]{:S(2)}, u32[]{:S(2)}) collective-permute-start(bf16[576,1152]{1,0:T(8,128)(2,1)} %get-tuple-element.443), channel_id=1, source_target_pairs={{0,2},{2,4},{4,6},{6,7},{7,5},{5,3},{3,1},{1,0},{8,10},{10,12},{12... | collective-permute-start | bytes 3981320 | tf_op jit(solution)/shard_map/ppermute | solution.py:825
  481.6 33.3 %collective-permute-start.45 = (bf16[576,1152]{1,0:T(8,128)(2,1)}, bf16[576,1152]{1,0:T(8,128)(2,1)S(1)}, u32[]{:S(2)}, u32[]{:S(2)}) collective-permute-start(bf16[576,1152]{1,0:T(8,128)(2,1)} %get-tuple-element.442), channel_id=1, source_target_pairs={{2,0},{4,2},{6,4},{7,6},{5,7},{3,5},{1,3},{0,1},{10,8},{12,10},{14... | collective-permute-start | bytes 3981320 | tf_op jit(solution)/shard_map/ppermute | solution.py:828
  501.8 34.9 %collective-permute-start.48 = (bf16[2,96,1152]{2,1,0:T(8,128)(2,1)}, bf16[2,96,1152]{2,1,0:T(8,128)(2,1)}, u32[]{:S(2)}, u32[]{:S(2)}) collective-permute-start(bf16[2,96,1152]{2,1,0:T(8,128)(2,1)} %pad_maximum_fusion.27), channel_id=1, source_target_pairs={{0,16},{8,24},{16,0},{24,8},{1,17},{9,25},{17,1},{25,9},{2,18},{10... | collective-permute-start | bytes 1327112 | tf_op jit(solution)/shard_map/ppermute | solution.py:806
  513.4 41.4 %collective-permute-start.51 = (bf16[2,96,1152]{2,1,0:T(8,128)(2,1)S(1)}, bf16[2,96,1152]{2,1,0:T(8,128)(2,1)}, u32[]{:S(2)}, u32[]{:S(2)}) collective-permute-start(bf16[2,96,1152]{2,1,0:T(8,128)(2,1)S(1)} %pad_maximum_fusion.28), channel_id=1, source_target_pairs={{0,16},{8,24},{16,0},{24,8},{1,17},{9,25},{17,1},{25,9},{2,18},{10... | collective-permute-start | bytes 1327112 | tf_op jit(solution)/shard_map/ppermute | solution.py:806
  536.8 35.4 %collective-permute-start.54 = (bf16[1,96,1152]{2,1,0:T(8,128)(2,1)}, bf16[1,96,1152]{2,1,0:T(8,128)(2,1)}, u32[]{:S(2)}, u32[]{:S(2)}) collective-permute-start(bf16[1,96,1152]{2,1,0:T(8,128)(2,1)} %get-tuple-element.430), channel_id=1, source_target_pairs={{0,16},{8,24},{16,0},{24,8},{1,17},{9,25},{17,1},{25,9},{2,18},{10... | collective-permute-start | bytes 663560 | tf_op jit(solution)/shard_map/ppermute | solution.py:806
  554.9 31.0 %collective-permute-start.67 = (bf16[576,1152]{1,0:T(8,128)(2,1)S(1)}, bf16[576,1152]{1,0:T(8,128)(2,1)}, u32[]{:S(2)}, u32[]{:S(2)}) collective-permute-start(bf16[576,1152]{1,0:T(8,128)(2,1)S(1)} %fusion.1), channel_id=1, source_target_pairs={{0,16},{8,24},{16,0},{24,8},{1,17},{9,25},{17,1},{25,9},{2,18},{10... | collective-permute-start | bytes 3981320 | tf_op jit(solution)/shard_map/ppermute | solution.py:806
  580.4 21.7 %collective-permute-start.55 = (bf16[528,1152]{1,0:T(8,128)(2,1)S(1)}, bf16[528,1152]{1,0:T(8,128)(2,1)}, u32[]{:S(2)}, u32[]{:S(2)}) collective-permute-start(bf16[528,1152]{1,0:T(8,128)(2,1)S(1)} %pad_maximum_fusion.6), channel_id=1, source_target_pairs={{0,8},{8,0},{16,24},{24,16},{1,9},{9,1},{17,25},{25,17},{2,10},{10... | collective-permute-start | bytes 3649544 | tf_op jit(solution)/shard_map/ppermute | solution.py:795
  580.5 49.7 %all-to-all-start.2 = ((bf16[8,104,1152]{2,1,0:T(8,128)(2,1)}), bf16[8,104,1152]{2,1,0:T(8,128)(2,1)}, u32[]{:S(2)}, u32[]{:S(2)}) async-start(bf16[8,104,1152]{2,1,0:T(8,128)(2,1)} %get-tuple-element.416), calls=%async_computation.2 | async-start | bytes 3833856 | tf_op jit(solution)/shard_map/all_to_all | solution.py:1142
  587.5 21.7 %collective-permute-start.68 = (bf16[4,144,1152]{2,1,0:T(8,128)(2,1)S(1)}, bf16[4,144,1152]{2,1,0:T(8,128)(2,1)S(1)}, u32[]{:S(2)}, u32[]{:S(2)}) collective-permute-start(bf16[4,144,1152]{2,1,0:T(8,128)(2,1)S(1)} %bitcast.267), channel_id=1, source_target_pairs={{0,8},{8,0},{16,24},{24,16},{1,9},{9,1},{17,25},{25,17},{2,10},{10... | collective-permute-start | bytes 3981320 | tf_op jit(solution)/shard_map/ppermute | solution.py:795
  632.8 26.7 %all-to-all-start.3 = ((bf16[8,48,1152]{2,1,0:T(8,128)(2,1)}), bf16[8,48,1152]{2,1,0:T(8,128)(2,1)S(1)}, u32[]{:S(2)}, u32[]{:S(2)}) async-start(bf16[8,48,1152]{2,1,0:T(8,128)(2,1)} %pad_maximum_fusion.17), calls=%async_computation.3 | async-start | bytes 1769472 | tf_op jit(solution)/shard_map/all_to_all | solution.py:1142
  (95 other events, 1169.1 us)

commit v8 on v7

--- a/solution.py
+++ b/solution.py
@@ -255,7 +255,7 @@
 
 heads_a_step = 2
 forward_groups = ((0, 8), (8, 8))
-back_groups = ((0, 4), (4, 8), (12, 4))
+back_groups = ((0, 2), (2, 8), (10, 6))
 groups = len(back_groups)
 
 
@@ -927,7 +927,7 @@
             for values in self.values
         )
 
-    def hop(self):
+    def prepare(self):
         ring, distance, split = self.ring, self.distance, self.split
         rows = self.values[0].shape[1]
         if distance == ring.size // 2:
@@ -941,7 +941,13 @@
             ahead = self.piece(distance, 0, rows) + ahead
             behind = self.piece(-distance, 0, rows) + behind
         self.distance -= 1
-        return ring.forward(ahead.astype(bf16)), ring.backward(behind.astype(bf16))
+        return ahead.astype(bf16), behind.astype(bf16)
+
+    def send(self, payload):
+        return self.ring.forward(payload[0]), self.ring.backward(payload[1])
+
+    def hop(self):
+        return self.send(self.prepare())
 
     def land(self, flight):
         self.ahead, self.behind = flight
@@ -1287,14 +1293,18 @@
     got_down, feed_chip, hidden = sync(swap_core(other_down), feed_chip, hidden)
     feed_chip = feed_weight_call(near, hidden, grad_two, got_down, feed_chip, 2, 4)
     feed_chip, grad_one = sync(feed_chip, grad_one)
-    mix_grad = mix_grad_call(core_row, places, grad_one, attention_chunks)
     if ringed:
         feed_scatter = Scatter(ring, feed_chip)
+        payload, grad_one = sync(feed_scatter.prepare(), grad_one)
+        flight = feed_scatter.send(payload)
+    mix_grad = mix_grad_call(core_row, places, grad_one, attention_chunks)
     grads = []
     for group, (first, heads) in enumerate(back_groups):
         grads.append(attend_back_call(projected, attended, mix_grad, first, heads))
         if ringed and group < 2:
-            flight, grads, mix_grad = sync(feed_scatter.hop(), grads, mix_grad)
+            if group:
+                flight = feed_scatter.hop()
+            flight, grads, mix_grad = sync(flight, grads, mix_grad)
             feed_scatter.land(flight)
     grads = [triple[block] for block in range(3) for triple in grads]
 

time: 671 us -> 671 us (level)
    convert_element_type x5 -> x2, other arithmetic: 14.7 us -> 3.79 us  [hop(): behind.astype(bf16)]
    convert_element_type x0 -> x3, other arithmetic: none -> 10.8 us  [prepare(): return (ahead.astype(bf16), behind.astype(bf16))]
  transfers between devices with their start and end apart: 73 -> 73, of which waited for: 28 -> 24; matrix products, arithmetic and copies ran while one was open for 15% -> 15% of each run, Pallas kernels for 33% -> 34%
where the time goes in v8:
time: 671 us; the launch traced here: 662 us
  Pallas kernels  332 us (49%)
  waiting for transfers between devices  103 us (15%)
  starting transfers between devices  96.8 us (14%)
  other arithmetic  90.4 us (13%)
  local copies, waits for them, and re-layouts  32.5 us (5%)
    pallas_call x1, Pallas kernels, feed_call(): pl.pallas_call(functools.partial(feed_kernel, source=source), grid=(steps...  83.2 us
    pallas_call x3, Pallas kernels, attend_back_call(): pl.pallas_call(functools.partial(attend_back_kernel, factor=1.0 / math.sq...  50.2 us
    pallas_call x4, Pallas kernels, start_back_call(): pl.pallas_call(functools.partial(start_back_kernel, chunks=chunks, first=...  45.4 us
    pallas_call x4, Pallas kernels, feed_weight_call(): pl.pallas_call(feed_weight_kernel, grid_spec=pltpu.PrefetchScalarGridSpec...  43.5 us
    ppermute x16, starting transfers between devices, forward(): return lax.ppermute(values, 'tok', self.ahead)  39.6 us
    ppermute x16, waiting for transfers between devices, forward(): return lax.ppermute(values, 'tok', self.ahead)  35.3 us
    ppermute x16, waiting for transfers between devices, swap_x(): return lax.ppermute(values, 'grp', swap_pairs(lax.axis_size('grp'), 2))  33.9 us
    pallas_call x2, Pallas kernels, attend_call(): pl.pallas_call(functools.partial(attend_kernel, factor=math.log2(math.e)...  29.8 us
  transfers between devices with their start and end apart: 73, of which 24 were waited for; matrix products, arithmetic and copies ran while one was open for 15% of the time, Pallas kernels for 34%

profile of v8, /device:TPU:0, one launch (start us, length us, event | category | flops | bytes accessed | tf_op | source)
XLA Modules:
  0.0 661.8 jit_solution(3616372843936386138)
XLA Ops:
  17.8 6.5 all-to-all-start
  46.0 23.3 %collective-permute-done.2 = bf16[240,1152]{1,0:T(8,128)(2,1)} collective-permute-done((bf16[240,1152]{1,0:T(8,128)(2,1)S(1)}, bf16[240,1152]{1,0:T(8,128)(2,1)}, u32[]{:S(2)}, u32[]{:S(2)}) %collective-permute-start.2) | collective-permute-done | bytes 552992 | tf_op jit(solution)/shard_map/ppermute | solution.py:825
  69.4 14.4 %collective-permute-start.5 = (bf16[240,1152]{1,0:T(8,128)(2,1)}, bf16[240,1152]{1,0:T(8,128)(2,1)S(1)}, u32[]{:S(2)}, u32[]{:S(2)}) collective-permute-start(bf16[240,1152]{1,0:T(8,128)(2,1)} %collective-permute-done.2), channel_id=1, source_target_pairs={{0,2},{2,4},{4,6},{6,7},{7,5},{5,3},{3,1},{1,0},{8,10},{10,12},{12... | collective-permute-start | bytes 1658888 | tf_op jit(solution)/shard_map/ppermute | solution.py:825
  117.2 5.6 all-to-all-start.1
  135.4 8.4 %shard_map.307 = (f32[1024,1152]{1,0:T(8,128)}, bf16[1024,1152]{1,0:T(8,128)(2,1)}) custom-call(s32[2]{0:T(128)} %pad_add_fusion.core_ref, s32[8]{0:T(128)} %compare_select_fusion.2.places_ref, s32[1]{0:T(128)S(6)} %copy.72.count_ref, s32[1,768]{1,0:T(1,128)} %index_row_ref.7, bf16[8,112,1152]{2,1,0:T(8,128)(2,1)} %all-to-all-done.kept_ref, ...), custom_call_target="tpu_custom_call" | custom-call | flops 1811939328 | bytes 16515072 | tf_op jit(solution)/shard_map/pallas_call | solution.py:106
  143.8 4.1 collective-permute-done.17
  158.1 16.8 %shard_map.308.query_ref.key_ref.value_ref = bf16[3,16,1024,128]{3,2,1,0:T(8,128)(2,1)} custom-call(s32[2]{0:T(128)} %pad_add_fusion.core_ref, s32[8]{0:T(128)} %compare_select_fusion.2.places_ref, bf16[1024,1152]{1,0:T(8,128)(2,1)} %get-tuple-element.337.norm_ref, f32[16,1152]{1,0:T(8,128)} %convert_reduce_fusion.1.small_ref, ...), custom_call_target="tpu_custom_call" | custom-call | flops 8153726976 | bytes 22118400 | tf_op jit(solution)/shard_map/pallas_call | solution.py:235
  183.1 14.9 %shard_map.309 = (bf16[16,1024,128]{2,1,0:T(8,128)(2,1)}, f32[16,1,1024]{2,1,0:T(1,128)}) custom-call(bf16[3,16,1024,128]{3,2,1,0:T(8,128)(2,1)} %shard_map.308.query_ref.key_ref.value_ref, bf16[3,16,1024,128]{3,2,1,0:T(8,128)(2,1)} %shard_map.308.query_ref.key_ref.value_ref, bf16[3,16,1024,128]{3,2,1,0:T(8,128)(2,1)} %shard_map.308.query_ref.key_ref.value_ref), custom_call_target="tpu_custom_call" | custom-call | flops 8589934592 | bytes 8388608 | tf_op jit(solution)/shard_map/pallas_call | solution.py:287
  204.5 14.9 %shard_map.310 = (bf16[16,1024,128]{2,1,0:T(8,128)(2,1)}, f32[16,1,1024]{2,1,0:T(1,128)}) custom-call(bf16[3,16,1024,128]{3,2,1,0:T(8,128)(2,1)} %shard_map.308.query_ref.key_ref.value_ref, bf16[3,16,1024,128]{3,2,1,0:T(8,128)(2,1)} %shard_map.308.query_ref.key_ref.value_ref, ...), custom_call_target="tpu_custom_call", output_to_operand_aliasing={{0}: (3, {}), {1}: (4, {})} | custom-call | flops 8589934592 | bytes 8388608 | tf_op jit(solution)/shard_map/pallas_call | solution.py:287
  230.4 11.7 %shard_map.311 = (bf16[1024,1152]{1,0:T(8,128)(2,1)}, bf16[1024,1152]{1,0:T(8,128)(2,1)}, f32[1024,1152]{1,0:T(8,128)}, bf16[1024,1152]{1,0:T(8,128)(2,1)}) custom-call(s32[2]{0:T(128)} %pad_add_fusion.core_ref, s32[8]{0:T(128)} %compare_select_fusion.2.places_ref, f32[1024,1152]{1,0:T(8,128)} %get-tuple-element.279.start_ref, ...), custom_call_target="tpu_custom_call" | custom-call | flops 2717908992 | bytes 21233664 | tf_op jit(solution)/shard_map/pallas_call | solution.py:375
  244.8 83.2 %shard_map.312 = (f32[1024,1152]{1,0:T(8,128)}, bf16[4,1024,1152]{2,1,0:T(8,128)(2,1)}, bf16[4,1024,1152]{2,1,0:T(8,128)(2,1)}, bf16[1024,1152]{1,0:T(8,128)(2,1...) custom-call(s32[2]{0:T(128)} %pad_add_fusion.core_ref, ...), custom_call_target="tpu_custom_call" | custom-call | flops 43486543872 | bytes 70778880 | tf_op jit(solution)/shard_map/pallas_call | solution.py:471
  328.0 10.4 %shard_map.313 = bf16[8,288,1152]{2,1,0:T(8,128)(2,1)} custom-call(s32[1]{0:T(128)S(6)} %sub.88.first_ref, bf16[1024,1152]{1,0:T(8,128)(2,1)} %get-tuple-element.299.norm_ref.left_ref, bf16[4,1024,1152]{2,1,0:T(8,128)(2,1)} %get-tuple-element.292.right_ref), custom_call_target="tpu_custom_call" | custom-call | flops 5435817984 | bytes 14745600 | tf_op jit(solution)/shard_map/pallas_call | solution.py:542
  338.7 10.4 %shard_map.314 = bf16[8,288,1152]{2,1,0:T(8,128)(2,1)} custom-call(s32[1]{0:T(128)S(6)} %sub.88.first_ref, bf16[4,1024,1152]{2,1,0:T(8,128)(2,1)} %get-tuple-element.301.left_ref, bf16[1024,1152]{1,0:T(8,128)(2,1)} %get-tuple-element.297.right_ref), custom_call_target="tpu_custom_call" | custom-call | flops 5435817984 | bytes 14745600 | tf_op jit(solution)/shard_map/pallas_call | solution.py:542
  349.4 11.3 %shard_map.315.rest_1_ = bf16[8,576,1152]{2,1,0:T(8,128)(2,1)} custom-call(s32[1]{0:T(128)S(6)} %mul.77.first_ref, bf16[1024,1152]{1,0:T(8,128)(2,1)} %get-tuple-element.299.norm_ref.left_ref, bf16[4,1024,1152]{2,1,0:T(8,128)(2,1)} %get-tuple-element.292.right_ref, bf16[8,288,1152]{2,1,0:T(8,128)(2,1)} %collective-permute-done.34.rest_0_), custom_call_target="tpu_custom_call" | custom-call | flops 5435817984 | bytes 14745600 | tf_op jit(solution)/shard_map/pallas_call | solution.py:542
  360.8 11.3 %shard_map.316 = bf16[8,576,1152]{2,1,0:T(8,128)(2,1)} custom-call(s32[1]{0:T(128)S(6)} %mul.77.first_ref, bf16[4,1024,1152]{2,1,0:T(8,128)(2,1)} %get-tuple-element.301.left_ref, bf16[1024,1152]{1,0:T(8,128)(2,1)} %get-tuple-element.297.right_ref, bf16[8,288,1152]{2,1,0:T(8,128)(2,1)} %collective-permute-done.35.rest_0_, ...), custom_call_target="tpu_custom_call", output_to_operand_aliasing={{}: (4, {})} | custom-call | flops 5435817984 | bytes 14745600 | tf_op jit(solution)/shard_map/pallas_call | solution.py:542
  375.5 8.9 %shard_map.317.grad_ref = bf16[16,1024,128]{2,1,0:T(8,128)(2,1)} custom-call(s32[2]{0:T(128)} %pad_add_fusion.core_ref, s32[8]{0:T(128)} %compare_select_fusion.2.places_ref, bf16[1024,1152]{1,0:T(8,128)(2,1)} %get-tuple-element.311.grad_ref, bf16[1,352,1152]{2,1,0:T(8,128)(2,1)} %copy-done.2, bf16[1,240,1152]{2,1,0:T(8,128)(2,1)} %bitcast.238, ...), custom_call_target="tpu_custom_call" | custom-call | flops 2717908992 | bytes 9437184 | tf_op jit(solution)/shard_map/pallas_call | solution.py:633
  384.4 7.9 %shard_map.318 = (bf16[2,1024,128]{2,1,0:T(8,128)(2,1)}, bf16[2,1024,128]{2,1,0:T(8,128)(2,1)}, bf16[2,1024,128]{2,1,0:T(8,128)(2,1)}) custom-call(bf16[3,16,1024,128]{3,2,1,0:T(8,128)(2,1)} %shard_map.308.query_ref.key_ref.value_ref, bf16[3,16,1024,128]{3,2,1,0:T(8,128)(2,1)} %shard_map.308.query_ref.key_ref.value_ref, ...), custom_call_target="tpu_custom_call" | custom-call | flops 5368709120 | bytes 4194304 | tf_op jit(solution)/shard_map/pallas_call | solution.py:329
  397.5 23.5 %shard_map.319 = (bf16[8,1024,128]{2,1,0:T(8,128)(2,1)}, bf16[8,1024,128]{2,1,0:T(8,128)(2,1)}, bf16[8,1024,128]{2,1,0:T(8,128)(2,1)}) custom-call(bf16[3,16,1024,128]{3,2,1,0:T(8,128)(2,1)} %shard_map.308.query_ref.key_ref.value_ref, bf16[3,16,1024,128]{3,2,1,0:T(8,128)(2,1)} %shard_map.308.query_ref.key_ref.value_ref, ...), custom_call_target="tpu_custom_call" | custom-call | flops 21474836480 | bytes 16777216 | tf_op jit(solution)/shard_map/pallas_call | solution.py:329
  421.1 5.3 collective-permute-done.38
  433.2 18.7 %shard_map.320 = (bf16[6,1024,128]{2,1,0:T(8,128)(2,1)}, bf16[6,1024,128]{2,1,0:T(8,128)(2,1)}, bf16[6,1024,128]{2,1,0:T(8,128)(2,1)}) custom-call(bf16[3,16,1024,128]{3,2,1,0:T(8,128)(2,1)} %shard_map.308.query_ref.key_ref.value_ref, bf16[3,16,1024,128]{3,2,1,0:T(8,128)(2,1)} %shard_map.308.query_ref.key_ref.value_ref, ...), custom_call_target="tpu_custom_call" | custom-call | flops 16106127360 | bytes 12582912 | tf_op jit(solution)/shard_map/pallas_call | solution.py:329
  452.0 12.1 %shard_map.321 = bf16[8,288,1152]{2,1,0:T(8,128)(2,1)} custom-call(s32[1]{0:T(128)S(6)} %sub.94.owner_ref, bf16[1024,1152]{1,0:T(8,128)(2,1)} %get-tuple-element.337.norm_ref, bf16[1024,1152]{1,0:T(8,128)(2,1)} %get-tuple-element.326.joined_ref, bf16[1024,1152]{1,0:T(8,128)(2,1)} %get-tuple-element.311.grad_ref, ...), custom_call_target="tpu_custom_call" | custom-call | flops 5435817984 | bytes 17104896 | tf_op jit(solution)/shard_map/pallas_call | solution.py:599
  465.7 4.4 collective-permute-done.59
  477.4 13.4 %shard_map.322 = bf16[8,288,1152]{2,1,0:T(8,128)(2,1)} custom-call(s32[1]{0:T(128)} %bitcast.owner_ref, bf16[1024,1152]{1,0:T(8,128)(2,1)} %get-tuple-element.337.norm_ref, bf16[1024,1152]{1,0:T(8,128)(2,1)} %get-tuple-element.326.joined_ref, bf16[1024,1152]{1,0:T(8,128)(2,1)} %get-tuple-element.311.grad_ref, ...), custom_call_target="tpu_custom_call" | custom-call | flops 5435817984 | bytes 17104896 | tf_op jit(solution)/shard_map/pallas_call | solution.py:599
  497.1 10.9 %shard_map.323 = (bf16[256,1152]{1,0:T(8,128)(2,1)}, bf16[8,104,1152]{2,1,0:T(8,128)(2,1)}, f32[8,1152]{1,0:T(8,128)}) custom-call(s32[2]{0:T(128)} %pad_add_fusion.core_ref, s32[8]{0:T(128)} %compare_select_fusion.2.places_ref, s32[1]{0:T(128)S(6)} %copy.72.count_ref, s32[1,768]{1,0:T(1,128)} %index_row_ref.7, s32[768,1]{1,0:T(8,128)} %copy.48.index_ref, ...), custom_call_target="tpu_custom_call" | custom-call | flops 2717908992 | bytes 8257536 | tf_op jit(solution)/shard_map/pallas_call | solution.py:706
  519.7 11.5 %shard_map.324 = (bf16[256,1152]{1,0:T(8,128)(2,1)}, bf16[8,104,1152]{2,1,0:T(8,128)(2,1)}, f32[8,1152]{1,0:T(8,128)}) custom-call(s32[2]{0:T(128)} %pad_add_fusion.core_ref, s32[8]{0:T(128)} %compare_select_fusion.2.places_ref, s32[1]{0:T(128)S(6)} %copy.72.count_ref, s32[1,768]{1,0:T(1,128)} %index_row_ref.7, s32[768,1]{1,0:T(8,128)} %copy.48.index_ref, ...), custom_call_target="tpu_custom_call" | custom-call | flops 2717908992 | bytes 8257536 | tf_op jit(solution)/shard_map/pallas_call | solution.py:706
  536.7 11.5 %shard_map.325 = (bf16[256,1152]{1,0:T(8,128)(2,1)}, bf16[8,104,1152]{2,1,0:T(8,128)(2,1)}, f32[8,1152]{1,0:T(8,128)}) custom-call(s32[2]{0:T(128)} %pad_add_fusion.core_ref, s32[8]{0:T(128)} %compare_select_fusion.2.places_ref, s32[1]{0:T(128)S(6)} %copy.72.count_ref, s32[1,768]{1,0:T(1,128)} %index_row_ref.7, s32[768,1]{1,0:T(8,128)} %copy.48.index_ref, ...), custom_call_target="tpu_custom_call" | custom-call | flops 2717908992 | bytes 8257536 | tf_op jit(solution)/shard_map/pallas_call | solution.py:706
  555.2 11.5 %shard_map.326 = (bf16[256,1152]{1,0:T(8,128)(2,1)}, bf16[8,104,1152]{2,1,0:T(8,128)(2,1)}, f32[8,1152]{1,0:T(8,128)}) custom-call(s32[2]{0:T(128)} %pad_add_fusion.core_ref, s32[8]{0:T(128)} %compare_select_fusion.2.places_ref, s32[1]{0:T(128)S(6)} %copy.72.count_ref, s32[1,768]{1,0:T(1,128)} %index_row_ref.7, s32[768,1]{1,0:T(8,128)} %copy.48.index_ref, ...), custom_call_target="tpu_custom_call" | custom-call | flops 2717908992 | bytes 8257536 | tf_op jit(solution)/shard_map/pallas_call | solution.py:706
  575.0 4.4 all-to-all-start.2
  586.5 9.8 %collective-permute-done.65 = bf16[192,1152]{1,0:T(8,128)(2,1)S(1)} collective-permute-done((bf16[192,1152]{1,0:T(8,128)(2,1)S(1)}, bf16[192,1152]{1,0:T(8,128)(2,1)S(1)}, u32[]{:S(2)}, u32[]{:S(2)}) %collective-permute-start.65) | collective-permute-done | bytes 442400 | tf_op jit(solution)/shard_map/ppermute | solution.py:806
  604.8 10.4 %collective-permute-done.56 = bf16[272,1152]{1,0:T(8,128)(2,1)S(1)} collective-permute-done((bf16[272,1152]{1,0:T(8,128)(2,1)S(1)}, bf16[272,1152]{1,0:T(8,128)(2,1)S(1)}, u32[]{:S(2)}, u32[]{:S(2)}) %collective-permute-start.56) | collective-permute-done | bytes 626720 | tf_op jit(solution)/shard_map/ppermute | solution.py:806
  616.2 8.9 %all-to-all-done.2 = bf16[8,104,1152]{2,1,0:T(8,128)(2,1)} async-done(((bf16[8,104,1152]{2,1,0:T(8,128)(2,1)}), bf16[8,104,1152]{2,1,0:T(8,128)(2,1)}, u32[]{:S(2)}, u32[]{:S(2)}) %all-to-all-start.2) | async-done | bytes 1916960 | tf_op jit(solution)/shard_map/all_to_all | solution.py:1148
  645.6 8.8 %all-to-all-done.3 = bf16[8,48,1152]{2,1,0:T(8,128)(2,1)S(1)} async-done(((bf16[8,48,1152]{2,1,0:T(8,128)(2,1)}), bf16[8,48,1152]{2,1,0:T(8,128)(2,1)S(1)}, u32[]{:S(2)}, u32[]{:S(2)}) %all-to-all-start.3) | async-done | bytes 884768 | tf_op jit(solution)/shard_map/all_to_all | solution.py:1148
  (394 shorter events, 229.4 us)
Async XLA Ops:
  6.8 19.4 %collective-permute-start = (bf16[240,1152]{1,0:T(8,128)(2,1)}, bf16[240,1152]{1,0:T(8,128)(2,1)S(1)}, u32[]{:S(2)}, u32[]{:S(2)}) collective-permute-start(bf16[240,1152]{1,0:T(8,128)(2,1)} %fusion.27), channel_id=1, source_target_pairs={{0,2},{2,4},{4,6},{6,7},{7,5},{5,3},{3,1},{1,0},{8,10},{10,12},{12... | collective-permute-start | bytes 1658888 | tf_op jit(solution)/shard_map/ppermute | solution.py:825
  17.8 74.1 %all-to-all-start = ((bf16[8,112,1152]{2,1,0:T(8,128)(2,1)}), bf16[8,112,1152]{2,1,0:T(8,128)(2,1)}, u32[]{:S(2)}, u32[]{:S(2)}) async-start(bf16[8,112,1152]{2,1,0:T(8,128)(2,1)} %pad_maximum_fusion.4), calls=%async_computation | async-start | bytes 4128768 | tf_op jit(solution)/shard_map/all_to_all | solution.py:1148
  26.3 43.1 %collective-permute-start.2 = (bf16[240,1152]{1,0:T(8,128)(2,1)S(1)}, bf16[240,1152]{1,0:T(8,128)(2,1)}, u32[]{:S(2)}, u32[]{:S(2)}) collective-permute-start(bf16[240,1152]{1,0:T(8,128)(2,1)S(1)} %collective-permute-done), channel_id=1, source_target_pairs={{0,2},{2,4},{4,6},{6,7},{7,5},{5,3},{3,1},{1,0},{8,10},{10,12},{12... | collective-permute-start | bytes 1658888 | tf_op jit(solution)/shard_map/ppermute | solution.py:825
  28.4 41.0 %collective-permute-start.3 = (bf16[240,1152]{1,0:T(8,128)(2,1)S(1)}, bf16[240,1152]{1,0:T(8,128)(2,1)}, u32[]{:S(2)}, u32[]{:S(2)}) collective-permute-start(bf16[240,1152]{1,0:T(8,128)(2,1)S(1)} %collective-permute-done.1), channel_id=1, source_target_pairs={{2,0},{4,2},{6,4},{7,6},{5,7},{3,5},{1,3},{0,1},{10,8},{12,10},{14... | collective-permute-start | bytes 1658888 | tf_op jit(solution)/shard_map/ppermute | solution.py:828
  69.4 28.3 %collective-permute-start.5 = (bf16[240,1152]{1,0:T(8,128)(2,1)}, bf16[240,1152]{1,0:T(8,128)(2,1)S(1)}, u32[]{:S(2)}, u32[]{:S(2)}) collective-permute-start(bf16[240,1152]{1,0:T(8,128)(2,1)} %collective-permute-done.2), channel_id=1, source_target_pairs={{0,2},{2,4},{4,6},{6,7},{7,5},{5,3},{3,1},{1,0},{8,10},{10,12},{12... | collective-permute-start | bytes 1658888 | tf_op jit(solution)/shard_map/ppermute | solution.py:825
  126.6 21.4 %collective-permute-start.17 = (bf16[384,1152]{1,0:T(8,128)(2,1)}, bf16[384,1152]{1,0:T(8,128)(2,1)}, u32[]{:S(2)}, u32[]{:S(2)}) collective-permute-start(bf16[384,1152]{1,0:T(8,128)(2,1)} %constant_dynamic-slice_fusion.3), channel_id=1, source_target_pairs={{0,2},{2,4},{4,6},{6,7},{7,5},{5,3},{3,1},{1,0},{8,10},{10,12},{12... | collective-permute-start | bytes 2654216 | tf_op jit(solution)/shard_map/ppermute | solution.py:825
  130.8 20.8 %collective-permute-start.18 = (bf16[384,1152]{1,0:T(8,128)(2,1)}, bf16[384,1152]{1,0:T(8,128)(2,1)}, u32[]{:S(2)}, u32[]{:S(2)}) collective-permute-start(bf16[384,1152]{1,0:T(8,128)(2,1)} %constant_dynamic-slice_fusion.3), channel_id=1, source_target_pairs={{2,0},{4,2},{6,4},{7,6},{5,7},{3,5},{1,3},{0,1},{10,8},{12,10},{14... | collective-permute-start | bytes 2654216 | tf_op jit(solution)/shard_map/ppermute | solution.py:828
  154.1 20.8 %collective-permute-start.21 = (bf16[2,192,1152]{2,1,0:T(8,128)(2,1)S(1)}, bf16[2,192,1152]{2,1,0:T(8,128)(2,1)S(1)}, u32[]{:S(2)}, u32[]{:S(2)}) collective-permute-start(bf16[2,192,1152]{2,1,0:T(8,128)(2,1)S(1)} %pad_maximum_fusion.14), channel_id=1, source_target_pairs={{0,16},{8,24},{16,0},{24,8},{1,17},{9,25},{17,1},{25,9},{2,18},{10... | collective-permute-start | bytes 2654216 | tf_op jit(solution)/shard_map/ppermute | solution.py:806
  155.8 19.8 %collective-permute-start.19 = (bf16[384,1152]{1,0:T(8,128)(2,1)}, bf16[384,1152]{1,0:T(8,128)(2,1)S(1)}, u32[]{:S(2)}, u32[]{:S(2)}) collective-permute-start(bf16[384,1152]{1,0:T(8,128)(2,1)} %collective-permute-done.17), channel_id=1, source_target_pairs={{0,2},{2,4},{4,6},{6,7},{7,5},{5,3},{3,1},{1,0},{8,10},{10,12},{12... | collective-permute-start | bytes 2654216 | tf_op jit(solution)/shard_map/ppermute | solution.py:825
  157.1 19.1 %collective-permute-start.20 = (bf16[384,1152]{1,0:T(8,128)(2,1)}, bf16[384,1152]{1,0:T(8,128)(2,1)S(1)}, u32[]{:S(2)}, u32[]{:S(2)}) collective-permute-start(bf16[384,1152]{1,0:T(8,128)(2,1)} %collective-permute-done.18), channel_id=1, source_target_pairs={{2,0},{4,2},{6,4},{7,6},{5,7},{3,5},{1,3},{0,1},{10,8},{12,10},{14... | collective-permute-start | bytes 2654216 | tf_op jit(solution)/shard_map/ppermute | solution.py:828
  176.3 21.7 %collective-permute-start.22 = (bf16[384,1152]{1,0:T(8,128)(2,1)S(1)}, bf16[384,1152]{1,0:T(8,128)(2,1)S(1)}, u32[]{:S(2)}, u32[]{:S(2)}) collective-permute-start(bf16[384,1152]{1,0:T(8,128)(2,1)S(1)} %collective-permute-done.19), channel_id=1, source_target_pairs={{0,2},{2,4},{4,6},{6,7},{7,5},{5,3},{3,1},{1,0},{8,10},{10,12},{12... | collective-permute-start | bytes 2654216 | tf_op jit(solution)/shard_map/ppermute | solution.py:825
  177.8 20.2 %collective-permute-start.23 = (bf16[384,1152]{1,0:T(8,128)(2,1)S(1)}, bf16[384,1152]{1,0:T(8,128)(2,1)S(1)}, u32[]{:S(2)}, u32[]{:S(2)}) collective-permute-start(bf16[384,1152]{1,0:T(8,128)(2,1)S(1)} %collective-permute-done.20), channel_id=1, source_target_pairs={{2,0},{4,2},{6,4},{7,6},{5,7},{3,5},{1,3},{0,1},{10,8},{12,10},{14... | collective-permute-start | bytes 2654216 | tf_op jit(solution)/shard_map/ppermute | solution.py:828
  198.1 25.1 %collective-permute-start.25 = (bf16[2,576,1152]{2,1,0:T(8,128)(2,1)}, bf16[2,576,1152]{2,1,0:T(8,128)(2,1)}, u32[]{:S(2)}, u32[]{:S(2)}) collective-permute-start(bf16[2,576,1152]{2,1,0:T(8,128)(2,1)} %pad_maximum_fusion), channel_id=1, source_target_pairs={{0,8},{8,0},{16,24},{24,16},{1,9},{9,1},{17,25},{25,17},{2,10},{10... | collective-permute-start | bytes 7962632 | tf_op jit(solution)/shard_map/ppermute | solution.py:795
  201.0 22.2 %collective-permute-start.28 = (bf16[2,192,1152]{2,1,0:T(8,128)(2,1)}, bf16[2,192,1152]{2,1,0:T(8,128)(2,1)}, u32[]{:S(2)}, u32[]{:S(2)}) collective-permute-start(bf16[2,192,1152]{2,1,0:T(8,128)(2,1)} %pad_maximum_fusion.16), channel_id=1, source_target_pairs={{0,16},{8,24},{16,0},{24,8},{1,17},{9,25},{17,1},{25,9},{2,18},{10... | collective-permute-start | bytes 2654216 | tf_op jit(solution)/shard_map/ppermute | solution.py:806
  202.5 19.8 %collective-permute-start.26 = (bf16[192,1152]{1,0:T(8,128)(2,1)}, bf16[192,1152]{1,0:T(8,128)(2,1)S(1)}, u32[]{:S(2)}, u32[]{:S(2)}) collective-permute-start(bf16[192,1152]{1,0:T(8,128)(2,1)} %get-tuple-element.488), channel_id=1, source_target_pairs={{0,2},{2,4},{4,6},{6,7},{7,5},{5,3},{3,1},{1,0},{8,10},{10,12},{12... | collective-permute-start | bytes 1327112 | tf_op jit(solution)/shard_map/ppermute | solution.py:825
  373.5 18.9 %collective-permute-start.36 = (bf16[288,1152]{1,0:T(8,128)(2,1)S(1)}, bf16[288,1152]{1,0:T(8,128)(2,1)S(1)}, u32[]{:S(2)}, u32[]{:S(2)}) collective-permute-start(bf16[288,1152]{1,0:T(8,128)(2,1)S(1)} %get-tuple-element.307), channel_id=1, source_target_pairs={{0,2},{2,4},{4,6},{6,7},{7,5},{5,3},{3,1},{1,0},{8,10},{10,12},{12... | collective-permute-start | bytes 1990664 | tf_op jit(solution)/shard_map/ppermute | solution.py:825
  395.5 30.9 %collective-permute-start.38 = (bf16[576,1152]{1,0:T(8,128)(2,1)}, bf16[576,1152]{1,0:T(8,128)(2,1)S(1)}, u32[]{:S(2)}, u32[]{:S(2)}) collective-permute-start(bf16[576,1152]{1,0:T(8,128)(2,1)} %get-tuple-element.453), channel_id=1, source_target_pairs={{0,2},{2,4},{4,6},{6,7},{7,5},{5,3},{3,1},{1,0},{8,10},{10,12},{12... | collective-permute-start | bytes 3981320 | tf_op jit(solution)/shard_map/ppermute | solution.py:825
  397.0 30.4 %collective-permute-start.39 = (bf16[576,1152]{1,0:T(8,128)(2,1)S(1)}, bf16[576,1152]{1,0:T(8,128)(2,1)S(1)}, u32[]{:S(2)}, u32[]{:S(2)}) collective-permute-start(bf16[576,1152]{1,0:T(8,128)(2,1)S(1)} %get-tuple-element.452), channel_id=1, source_target_pairs={{2,0},{4,2},{6,4},{7,6},{5,7},{3,5},{1,3},{0,1},{10,8},{12,10},{14... | collective-permute-start | bytes 3981320 | tf_op jit(solution)/shard_map/ppermute | solution.py:828
  431.2 32.9 %collective-permute-start.40 = (bf16[576,1152]{1,0:T(8,128)(2,1)}, bf16[576,1152]{1,0:T(8,128)(2,1)S(1)}, u32[]{:S(2)}, u32[]{:S(2)}) collective-permute-start(bf16[576,1152]{1,0:T(8,128)(2,1)} %get-tuple-element.451), channel_id=1, source_target_pairs={{0,2},{2,4},{4,6},{6,7},{7,5},{5,3},{3,1},{1,0},{8,10},{10,12},{12... | collective-permute-start | bytes 3981320 | tf_op jit(solution)/shard_map/ppermute | solution.py:825
  432.9 31.2 %collective-permute-start.41 = (bf16[576,1152]{1,0:T(8,128)(2,1)}, bf16[576,1152]{1,0:T(8,128)(2,1)S(1)}, u32[]{:S(2)}, u32[]{:S(2)}) collective-permute-start(bf16[576,1152]{1,0:T(8,128)(2,1)} %get-tuple-element.450), channel_id=1, source_target_pairs={{2,0},{4,2},{6,4},{7,6},{5,7},{3,5},{1,3},{0,1},{10,8},{12,10},{14... | collective-permute-start | bytes 3981320 | tf_op jit(solution)/shard_map/ppermute | solution.py:828
  464.2 26.6 %collective-permute-start.42 = (bf16[8,288,1152]{2,1,0:T(8,128)(2,1)}, bf16[8,288,1152]{2,1,0:T(8,128)(2,1)}, u32[]{:S(2)}, u32[]{:S(2)}) collective-permute-start(bf16[8,288,1152]{2,1,0:T(8,128)(2,1)} %shard_map.321), channel_id=1, source_target_pairs={{0,8},{8,0},{16,24},{24,16},{1,9},{9,1},{17,25},{25,17},{2,10},{10... | collective-permute-start | bytes 15925256 | tf_op jit(solution)/shard_map/ppermute | solution.py:795
  470.7 171.3 %collective-permute-start.60 = (bf16[16,1152]{1,0:T(8,128)(2,1)}, bf16[16,1152]{1,0:T(8,128)(2,1)}, u32[]{:S(2)}, u32[]{:S(2)}) collective-permute-start(bf16[16,1152]{1,0:T(8,128)(2,1)} %pad_maximum_fusion.32), channel_id=1, source_target_pairs={{0,16},{8,24},{16,0},{24,8},{1,17},{9,25},{17,1},{25,9},{2,18},{10... | collective-permute-start | bytes 110600 | tf_op jit(solution)/shard_map/ppermute | solution.py:1052
  475.3 32.6 %collective-permute-start.44 = (bf16[576,1152]{1,0:T(8,128)(2,1)}, bf16[576,1152]{1,0:T(8,128)(2,1)S(1)}, u32[]{:S(2)}, u32[]{:S(2)}) collective-permute-start(bf16[576,1152]{1,0:T(8,128)(2,1)} %get-tuple-element.449), channel_id=1, source_target_pairs={{0,2},{2,4},{4,6},{6,7},{7,5},{5,3},{3,1},{1,0},{8,10},{10,12},{12... | collective-permute-start | bytes 3981320 | tf_op jit(solution)/shard_map/ppermute | solution.py:825
  477.0 32.4 %collective-permute-start.45 = (bf16[576,1152]{1,0:T(8,128)(2,1)}, bf16[576,1152]{1,0:T(8,128)(2,1)S(1)}, u32[]{:S(2)}, u32[]{:S(2)}) collective-permute-start(bf16[576,1152]{1,0:T(8,128)(2,1)} %get-tuple-element.448), channel_id=1, source_target_pairs={{2,0},{4,2},{6,4},{7,6},{5,7},{3,5},{1,3},{0,1},{10,8},{12,10},{14... | collective-permute-start | bytes 3981320 | tf_op jit(solution)/shard_map/ppermute | solution.py:828
  496.3 35.0 %collective-permute-start.48 = (bf16[2,96,1152]{2,1,0:T(8,128)(2,1)}, bf16[2,96,1152]{2,1,0:T(8,128)(2,1)}, u32[]{:S(2)}, u32[]{:S(2)}) collective-permute-start(bf16[2,96,1152]{2,1,0:T(8,128)(2,1)} %pad_maximum_fusion.27), channel_id=1, source_target_pairs={{0,16},{8,24},{16,0},{24,8},{1,17},{9,25},{17,1},{25,9},{2,18},{10... | collective-permute-start | bytes 1327112 | tf_op jit(solution)/shard_map/ppermute | solution.py:806
  507.9 41.4 %collective-permute-start.51 = (bf16[2,96,1152]{2,1,0:T(8,128)(2,1)S(1)}, bf16[2,96,1152]{2,1,0:T(8,128)(2,1)}, u32[]{:S(2)}, u32[]{:S(2)}) collective-permute-start(bf16[2,96,1152]{2,1,0:T(8,128)(2,1)S(1)} %pad_maximum_fusion.28), channel_id=1, source_target_pairs={{0,16},{8,24},{16,0},{24,8},{1,17},{9,25},{17,1},{25,9},{2,18},{10... | collective-permute-start | bytes 1327112 | tf_op jit(solution)/shard_map/ppermute | solution.py:806
  531.3 35.4 %collective-permute-start.54 = (bf16[1,96,1152]{2,1,0:T(8,128)(2,1)}, bf16[1,96,1152]{2,1,0:T(8,128)(2,1)}, u32[]{:S(2)}, u32[]{:S(2)}) collective-permute-start(bf16[1,96,1152]{2,1,0:T(8,128)(2,1)} %get-tuple-element.436), channel_id=1, source_target_pairs={{0,16},{8,24},{16,0},{24,8},{1,17},{9,25},{17,1},{25,9},{2,18},{10... | collective-permute-start | bytes 663560 | tf_op jit(solution)/shard_map/ppermute | solution.py:806
  549.3 31.0 %collective-permute-start.67 = (bf16[576,1152]{1,0:T(8,128)(2,1)S(1)}, bf16[576,1152]{1,0:T(8,128)(2,1)}, u32[]{:S(2)}, u32[]{:S(2)}) collective-permute-start(bf16[576,1152]{1,0:T(8,128)(2,1)S(1)} %fusion.1), channel_id=1, source_target_pairs={{0,16},{8,24},{16,0},{24,8},{1,17},{9,25},{17,1},{25,9},{2,18},{10... | collective-permute-start | bytes 3981320 | tf_op jit(solution)/shard_map/ppermute | solution.py:806
  574.9 21.7 %collective-permute-start.55 = (bf16[528,1152]{1,0:T(8,128)(2,1)S(1)}, bf16[528,1152]{1,0:T(8,128)(2,1)}, u32[]{:S(2)}, u32[]{:S(2)}) collective-permute-start(bf16[528,1152]{1,0:T(8,128)(2,1)S(1)} %pad_maximum_fusion.6), channel_id=1, source_target_pairs={{0,8},{8,0},{16,24},{24,16},{1,9},{9,1},{17,25},{25,17},{2,10},{10... | collective-permute-start | bytes 3649544 | tf_op jit(solution)/shard_map/ppermute | solution.py:795
  575.0 50.0 %all-to-all-start.2 = ((bf16[8,104,1152]{2,1,0:T(8,128)(2,1)}), bf16[8,104,1152]{2,1,0:T(8,128)(2,1)}, u32[]{:S(2)}, u32[]{:S(2)}) async-start(bf16[8,104,1152]{2,1,0:T(8,128)(2,1)} %get-tuple-element.422), calls=%async_computation.2 | async-start | bytes 3833856 | tf_op jit(solution)/shard_map/all_to_all | solution.py:1148
  582.0 21.6 %collective-permute-start.68 = (bf16[4,144,1152]{2,1,0:T(8,128)(2,1)S(1)}, bf16[4,144,1152]{2,1,0:T(8,128)(2,1)S(1)}, u32[]{:S(2)}, u32[]{:S(2)}) collective-permute-start(bf16[4,144,1152]{2,1,0:T(8,128)(2,1)S(1)} %bitcast.267), channel_id=1, source_target_pairs={{0,8},{8,0},{16,24},{24,16},{1,9},{9,1},{17,25},{25,17},{2,10},{10... | collective-permute-start | bytes 3981320 | tf_op jit(solution)/shard_map/ppermute | solution.py:795
  627.7 26.7 %all-to-all-start.3 = ((bf16[8,48,1152]{2,1,0:T(8,128)(2,1)}), bf16[8,48,1152]{2,1,0:T(8,128)(2,1)S(1)}, u32[]{:S(2)}, u32[]{:S(2)}) async-start(bf16[8,48,1152]{2,1,0:T(8,128)(2,1)} %pad_maximum_fusion.17), calls=%async_computation.3 | async-start | bytes 1769472 | tf_op jit(solution)/shard_map/all_to_all | solution.py:1148
  (95 other events, 1163.7 us)
